TPU v7x, 32 devices: a whole 2x2x4 slice. The times are simulated.
32 devices in a mesh: dp: 4 (over x, core), fsdp: 8 (over z, y).
Axes of the slice: x: 2, y: 2, z: 4, core: 2. Of those that a mesh axis runs over, the one named last changes fastest.
Arguments:
- tokens: bfloat16 [2, 32, 128, 1024], P(None, ('dp', 'fsdp')), may hold values from -6 to 6
- states: bfloat16 [2, 32, 1024, 1024], P(None, ('dp', 'fsdp')), may hold values from -6 to 6
- cotangent: bfloat16 [2, 32, 128, 1024], P(None, ('dp', 'fsdp')), may hold values from -6 to 6
- seq_len: int32 [2, 32], P(None, ('dp', 'fsdp')), may hold values from 1 to 128, as said below
- enc_len: int32 [2, 32], P(None, ('dp', 'fsdp')), may hold values from 1 to 1024, as said below
- attn_w: float32 [8, 1024, 1024], P(None, 'fsdp'), may hold values from -0.5 to 0.5
- attn_m: float32 [8, 1024, 1024], P(None, 'fsdp'), may hold values from -39.824254 to 39.824254
- attn_v: float32 [8, 1024, 1024], P(None, 'fsdp'), as said below
- fc1_w: float32 [1024, 4096], P('fsdp'), may hold values from -0.1875 to 0.1875
- fc1_m: float32 [1024, 4096], P('fsdp'), may hold values from -39.824254 to 39.824254
- fc1_v: float32 [1024, 4096], P('fsdp'), as said below
- fc2_w: float32 [4096, 1024], P('fsdp'), may hold values from -0.09375 to 0.09375
- fc2_m: float32 [4096, 1024], P('fsdp'), may hold values from -39.824254 to 39.824254
- fc2_v: float32 [4096, 1024], P('fsdp'), as said below
- vec_w: float32 [17, 1024], P(None, 'fsdp'), may hold values from -0.8 to 1.4
- vec_m: float32 [17, 1024], P(None, 'fsdp'), may hold values from -39.824254 to 39.824254
- vec_v: float32 [17, 1024], P(None, 'fsdp'), as said below
Outputs:
- mixed: bfloat16 [2, 32, 128, 1024], P(None, ('dp', 'fsdp'))
- grad_tokens: bfloat16 [2, 32, 128, 1024], P(None, ('dp', 'fsdp'))
- grad_states: bfloat16 [2, 32, 1024, 1024], P(None, ('dp', 'fsdp'))
- stream_rms: float32 [4], replicated
- attn_new: float32 [8, 1024, 1024], P(None, 'fsdp')
- attn_m_new: float32 [8, 1024, 1024], P(None, 'fsdp')
- attn_v_new: float32 [8, 1024, 1024], P(None, 'fsdp')
- fc1_new: float32 [1024, 4096], P('fsdp')
- fc1_m_new: float32 [1024, 4096], P('fsdp')
- fc1_v_new: float32 [1024, 4096], P('fsdp')
- fc2_new: float32 [4096, 1024], P('fsdp')
- fc2_m_new: float32 [4096, 1024], P('fsdp')
- fc2_v_new: float32 [4096, 1024], P('fsdp')
- vec_new: float32 [17, 1024], P(None, 'fsdp')
- vec_m_new: float32 [17, 1024], P(None, 'fsdp')
- vec_v_new: float32 [17, 1024], P(None, 'fsdp')
Inputs may be any that keep to these rules, and one draw needn't show every extreme that they name: `seq_len`: valid tokens rise on the whole from the first sequences to the last, each sequence lying below that rise by a random dip of up to 17; in every draw some sequence has all 128. `enc_len`: in every draw some sequence has all 1024 encoder states valid. `attn_v`: Positive. `fc1_v`: Positive. `fc2_v`: Positive. `vec_v`: Positive.
All inputs are finite; a program needn't handle non-finite values.
Results may differ from a plain program's by a relative error of at most 0.03.
Values may be sent and summed in bfloat16 or wider, within the bound.
No kernel may reach another device: no remote copies, remote signals or barrier semaphores. Data moves between devices by JAX's collectives and lax.ppermute only.
A program may use at most 384 MiB of HBM per device.

v0:
```python
from functools import partial

import jax
import jax.numpy as jnp
from jax import lax
from jax.sharding import PartitionSpec as P

D = 1024
H = 16
DH = 64
STEP = 7


momentum_decay = 0.9
square_decay = 0.999
matrix_rate = 0.08
vector_rate = 0.3
matrix_decay = 0.01
epsilon = 1e-08
norm_epsilon = 1e-05


def layer_norm(stream, gains, biases):
    centred = stream - jnp.mean(stream, axis=-1, keepdims=True)
    spread = jnp.mean(centred * centred, axis=-1, keepdims=True)
    return centred * lax.rsqrt(spread + norm_epsilon) * gains + biases


def gelu_exact(values):
    return jax.nn.gelu(values, approximate=False)


def matmul(left, right):
    return jnp.dot(left, right, preferred_element_type=jnp.float32)


def matmul_back(left, right):
    return jnp.einsum("rf,df->rd", left, right, preferred_element_type=jnp.float32)


def weight_grad(inputs, grads):
    return jnp.einsum("rd,rf->df", inputs, grads, preferred_element_type=jnp.float32)


def row_total(values):
    return jnp.sum(values.astype(jnp.float32), axis=0)


def block_scores(segment, offset, key_heads, key_valid, causal):
    raw_scores = jnp.einsum(
        "qhd,khd->hqk", segment, key_heads, preferred_element_type=jnp.float32
    ) * DH ** (-0.5)
    key_place = jnp.arange(key_heads.shape[0], dtype=jnp.int32)
    allowed = jnp.broadcast_to(key_valid[None, :], (segment.shape[0], key_heads.shape[0]))
    if causal:
        query_place = offset + jnp.arange(segment.shape[0], dtype=jnp.int32)
        allowed = allowed & (key_place[None, :] <= query_place[:, None])
    return (jnp.where(allowed[None], raw_scores, -1e30), allowed)


def attend_forward(queries, key_rows, value_rows, key_valid, causal):
    length = queries.shape[0]
    block_size = min(512, length)
    query_blocks = queries.reshape(length // block_size, block_size, H, DH)
    offsets = jnp.arange(length // block_size, dtype=jnp.int32) * block_size
    key_heads = key_rows.reshape(-1, H, DH)
    value_heads = value_rows.reshape(-1, H, DH)

    def one_block(block_pair):
        segment, offset = block_pair
        scores, allowed = block_scores(segment, offset, key_heads, key_valid, causal)
        row_peak = jnp.max(scores, axis=-1, keepdims=True)
        exponent = jnp.exp(scores - row_peak)
        totals = jnp.sum(exponent, axis=-1, keepdims=True)
        softmax_w = (exponent / totals).astype(jnp.bfloat16)
        context = jnp.einsum(
            "hqk,khd->qhd", softmax_w, value_heads, preferred_element_type=jnp.float32
        )
        return (context, (row_peak + jnp.log(totals))[..., 0])

    context, log_total = lax.map(one_block, (query_blocks, offsets))
    return (context.reshape(length, H * DH), log_total)


def attend_backward(queries, key_rows, value_rows, key_valid, log_total, grad_ctx, causal):
    length = queries.shape[0]
    block_size = min(512, length)
    query_blocks = queries.reshape(length // block_size, block_size, H, DH)
    grad_blocks = grad_ctx.reshape(length // block_size, block_size, H, DH)
    offsets = jnp.arange(length // block_size, dtype=jnp.int32) * block_size
    key_heads = key_rows.reshape(-1, H, DH)
    value_heads = value_rows.reshape(-1, H, DH)

    def one_block(carry_in, block_in):
        grad_keys, grad_values = carry_in
        segment, offset, block_lse, grad_seg = block_in
        scores, allowed = block_scores(segment, offset, key_heads, key_valid, causal)
        softmax_w = jnp.where(allowed[None], jnp.exp(scores - block_lse[..., None]), 0.0)
        grad_probs = jnp.einsum(
            "qhd,khd->hqk", grad_seg, value_heads, preferred_element_type=jnp.float32
        )
        row_dot = jnp.sum(softmax_w * grad_probs, axis=-1, keepdims=True)
        grad_scores = (softmax_w * (grad_probs - row_dot)).astype(jnp.bfloat16)
        grad_query = jnp.einsum(
            "hqk,khd->qhd", grad_scores, key_heads, preferred_element_type=jnp.float32
        ) * DH ** (-0.5)
        grad_keys = grad_keys + jnp.einsum(
            "hqk,qhd->khd", grad_scores, segment, preferred_element_type=jnp.float32
        ) * DH ** (-0.5)
        grad_values = grad_values + jnp.einsum(
            "hqk,qhd->khd",
            softmax_w.astype(jnp.bfloat16),
            grad_seg,
            preferred_element_type=jnp.float32,
        )
        return ((grad_keys, grad_values), grad_query)

    empty = jnp.zeros(key_heads.shape, jnp.float32)
    (grad_keys, grad_values), grad_query = lax.scan(
        one_block, (empty, empty), (query_blocks, offsets, log_total, grad_blocks)
    )
    return (
        grad_query.reshape(length, H * DH),
        grad_keys.reshape(-1, H * DH),
        grad_values.reshape(-1, H * DH),
    )


def forward_pass(weights, tokens_mb, states_mb, tok_lens, enc_lens):
    attn, fc_in, fc_out, vectors = weights
    seqs_here, length, width = tokens_mb.shape
    enc_length = states_mb.shape[1]
    token_rows = tokens_mb.reshape(seqs_here * length, width)
    state_rows = states_mb.reshape(seqs_here * enc_length, width)
    vector_f = vectors.astype(jnp.float32)
    fc_bias = vector_f[13:].reshape(-1)
    tok_valid = jnp.arange(length, dtype=jnp.int32)[None, :] < tok_lens[:, None]
    enc_valid = jnp.arange(enc_length, dtype=jnp.int32)[None, :] < enc_lens[:, None]

    def by_seq(rows):
        return rows.reshape(seqs_here, -1, rows.shape[-1])

    queries = (matmul(token_rows, attn[0]) + vector_f[0]).astype(jnp.bfloat16)
    key_rows = matmul(token_rows, attn[1]).astype(jnp.bfloat16)
    value_rows = (matmul(token_rows, attn[2]) + vector_f[1]).astype(jnp.bfloat16)
    context, self_lse = jax.vmap(partial(attend_forward, causal=True))(
        by_seq(queries), by_seq(key_rows), by_seq(value_rows), tok_valid
    )
    context_low = context.reshape(-1, width).astype(jnp.bfloat16)
    self_out = matmul(context_low, attn[3]) + vector_f[2]
    stream_one = token_rows.astype(jnp.float32) + self_out
    normed_one = layer_norm(stream_one, vector_f[7], vector_f[8])
    normed_low = normed_one.astype(jnp.bfloat16)
    cross_q = (matmul(normed_low, attn[4]) + vector_f[3]).astype(jnp.bfloat16)
    cross_k = matmul(state_rows, attn[5]).astype(jnp.bfloat16)
    cross_v = (matmul(state_rows, attn[6]) + vector_f[4]).astype(jnp.bfloat16)
    cross_ctx, cross_lse = jax.vmap(partial(attend_forward, causal=False))(
        by_seq(cross_q), by_seq(cross_k), by_seq(cross_v), enc_valid
    )
    cross_low = cross_ctx.reshape(-1, width).astype(jnp.bfloat16)
    cross_out = matmul(cross_low, attn[7]) + vector_f[5]
    stream_two = normed_one + cross_out
    normed_two = layer_norm(stream_two, vector_f[9], vector_f[10])
    normed_two_low = normed_two.astype(jnp.bfloat16)
    hidden_pre = matmul(normed_two_low, fc_in) + fc_bias
    hidden = gelu_exact(hidden_pre).astype(jnp.bfloat16)
    ffn_out = matmul(hidden, fc_out) + vector_f[6]
    stream_three = normed_two + ffn_out
    result = layer_norm(stream_three, vector_f[11], vector_f[12])
    valid_rows = tok_valid.reshape(-1, 1).astype(jnp.float32)
    sums = jnp.stack(
        [
            jnp.sum(valid_rows * result * result),
            jnp.sum(valid_rows * self_out * self_out),
            jnp.sum(valid_rows * cross_out * cross_out),
            jnp.sum(valid_rows * ffn_out * ffn_out),
        ]
    )
    kept = (
        token_rows,
        state_rows,
        tok_valid,
        enc_valid,
        queries,
        key_rows,
        value_rows,
        self_lse,
        context_low,
        stream_one,
        normed_low,
        cross_q,
        cross_k,
        cross_v,
        cross_lse,
        cross_low,
        stream_two,
        normed_two_low,
        hidden_pre,
        hidden,
        stream_three,
    )
    return (result.astype(jnp.bfloat16).reshape(seqs_here, length, width), sums, kept)


def backward_pass(weights, kept, cotan_mb):
    attn, fc_in, fc_out, vectors = weights
    (
        token_rows,
        state_rows,
        tok_valid,
        enc_valid,
        queries,
        key_rows,
        value_rows,
        self_lse,
        context_low,
        stream_one,
        normed_low,
        cross_q,
        cross_k,
        cross_v,
        cross_lse,
        cross_low,
        stream_two,
        normed_two_low,
        hidden_pre,
        hidden,
        stream_three,
    ) = kept
    seqs_here, length, width = cotan_mb.shape
    vector_f = vectors.astype(jnp.float32)

    def by_seq(rows):
        return rows.reshape(seqs_here, -1, rows.shape[-1])

    def flat(rows):
        return rows.reshape(-1, rows.shape[-1])

    grad_out = cotan_mb.reshape(-1, width).astype(jnp.float32)
    grad_three, grad_g3, grad_b3 = jax.vjp(layer_norm, stream_three, vector_f[11], vector_f[12])[1](
        grad_out
    )
    grad_ffn = grad_three.astype(jnp.bfloat16)
    grad_fc_out = weight_grad(hidden, grad_ffn)
    grad_b_fc2 = row_total(grad_ffn)
    grad_hidden = matmul_back(grad_ffn, fc_out)
    grad_pre = jax.vjp(gelu_exact, hidden_pre)[1](grad_hidden)[0].astype(jnp.bfloat16)
    grad_fc_in = weight_grad(normed_two_low, grad_pre)
    grad_fc_bias = row_total(grad_pre)
    grad_normed_two = grad_three + matmul_back(grad_pre, fc_in)
    grad_two, grad_g2, grad_b2 = jax.vjp(layer_norm, stream_two, vector_f[9], vector_f[10])[1](
        grad_normed_two
    )
    grad_cross = grad_two.astype(jnp.bfloat16)
    grad_w_co = weight_grad(cross_low, grad_cross)
    grad_b_co = row_total(grad_cross)
    grad_cross_ctx = matmul_back(grad_cross, attn[7]).astype(jnp.bfloat16)
    cross_gq, cross_gk, cross_gv = jax.vmap(partial(attend_backward, causal=False))(
        by_seq(cross_q),
        by_seq(cross_k),
        by_seq(cross_v),
        enc_valid,
        cross_lse,
        by_seq(grad_cross_ctx),
    )
    cross_gq = flat(cross_gq).astype(jnp.bfloat16)
    cross_gk = flat(cross_gk).astype(jnp.bfloat16)
    cross_gv = flat(cross_gv).astype(jnp.bfloat16)
    grad_w_cq = weight_grad(normed_low, cross_gq)
    grad_b_cq = row_total(cross_gq)
    grad_w_ck = weight_grad(state_rows, cross_gk)
    grad_w_cv = weight_grad(state_rows, cross_gv)
    grad_b_cv = row_total(cross_gv)
    grad_states = (matmul_back(cross_gk, attn[5]) + matmul_back(cross_gv, attn[6])).astype(
        jnp.bfloat16
    )
    grad_normed_one = grad_two + matmul_back(cross_gq, attn[4])
    grad_one, grad_g1, grad_b1 = jax.vjp(layer_norm, stream_one, vector_f[7], vector_f[8])[1](
        grad_normed_one
    )
    grad_self = grad_one.astype(jnp.bfloat16)
    grad_w_so = weight_grad(context_low, grad_self)
    grad_b_so = row_total(grad_self)
    grad_ctx = matmul_back(grad_self, attn[3]).astype(jnp.bfloat16)
    self_gq, self_gk, self_gv = jax.vmap(partial(attend_backward, causal=True))(
        by_seq(queries), by_seq(key_rows), by_seq(value_rows), tok_valid, self_lse, by_seq(grad_ctx)
    )
    self_gq = flat(self_gq).astype(jnp.bfloat16)
    self_gk = flat(self_gk).astype(jnp.bfloat16)
    self_gv = flat(self_gv).astype(jnp.bfloat16)
    grad_w_sq = weight_grad(token_rows, self_gq)
    grad_b_sq = row_total(self_gq)
    grad_w_sk = weight_grad(token_rows, self_gk)
    grad_w_sv = weight_grad(token_rows, self_gv)
    grad_b_sv = row_total(self_gv)
    grad_tokens = (
        grad_one
        + matmul_back(self_gq, attn[0])
        + matmul_back(self_gk, attn[1])
        + matmul_back(self_gv, attn[2])
    ).astype(jnp.bfloat16)
    grad_attn = jnp.stack(
        [grad_w_sq, grad_w_sk, grad_w_sv, grad_w_so, grad_w_cq, grad_w_ck, grad_w_cv, grad_w_co]
    )
    grad_vec = jnp.concatenate(
        [
            jnp.stack(
                [
                    grad_b_sq,
                    grad_b_sv,
                    grad_b_so,
                    grad_b_cq,
                    grad_b_cv,
                    grad_b_co,
                    grad_b_fc2,
                    grad_g1,
                    grad_b1,
                    grad_g2,
                    grad_b2,
                    grad_g3,
                    grad_b3,
                ]
            ),
            grad_fc_bias.reshape(-1, width),
        ],
        axis=0,
    )
    grads = (grad_attn, grad_fc_in, grad_fc_out, grad_vec)
    return (
        grads,
        grad_tokens.reshape(seqs_here, length, width),
        grad_states.reshape(seqs_here, -1, width),
    )


def adam_update(weight, first, second, grad, rate, decay):
    first = momentum_decay * first + (1.0 - momentum_decay) * grad
    second = square_decay * second + (1.0 - square_decay) * grad * grad
    fix_first = 1.0 - momentum_decay**STEP
    fix_second = 1.0 - square_decay**STEP
    update = first / fix_first / (jnp.sqrt(second / fix_second) + epsilon) + decay * weight
    return (weight - rate * update, first, second)


def on_device(
    tokens,
    states,
    cotangent,
    seq_len,
    enc_len,
    attn_w,
    attn_m,
    attn_v,
    fc1_w,
    fc1_m,
    fc1_v,
    fc2_w,
    fc2_m,
    fc2_v,
    vec_w,
    vec_m,
    vec_v,
):
    micro_count = tokens.shape[0]
    attn_low = attn_w.astype(jnp.bfloat16)
    fc1_low = fc1_w.astype(jnp.bfloat16)
    fc2_low = fc2_w.astype(jnp.bfloat16)
    vec_low = vec_w.astype(jnp.bfloat16)
    grad_acc = None
    results = []
    grad_tok_list = []
    grad_state_list = []
    sums_total = jnp.zeros((4,), jnp.float32)
    for micro_index in range(micro_count):
        fwd_weights = (
            lax.all_gather(attn_low, "fsdp", axis=1, tiled=True),
            lax.all_gather(fc1_low, "fsdp", axis=0, tiled=True),
            lax.all_gather(fc2_low, "fsdp", axis=0, tiled=True),
            lax.all_gather(vec_low, "fsdp", axis=1, tiled=True),
        )
        result, sums, kept = forward_pass(
            fwd_weights,
            tokens[micro_index],
            states[micro_index],
            seq_len[micro_index],
            enc_len[micro_index],
        )
        sums_total = sums_total + sums
        back_weights = (
            lax.all_gather(attn_low, "fsdp", axis=1, tiled=True),
            lax.all_gather(fc1_low, "fsdp", axis=0, tiled=True),
            lax.all_gather(fc2_low, "fsdp", axis=0, tiled=True),
            lax.all_gather(vec_low, "fsdp", axis=1, tiled=True),
        )
        grads, grad_tok, grad_state = backward_pass(back_weights, kept, cotangent[micro_index])
        if grad_acc is None:
            grad_acc = grads
        else:
            grad_acc = jax.tree.map(jnp.add, grad_acc, grads)
        results.append(result)
        grad_tok_list.append(grad_tok)
        grad_state_list.append(grad_state)
    grad_acc = (
        lax.psum_scatter(
            grad_acc[0].astype(jnp.bfloat16), "fsdp", scatter_dimension=1, tiled=True
        ).astype(jnp.float32),
        lax.psum_scatter(
            grad_acc[1].astype(jnp.bfloat16), "fsdp", scatter_dimension=0, tiled=True
        ).astype(jnp.float32),
        lax.psum_scatter(
            grad_acc[2].astype(jnp.bfloat16), "fsdp", scatter_dimension=0, tiled=True
        ).astype(jnp.float32),
        lax.psum_scatter(
            grad_acc[3].astype(jnp.bfloat16), "fsdp", scatter_dimension=1, tiled=True
        ).astype(jnp.float32),
    )
    shard_grads = (
        lax.psum(grad_acc[0].astype(jnp.bfloat16), "dp").astype(jnp.float32),
        lax.psum(grad_acc[1].astype(jnp.bfloat16), "dp").astype(jnp.float32),
        lax.psum(grad_acc[2].astype(jnp.bfloat16), "dp").astype(jnp.float32),
        lax.psum(grad_acc[3].astype(jnp.bfloat16), "dp").astype(jnp.float32),
    )
    local_count = jnp.sum(seq_len).astype(jnp.float32)
    total_sums, total_count = lax.psum((sums_total, local_count), ("dp", "fsdp"))
    stream_rms = jnp.sqrt(total_sums / (total_count * D))
    attn_new, attn_m_new, attn_v_new = adam_update(
        attn_w, attn_m, attn_v, shard_grads[0], matrix_rate, matrix_decay
    )
    fc1_new, fc1_m_new, fc1_v_new = adam_update(
        fc1_w, fc1_m, fc1_v, shard_grads[1], matrix_rate, matrix_decay
    )
    fc2_new, fc2_m_new, fc2_v_new = adam_update(
        fc2_w, fc2_m, fc2_v, shard_grads[2], matrix_rate, matrix_decay
    )
    vec_new, vec_m_new, vec_v_new = adam_update(
        vec_w, vec_m, vec_v, shard_grads[3], vector_rate, 0.0
    )
    return (
        jnp.stack(results),
        jnp.stack(grad_tok_list),
        jnp.stack(grad_state_list),
        stream_rms,
        attn_new,
        attn_m_new,
        attn_v_new,
        fc1_new,
        fc1_m_new,
        fc1_v_new,
        fc2_new,
        fc2_m_new,
        fc2_v_new,
        vec_new,
        vec_m_new,
        vec_v_new,
    )


def solution(mesh):
    in_specs = (
        P(None, ("dp", "fsdp"), None, None),
        P(None, ("dp", "fsdp"), None, None),
        P(None, ("dp", "fsdp"), None, None),
        P(None, ("dp", "fsdp")),
        P(None, ("dp", "fsdp")),
        P(None, "fsdp", None),
        P(None, "fsdp", None),
        P(None, "fsdp", None),
        P("fsdp", None),
        P("fsdp", None),
        P("fsdp", None),
        P("fsdp", None),
        P("fsdp", None),
        P("fsdp", None),
        P(None, "fsdp"),
        P(None, "fsdp"),
        P(None, "fsdp"),
    )
    out_specs = (
        P(None, ("dp", "fsdp"), None, None),
        P(None, ("dp", "fsdp"), None, None),
        P(None, ("dp", "fsdp"), None, None),
        P(),
        P(None, "fsdp", None),
        P(None, "fsdp", None),
        P(None, "fsdp", None),
        P("fsdp", None),
        P("fsdp", None),
        P("fsdp", None),
        P("fsdp", None),
        P("fsdp", None),
        P("fsdp", None),
        P(None, "fsdp"),
        P(None, "fsdp"),
        P(None, "fsdp"),
    )
    return jax.shard_map(
        on_device, mesh=mesh, in_specs=in_specs, out_specs=out_specs, check_vma=False
    )
```

profile of v0, /device:TPU:0, one launch (start us, length us, event | category | flops | bytes accessed | tf_op | source)
XLA Modules:
  0.0 1499.0 jit_solution(11202320513036617973)
XLA Ops:
  7.2 3.8 convert_element_type.540
  20.5 28.6 %all_gather.9 = bf16[17,1024]{1,0:T(8,128)(2,1)S(1)} all-gather(bf16[17,128]{1,0:T(8,128)(2,1)S(1)} %convert_element_type.541), channel_id=1, replica_groups=mesh['dp'=4,'fsdp'=8] {'fsdp'}, dimensions={1}, use_global_device_ids=true | all-gather | bytes 39168 | tf_op jit(solution)/shard_map/all_gather | solution.py:379
  51.3 191.0 %all-gather.4.cloned.1.call-done = bf16[8,1024,1024]{2,1,0:T(8,128)(2,1)} async-done(((bf16[8,128,1024]{2,1,0:T(8,128)(2,1)}), bf16[8,1024,1024]{2,1,0:T(8,128)(2,1)}) %all-gather.4.cloned.1.call-update) | async-done | bytes 16777232 | tf_op jit(solution)/shard_map/all_gather | solution.py:376
  269.6 4.8 fusion.45
  289.8 4.2 fusion.42
  306.3 61.8 %all-gather.6.cloned.1.call-done = bf16[1024,4096]{1,0:T(8,128)(2,1)} async-done(((bf16[128,4096]{1,0:T(8,128)(2,1)}), bf16[1024,4096]{1,0:T(8,128)(2,1)}) %all-gather.6.cloned.1.call-update) | async-done | bytes 8388624 | tf_op jit(solution)/shard_map/all_gather | solution.py:377
  368.1 22.0 %multiply_convert_fusion.5 = (bf16[128,4096]{1,0:T(8,128)(2,1)S(1)}, f32[128,4096]{1,0:T(8,128)}, f32[128,4096]{1,0:T(8,128)}) fusion(f32[4096]{0:T(1024)S(1)} %bitcast.658, bf16[1024,4096]{1,0:T(8,128)(2,1)} %all-gather.6.cloned.1.call-done, f32[128,1024]{1,0:T(8,128)S(1)} %get-tuple-element.346, f32[1024]{0:T(1024)S(1)} %bitcast.620, ...), kind=kOutput, calls=%fused_computation.110 | convolution fusion | flops 1109000192 | bytes 14181376 | tf_op jit(solution)/shard_map/dot_general | solution.py:34
  390.1 8.9 multiply_convert_fusion.4
  399.0 94.9 %all-gather.8.cloned.1.call-done = bf16[4096,1024]{1,0:T(8,128)(2,1)} async-done(((bf16[512,1024]{1,0:T(8,128)(2,1)}), bf16[4096,1024]{1,0:T(8,128)(2,1)}) %all-gather.8.cloned.1.call-update) | async-done | bytes 8388624 | tf_op jit(solution)/shard_map/all_gather | solution.py:378
  494.0 4.8 convolution_add_fusion.5
  506.6 5.8 convert_reduce_fusion.2
  515.4 6.3 convert_reduce_fusion.3
  521.7 4.0 multiply_reduce_fusion.6
  530.9 7.5 multiply_reduce_fusion
  547.3 7.5 multiply_reduce_fusion.1
  589.2 8.4 convert_reduce_fusion
  610.2 4.0 bitcast_dynamic-update-slice_fusion.5
  625.5 4.6 copy-done.3
  635.7 4.7 bitcast_dynamic-update-slice_fusion.1
  640.4 4.3 bitcast_dynamic-update-slice_fusion
  647.4 27.6 %add_convert_fusion = bf16[8,1024,1024]{1,2,0:T(8,128)(2,1)} fusion(f32[8,1024,1024]{1,2,0:T(8,128)} %copy-done.3, f32[8,1024,1024]{1,2,0:T(8,128)} %bitcast_dynamic-update-slice_fusion.10), kind=kLoop, calls=%fused_computation | loop fusion | flops 16777216 | bytes 83886080 | tf_op jit(solution)/shard_map/convert_element_type | solution.py:405
  675.0 23.9 %copy.158 = bf16[8,1024,1024]{2,0,1:T(8,128)(2,1)} copy(bf16[8,1024,1024]{1,2,0:T(8,128)(2,1)} %add_convert_fusion) | data formatting | bytes 33554432
  698.8 18.6 %copy.163 = bf16[128,8,8,1024]{3,1,2,0:T(8,128)(2,1)} copy(bf16[128,8,8,1024]{3,2,1,0:T(8,128)(2,1)} %bitcast.545) | data formatting | bytes 33554432
  718.7 8.7 fusion.232
  727.4 11.5 add_convert_fusion.2
  740.2 8.1 fusion.268
  748.4 11.6 add_convert_fusion.1
  760.1 5.3 copy.140
  766.7 5.5 copy.131
  772.2 5.0 maximum_add_fusion
  777.4 5.5 copy.138
  782.9 41.4 %all-reduce = (f32[4]{0:T(128)S(1)}, f32[]{:T(128)}) all-reduce(f32[4]{0:T(128)S(1)} %maximum_add_fusion, f32[]{:T(128)S(6)} %convert_element_type.664), channel_id=1, replica_groups=mesh['dp'=4,'fsdp'=8] {'dp','fsdp'}, use_global_device_ids=true, to_apply=%region_44.45 | all-reduce | flops 5 | bytes 40 | tf_op jit(solution)/shard_map/psum | solution.py:424
  838.6 6.2 fusion.80
  844.8 6.1 fusion.81
  856.7 142.9 %reduce-scatter.13.cloned.1.call-done = bf16[128,8192]{1,0:T(8,128)(2,1)} async-done(((bf16[1024,8192]{1,0:T(8,128)(2,1)}), bf16[128,8192]{1,0:T(8,128)(2,1)}) %reduce-scatter.13.cloned.1.call-update) | async-done | bytes 2097168
  1005.6 145.9 %reduce-scatter.9.cloned.1.call-done = bf16[128,4096]{1,0:T(8,128)(2,1)} async-done(((bf16[1024,4096]{1,0:T(8,128)(2,1)}), bf16[128,4096]{1,0:T(8,128)(2,1)}) %reduce-scatter.9.cloned.1.call-update) | async-done | bytes 1048592 | tf_op jit(solution)/shard_map/reduce_scatter | solution.py:407
  1151.5 151.5 %reduce-scatter.11.cloned.1.call-done = bf16[512,1024]{1,0:T(8,128)(2,1)} async-done(((bf16[4096,1024]{1,0:T(8,128)(2,1)}), bf16[512,1024]{1,0:T(8,128)(2,1)}) %reduce-scatter.11.cloned.1.call-update) | async-done | bytes 1048592 | tf_op jit(solution)/shard_map/reduce_scatter | solution.py:410
  1304.7 5.3 fusion.19
  1310.0 4.0 fusion.18
  1317.0 49.9 %reduce-scatter.15.cloned.1.call-done = bf16[128,17]{1,0:T(8,128)(2,1)} async-done(((bf16[1024,17]{1,0:T(8,128)(2,1)}), bf16[128,17]{1,0:T(8,128)(2,1)}) %reduce-scatter.15.cloned.1.call-update) | async-done | bytes 4368
  1367.8 5.8 psum.47
  1374.2 80.9 %all-reduce.4.cloned.1.call-done = (bf16[8,128,1024]{1,2,0:T(8,128)(2,1)}, bf16[128,4096]{1,0:T(8,128)(2,1)}, bf16[512,1024]{1,0:T(8,128)(2,1)}) async-done(((bf16[8,128,1024]{1,2,0:T(8,128)(2,1)}, bf16[128,4096]{1,0:T(8,128)(2,1)}, bf16[512,1024]{1,0:T(8,128)(2,1)}), (bf16[8,128,1024]{1,2,0:T(8,128)(2,1)}, bf16[128,4096]{1,0:T(8,128)(2,1)}, bf16[512,1024]{1,0:T(8,128)(2,1)})) %all-reduce.4.cloned.1.call-update) | async-done | bytes 4194320 | tf_op jit(solution)/shard_map/psum | solution.py:418
  1455.1 10.2 multiply_subtract_fusion
  1465.3 5.3 copy.141
  1470.7 5.3 copy.142
  1476.0 5.5 copy.143
  1481.6 6.2 multiply_subtract_fusion.2
  1487.7 3.9 multiply_subtract_fusion.1
  (531 shorter events, 190.8 us)
Async XLA Ops:
  7.2 235.1 %all-gather.4.cloned.1.call-start = ((), (), s32[]{:S(2)}) async-start(), calls=%async_computation.4 | async-start | bytes 18874368 | tf_op jit(solution)/shard_map/all_gather | solution.py:376
  11.1 357.0 %all-gather.6.cloned.1.call-start = ((), (), s32[]{:S(2)}) async-start(), calls=%async_computation.5 | async-start | bytes 9437184 | tf_op jit(solution)/shard_map/all_gather | solution.py:377
  13.8 35.5 %copy-start.142 = (s32[2,1]{0,1:T(1,128)S(1)}, s32[2,1]{0,1:T(1,128)}, u32[]{:S(2)}) copy-start(s32[2,1]{0,1:T(1,128)} %param.21) | copy-start | bytes 28
  13.8 228.5 %copy-start.24 = (bf16[2,1,128,1024]{3,2,1,0:T(8,128)(2,1)S(1)}, bf16[2,1,128,1024]{3,2,1,0:T(8,128)(2,1)}, u32[]{:S(2)}) copy-start(bf16[2,1,128,1024]{3,2,1,0:T(8,128)(2,1)} %param.17) | copy-start | bytes 1572868
  13.8 480.2 %all-gather.8.cloned.1.call-start = ((), (), s32[]{:S(2)}) async-start(), calls=%async_computation.6 | async-start | bytes 9437184 | tf_op jit(solution)/shard_map/all_gather | solution.py:378
  16.7 982.9 %reduce-scatter.13.cloned.1.call-start = ((), (), s32[]{:S(2)}) async-start(), calls=%async_computation.9 | async-start | bytes 18874368
  49.1 449.6 %copy-start.112 = (f32[1,1024]{1,0:T(1,128)}, f32[1,1024]{1,0:T(1,128)S(1)}, u32[]{:S(2)}) copy-start(f32[1,1024]{1,0:T(1,128)S(1)} %get-tuple-element.368) | copy-start | bytes 12292
  49.2 207.2 %copy-start.110 = (pred[128,128]{0,1:T(8,128)(4,1)}, pred[128,128]{0,1:T(8,128)(4,1)S(1)}, u32[]{:S(2)}) copy-start(pred[128,128]{0,1:T(8,128)(4,1)S(1)} %fusion.204) | copy-start | bytes 49156
  49.4 208.5 %copy-start.108 = (pred[128,128]{0,1:T(8,128)(4,1)}, pred[128,128]{0,1:T(8,128)(4,1)S(1)}, u32[]{:S(2)}) copy-start(pred[128,128]{0,1:T(8,128)(4,1)S(1)} %fusion.205) | copy-start | bytes 49156
  244.5 12.6 copy-start.105
  267.1 298.3 %copy-start.135 = (f32[128]{0:T(128)}, f32[128]{0:T(128)S(1)}, u32[]{:S(2)}) copy-start(f32[128]{0:T(128)S(1)} %fusion.208) | copy-start | bytes 1540
  269.5 24.5 %copy-start.44 = (bf16[128,1024]{0,1:T(8,128)(2,1)}, bf16[128,1024]{0,1:T(8,128)(2,1)S(1)}, u32[]{:S(2)}) copy-start(bf16[128,1024]{0,1:T(8,128)(2,1)S(1)} %copy.115) | copy-start | bytes 786436
  289.8 14.7 copy-start.30
  368.1 22.0 %copy-start.8 = (bf16[1024,4096]{1,0:T(8,128)(2,1)S(1)}, bf16[1024,4096]{1,0:T(8,128)(2,1)}, u32[]{:S(2)}) copy-start(bf16[1024,4096]{1,0:T(8,128)(2,1)} %all-gather.6.cloned.1.call-done) | copy-start | bytes 25165828
  390.1 103.9 %copy-start.20 = (bf16[128,4096]{1,0:T(8,128)(2,1)}, bf16[128,4096]{1,0:T(8,128)(2,1)S(1)}, u32[]{:S(2)}) copy-start(bf16[128,4096]{1,0:T(8,128)(2,1)S(1)} %get-tuple-element.343) | copy-start | bytes 3145732
  543.2 16.3 %copy-start.42 = (bf16[16,64,128]{2,1,0:T(8,128)(2,1)}, bf16[16,64,128]{2,1,0:T(8,128)(2,1)S(1)}, u32[]{:S(2)}) copy-start(bf16[16,64,128]{2,1,0:T(8,128)(2,1)S(1)} %get-tuple-element.430) | copy-start | bytes 786436
  584.2 19.5 %copy-start.86 = (bf16[16,64,128]{2,1,0:T(8,128)(2,1)}, bf16[16,64,128]{2,1,0:T(8,128)(2,1)S(1)}, u32[]{:S(2)}) copy-start(bf16[16,64,128]{2,1,0:T(8,128)(2,1)S(1)} %get-tuple-element.420) | copy-start | bytes 786436
  586.7 15.5 %copy-start.50 = (bf16[16,64,128]{2,1,0:T(8,128)(2,1)}, bf16[16,64,128]{2,1,0:T(8,128)(2,1)S(1)}, u32[]{:S(2)}) copy-start(bf16[16,64,128]{2,1,0:T(8,128)(2,1)S(1)} %get-tuple-element.418) | copy-start | bytes 786436
  588.2 14.8 copy-start.40
  589.2 46.5 %copy-start.60 = (bf16[16,64,1024]{2,1,0:T(8,128)(2,1)}, bf16[16,64,1024]{2,1,0:T(8,128)(2,1)S(1)}, u32[]{:S(2)}) copy-start(bf16[16,64,1024]{2,1,0:T(8,128)(2,1)S(1)} %multiply_convert_fusion.2) | copy-start | bytes 6291460
  615.0 15.1 %copy-start.3 = (f32[8,1024,1024]{1,2,0:T(8,128)}, f32[8,1024,1024]{1,2,0:T(8,128)S(1)}, u32[]{:S(2)}) copy-start(f32[8,1024,1024]{1,2,0:T(8,128)S(1)} %bitcast_dynamic-update-slice_fusion.13) | copy-start | bytes 100663296
  717.5 434.0 %reduce-scatter.9.cloned.1.call-start = ((), (), s32[]{:S(2)}) async-start(), calls=%async_computation.7 | async-start | bytes 9437184 | tf_op jit(solution)/shard_map/reduce_scatter | solution.py:407
  739.0 564.1 %reduce-scatter.11.cloned.1.call-start = ((), (), s32[]{:S(2)}) async-start(), calls=%async_computation.8 | async-start | bytes 9437184 | tf_op jit(solution)/shard_map/reduce_scatter | solution.py:410
  760.0 606.9 %reduce-scatter.15.cloned.1.call-start = ((), (), s32[]{:S(2)}) async-start(), calls=%async_computation.10 | async-start | bytes 294912
  777.3 47.4 %copy-start.130 = (f32[4096]{0:T(1024)S(1)}, f32[4096]{0:T(1024)}, u32[]{:S(2)}) copy-start(f32[4096]{0:T(1024)} %get-tuple-element.312) | copy-start | bytes 49156
  777.3 47.6 %copy-start.120 = (f32[16,64]{1,0:T(8,128)S(1)}, f32[16,64]{1,0:T(8,128)}, u32[]{:S(2)}) copy-start(f32[16,64]{1,0:T(8,128)} %get-tuple-element.429) | copy-start | bytes 12292
  777.3 47.8 %copy-start.129 = (f32[4096]{0:T(1024)S(1)}, f32[4096]{0:T(1024)}, u32[]{:S(2)}) copy-start(f32[4096]{0:T(1024)} %get-tuple-element.304) | copy-start | bytes 49156
  777.3 47.8 %copy-start.123 = (f32[1024]{0:T(1024)S(1)}, f32[1024]{0:T(1024)}, u32[]{:S(2)}) copy-start(f32[1024]{0:T(1024)} %get-tuple-element.276) | copy-start | bytes 12292
  777.3 47.8 %copy-start.124 = (f32[1024]{0:T(1024)S(1)}, f32[1024]{0:T(1024)}, u32[]{:S(2)}) copy-start(f32[1024]{0:T(1024)} %get-tuple-element.289) | copy-start | bytes 12292
  777.3 47.8 %copy-start.126 = (f32[1024]{0:T(1024)S(1)}, f32[1024]{0:T(1024)}, u32[]{:S(2)}) copy-start(f32[1024]{0:T(1024)} %get-tuple-element.314) | copy-start | bytes 12292
  777.3 47.8 %copy-start.128 = (f32[1024]{0:T(1024)S(1)}, f32[1024]{0:T(1024)}, u32[]{:S(2)}) copy-start(f32[1024]{0:T(1024)} %get-tuple-element.316) | copy-start | bytes 12292
  777.3 47.8 %copy-start.132 = (f32[1024]{0:T(1024)S(1)}, f32[1024]{0:T(1024)}, u32[]{:S(2)}) copy-start(f32[1024]{0:T(1024)} %get-tuple-element.284) | copy-start | bytes 12292
  777.3 47.8 %copy-start.139 = (f32[1024]{0:T(1024)S(1)}, f32[1024]{0:T(1024)}, u32[]{:S(2)}) copy-start(f32[1024]{0:T(1024)} %get-tuple-element.278) | copy-start | bytes 12292
  777.3 47.8 %copy-start.140 = (f32[1024]{0:T(1024)S(1)}, f32[1024]{0:T(1024)}, u32[]{:S(2)}) copy-start(f32[1024]{0:T(1024)} %get-tuple-element.290) | copy-start | bytes 12292
  777.3 48.0 %copy-start.121 = (f32[1024]{0:T(1024)S(1)}, f32[1024]{0:T(1024)}, u32[]{:S(2)}) copy-start(f32[1024]{0:T(1024)} %get-tuple-element.388) | copy-start | bytes 12292
  777.4 48.0 %copy-start.122 = (f32[1024]{0:T(1024)S(1)}, f32[1024]{0:T(1024)}, u32[]{:S(2)}) copy-start(f32[1024]{0:T(1024)} %get-tuple-element.390) | copy-start | bytes 12292
  777.4 48.0 %copy-start.125 = (f32[1024]{0:T(1024)S(1)}, f32[1024]{0:T(1024)}, u32[]{:S(2)}) copy-start(f32[1024]{0:T(1024)} %get-tuple-element.306) | copy-start | bytes 12292
  777.4 48.0 %copy-start.127 = (f32[1024]{0:T(1024)S(1)}, f32[1024]{0:T(1024)}, u32[]{:S(2)}) copy-start(f32[1024]{0:T(1024)} %get-tuple-element.308) | copy-start | bytes 12292
  777.4 48.0 %copy-start.131 = (f32[1024]{0:T(1024)S(1)}, f32[1024]{0:T(1024)}, u32[]{:S(2)}) copy-start(f32[1024]{0:T(1024)} %get-tuple-element.258) | copy-start | bytes 12292
  777.4 48.0 %copy-start.137 = (f32[1024]{0:T(1024)S(1)}, f32[1024]{0:T(1024)}, u32[]{:S(2)}) copy-start(f32[1024]{0:T(1024)} %get-tuple-element.383) | copy-start | bytes 12292
  777.4 48.0 %copy-start.138 = (f32[1024]{0:T(1024)S(1)}, f32[1024]{0:T(1024)}, u32[]{:S(2)}) copy-start(f32[1024]{0:T(1024)} %get-tuple-element.385) | copy-start | bytes 12292
  777.4 49.8 %copy-start.90 = (bf16[1,1,128,1024]{3,2,1,0:T(8,128)(2,1)S(1)}, bf16[1,1,128,1024]{3,2,1,0:T(8,128)(2,1)}, u32[]{:S(2)}) copy-start(bf16[1,1,128,1024]{3,2,1,0:T(8,128)(2,1)} %get-tuple-element.357) | copy-start | bytes 786436
  777.4 49.8 %copy-start.91 = (bf16[1,1,128,1024]{3,2,1,0:T(8,128)(2,1)S(1)}, bf16[1,1,128,1024]{3,2,1,0:T(8,128)(2,1)}, u32[]{:S(2)}) copy-start(bf16[1,1,128,1024]{3,2,1,0:T(8,128)(2,1)} %get-tuple-element.358) | copy-start | bytes 786436
  782.9 45.4 %copy-start.85 = (bf16[16,64,128]{2,1,0:T(8,128)(2,1)S(1)}, bf16[16,64,128]{2,1,0:T(8,128)(2,1)}, u32[]{:S(2)}) copy-start(bf16[16,64,128]{2,1,0:T(8,128)(2,1)} %get-tuple-element.428) | copy-start | bytes 786436
  828.1 627.0 %all-reduce.4.cloned.1.call-start = ((), (), s32[]{:S(2)}) async-start(), calls=%async_computation.11 | async-start | bytes 8388608 | tf_op jit(solution)/shard_map/psum | solution.py:418
  1314.1 59.5 %copy-start.117 = (f32[17,128]{1,0:T(8,128)S(1)}, f32[17,128]{1,0:T(8,128)}, u32[]{:S(2)}) copy-start(f32[17,128]{1,0:T(8,128)} %param.31) | copy-start | bytes 26116
  1314.1 59.5 %copy-start.133 = (f32[17,128]{1,0:T(8,128)S(1)}, f32[17,128]{1,0:T(8,128)}, u32[]{:S(2)}) copy-start(f32[17,128]{1,0:T(8,128)} %param.32) | copy-start | bytes 26116
  1314.1 59.5 %copy-start.134 = (f32[17,128]{1,0:T(8,128)S(1)}, f32[17,128]{1,0:T(8,128)}, u32[]{:S(2)}) copy-start(f32[17,128]{1,0:T(8,128)} %param.33) | copy-start | bytes 26116
  (133 other events, 551.7 us)
Sparse Core Ops, SparseCore 0:
  11.2 231.0 all-gather.3
  245.0 123.1 all-gather.5
  370.8 123.1 all-gather.7
  717.6 281.9 reduce-scatter.12
  1003.5 148.0 reduce-scatter.8
  1155.0 148.0 reduce-scatter.10
  1306.8 60.1 reduce-scatter.14
  1370.2 84.8 all-reduce.3
where the time goes:
time: 1510 us; the launch traced here: 1500 us
  waiting for transfers between devices  919 us (61%)
  matrix products  277 us (18%)
  local copies, waits for them, and re-layouts  118 us (8%)
  other arithmetic  90.3 us (6%)
  blocking collectives  75.8 us (5%)
  between operations  18.4 us (1%)
    unnamed x10, waiting for transfers between devices  193 us
    all_gather x1, waiting for transfers between devices, on_device(): lax.all_gather(attn_low, 'fsdp', axis=1, tiled=True)  191 us
    reduce_scatter x1, waiting for transfers between devices, on_device(): lax.psum_scatter(grad_acc[2].astype(jnp.bfloat16), 'fsdp', scatter_dimens...  152 us
    reduce_scatter x1, waiting for transfers between devices, on_device(): lax.psum_scatter(grad_acc[1].astype(jnp.bfloat16), 'fsdp', scatter_dimens...  146 us
    unnamed x360, local copies, waits for them, and re-layouts  111 us
    all_gather x1, waiting for transfers between devices, on_device(): lax.all_gather(fc2_low, 'fsdp', axis=0, tiled=True)  94.9 us
    psum x1, waiting for transfers between devices, on_device(): lax.psum(grad_acc[0].astype(jnp.bfloat16), 'dp').astype(jnp.float32)  80.9 us
    dot_general x20, matrix products, weight_grad(): jnp.einsum('rd,rf->df', inputs, grads, preferred_element_type=jnp.float32)  78.2 us
  transfers between devices with their start and end apart: 8, of which 8 were waited for; matrix products, arithmetic and copies ran while one was open for 14% of the time, Pallas kernels for 0%

commit v1 on v0

v1 whole, which is shorter than its diff:
```python
from functools import partial

import jax
import jax.numpy as jnp
from jax import lax
from jax.experimental import pallas as pl
from jax.experimental.pallas import tpu as pltpu
from jax.sharding import PartitionSpec as P

D = 1024
H = 16
DH = 64
STEP = 7
PAIRS = H // 2
UNITS = 4

momentum_decay = 0.9
square_decay = 0.999
matrix_rate = 0.08
vector_rate = 0.3
matrix_decay = 0.01
epsilon = 1e-08
norm_epsilon = 1e-05
fix_first = 1.0 - momentum_decay**STEP
fix_second = 1.0 - square_decay**STEP

f32 = jnp.float32
bf16 = jnp.bfloat16
ANY = pl.BlockSpec(memory_space=pl.ANY)
VMEM_BYTES = 40 * 1024 * 1024
CROSS_ORDER = (4, 7, 5, 6)


def params(**more):
    return pltpu.CompilerParams(vmem_limit_bytes=VMEM_BYTES, **more)


def cost(flops, nbytes, exps=0):
    return pl.CostEstimate(flops=int(flops), bytes_accessed=int(nbytes), transcendentals=int(exps))


def dot(left, right):
    return jnp.dot(left, right, preferred_element_type=f32)


def dot_back(left, right):
    return lax.dot_general(left, right, (((1,), (1,)), ((), ())), preferred_element_type=f32)


def dot_grad(inputs, grads):
    return lax.dot_general(inputs, grads, (((0,), (0,)), ((), ())), preferred_element_type=f32)


def two_heads(rows):
    low_half = lax.broadcasted_iota(jnp.int32, rows.shape, 1) < DH
    zero = jnp.zeros_like(rows)
    return jnp.concatenate([jnp.where(low_half, rows, zero), jnp.where(low_half, zero, rows)], axis=0)


def one_row(both):
    half = both.shape[0] // 2
    low_half = lax.broadcasted_iota(jnp.int32, (half, both.shape[1]), 1) < DH
    return jnp.where(low_half, both[:half], both[half:])


def masked_exp(queries, keys, valid, causal):
    scores = dot_back(queries, keys)
    place = lax.broadcasted_iota(jnp.int32, (1, scores.shape[1]), 1)
    if causal:
        rows = scores.shape[0] // 2
        spot = lax.broadcasted_iota(jnp.int32, scores.shape, 0)
        spot = jnp.where(spot >= rows, spot - rows, spot)
        spots = lax.broadcasted_iota(jnp.int32, scores.shape, 1)
        allowed = (spots <= spot) & (spots < valid)
        scores = jnp.where(allowed, scores, -1e30)
    else:
        scores = scores + jnp.where(place < valid, 0.0, -1e30)
    top = jnp.max(scores, axis=-1, keepdims=True)
    exponent = jnp.exp(scores - top)
    return exponent, 1.0 / jnp.sum(exponent, axis=-1, keepdims=True)


def attend_kernel(causal, len_ref, q_ref, k_ref, v_ref, o_ref):
    queries = two_heads(q_ref[...] * DH**-0.5)
    exponent, inverse = masked_exp(queries, k_ref[...], len_ref[pl.program_id(0)], causal)
    o_ref[...] = one_row(dot(exponent.astype(bf16), v_ref[...]) * inverse).astype(bf16)


def attend_back_kernel(causal, len_ref, q_ref, k_ref, v_ref, do_ref, dq_ref, dk_ref, dv_ref):
    queries = two_heads(q_ref[...] * DH**-0.5)
    exponent, inverse = masked_exp(queries, k_ref[...], len_ref[pl.program_id(0)], causal)
    grads = two_heads(do_ref[...])
    grad_probs = dot_back(grads, v_ref[...])
    row_dot = jnp.sum(exponent * grad_probs, axis=-1, keepdims=True) * inverse
    grad_scores = (exponent * (grad_probs - row_dot)).astype(bf16)
    dq_ref[...] = one_row(dot(grad_scores, k_ref[...]) * (inverse * DH**-0.5)).astype(bf16)
    dk_ref[...] = dot_grad(grad_scores, (queries * inverse).astype(bf16)).astype(bf16)
    dv_ref[...] = dot_grad(exponent.astype(bf16), (grads * inverse).astype(bf16)).astype(bf16)


def attend(lengths, queries, keys, values, seqs, causal, q_at, k_at, v_at):
    q_rows, k_rows = queries.shape[0] // seqs, keys.shape[0] // seqs

    def block(rows, at):
        return pl.BlockSpec((rows, 2 * DH), lambda m, p, n: (m, at + p))

    return pl.pallas_call(
        partial(attend_kernel, causal),
        out_shape=jax.ShapeDtypeStruct((seqs * q_rows, D), bf16),
        grid_spec=pltpu.PrefetchScalarGridSpec(
            num_scalar_prefetch=1,
            grid=(seqs, PAIRS),
            in_specs=[block(q_rows, q_at), block(k_rows, k_at), block(k_rows, v_at)],
            out_specs=block(q_rows, 0),
        ),
        compiler_params=params(),
        cost_estimate=cost(8 * seqs * q_rows * k_rows * D, 4 * seqs * (q_rows + k_rows) * D, seqs * H * q_rows * k_rows),
    )(lengths, queries, keys, values)


def attend_back(lengths, queries, keys, values, grads, seqs, causal, q_at, k_at, v_at):
    q_rows, k_rows = queries.shape[0] // seqs, keys.shape[0] // seqs

    def block(rows, at):
        return pl.BlockSpec((rows, 2 * DH), lambda m, p, n: (m, at + p))

    return pl.pallas_call(
        partial(attend_back_kernel, causal),
        out_shape=[
            jax.ShapeDtypeStruct((seqs * q_rows, D), bf16),
            jax.ShapeDtypeStruct((seqs * k_rows, D), bf16),
            jax.ShapeDtypeStruct((seqs * k_rows, D), bf16),
        ],
        grid_spec=pltpu.PrefetchScalarGridSpec(
            num_scalar_prefetch=1,
            grid=(seqs, PAIRS),
            in_specs=[block(q_rows, q_at), block(k_rows, k_at), block(k_rows, v_at), block(q_rows, 0)],
            out_specs=[block(q_rows, 0), block(k_rows, 0), block(k_rows, 0)],
        ),
        compiler_params=params(),
        cost_estimate=cost(20 * seqs * q_rows * k_rows * D, 8 * seqs * (q_rows + k_rows) * D, seqs * H * q_rows * k_rows),
    )(lengths, queries, keys, values, grads)


def place_kernel(count, rows, idx_ref, *refs):
    pieces, out_ref, sems = refs[:count], refs[count], refs[count + 1]
    copies = [
        pltpu.make_async_copy(
            piece, out_ref.at[pl.ds(pl.multiple_of(idx_ref[i] * rows, rows), rows), :], sems.at[i]
        )
        for i, piece in enumerate(pieces)
    ]
    for copy in copies:
        copy.start()
    for copy in copies:
        copy.wait()


def place(pieces, slots):
    count, (rows, width) = len(pieces), pieces[0].shape
    return pl.pallas_call(
        partial(place_kernel, count, rows),
        out_shape=jax.ShapeDtypeStruct((count * rows, width), pieces[0].dtype),
        grid_spec=pltpu.PrefetchScalarGridSpec(
            num_scalar_prefetch=1,
            grid=(),
            in_specs=[ANY] * count,
            out_specs=ANY,
            scratch_shapes=[pltpu.SemaphoreType.DMA((count,))],
        ),
        compiler_params=params(),
        cost_estimate=cost(0, 4 * count * rows * width),
    )(jnp.stack(slots).astype(jnp.int32), *pieces)


def assemble_kernel(wide, depth, rows, idx_ref, *refs):
    pieces, out_ref, sems = refs[:8], refs[8], refs[9]
    copies = []
    for i, piece in enumerate(pieces):
        unit, plane = idx_ref[2 * i], idx_ref[2 * i + 1]
        for z in range(depth):
            if wide:
                row = (2 * z + plane) * rows
                target = out_ref.at[
                    pl.ds(pl.multiple_of(row, rows), rows), pl.ds(pl.multiple_of(unit * D, D), D)
                ]
            else:
                row = ((2 * z + plane) * UNITS + unit) * rows
                target = out_ref.at[pl.ds(pl.multiple_of(row, rows), rows), :]
            copies.append(
                pltpu.make_async_copy(piece.at[pl.ds(z * rows, rows), :], target, sems.at[i * depth + z])
            )
    for copy in copies:
        copy.start()
    for copy in copies:
        copy.wait()


def assemble(pieces, places, depth, wide):
    total, width = pieces[0].shape
    rows = total // depth
    shape = (2 * total, UNITS * D) if wide else (2 * UNITS * total, D)
    return pl.pallas_call(
        partial(assemble_kernel, wide, depth, rows),
        out_shape=jax.ShapeDtypeStruct(shape, bf16),
        grid_spec=pltpu.PrefetchScalarGridSpec(
            num_scalar_prefetch=1,
            grid=(),
            in_specs=[ANY] * 8,
            out_specs=ANY,
            scratch_shapes=[pltpu.SemaphoreType.DMA((8 * depth,))],
        ),
        compiler_params=params(),
        cost_estimate=cost(0, 32 * total * width),
    )(jnp.stack([i for pair in places for i in pair]).astype(jnp.int32), *pieces)


def grad_kernel(idx_ref, xm_ref, xr_ref, ym_ref, yr_ref, out_ref):
    out_ref[...] = (dot_grad(xm_ref[...], ym_ref[...]) + dot_grad(xr_ref[...], yr_ref[...])).astype(bf16)


def plane_grad(x_mine, x_peer, y_mine, y_peer, x_at, y_at, stride, depth, rows):
    tokens = x_mine.shape[0]
    x_spec = pl.BlockSpec((tokens, rows), lambda z, i: (0, i[0] + stride * z))
    y_spec = pl.BlockSpec((tokens, D), lambda z, i: (0, i[1]))
    return pl.pallas_call(
        grad_kernel,
        out_shape=jax.ShapeDtypeStruct((depth * rows, D), bf16),
        grid_spec=pltpu.PrefetchScalarGridSpec(
            num_scalar_prefetch=1,
            grid=(depth,),
            in_specs=[x_spec, x_spec, y_spec, y_spec],
            out_specs=pl.BlockSpec((rows, D), lambda z, i: (z, 0)),
        ),
        compiler_params=params(),
        cost_estimate=cost(4 * tokens * depth * rows * D, 2 * depth * rows * D + 8 * tokens * D),
    )(jnp.stack([x_at, y_at]).astype(jnp.int32), x_mine, x_peer, y_mine, y_peer)


def adam_update(weight, first, second, grad, rate, decay):
    first = momentum_decay * first + (1.0 - momentum_decay) * grad
    second = square_decay * second + (1.0 - square_decay) * grad * grad
    update = first / fix_first / (jnp.sqrt(second / fix_second) + epsilon) + decay * weight
    return (weight - rate * update, first, second)


def adam_kernel(idx_ref, g0_ref, g1_ref, g2_ref, g3_ref, w_ref, m_ref, v_ref, *rest):
    w_out, m_out, v_out = rest[-3:]
    away = pl.program_id(0) ^ idx_ref[0]
    grad = jnp.where(
        away < 2,
        jnp.where(away == 0, g0_ref[...], g1_ref[...]),
        jnp.where(away == 2, g2_ref[...], g3_ref[...]),
    ).astype(f32)
    if len(w_ref.shape) == 3:
        grad = grad[None]
    w_out[...], m_out[...], v_out[...] = adam_update(
        w_ref[...], m_ref[...], v_ref[...], grad, matrix_rate, matrix_decay
    )


def adam_units(spot, grads, state, block_shape, at, earlier=None):
    spec = pl.BlockSpec(block_shape, lambda u, i: at(u))
    g_spec = pl.BlockSpec(grads[0].shape, lambda u, i: (0, 0))
    extra = list(earlier) if earlier is not None else []
    return pl.pallas_call(
        adam_kernel,
        out_shape=[jax.ShapeDtypeStruct(a.shape, f32) for a in state],
        grid_spec=pltpu.PrefetchScalarGridSpec(
            num_scalar_prefetch=1,
            grid=(UNITS,),
            in_specs=[g_spec] * 4 + [spec] * 3 + [ANY] * len(extra),
            out_specs=[spec] * 3,
        ),
        input_output_aliases={8 + i: i for i in range(len(extra))},
        compiler_params=params(),
        cost_estimate=cost(20 * UNITS * grads[0].size, 26 * UNITS * grads[0].size),
    )(jnp.stack([spot]).astype(jnp.int32), *grads, *state, *extra)


class Links:
    def __init__(self, n_dp, n_fsdp):
        self.n_fsdp, self.depth = n_fsdp, n_fsdp // 2
        spot = lax.axis_index("dp")
        shard = lax.axis_index("fsdp")
        self.spot, self.shard = spot, shard
        self.x, self.core = spot // 2, spot % 2
        self.z, self.y = shard // 2, shard % 2
        ids = [
            (x, c, z, y) for x in range(2) for c in range(2) for z in range(self.depth) for y in range(2)
        ]

        def number(x, c, z, y):
            return ((x * 2 + c) * self.depth + z) * 2 + y

        def perm(to):
            return [(number(*i), number(*to(*i))) for i in ids]

        flip_x = lambda x, c, z, y: (1 - x, c, z, y)
        flip_y = lambda x, c, z, y: (x, c, z, 1 - y)
        self.to_core = perm(lambda x, c, z, y: (x, 1 - c, z, y))
        self.to_x = perm(flip_x)
        self.to_y = perm(flip_y)
        self.swap1 = perm(lambda x, c, z, y: flip_y(x, c, z, y) if c == 0 else flip_x(x, c, z, y))
        self.swap2 = perm(lambda x, c, z, y: flip_x(x, c, z, y) if c == 0 else flip_y(x, c, z, y))
        self.shift_z = [
            perm(lambda x, c, z, y, s=s: (x, c, (z + s) % self.depth, y)) for s in range(self.depth)
        ]

    def send(self, block, perm):
        return lax.ppermute(block, ("dp", "fsdp"), perm)

    def along_z(self, block):
        arrived = [block] + [self.send(block, self.shift_z[s]) for s in range(1, self.depth)]
        return place(arrived, [(self.z + self.depth - s) % self.depth for s in range(self.depth)])

    def gather(self, block, wide):
        x, y, c = self.x, self.y, self.core
        own = self.along_z(block)
        near = self.send(own, self.swap1)
        far = self.send(own, self.swap2)
        both = self.send(near, self.swap2)
        here = [own, near, far, both]
        pieces = here + [self.send(piece, self.to_core) for piece in here]
        places = []
        for core in (c, 1 - c):
            for ux, uy in ((x, y), (x ^ core, y ^ (1 - core)), (x ^ (1 - core), y ^ core), (1 - x, 1 - y)):
                places.append((ux * 2 + core, uy))
        return assemble(pieces, places, self.depth, wide)

    def gather_vectors(self, block):
        rows, cols = block.shape
        padded = jnp.pad(block, ((0, -rows % 16), (0, 0)))
        own = self.along_z(padded)
        other = self.send(own, self.to_y)
        pair = jnp.stack([own, other])
        pair = jnp.where(self.y == 0, pair, pair[::-1])
        pair = pair.reshape(2, self.depth, -1, cols)[:, :, :rows]
        return pair.transpose(2, 1, 0, 3).reshape(rows, -1)

    def plane_order(self):
        x, y, c = self.x, self.y, self.core
        return ((x, y), (x ^ (1 - c), y ^ c), (1 - x, 1 - y), (x ^ c, y ^ (1 - c)))

    def reduce(self, planes):
        kept, first, corner, second = planes
        got_first = self.send(first, self.swap2)
        got_corner = self.send(corner, self.swap2)
        second = (second.astype(f32) + got_corner.astype(f32)).astype(bf16)
        got_second = self.send(second, self.swap1)
        kept = (kept.astype(f32) + got_first.astype(f32) + got_second.astype(f32)).astype(bf16)
        rows = kept.shape[0] // self.depth

        def block_of(z):
            return lax.dynamic_slice_in_dim(kept, z * rows, rows, 0)

        total = block_of(self.z).astype(f32)
        for s in range(1, self.depth):
            got = self.send(block_of((self.z + s) % self.depth), self.shift_z[s])
            total = total + got.astype(f32)
        total = total.astype(bf16)
        from_x = self.send(total, self.to_x)
        return [total, self.send(total, self.to_core), from_x, self.send(from_x, self.to_core)]

    def sum_all(self, values):
        for perm in (self.to_core, self.to_x, self.to_y):
            values = values + self.send(values, perm)
        step = 1
        while step < self.depth:
            flip = [
                (a, b)
                for a in range(4 * self.n_fsdp)
                for b in [(a // self.n_fsdp) * self.n_fsdp + ((((a % self.n_fsdp) // 2) ^ step) * 2 + a % 2)]
            ]
            values = values + self.send(values, flip)
            step *= 2
        return values


def norm_forward(stream, gain, bias):
    centred = stream - jnp.mean(stream, axis=-1, keepdims=True)
    spread = jnp.mean(centred * centred, axis=-1, keepdims=True)
    scale = lax.rsqrt(spread + norm_epsilon)
    unit = centred * scale
    return unit * gain + bias, unit, scale


def norm_backward(grad, unit, scale, gain):
    grad_gain = jnp.sum(grad * unit, axis=0)
    grad_bias = jnp.sum(grad, axis=0)
    scaled = grad * gain
    mean = jnp.mean(scaled, axis=-1, keepdims=True)
    along = jnp.mean(scaled * unit, axis=-1, keepdims=True)
    return scale * (scaled - mean - unit * along), grad_gain, grad_bias


def row_total(values):
    return jnp.sum(values.astype(f32), axis=0)


def column_units(shard):
    return [shard[:, u * D : (u + 1) * D] for u in range(UNITS)]


def on_device(
    n_dp,
    n_fsdp,
    tokens,
    states,
    cotangent,
    seq_len,
    enc_len,
    attn_w,
    attn_m,
    attn_v,
    fc1_w,
    fc1_m,
    fc1_v,
    fc2_w,
    fc2_m,
    fc2_v,
    vec_w,
    vec_m,
    vec_v,
):
    micro, local, length, width = tokens.shape
    enc_length = states.shape[2]
    seqs = micro * local
    shard_rows = attn_w.shape[1]
    linked = n_dp == 4 and n_fsdp == 8
    token_rows = tokens.reshape(seqs * length, width)
    state_rows = states.reshape(seqs * enc_length, width)
    cotan_rows = cotangent.reshape(seqs * length, width)
    tok_lens = seq_len.reshape(seqs)
    enc_lens = enc_len.reshape(seqs)

    if linked:
        links = Links(n_dp, n_fsdp)
        spot = links.spot
        vectors = links.gather_vectors(vec_w.astype(bf16))
        part_a = lax.dynamic_index_in_dim(attn_w, spot, 0, keepdims=False).astype(bf16)
        cross_at = 4 + jnp.where(spot < 2, 3 * spot, spot - 1)
        part_b = lax.dynamic_index_in_dim(attn_w, cross_at, 0, keepdims=False).astype(bf16)
        part_1 = lax.dynamic_slice_in_dim(fc1_w, spot * D, D, 1).astype(bf16)
        part_2 = lax.dynamic_slice_in_dim(fc2_w, spot * shard_rows, shard_rows, 0).astype(bf16)
        self_w = links.gather(part_a, True)
        cross_w = links.gather(part_b, True)
        fc_in = links.gather(part_1, True)
        fc_out = links.gather(part_2, False)
    else:
        vectors = lax.all_gather(vec_w.astype(bf16), "fsdp", axis=1, tiled=True)
        attn = lax.all_gather(attn_w.astype(bf16), "fsdp", axis=1, tiled=True)
        self_w = jnp.concatenate([attn[u] for u in range(4)], axis=1)
        cross_w = jnp.concatenate([attn[u] for u in CROSS_ORDER], axis=1)
        fc_in = lax.all_gather(fc1_w.astype(bf16), "fsdp", axis=0, tiled=True)
        fc_out = lax.all_gather(fc2_w.astype(bf16), "fsdp", axis=0, tiled=True)
    vec = vectors.astype(f32)
    fc_bias = vec[13:].reshape(-1)
    zeros = jnp.zeros((width,), f32)

    qkv_bias = jnp.concatenate([vec[0], zeros, vec[1]])
    qkv = (dot(token_rows, self_w[:, : 3 * D]) + qkv_bias).astype(bf16)
    context = attend(tok_lens, qkv, qkv, qkv, seqs, True, 0, PAIRS, 2 * PAIRS)
    self_out = dot(context, self_w[:, 3 * D :]) + vec[2]
    normed_one, unit_one, scale_one = norm_forward(token_rows.astype(f32) + self_out, vec[7], vec[8])
    normed_one_low = normed_one.astype(bf16)
    cross_q = (dot(normed_one_low, cross_w[:, :D]) + vec[3]).astype(bf16)
    kv_bias = jnp.concatenate([zeros, vec[4]])
    cross_kv = (dot(state_rows, cross_w[:, 2 * D :]) + kv_bias).astype(bf16)
    cross_ctx = attend(enc_lens, cross_q, cross_kv, cross_kv, seqs, False, 0, 0, PAIRS)
    cross_out = dot(cross_ctx, cross_w[:, D : 2 * D]) + vec[5]
    normed_two, unit_two, scale_two = norm_forward(normed_one + cross_out, vec[9], vec[10])
    normed_two_low = normed_two.astype(bf16)
    hidden_pre = dot(normed_two_low, fc_in) + fc_bias
    phi = 0.5 * (1.0 + lax.erf(hidden_pre * 2.0**-0.5))
    hidden = (hidden_pre * phi).astype(bf16)
    slope = phi + hidden_pre * jnp.exp(-0.5 * hidden_pre * hidden_pre) * (2.0 * jnp.pi) ** -0.5
    ffn_out = dot(hidden, fc_out) + vec[6]
    result, unit_three, scale_three = norm_forward(normed_two + ffn_out, vec[11], vec[12])
    mixed = result.astype(bf16).reshape(tokens.shape)
    valid = (jnp.arange(length, dtype=jnp.int32)[None, :] < tok_lens[:, None]).reshape(-1, 1)
    sums = [jnp.sum(jnp.where(valid, a * a, 0.0)) for a in (result, self_out, cross_out, ffn_out)]
    count = jnp.sum(seq_len).astype(f32)

    if linked:
        peer = lambda rows: links.send(rows, links.to_core)
        order = links.plane_order()
        self_in = jnp.concatenate([token_rows, context], axis=1)
        cross_in = jnp.concatenate([normed_one_low, cross_ctx], axis=1)
        self_in_peer, cross_in_peer = peer(self_in), peer(cross_in)
        hidden_peer, normed_two_peer = peer(hidden), peer(normed_two_low)
        core = links.core

    grad_three, grad_g3, grad_b3 = norm_backward(cotan_rows.astype(f32), unit_three, scale_three, vec[11])
    grad_ffn = grad_three.astype(bf16)
    if linked:
        grad_ffn_peer = peer(grad_ffn)
        planes = [
            plane_grad(
                hidden, hidden_peer, grad_ffn, grad_ffn_peer,
                y * UNITS + ux * 2 + core, 0 * y, 2 * UNITS, links.depth, shard_rows,
            )
            for ux, y in order
        ]
        blocks_2 = links.reduce(planes)
    else:
        grad_fc2 = dot_grad(hidden, grad_ffn).astype(bf16)
    grad_pre = (dot_back(grad_ffn, fc_out) * slope).astype(bf16)
    if linked:
        grad_pre_peer = peer(grad_pre)
        planes = [
            plane_grad(
                normed_two_low, normed_two_peer, grad_pre, grad_pre_peer,
                y, ux * 2 + core, 2, links.depth, shard_rows,
            )
            for ux, y in order
        ]
        blocks_1 = links.reduce(planes)
    else:
        grad_fc1 = dot_grad(normed_two_low, grad_pre).astype(bf16)
    grad_normed_two = grad_three + dot_back(grad_pre, fc_in)
    grad_two, grad_g2, grad_b2 = norm_backward(grad_normed_two, unit_two, scale_two, vec[9])
    grad_cross = grad_two.astype(bf16)
    grad_ctx = dot_back(grad_cross, cross_w[:, D : 2 * D]).astype(bf16)
    cross_gq, cross_gk, cross_gv = attend_back(
        enc_lens, cross_q, cross_kv, cross_kv, grad_ctx, seqs, False, 0, 0, PAIRS
    )
    if linked:
        cross_grads = jnp.concatenate([cross_gq, grad_cross], axis=1)
        cross_grads_peer = peer(cross_grads)
        grad_ck = dot_grad(state_rows, cross_gk).astype(bf16)
        grad_cv = dot_grad(state_rows, cross_gv).astype(bf16)
        mine = jnp.where(core == 0, grad_ck, grad_cv)
        theirs = peer(jnp.where(core == 0, grad_cv, grad_ck))
        enc_grad = (mine.astype(f32) + theirs.astype(f32)).astype(bf16)
        enc_grad = enc_grad.reshape(links.depth, 2, shard_rows, D)
        enc_planes = [
            lax.dynamic_index_in_dim(enc_grad, y, 1, keepdims=False).reshape(-1, D)
            for y in (links.y, 1 - links.y)
        ]
        tok_planes = [
            plane_grad(
                cross_in, cross_in_peer, cross_grads, cross_grads_peer,
                core * 2 * links.depth + y, core, 2, links.depth, shard_rows,
            )
            for y in (links.y, 1 - links.y)
        ]
        planes = []
        for ux, y in order:
            tok_plane = jnp.where(y == links.y, tok_planes[0], tok_planes[1])
            enc_plane = jnp.where(y == links.y, enc_planes[0], enc_planes[1])
            planes.append(jnp.where(ux == 0, tok_plane, enc_plane))
        blocks_b = links.reduce(planes)
    else:
        grad_b = [
            dot_grad(normed_one_low, cross_gq),
            dot_grad(state_rows, cross_gk),
            dot_grad(state_rows, cross_gv),
            dot_grad(cross_ctx, grad_cross),
        ]
    grad_states = (
        dot_back(cross_gk, cross_w[:, 2 * D : 3 * D]) + dot_back(cross_gv, cross_w[:, 3 * D :])
    ).astype(bf16)
    grad_normed_one = grad_two + dot_back(cross_gq, cross_w[:, :D])
    grad_one, grad_g1, grad_b1 = norm_backward(grad_normed_one, unit_one, scale_one, vec[7])
    grad_self = grad_one.astype(bf16)
    grad_ctx = dot_back(grad_self, self_w[:, 3 * D :]).astype(bf16)
    self_gq, self_gk, self_gv = attend_back(tok_lens, qkv, qkv, qkv, grad_ctx, seqs, True, 0, PAIRS, 2 * PAIRS)
    if linked:
        self_grads = jnp.concatenate([self_gq, self_gk, self_gv, grad_self], axis=1)
        self_grads_peer = peer(self_grads)
        planes = [
            plane_grad(
                self_in, self_in_peer, self_grads, self_grads_peer,
                y + 2 * links.depth * (ux * core), ux * 2 + core, 2, links.depth, shard_rows,
            )
            for ux, y in order
        ]
        blocks_a = links.reduce(planes)
    else:
        grad_a = [
            dot_grad(token_rows, self_gq),
            dot_grad(token_rows, self_gk),
            dot_grad(token_rows, self_gv),
            dot_grad(context, grad_self),
        ]
        grad_attn = jnp.stack(grad_a + grad_b).astype(bf16)
    grad_tokens = (
        grad_one
        + dot_back(self_gq, self_w[:, :D])
        + dot_back(self_gk, self_w[:, D : 2 * D])
        + dot_back(self_gv, self_w[:, 2 * D : 3 * D])
    ).astype(bf16)
    stat_row = jnp.pad(jnp.stack(sums + [count]), (0, width - 5))
    grad_vec = jnp.concatenate(
        [
            jnp.stack(
                [
                    row_total(self_gq),
                    row_total(self_gv),
                    row_total(grad_self),
                    row_total(cross_gq),
                    row_total(cross_gv),
                    row_total(grad_cross),
                    row_total(grad_ffn),
                    grad_g1,
                    grad_b1,
                    grad_g2,
                    grad_b2,
                    grad_g3,
                    grad_b3,
                ]
            ),
            row_total(grad_pre).reshape(-1, width),
            stat_row[None],
        ],
        axis=0,
    )

    if linked:
        grad_vec = links.sum_all(grad_vec)
        fc2_new = adam_units(
            spot, blocks_2, (fc2_w, fc2_m, fc2_v), (shard_rows, D), lambda u: (u, 0)
        )
        fc1_new = adam_units(
            spot, blocks_1, (fc1_w, fc1_m, fc1_v), (shard_rows, D), lambda u: (0, u)
        )
        attn_state = (attn_w, attn_m, attn_v)
        attn_new = adam_units(
            spot, blocks_b, attn_state, (1, shard_rows, D),
            lambda u: (4 + jnp.where(u < 2, 3 * u, u - 1), 0, 0),
        )
        attn_new = adam_units(
            spot, blocks_a, attn_state, (1, shard_rows, D), lambda u: (u, 0, 0), attn_new
        )
    else:
        grad_vec = lax.psum(grad_vec, ("dp", "fsdp"))

        def owned(grad, dim):
            part = lax.psum_scatter(grad, "fsdp", scatter_dimension=dim, tiled=True)
            return lax.psum(part, "dp").astype(f32)

        attn_new = adam_update(attn_w, attn_m, attn_v, owned(grad_attn, 1), matrix_rate, matrix_decay)
        fc1_new = adam_update(fc1_w, fc1_m, fc1_v, owned(grad_fc1, 0), matrix_rate, matrix_decay)
        fc2_new = adam_update(fc2_w, fc2_m, fc2_v, owned(grad_fc2, 0), matrix_rate, matrix_decay)
    stats = grad_vec[17]
    stream_rms = jnp.sqrt(stats[:4] / (stats[4] * D))
    cols = vec_w.shape[1]
    vec_grad = lax.dynamic_slice_in_dim(grad_vec[:17], lax.axis_index("fsdp") * cols, cols, 1)
    vec_new = adam_update(vec_w, vec_m, vec_v, vec_grad, vector_rate, 0.0)
    return (
        mixed,
        grad_tokens.reshape(tokens.shape),
        grad_states.reshape(states.shape),
        stream_rms,
        *attn_new,
        *fc1_new,
        *fc2_new,
        *vec_new,
    )


def solution(mesh):
    rows = P(None, ("dp", "fsdp"), None, None)
    lens = P(None, ("dp", "fsdp"))
    attn, fc, vec = P(None, "fsdp", None), P("fsdp", None), P(None, "fsdp")
    state = (attn,) * 3 + (fc,) * 6 + (vec,) * 3
    return jax.shard_map(
        partial(on_device, mesh.shape["dp"], mesh.shape["fsdp"]),
        mesh=mesh,
        in_specs=(rows, rows, rows, lens, lens) + state,
        out_specs=(rows, rows, rows, P()) + state,
        check_vma=False,
    )
```

time: 1510 us -> 782 us (0.52)
  waiting for transfers between devices: 919 us -> 196 us
  Pallas kernels: 0 us -> 288 us
  matrix products: 277 us -> 102 us
  starting transfers between devices: 0.72 us -> 122 us
  local copies, waits for them, and re-layouts: 118 us -> 31.2 us
  blocking collectives: 75.8 us -> 0 us
  other arithmetic: 90.3 us -> 33.8 us
    all_gather x3 -> x0, waiting for transfers between devices: 348 us -> none  [the longest x1 191 us: on_device(): lax.all_gather(attn_low, 'fsdp', axis=1, tiled=True)]
    reduce_scatter x2 -> x0, waiting for transfers between devices: 297 us -> none  [the longest x1 152 us: on_device(): lax.psum_scatter(grad_acc[2].astype(jnp.bfloat16), 'fsdp', scatter_dimens...]
    pallas_call x0 -> x31, Pallas kernels: none -> 288 us  [the longest x4 171 us: assemble(): pl.pallas_call(partial(assemble_kernel, wide, depth, rows), out_shape=jax...]
    ppermute x0 -> x94, waiting for transfers between devices: none -> 196 us  [send(): return lax.ppermute(block, ('dp', 'fsdp'), perm)]
    unnamed x10 -> x0, waiting for transfers between devices: 193 us -> none
    dot_general x84 -> x19, matrix products: 277 us -> 102 us  [the longest x10 48.2 us: dot_back(): lax.dot_general(left, right, (((1,), (1,)), ((), ())), preferred_element_...]
    ppermute x0 -> x94, starting transfers between devices: none -> 122 us  [send(): return lax.ppermute(block, ('dp', 'fsdp'), perm)]
    unnamed x360 -> x129, local copies, waits for them, and re-layouts: 111 us -> 23.6 us
  transfers between devices with their start and end apart: 8 -> 94, of which waited for: 8 -> 27; matrix products, arithmetic and copies ran while one was open for 14% -> 14% of each run, Pallas kernels for 0% -> 33%
where the time goes in v1:
time: 782 us; the launch traced here: 778 us
  Pallas kernels  288 us (37%)
  waiting for transfers between devices  196 us (25%)
  starting transfers between devices  122 us (16%)
  matrix products  102 us (13%)
  other arithmetic  33.8 us (4%)
  local copies, waits for them, and re-layouts  31.2 us (4%)
    ppermute x94, waiting for transfers between devices, send(): return lax.ppermute(block, ('dp', 'fsdp'), perm)  196 us
    pallas_call x4, Pallas kernels, assemble(): pl.pallas_call(partial(assemble_kernel, wide, depth, rows), out_shape=jax...  171 us
    ppermute x94, starting transfers between devices, send(): return lax.ppermute(block, ('dp', 'fsdp'), perm)  122 us
    dot_general x10, matrix products, dot_back(): lax.dot_general(left, right, (((1,), (1,)), ((), ())), preferred_element_...  48.2 us
    dot_general x7, matrix products, dot(): return jnp.dot(left, right, preferred_element_type=f32)  40.2 us
    pallas_call x14, Pallas kernels, plane_grad(): pl.pallas_call(grad_kernel, out_shape=jax.ShapeDtypeStruct((depth * rows,...  39 us
    pallas_call x2, Pallas kernels, attend_back(): pl.pallas_call(partial(attend_back_kernel, causal), out_shape=[jax.ShapeD...  35.6 us
    unnamed x129, local copies, waits for them, and re-layouts  23.6 us
  transfers between devices with their start and end apart: 94, of which 27 were waited for; matrix products, arithmetic and copies ran while one was open for 14% of the time, Pallas kernels for 33%

profile of v1, /device:TPU:0, one launch (start us, length us, event | category | flops | bytes accessed | tf_op | source)
XLA Modules:
  0.0 777.5 jit_solution(4506411236437946224)
XLA Ops:
  1.9 5.1 collective-permute-start.2
  8.1 5.7 collective-permute-done.2.refs_3_
  13.8 15.6 %collective-permute-done.1.refs_2_ = bf16[128,1024]{1,0:T(8,128)(2,1)S(1)} collective-permute-done((bf16[128,1024]{1,0:T(8,128)(2,1)S(1)}, bf16[128,1024]{1,0:T(8,128)(2,1)S(1)}, u32[]{:S(2)}, u32[]{:S(2)}) %collective-permute-start.1) | collective-permute-done | bytes 262176 | tf_op jit(solution)/shard_map/ppermute | solution.py:311
  42.6 7.5 collective-permute-done.10.refs_1_
  50.8 14.6 %collective-permute-start.35 = (bf16[128,1024]{1,0:T(8,128)(2,1)S(1)}, bf16[128,1024]{1,0:T(8,128)(2,1)S(1)}, u32[]{:S(2)}, u32[]{:S(2)}) collective-permute-start(bf16[128,1024]{1,0:T(8,128)(2,1)S(1)} %dynamic-slice_convert_fusion.refs_0_), channel_id=1, source_target_pairs={{0,4},{1,5},{2,6},{3,7},{4,0},{5,1},{6,2},{7,3},{8,12},{9,13},{10,... | collective-permute-start | bytes 786440 | tf_op jit(solution)/shard_map/ppermute | solution.py:311
  76.3 6.4 collective-permute-done.35.refs_2_
  85.1 6.1 collective-permute-done.26.refs_3_
  91.4 10.5 %collective-permute-done.25.refs_2_ = bf16[128,1024]{1,0:T(8,128)(2,1)} collective-permute-done((bf16[128,1024]{1,0:T(8,128)(2,1)S(1)}, bf16[128,1024]{1,0:T(8,128)(2,1)}, u32[]{:S(2)}, u32[]{:S(2)}) %collective-permute-start.25) | collective-permute-done | bytes 262176 | tf_op jit(solution)/shard_map/ppermute | solution.py:311
  103.6 7.0 collective-permute-done.24.refs_1_
  118.3 7.3 collective-permute-done.18.refs_2_
  127.8 16.8 %collective-permute-done.19.refs_3_ = bf16[512,1024]{1,0:T(8,128)(2,1)S(1)} collective-permute-done((bf16[512,1024]{1,0:T(8,128)(2,1)}, bf16[512,1024]{1,0:T(8,128)(2,1)S(1)}, u32[]{:S(2)}, u32[]{:S(2)}) %collective-permute-start.19) | collective-permute-done | bytes 1048608 | tf_op jit(solution)/shard_map/ppermute | solution.py:311
  145.1 129.0 %shard_map.289 = bf16[1024,4096]{1,0:T(8,128)(2,1)} custom-call(s32[16]{0:T(128)S(1)} %stack.144.idx_ref, bf16[512,1024]{1,0:T(8,128)(2,1)S(1)} %shard_map.288.refs_0_, bf16[512,1024]{1,0:T(8,128)(2,1)} %collective-permute-done.3.refs_1_, bf16[512,1024]{1,0:T(8,128)(2,1)} %collective-permute-done.4.refs_2_, ...), custom_call_target="tpu_custom_call" | custom-call | bytes 16777216 | tf_op jit(solution)/shard_map/pallas_call | solution.py:203
  274.1 4.6 fusion.16.q_ref.k_ref.v_ref
  278.7 7.7 shard_map.291
  287.3 3.6 fusion.99
  299.8 33.7 %shard_map.293 = bf16[1024,4096]{1,0:T(8,128)(2,1)} custom-call(s32[16]{0:T(128)S(1)} %stack.144.idx_ref, bf16[512,1024]{1,0:T(8,128)(2,1)S(1)} %shard_map.292.refs_0_, bf16[512,1024]{1,0:T(8,128)(2,1)} %collective-permute-done.17.refs_1_, bf16[512,1024]{1,0:T(8,128)(2,1)S(1)} %collective-permute-done.18.refs_2_, ...), custom_call_target="tpu_custom_call" | custom-call | bytes 16777216 | tf_op jit(solution)/shard_map/pallas_call | solution.py:203
  333.5 12.0 %fusion.k_ref.v_ref = bf16[2048,2048]{1,0:T(8,128)(2,1)S(1)} fusion(f32[2048]{0:T(1024)S(1)} %concatenate.22, bf16[2048,1024]{1,0:T(8,128)(2,1)} %bitcast.225, bf16[1024,4096]{1,0:T(8,128)(2,1)} %shard_map.293), kind=kOutput, calls=%fused_computation.1 | convolution fusion | flops 8598323200 | bytes 16785408 | tf_op jit(solution)/shard_map/dot_general | solution.py:43
  346.1 3.9 fusion.70.q_ref
  350.0 13.9 %shard_map.294 = bf16[256,1024]{1,0:T(8,128)(2,1)S(1)} custom-call(s32[2]{0:T(128)S(1)} %bitcast.173, bf16[256,1024]{1,0:T(8,128)(2,1)S(1)} %fusion.70.q_ref, bf16[2048,2048]{1,0:T(8,128)(2,1)S(1)} %fusion.k_ref.v_ref, bf16[2048,2048]{1,0:T(8,128)(2,1)S(1)} %fusion.k_ref.v_ref), custom_call_target="tpu_custom_call" | custom-call | flops 2147483648 | bytes 9437184 | tf_op jit(solution)/shard_map/pallas_call | solution.py:107
  372.1 7.2 collective-permute-done.39.refs_3_
  379.3 4.1 shard_map.296
  383.7 6.7 multiply_convert_fusion
  390.5 4.1 shard_map.298
  394.7 6.0 fusion.95
  404.6 6.6 convert_reduce_fusion.1
  411.1 6.7 multiply_reduce_fusion
  420.0 24.1 %shard_map.299 = (bf16[256,1024]{1,0:T(8,128)(2,1)S(1)}, bf16[2048,1024]{1,0:T(8,128)(2,1)S(1)}, bf16[2048,1024]{1,0:T(8,128)(2,1)S(1)}) custom-call(s32[2]{0:T(128)S(1)} %bitcast.174, bf16[256,1024]{1,0:T(8,128)(2,1)S(1)} %fusion.70.q_ref, bf16[2048,2048]{1,0:T(8,128)(2,1)} %copy-done.2, bf16[2048,2048]{1,0:T(8,128)(2,1)} %copy-done.2, ...), custom_call_target="tpu_custom_call" | custom-call | flops 5368709120 | bytes 18874368 | tf_op jit(solution)/shard_map/pallas_call | solution.py:127
  448.0 5.8 convolution_convert_fusion
  454.3 6.8 fusion.19
  471.8 11.6 %shard_map.300 = (bf16[256,1024]{1,0:T(8,128)(2,1)S(1)}, bf16[256,1024]{1,0:T(8,128)(2,1)S(1)}, bf16[256,1024]{1,0:T(8,128)(2,1)S(1)}) custom-call(s32[2]{0:T(128)S(1)} %bitcast.172, bf16[256,3072]{1,0:T(8,128)(2,1)S(1)} %fusion.16.q_ref.k_ref.v_ref, bf16[256,3072]{1,0:T(8,128)(2,1)S(1)} %fusion.16.q_ref.k_ref.v_ref, ...), custom_call_target="tpu_custom_call" | custom-call | flops 671088640 | bytes 4194304 | tf_op jit(solution)/shard_map/pallas_call | solution.py:127
  485.3 8.2 %convolution_convert_fusion.1 = bf16[1024,1024]{0,1:T(8,128)(2,1)S(1)} fusion(bf16[2048,1024]{1,0:T(8,128)(2,1)} %copy-done.36, bf16[2048,1024]{1,0:T(8,128)(2,1)} %bitcast.226), kind=kOutput, calls=%fused_computation.43 | convolution fusion | flops 4296015872 | bytes 10485760 | tf_op jit(solution)/shard_map/dot_general | solution.py:51
  505.2 11.8 %add_convert_fusion.1 = bf16[2048,1024]{1,0:T(8,128)(2,1)} fusion(f32[2048,1024]{1,0:T(8,128)} %fusion.19, bf16[2048,1024]{1,0:T(8,128)(2,1)} %copy-done.36, bf16[1024,4096]{1,0:T(8,128)(2,1)} %shard_map.293), kind=kOutput, calls=%fused_computation.3 | convolution fusion | flops 4299161600 | bytes 18874368 | tf_op jit(solution)/shard_map/dot_general | solution.py:47
  524.9 3.7 fusion.9
  584.8 19.3 %collective-permute-done.86 = bf16[512,1024]{1,0:T(8,128)(2,1)} collective-permute-done((bf16[512,1024]{1,0:T(8,128)(2,1)S(1)}, bf16[512,1024]{1,0:T(8,128)(2,1)}, u32[]{:S(2)}, u32[]{:S(2)}) %collective-permute-start.86) | collective-permute-done | bytes 1048608 | tf_op jit(solution)/shard_map/ppermute | solution.py:311
  613.6 10.6 %collective-permute-done.74 = bf16[512,1024]{1,0:T(8,128)(2,1)S(1)} collective-permute-done((bf16[512,1024]{1,0:T(8,128)(2,1)S(1)}, bf16[512,1024]{1,0:T(8,128)(2,1)S(1)}, u32[]{:S(2)}, u32[]{:S(2)}) %collective-permute-start.74) | collective-permute-done | bytes 1048608 | tf_op jit(solution)/shard_map/ppermute | solution.py:311
  626.4 3.7 collective-permute-done.76
  631.7 15.0 %collective-permute-done.85 = bf16[512,1024]{1,0:T(8,128)(2,1)S(1)} collective-permute-done((bf16[512,1024]{1,0:T(8,128)(2,1)S(1)}, bf16[512,1024]{1,0:T(8,128)(2,1)S(1)}, u32[]{:S(2)}, u32[]{:S(2)}) %collective-permute-start.85) | collective-permute-done | bytes 1048608 | tf_op jit(solution)/shard_map/ppermute | solution.py:311
  655.4 13.7 %collective-permute-done.51 = bf16[512,1024]{1,0:T(8,128)(2,1)S(1)} collective-permute-done((bf16[512,1024]{1,0:T(8,128)(2,1)S(1)}, bf16[512,1024]{1,0:T(8,128)(2,1)S(1)}, u32[]{:S(2)}, u32[]{:S(2)}) %collective-permute-start.51) | collective-permute-done | bytes 1048608 | tf_op jit(solution)/shard_map/ppermute | solution.py:311
  680.0 4.7 collective-permute-done.88
  684.7 21.3 %collective-permute-start.54 = (bf16[128,1024]{1,0:T(8,128)(2,1)S(1)}, bf16[128,1024]{1,0:T(8,128)(2,1)S(1)}, u32[]{:S(2)}, u32[]{:S(2)}) collective-permute-start(bf16[128,1024]{1,0:T(8,128)(2,1)S(1)} %get-tuple-element.134), channel_id=1, source_target_pairs={{0,2},{1,3},{2,4},{3,5},{4,6},{5,7},{6,0},{7,1},{8,10},{9,11},{10,... | collective-permute-start | bytes 786440 | tf_op jit(solution)/shard_map/ppermute | solution.py:311
  706.0 3.9 collective-permute-start.55
  710.2 15.0 %collective-permute-done.78 = bf16[128,1024]{1,0:T(8,128)(2,1)S(1)} collective-permute-done((bf16[128,1024]{1,0:T(8,128)(2,1)S(1)}, bf16[128,1024]{1,0:T(8,128)(2,1)S(1)}, u32[]{:S(2)}, u32[]{:S(2)}) %collective-permute-start.78) | collective-permute-done | bytes 262176 | tf_op jit(solution)/shard_map/ppermute | solution.py:311
  727.4 9.6 %collective-permute-start.48 = (f32[18,1024]{1,0:T(8,128)S(1)}, f32[18,1024]{1,0:T(8,128)S(1)}, u32[]{:S(2)}, u32[]{:S(2)}) collective-permute-start(f32[18,1024]{1,0:T(8,128)S(1)} %copy-done.57), channel_id=1, source_target_pairs={{0,4},{1,5},{2,6},{3,7},{4,0},{5,1},{6,2},{7,3},{8,12},{9,13},{10,... | collective-permute-start | bytes 221192 | tf_op jit(solution)/shard_map/ppermute | solution.py:311
  737.6 3.7 collective-permute-done.55
  755.3 3.7 shard_map.318
  765.7 3.9 shard_map.313
  769.6 3.8 shard_map.307
  773.5 3.8 shard_map.308
  (409 shorter events, 213.5 us)
Async XLA Ops:
  30.0 54.2 %collective-permute-start.3 = (bf16[512,1024]{1,0:T(8,128)(2,1)S(1)}, bf16[512,1024]{1,0:T(8,128)(2,1)}, u32[]{:S(2)}, u32[]{:S(2)}) collective-permute-start(bf16[512,1024]{1,0:T(8,128)(2,1)S(1)} %shard_map.288.refs_0_), channel_id=1, source_target_pairs={{0,1},{1,0},{2,3},{3,2},{4,5},{5,4},{6,7},{7,6},{8,24},{9,25},{10,... | collective-permute-start | bytes 3145736 | tf_op jit(solution)/shard_map/ppermute | solution.py:311
  36.7 31.7 %collective-permute-start.15 = (bf16[128,1024]{1,0:T(8,128)(2,1)S(1)}, bf16[128,1024]{1,0:T(8,128)(2,1)S(1)}, u32[]{:S(2)}, u32[]{:S(2)}) collective-permute-start(bf16[128,1024]{1,0:T(8,128)(2,1)S(1)} %get-tuple-element.120.refs_0_), channel_id=1, source_target_pairs={{0,4},{1,5},{2,6},{3,7},{4,0},{5,1},{6,2},{7,3},{8,12},{9,13},{10,... | collective-permute-start | bytes 786440 | tf_op jit(solution)/shard_map/ppermute | solution.py:311
  40.9 28.9 %collective-permute-start.14 = (bf16[128,1024]{1,0:T(8,128)(2,1)S(1)}, bf16[128,1024]{1,0:T(8,128)(2,1)S(1)}, u32[]{:S(2)}, u32[]{:S(2)}) collective-permute-start(bf16[128,1024]{1,0:T(8,128)(2,1)S(1)} %get-tuple-element.120.refs_0_), channel_id=1, source_target_pairs={{0,2},{1,3},{2,4},{3,5},{4,6},{5,7},{6,0},{7,1},{8,10},{9,11},{10,... | collective-permute-start | bytes 786440 | tf_op jit(solution)/shard_map/ppermute | solution.py:311
  50.1 24.8 %collective-permute-start.36 = (bf16[128,1024]{1,0:T(8,128)(2,1)S(1)}, bf16[128,1024]{1,0:T(8,128)(2,1)S(1)}, u32[]{:S(2)}, u32[]{:S(2)}) collective-permute-start(bf16[128,1024]{1,0:T(8,128)(2,1)S(1)} %dynamic-slice_convert_fusion.refs_0_), channel_id=1, source_target_pairs={{0,6},{1,7},{2,0},{3,1},{4,2},{5,3},{6,4},{7,5},{8,14},{9,15},{10,... | collective-permute-start | bytes 786440 | tf_op jit(solution)/shard_map/ppermute | solution.py:311
  50.8 32.0 %collective-permute-start.35 = (bf16[128,1024]{1,0:T(8,128)(2,1)S(1)}, bf16[128,1024]{1,0:T(8,128)(2,1)S(1)}, u32[]{:S(2)}, u32[]{:S(2)}) collective-permute-start(bf16[128,1024]{1,0:T(8,128)(2,1)S(1)} %dynamic-slice_convert_fusion.refs_0_), channel_id=1, source_target_pairs={{0,4},{1,5},{2,6},{3,7},{4,0},{5,1},{6,2},{7,3},{8,12},{9,13},{10,... | collective-permute-start | bytes 786440 | tf_op jit(solution)/shard_map/ppermute | solution.py:311
  74.7 38.1 %collective-permute-start.6 = (bf16[512,1024]{1,0:T(8,128)(2,1)S(1)}, bf16[512,1024]{1,0:T(8,128)(2,1)}, u32[]{:S(2)}, u32[]{:S(2)}) collective-permute-start(bf16[512,1024]{1,0:T(8,128)(2,1)S(1)} %shard_map.288.refs_0_), channel_id=1, source_target_pairs={{0,8},{1,9},{2,10},{3,11},{4,12},{5,13},{6,14},{7,15},{8,0},{9,1},... | collective-permute-start | bytes 3145736 | tf_op jit(solution)/shard_map/ppermute | solution.py:311
  74.8 38.0 %collective-permute-start.4 = (bf16[512,1024]{1,0:T(8,128)(2,1)S(1)}, bf16[512,1024]{1,0:T(8,128)(2,1)}, u32[]{:S(2)}, u32[]{:S(2)}) collective-permute-start(bf16[512,1024]{1,0:T(8,128)(2,1)S(1)} %shard_map.288.refs_0_), channel_id=1, source_target_pairs={{0,16},{1,17},{2,18},{3,19},{4,20},{5,21},{6,22},{7,23},{8,9},{9,8... | collective-permute-start | bytes 3145736 | tf_op jit(solution)/shard_map/ppermute | solution.py:311
  82.8 30.6 %collective-permute-start.17 = (bf16[512,1024]{1,0:T(8,128)(2,1)S(1)}, bf16[512,1024]{1,0:T(8,128)(2,1)}, u32[]{:S(2)}, u32[]{:S(2)}) collective-permute-start(bf16[512,1024]{1,0:T(8,128)(2,1)S(1)} %shard_map.292.refs_0_), channel_id=1, source_target_pairs={{0,1},{1,0},{2,3},{3,2},{4,5},{5,4},{6,7},{7,6},{8,24},{9,25},{10,... | collective-permute-start | bytes 3145736 | tf_op jit(solution)/shard_map/ppermute | solution.py:311
  84.2 29.1 %collective-permute-start.5 = (bf16[512,1024]{1,0:T(8,128)(2,1)}, bf16[512,1024]{1,0:T(8,128)(2,1)}, u32[]{:S(2)}, u32[]{:S(2)}) collective-permute-start(bf16[512,1024]{1,0:T(8,128)(2,1)} %collective-permute-done.3.refs_1_), channel_id=1, source_target_pairs={{0,16},{1,17},{2,18},{3,19},{4,20},{5,21},{6,22},{7,23},{8,9},{9,8... | collective-permute-start | bytes 3145736 | tf_op jit(solution)/shard_map/ppermute | solution.py:311
  113.3 31.3 %collective-permute-start.19 = (bf16[512,1024]{1,0:T(8,128)(2,1)}, bf16[512,1024]{1,0:T(8,128)(2,1)S(1)}, u32[]{:S(2)}, u32[]{:S(2)}) collective-permute-start(bf16[512,1024]{1,0:T(8,128)(2,1)} %collective-permute-done.17.refs_1_), channel_id=1, source_target_pairs={{0,16},{1,17},{2,18},{3,19},{4,20},{5,21},{6,22},{7,23},{8,9},{9,8... | collective-permute-start | bytes 3145736 | tf_op jit(solution)/shard_map/ppermute | solution.py:311
  113.3 31.3 %collective-permute-start.9 = (bf16[512,1024]{1,0:T(8,128)(2,1)}, bf16[512,1024]{1,0:T(8,128)(2,1)S(1)}, u32[]{:S(2)}, u32[]{:S(2)}) collective-permute-start(bf16[512,1024]{1,0:T(8,128)(2,1)} %collective-permute-done.5.refs_3_), channel_id=1, source_target_pairs={{0,8},{1,9},{2,10},{3,11},{4,12},{5,13},{6,14},{7,15},{8,0},{9,1},... | collective-permute-start | bytes 3145736 | tf_op jit(solution)/shard_map/ppermute | solution.py:311
  125.6 165.4 %collective-permute-start.20 = (bf16[512,1024]{1,0:T(8,128)(2,1)S(1)}, bf16[512,1024]{1,0:T(8,128)(2,1)S(1)}, u32[]{:S(2)}, u32[]{:S(2)}) collective-permute-start(bf16[512,1024]{1,0:T(8,128)(2,1)S(1)} %shard_map.292.refs_0_), channel_id=1, source_target_pairs={{0,8},{1,9},{2,10},{3,11},{4,12},{5,13},{6,14},{7,15},{8,0},{9,1},... | collective-permute-start | bytes 3145736 | tf_op jit(solution)/shard_map/ppermute | solution.py:311
  125.6 165.4 %collective-permute-start.27 = (bf16[512,1024]{1,0:T(8,128)(2,1)S(1)}, bf16[512,1024]{1,0:T(8,128)(2,1)S(1)}, u32[]{:S(2)}, u32[]{:S(2)}) collective-permute-start(bf16[512,1024]{1,0:T(8,128)(2,1)S(1)} %shard_map.295.refs_0_), channel_id=1, source_target_pairs={{0,1},{1,0},{2,3},{3,2},{4,5},{5,4},{6,7},{7,6},{8,24},{9,25},{10,... | collective-permute-start | bytes 3145736 | tf_op jit(solution)/shard_map/ppermute | solution.py:311
  127.5 166.9 %collective-permute-start.21 = (bf16[512,1024]{1,0:T(8,128)(2,1)}, bf16[512,1024]{1,0:T(8,128)(2,1)S(1)}, u32[]{:S(2)}, u32[]{:S(2)}) collective-permute-start(bf16[512,1024]{1,0:T(8,128)(2,1)} %collective-permute-done.17.refs_1_), channel_id=1, source_target_pairs={{0,8},{1,9},{2,10},{3,11},{4,12},{5,13},{6,14},{7,15},{8,0},{9,1},... | collective-permute-start | bytes 3145736 | tf_op jit(solution)/shard_map/ppermute | solution.py:311
  144.6 148.7 %collective-permute-start.22 = (bf16[512,1024]{1,0:T(8,128)(2,1)S(1)}, bf16[512,1024]{1,0:T(8,128)(2,1)S(1)}, u32[]{:S(2)}, u32[]{:S(2)}) collective-permute-start(bf16[512,1024]{1,0:T(8,128)(2,1)S(1)} %collective-permute-done.18.refs_2_), channel_id=1, source_target_pairs={{0,8},{1,9},{2,10},{3,11},{4,12},{5,13},{6,14},{7,15},{8,0},{9,1},... | collective-permute-start | bytes 3145736 | tf_op jit(solution)/shard_map/ppermute | solution.py:311
  144.6 151.6 %collective-permute-start.23 = (bf16[512,1024]{1,0:T(8,128)(2,1)S(1)}, bf16[512,1024]{1,0:T(8,128)(2,1)S(1)}, u32[]{:S(2)}, u32[]{:S(2)}) collective-permute-start(bf16[512,1024]{1,0:T(8,128)(2,1)S(1)} %collective-permute-done.19.refs_3_), channel_id=1, source_target_pairs={{0,8},{1,9},{2,10},{3,11},{4,12},{5,13},{6,14},{7,15},{8,0},{9,1},... | collective-permute-start | bytes 3145736 | tf_op jit(solution)/shard_map/ppermute | solution.py:311
  291.0 73.0 %collective-permute-start.30 = (bf16[512,1024]{1,0:T(8,128)(2,1)S(1)}, bf16[512,1024]{1,0:T(8,128)(2,1)S(1)}, u32[]{:S(2)}, u32[]{:S(2)}) collective-permute-start(bf16[512,1024]{1,0:T(8,128)(2,1)S(1)} %shard_map.295.refs_0_), channel_id=1, source_target_pairs={{0,8},{1,9},{2,10},{3,11},{4,12},{5,13},{6,14},{7,15},{8,0},{9,1},... | collective-permute-start | bytes 3145736 | tf_op jit(solution)/shard_map/ppermute | solution.py:311
  291.0 73.0 %collective-permute-start.28 = (bf16[512,1024]{1,0:T(8,128)(2,1)S(1)}, bf16[512,1024]{1,0:T(8,128)(2,1)S(1)}, u32[]{:S(2)}, u32[]{:S(2)}) collective-permute-start(bf16[512,1024]{1,0:T(8,128)(2,1)S(1)} %shard_map.295.refs_0_), channel_id=1, source_target_pairs={{0,16},{1,17},{2,18},{3,19},{4,20},{5,21},{6,22},{7,23},{8,9},{9,8... | collective-permute-start | bytes 3145736 | tf_op jit(solution)/shard_map/ppermute | solution.py:311
  294.3 76.8 %collective-permute-start.38 = (bf16[512,1024]{1,0:T(8,128)(2,1)S(1)}, bf16[512,1024]{1,0:T(8,128)(2,1)S(1)}, u32[]{:S(2)}, u32[]{:S(2)}) collective-permute-start(bf16[512,1024]{1,0:T(8,128)(2,1)S(1)} %shard_map.297.refs_0_), channel_id=1, source_target_pairs={{0,16},{1,17},{2,18},{3,19},{4,20},{5,21},{6,22},{7,23},{8,9},{9,8... | collective-permute-start | bytes 3145736 | tf_op jit(solution)/shard_map/ppermute | solution.py:311
  294.3 70.2 %collective-permute-start.37 = (bf16[512,1024]{1,0:T(8,128)(2,1)S(1)}, bf16[512,1024]{1,0:T(8,128)(2,1)S(1)}, u32[]{:S(2)}, u32[]{:S(2)}) collective-permute-start(bf16[512,1024]{1,0:T(8,128)(2,1)S(1)} %shard_map.297.refs_0_), channel_id=1, source_target_pairs={{0,1},{1,0},{2,3},{3,2},{4,5},{5,4},{6,7},{7,6},{8,24},{9,25},{10,... | collective-permute-start | bytes 3145736 | tf_op jit(solution)/shard_map/ppermute | solution.py:311
  297.2 69.2 %collective-permute-start.29 = (bf16[512,1024]{1,0:T(8,128)(2,1)S(1)}, bf16[512,1024]{1,0:T(8,128)(2,1)S(1)}, u32[]{:S(2)}, u32[]{:S(2)}) collective-permute-start(bf16[512,1024]{1,0:T(8,128)(2,1)S(1)} %collective-permute-done.27.refs_1_), channel_id=1, source_target_pairs={{0,16},{1,17},{2,18},{3,19},{4,20},{5,21},{6,22},{7,23},{8,9},{9,8... | collective-permute-start | bytes 3145736 | tf_op jit(solution)/shard_map/ppermute | solution.py:311
  453.7 79.0 %collective-permute-start.73 = (bf16[256,4096]{1,0:T(8,128)(2,1)}, bf16[256,4096]{1,0:T(8,128)(2,1)}, u32[]{:S(2)}, u32[]{:S(2)}) collective-permute-start(bf16[256,4096]{1,0:T(8,128)(2,1)} %get-tuple-element.158.ym_ref), channel_id=1, source_target_pairs={{0,8},{1,9},{2,10},{3,11},{4,12},{5,13},{6,14},{7,15},{8,0},{9,1},... | collective-permute-start | bytes 6291464 | tf_op jit(solution)/shard_map/ppermute | solution.py:311
  461.2 55.8 %collective-permute-start.60 = (bf16[256,2048]{1,0:T(8,128)(2,1)}, bf16[256,2048]{1,0:T(8,128)(2,1)}, u32[]{:S(2)}, u32[]{:S(2)}) collective-permute-start(bf16[256,2048]{1,0:T(8,128)(2,1)} %pad_maximum_fusion.2.xm_ref), channel_id=1, source_target_pairs={{0,8},{1,9},{2,10},{3,11},{4,12},{5,13},{6,14},{7,15},{8,0},{9,1},... | collective-permute-start | bytes 3145736 | tf_op jit(solution)/shard_map/ppermute | solution.py:311
  495.1 29.7 %collective-permute-start.62 = (bf16[1024,1024]{1,0:T(8,128)(2,1)}, bf16[1024,1024]{1,0:T(8,128)(2,1)}, u32[]{:S(2)}, u32[]{:S(2)}) collective-permute-start(bf16[1024,1024]{1,0:T(8,128)(2,1)} %select_bitcast_fusion), channel_id=1, source_target_pairs={{0,8},{1,9},{2,10},{3,11},{4,12},{5,13},{6,14},{7,15},{8,0},{9,1},... | collective-permute-start | bytes 6291464 | tf_op jit(solution)/shard_map/ppermute | solution.py:311
  505.1 40.3 %collective-permute-start.50 = (bf16[256,4096]{1,0:T(8,128)(2,1)S(1)}, bf16[256,4096]{1,0:T(8,128)(2,1)S(1)}, u32[]{:S(2)}, u32[]{:S(2)}) collective-permute-start(bf16[256,4096]{1,0:T(8,128)(2,1)S(1)} %pad_maximum_fusion.ym_ref), channel_id=1, source_target_pairs={{0,8},{1,9},{2,10},{3,11},{4,12},{5,13},{6,14},{7,15},{8,0},{9,1},... | collective-permute-start | bytes 6291464 | tf_op jit(solution)/shard_map/ppermute | solution.py:311
  517.0 33.7 %collective-permute-start.83 = (bf16[256,4096]{1,0:T(8,128)(2,1)S(1)}, bf16[256,4096]{1,0:T(8,128)(2,1)S(1)}, u32[]{:S(2)}, u32[]{:S(2)}) collective-permute-start(bf16[256,4096]{1,0:T(8,128)(2,1)S(1)} %copy-done.1), channel_id=1, source_target_pairs={{0,8},{1,9},{2,10},{3,11},{4,12},{5,13},{6,14},{7,15},{8,0},{9,1},... | collective-permute-start | bytes 6291464 | tf_op jit(solution)/shard_map/ppermute | solution.py:311
  532.7 38.8 %collective-permute-start.64 = (bf16[512,1024]{1,0:T(8,128)(2,1)}, bf16[512,1024]{1,0:T(8,128)(2,1)}, u32[]{:S(2)}, u32[]{:S(2)}) collective-permute-start(bf16[512,1024]{1,0:T(8,128)(2,1)} %get-tuple-element.119), channel_id=1, source_target_pairs={{0,16},{1,17},{2,18},{3,19},{4,20},{5,21},{6,22},{7,23},{8,9},{9,8... | collective-permute-start | bytes 3145736 | tf_op jit(solution)/shard_map/ppermute | solution.py:311
  541.1 40.2 %collective-permute-start.75 = (bf16[512,1024]{1,0:T(8,128)(2,1)S(1)}, bf16[512,1024]{1,0:T(8,128)(2,1)}, u32[]{:S(2)}, u32[]{:S(2)}) collective-permute-start(bf16[512,1024]{1,0:T(8,128)(2,1)S(1)} %shard_map.312), channel_id=1, source_target_pairs={{0,16},{1,17},{2,18},{3,19},{4,20},{5,21},{6,22},{7,23},{8,9},{9,8... | collective-permute-start | bytes 3145736 | tf_op jit(solution)/shard_map/ppermute | solution.py:311
  545.4 62.2 %collective-permute-start.63 = (bf16[512,1024]{1,0:T(8,128)(2,1)}, bf16[512,1024]{1,0:T(8,128)(2,1)}, u32[]{:S(2)}, u32[]{:S(2)}) collective-permute-start(bf16[512,1024]{1,0:T(8,128)(2,1)} %get-tuple-element.118), channel_id=1, source_target_pairs={{0,16},{1,17},{2,18},{3,19},{4,20},{5,21},{6,22},{7,23},{8,9},{9,8... | collective-permute-start | bytes 3145736 | tf_op jit(solution)/shard_map/ppermute | solution.py:311
  550.4 57.5 %collective-permute-start.52 = (bf16[512,1024]{1,0:T(8,128)(2,1)}, bf16[512,1024]{1,0:T(8,128)(2,1)}, u32[]{:S(2)}, u32[]{:S(2)}) collective-permute-start(bf16[512,1024]{1,0:T(8,128)(2,1)} %shard_map.304), channel_id=1, source_target_pairs={{0,16},{1,17},{2,18},{3,19},{4,20},{5,21},{6,22},{7,23},{8,9},{9,8... | collective-permute-start | bytes 3145736 | tf_op jit(solution)/shard_map/ppermute | solution.py:311
  552.9 51.2 %collective-permute-start.86 = (bf16[512,1024]{1,0:T(8,128)(2,1)S(1)}, bf16[512,1024]{1,0:T(8,128)(2,1)}, u32[]{:S(2)}, u32[]{:S(2)}) collective-permute-start(bf16[512,1024]{1,0:T(8,128)(2,1)S(1)} %shard_map.317), channel_id=1, source_target_pairs={{0,16},{1,17},{2,18},{3,19},{4,20},{5,21},{6,22},{7,23},{8,9},{9,8... | collective-permute-start | bytes 3145736 | tf_op jit(solution)/shard_map/ppermute | solution.py:311
  574.3 36.8 %collective-permute-start.65 = (bf16[512,1024]{1,0:T(8,128)(2,1)S(1)}, bf16[512,1024]{1,0:T(8,128)(2,1)S(1)}, u32[]{:S(2)}, u32[]{:S(2)}) collective-permute-start(bf16[512,1024]{1,0:T(8,128)(2,1)S(1)} %add_convert_fusion.7), channel_id=1, source_target_pairs={{0,1},{1,0},{2,3},{3,2},{4,5},{5,4},{6,7},{7,6},{8,24},{9,25},{10,... | collective-permute-start | bytes 3145736 | tf_op jit(solution)/shard_map/ppermute | solution.py:311
  581.3 42.9 %collective-permute-start.74 = (bf16[512,1024]{1,0:T(8,128)(2,1)S(1)}, bf16[512,1024]{1,0:T(8,128)(2,1)S(1)}, u32[]{:S(2)}, u32[]{:S(2)}) collective-permute-start(bf16[512,1024]{1,0:T(8,128)(2,1)S(1)} %shard_map.310), channel_id=1, source_target_pairs={{0,16},{1,17},{2,18},{3,19},{4,20},{5,21},{6,22},{7,23},{8,9},{9,8... | collective-permute-start | bytes 3145736 | tf_op jit(solution)/shard_map/ppermute | solution.py:311
  604.0 26.1 %collective-permute-start.76 = (bf16[512,1024]{1,0:T(8,128)(2,1)S(1)}, bf16[512,1024]{1,0:T(8,128)(2,1)S(1)}, u32[]{:S(2)}, u32[]{:S(2)}) collective-permute-start(bf16[512,1024]{1,0:T(8,128)(2,1)S(1)} %add_convert_fusion.5), channel_id=1, source_target_pairs={{0,1},{1,0},{2,3},{3,2},{4,5},{5,4},{6,7},{7,6},{8,24},{9,25},{10,... | collective-permute-start | bytes 3145736 | tf_op jit(solution)/shard_map/ppermute | solution.py:311
  607.6 39.0 %collective-permute-start.85 = (bf16[512,1024]{1,0:T(8,128)(2,1)S(1)}, bf16[512,1024]{1,0:T(8,128)(2,1)S(1)}, u32[]{:S(2)}, u32[]{:S(2)}) collective-permute-start(bf16[512,1024]{1,0:T(8,128)(2,1)S(1)} %shard_map.315), channel_id=1, source_target_pairs={{0,16},{1,17},{2,18},{3,19},{4,20},{5,21},{6,22},{7,23},{8,9},{9,8... | collective-permute-start | bytes 3145736 | tf_op jit(solution)/shard_map/ppermute | solution.py:311
  608.0 44.6 %collective-permute-start.87 = (bf16[512,1024]{1,0:T(8,128)(2,1)S(1)}, bf16[512,1024]{1,0:T(8,128)(2,1)S(1)}, u32[]{:S(2)}, u32[]{:S(2)}) collective-permute-start(bf16[512,1024]{1,0:T(8,128)(2,1)S(1)} %add_convert_fusion.3), channel_id=1, source_target_pairs={{0,1},{1,0},{2,3},{3,2},{4,5},{5,4},{6,7},{7,6},{8,24},{9,25},{10,... | collective-permute-start | bytes 3145736 | tf_op jit(solution)/shard_map/ppermute | solution.py:311
  611.1 58.0 %collective-permute-start.51 = (bf16[512,1024]{1,0:T(8,128)(2,1)S(1)}, bf16[512,1024]{1,0:T(8,128)(2,1)S(1)}, u32[]{:S(2)}, u32[]{:S(2)}) collective-permute-start(bf16[512,1024]{1,0:T(8,128)(2,1)S(1)} %shard_map.302), channel_id=1, source_target_pairs={{0,16},{1,17},{2,18},{3,19},{4,20},{5,21},{6,22},{7,23},{8,9},{9,8... | collective-permute-start | bytes 3145736 | tf_op jit(solution)/shard_map/ppermute | solution.py:311
  624.2 46.5 %collective-permute-start.53 = (bf16[512,1024]{1,0:T(8,128)(2,1)S(1)}, bf16[512,1024]{1,0:T(8,128)(2,1)S(1)}, u32[]{:S(2)}, u32[]{:S(2)}) collective-permute-start(bf16[512,1024]{1,0:T(8,128)(2,1)S(1)} %add_convert_fusion.9), channel_id=1, source_target_pairs={{0,1},{1,0},{2,3},{3,2},{4,5},{5,4},{6,7},{7,6},{8,24},{9,25},{10,... | collective-permute-start | bytes 3145736 | tf_op jit(solution)/shard_map/ppermute | solution.py:311
  630.1 42.6 %collective-permute-start.66 = (bf16[128,1024]{1,0:T(8,128)(2,1)S(1)}, bf16[128,1024]{1,0:T(8,128)(2,1)S(1)}, u32[]{:S(2)}, u32[]{:S(2)}) collective-permute-start(bf16[128,1024]{1,0:T(8,128)(2,1)S(1)} %get-tuple-element.131), channel_id=1, source_target_pairs={{0,2},{1,3},{2,4},{3,5},{4,6},{5,7},{6,0},{7,1},{8,10},{9,11},{10,... | collective-permute-start | bytes 786440 | tf_op jit(solution)/shard_map/ppermute | solution.py:311
  646.7 28.6 %collective-permute-start.68 = (bf16[128,1024]{1,0:T(8,128)(2,1)S(1)}, bf16[128,1024]{1,0:T(8,128)(2,1)S(1)}, u32[]{:S(2)}, u32[]{:S(2)}) collective-permute-start(bf16[128,1024]{1,0:T(8,128)(2,1)S(1)} %get-tuple-element.132), channel_id=1, source_target_pairs={{0,6},{1,7},{2,0},{3,1},{4,2},{5,3},{6,4},{7,5},{8,14},{9,15},{10,... | collective-permute-start | bytes 786440 | tf_op jit(solution)/shard_map/ppermute | solution.py:311
  672.7 33.3 %collective-permute-start.90 = (bf16[128,1024]{1,0:T(8,128)(2,1)S(1)}, bf16[128,1024]{1,0:T(8,128)(2,1)S(1)}, u32[]{:S(2)}, u32[]{:S(2)}) collective-permute-start(bf16[128,1024]{1,0:T(8,128)(2,1)S(1)} %get-tuple-element.126), channel_id=1, source_target_pairs={{0,6},{1,7},{2,0},{3,1},{4,2},{5,3},{6,4},{7,5},{8,14},{9,15},{10,... | collective-permute-start | bytes 786440 | tf_op jit(solution)/shard_map/ppermute | solution.py:311
  675.2 30.7 %collective-permute-start.89 = (bf16[128,1024]{1,0:T(8,128)(2,1)S(1)}, bf16[128,1024]{1,0:T(8,128)(2,1)S(1)}, u32[]{:S(2)}, u32[]{:S(2)}) collective-permute-start(bf16[128,1024]{1,0:T(8,128)(2,1)S(1)} %get-tuple-element.127), channel_id=1, source_target_pairs={{0,4},{1,5},{2,6},{3,7},{4,0},{5,1},{6,2},{7,3},{8,12},{9,13},{10,... | collective-permute-start | bytes 786440 | tf_op jit(solution)/shard_map/ppermute | solution.py:311
  675.4 34.7 %collective-permute-start.79 = (bf16[128,1024]{1,0:T(8,128)(2,1)S(1)}, bf16[128,1024]{1,0:T(8,128)(2,1)S(1)}, u32[]{:S(2)}, u32[]{:S(2)}) collective-permute-start(bf16[128,1024]{1,0:T(8,128)(2,1)S(1)} %get-tuple-element.129), channel_id=1, source_target_pairs={{0,6},{1,7},{2,0},{3,1},{4,2},{5,3},{6,4},{7,5},{8,14},{9,15},{10,... | collective-permute-start | bytes 786440 | tf_op jit(solution)/shard_map/ppermute | solution.py:311
  679.2 45.9 %collective-permute-start.78 = (bf16[128,1024]{1,0:T(8,128)(2,1)S(1)}, bf16[128,1024]{1,0:T(8,128)(2,1)S(1)}, u32[]{:S(2)}, u32[]{:S(2)}) collective-permute-start(bf16[128,1024]{1,0:T(8,128)(2,1)S(1)} %get-tuple-element.130), channel_id=1, source_target_pairs={{0,4},{1,5},{2,6},{3,7},{4,0},{5,1},{6,2},{7,3},{8,12},{9,13},{10,... | collective-permute-start | bytes 786440 | tf_op jit(solution)/shard_map/ppermute | solution.py:311
  684.7 42.7 %collective-permute-start.54 = (bf16[128,1024]{1,0:T(8,128)(2,1)S(1)}, bf16[128,1024]{1,0:T(8,128)(2,1)S(1)}, u32[]{:S(2)}, u32[]{:S(2)}) collective-permute-start(bf16[128,1024]{1,0:T(8,128)(2,1)S(1)} %get-tuple-element.134), channel_id=1, source_target_pairs={{0,2},{1,3},{2,4},{3,5},{4,6},{5,7},{6,0},{7,1},{8,10},{9,11},{10,... | collective-permute-start | bytes 786440 | tf_op jit(solution)/shard_map/ppermute | solution.py:311
  706.0 31.1 %collective-permute-start.56 = (bf16[128,1024]{1,0:T(8,128)(2,1)S(1)}, bf16[128,1024]{1,0:T(8,128)(2,1)S(1)}, u32[]{:S(2)}, u32[]{:S(2)}) collective-permute-start(bf16[128,1024]{1,0:T(8,128)(2,1)S(1)} %get-tuple-element.135), channel_id=1, source_target_pairs={{0,6},{1,7},{2,0},{3,1},{4,2},{5,3},{6,4},{7,5},{8,14},{9,15},{10,... | collective-permute-start | bytes 786440 | tf_op jit(solution)/shard_map/ppermute | solution.py:311
  706.0 35.3 %collective-permute-start.55 = (bf16[128,1024]{1,0:T(8,128)(2,1)S(1)}, bf16[128,1024]{1,0:T(8,128)(2,1)S(1)}, u32[]{:S(2)}, u32[]{:S(2)}) collective-permute-start(bf16[128,1024]{1,0:T(8,128)(2,1)S(1)} %get-tuple-element.136), channel_id=1, source_target_pairs={{0,4},{1,5},{2,6},{3,7},{4,0},{5,1},{6,2},{7,3},{8,12},{9,13},{10,... | collective-permute-start | bytes 786440 | tf_op jit(solution)/shard_map/ppermute | solution.py:311
  710.1 33.3 %collective-permute-start.70 = (bf16[128,1024]{1,0:T(8,128)(2,1)S(1)}, bf16[128,1024]{1,0:T(8,128)(2,1)S(1)}, u32[]{:S(2)}, u32[]{:S(2)}) collective-permute-start(bf16[128,1024]{1,0:T(8,128)(2,1)S(1)} %add_convert_fusion.12.g0_ref), channel_id=1, source_target_pairs={{0,16},{1,17},{2,18},{3,19},{4,20},{5,21},{6,22},{7,23},{8,24},{9,... | collective-permute-start | bytes 786440 | tf_op jit(solution)/shard_map/ppermute | solution.py:311
  (110 other events, 1674.2 us)

commit v2 on v1

v2 whole, which is shorter than its diff:
```python
from functools import partial

import jax
import jax.numpy as jnp
from jax import lax
from jax.experimental import pallas as pl
from jax.experimental.pallas import tpu as pltpu
from jax.sharding import PartitionSpec as P

D = 1024
H = 16
DH = 64
STEP = 7
PAIRS = H // 2
UNITS = 4
LANES = 128
TAIL = 16

momentum_decay = 0.9
square_decay = 0.999
matrix_rate = 0.08
vector_rate = 0.3
matrix_decay = 0.01
epsilon = 1e-08
norm_epsilon = 1e-05
fix_first = 1.0 - momentum_decay**STEP
fix_second = 1.0 - square_decay**STEP

f32 = jnp.float32
bf16 = jnp.bfloat16
ANY = pl.BlockSpec(memory_space=pl.ANY)
VMEM_BYTES = 44 * 1024 * 1024
FIRST, SECOND = (0, 1, 5, 6), (2, 3, 4, 7)


def params(**more):
    return pltpu.CompilerParams(vmem_limit_bytes=VMEM_BYTES, **more)


def cost(nbytes):
    return pl.CostEstimate(flops=0, bytes_accessed=int(nbytes), transcendentals=0)


def array(shape, kind=bf16):
    return jax.ShapeDtypeStruct(shape, kind)


def whole(shape):
    return pl.BlockSpec(shape, lambda *at: (0,) * len(shape))


def dot(left, right):
    return jnp.dot(left, right, preferred_element_type=f32)


def dot_back(left, right):
    return lax.dot_general(left, right, (((1,), (1,)), ((), ())), preferred_element_type=f32)


def dot_grad(inputs, grads):
    return lax.dot_general(inputs, grads, (((0,), (0,)), ((), ())), preferred_element_type=f32)


def norm_forward(stream, gain, bias):
    centred = stream - jnp.mean(stream, axis=-1, keepdims=True)
    spread = jnp.mean(centred * centred, axis=-1, keepdims=True)
    scale = lax.rsqrt(spread + norm_epsilon)
    unit = centred * scale
    return unit * gain + bias, unit, scale


def norm_backward(grad, unit, scale, gain):
    scaled = grad * gain
    mean = jnp.mean(scaled, axis=-1, keepdims=True)
    along = jnp.mean(scaled * unit, axis=-1, keepdims=True)
    return scale * (scaled - mean - unit * along), column_sum(grad * unit), column_sum(grad)


def column_sum(values):
    return jnp.sum(values.astype(f32), axis=0, keepdims=True)


def valid_rows(len_ref, rows, length):
    spot = lax.broadcasted_iota(jnp.int32, (rows, 1), 0)
    limit = jnp.full((rows, 1), len_ref[0], jnp.int32)
    for m in range(1, rows // length):
        limit = jnp.where(spot >= m * length, m * length + len_ref[m], limit)
    return spot < limit


def add_up(total_ref, step, part):
    @pl.when(step == 0)
    def _():
        total_ref[...] = part

    @pl.when(step > 0)
    def _():
        total_ref[...] += part


BLOCK = 1024


def project_kernel(x_ref, w_ref, b_ref, o_ref):
    o_ref[...] = (dot(x_ref[...], w_ref[...]) + b_ref[...]).astype(bf16)


def project(rows, weights, bias, at):
    n_rows, depth = rows.shape
    width = bias.shape[1]
    return pl.pallas_call(
        project_kernel,
        out_shape=array((n_rows, width)),
        grid=(width // BLOCK,),
        in_specs=[
            whole((n_rows, depth)),
            pl.BlockSpec((depth, BLOCK), lambda n: (0, at // BLOCK + n)),
            pl.BlockSpec((1, BLOCK), lambda n: (0, n)),
        ],
        out_specs=pl.BlockSpec((n_rows, BLOCK), lambda n: (0, n)),
        compiler_params=params(),
        cost_estimate=cost(1024),
    )(rows, weights, bias)


def join_kernel(length, rows_at, len_ref, x_ref, w_ref, res_ref, vec_ref, *outs):
    h_ref, low_ref, unit_ref, scale_ref, sums_ref, total_ref = outs
    step = pl.program_id(0)
    add_up(total_ref, step, dot(x_ref[...], w_ref[...]))

    @pl.when(step == pl.num_programs(0) - 1)
    def _():
        bias, gain, offset = (vec_ref[r : r + 1, :] for r in rows_at)
        branch = total_ref[...] + bias
        out, unit, scale = norm_forward(res_ref[...].astype(f32) + branch, gain, offset)
        h_ref[...] = out
        low_ref[...] = out.astype(bf16)
        unit_ref[...] = unit
        scale_ref[...] = jnp.broadcast_to(scale, scale_ref.shape)
        valid = valid_rows(len_ref, branch.shape[0], length)
        sums_ref[...] = column_sum(jnp.where(valid, branch * branch, 0.0))


def join(lengths, rows, weights, at, residual, vec, rows_at):
    n_rows = residual.shape[0]
    slot = rows.ndim == 3
    x_spec = (
        pl.BlockSpec((None, n_rows, BLOCK), lambda k, n: (1, 0, k))
        if slot
        else pl.BlockSpec((n_rows, BLOCK), lambda k, n: (0, k))
    )
    return pl.pallas_call(
        partial(join_kernel, n_rows // lengths.shape[0], rows_at),
        out_shape=[
            array((n_rows, D), f32),
            array((n_rows, D)),
            array((n_rows, D), f32),
            array((n_rows, LANES), f32),
            array((1, D), f32),
        ],
        grid_spec=pltpu.PrefetchScalarGridSpec(
            num_scalar_prefetch=1,
            grid=(D // BLOCK,),
            in_specs=[
                x_spec,
                pl.BlockSpec((BLOCK, D), lambda k, n: (k, at // D)),
                whole((n_rows, D)),
                whole(vec.shape),
            ],
            out_specs=[whole((n_rows, D))] * 3 + [whole((n_rows, LANES)), whole((1, D))],
            scratch_shapes=[pltpu.VMEM((n_rows, D), f32)],
        ),
        compiler_params=params(),
        cost_estimate=cost(1024),
    )(lengths, rows, weights, residual, vec)


def hidden_kernel(x_ref, w_ref, b_ref, g_ref, slope_ref):
    u = dot(x_ref[...], w_ref[...]) + b_ref[...]
    phi = 0.5 * (1.0 + lax.erf(u * 2.0**-0.5))
    g_ref[...] = (u * phi).astype(bf16)
    slope_ref[...] = (phi + u * jnp.exp(-0.5 * u * u) * (2.0 * jnp.pi) ** -0.5).astype(bf16)


def hidden_layer(rows, weights, bias):
    n_rows, depth = rows.shape
    width = weights.shape[1]
    out_spec = pl.BlockSpec((n_rows, BLOCK), lambda n: (0, n))
    return pl.pallas_call(
        hidden_kernel,
        out_shape=[array((n_rows, width))] * 2,
        grid=(width // BLOCK,),
        in_specs=[
            whole((n_rows, depth)),
            pl.BlockSpec((depth, BLOCK), lambda n: (0, n)),
            pl.BlockSpec((1, BLOCK), lambda n: (0, n)),
        ],
        out_specs=[out_spec] * 2,
        compiler_params=params(),
        cost_estimate=cost(1024),
    )(rows, weights, bias)


def turn_kernel(length, rows_at, len_ref, x_ref, w_ref, res_ref, cot_ref, vec_ref, *outs):
    mixed_ref, dr_ref, low_ref, sums_ref, total_ref = outs
    step = pl.program_id(0)
    add_up(total_ref, step, dot(x_ref[...], w_ref[...]))

    @pl.when(step == pl.num_programs(0) - 1)
    def _():
        bias, gain, offset = (vec_ref[r : r + 1, :] for r in rows_at)
        branch = total_ref[...] + bias
        out, unit, scale = norm_forward(res_ref[...] + branch, gain, offset)
        mixed_ref[...] = out.astype(bf16)
        valid = valid_rows(len_ref, branch.shape[0], length)
        grad, grad_gain, grad_bias = norm_backward(cot_ref[...].astype(f32), unit, scale, gain)
        low = grad.astype(bf16)
        dr_ref[...] = grad
        low_ref[...] = low
        sums_ref[0:1, :] = column_sum(jnp.where(valid, out * out, 0.0))
        sums_ref[1:2, :] = column_sum(jnp.where(valid, branch * branch, 0.0))
        sums_ref[2:3, :] = grad_gain
        sums_ref[3:4, :] = grad_bias
        sums_ref[4:5, :] = column_sum(low)
        sums_ref[5:8, :] = jnp.zeros((3, D), f32)


def turn(lengths, rows, weights, residual, cotangent, vec, rows_at):
    n_rows, depth = rows.shape
    return pl.pallas_call(
        partial(turn_kernel, n_rows // lengths.shape[0], rows_at),
        out_shape=[array((n_rows, D)), array((n_rows, D), f32), array((n_rows, D)), array((8, D), f32)],
        grid_spec=pltpu.PrefetchScalarGridSpec(
            num_scalar_prefetch=1,
            grid=(depth // BLOCK,),
            in_specs=[
                pl.BlockSpec((n_rows, BLOCK), lambda k, n: (0, k)),
                pl.BlockSpec((BLOCK, D), lambda k, n: (k, 0)),
                whole((n_rows, D)),
                whole((n_rows, D)),
                whole(vec.shape),
            ],
            out_specs=[whole((n_rows, D))] * 3 + [whole((8, D))],
            scratch_shapes=[pltpu.VMEM((n_rows, D), f32)],
        ),
        compiler_params=params(),
        cost_estimate=cost(1024),
    )(lengths, rows, weights, residual, cotangent, vec)


def hidden_back_kernel(e_ref, w_ref, slope_ref, du_ref, sums_ref):
    du = (dot_back(e_ref[...], w_ref[...]) * slope_ref[...].astype(f32)).astype(bf16)
    du_ref[...] = du
    sums_ref[...] = column_sum(du)


def hidden_back(grads, weights, slope):
    n_rows, width = slope.shape
    block = pl.BlockSpec((n_rows, BLOCK), lambda n: (0, n))
    return pl.pallas_call(
        hidden_back_kernel,
        out_shape=[array((n_rows, width)), array((1, width), f32)],
        grid=(width // BLOCK,),
        in_specs=[whole((n_rows, D)), pl.BlockSpec((BLOCK, D), lambda n: (n, 0)), block],
        out_specs=[block, pl.BlockSpec((1, BLOCK), lambda n: (0, n))],
        compiler_params=params(),
        cost_estimate=cost(1024),
    )(grads, weights, slope)


def join_back_kernel(row_at, g_ref, w_ref, dr_ref, unit_ref, scale_ref, vec_ref, after_ref, *outs):
    out_ref, low_ref, next_ref, sums_ref, total_ref = outs
    step = pl.program_id(0)
    add_up(total_ref, step, dot_back(g_ref[...], w_ref[...]))

    @pl.when(step == pl.num_programs(0) - 1)
    def _():
        grad, grad_gain, grad_bias = norm_backward(
            dr_ref[...] + total_ref[...], unit_ref[...], scale_ref[:, 0:1], vec_ref[row_at : row_at + 1, :]
        )
        low = grad.astype(bf16)
        out_ref[...] = grad
        low_ref[...] = low
        next_ref[...] = dot_back(low, after_ref[...]).astype(bf16)
        sums_ref[0:1, :] = grad_gain
        sums_ref[1:2, :] = grad_bias
        sums_ref[2:3, :] = column_sum(low)
        sums_ref[3:8, :] = jnp.zeros((5, D), f32)


def join_back(grads, weights, at, above, unit, scale, vec, row_at, after, after_at):
    slot = grads.ndim == 3
    n_rows, width = grads.shape[-2:]
    g_spec = (
        pl.BlockSpec((None, n_rows, BLOCK), lambda k: (0, 0, k))
        if slot
        else pl.BlockSpec((n_rows, BLOCK), lambda k: (0, k))
    )
    return pl.pallas_call(
        partial(join_back_kernel, row_at),
        out_shape=[array((n_rows, D), f32), array((n_rows, D)), array((n_rows, D)), array((8, D), f32)],
        grid=(width // BLOCK,),
        in_specs=[
            g_spec,
            pl.BlockSpec((D, BLOCK), lambda k: (0, at // BLOCK + k)),
            whole((n_rows, D)),
            whole((n_rows, D)),
            whole((n_rows, LANES)),
            whole(vec.shape),
            pl.BlockSpec((D, D), lambda k: (0, after_at // D)),
        ],
        out_specs=[whole((n_rows, D))] * 3 + [whole((8, D))],
        scratch_shapes=[pltpu.VMEM((n_rows, D), f32)],
        compiler_params=params(),
        cost_estimate=cost(1024),
    )(grads, weights, above, unit, scale, vec, after)


def input_grad_kernel(count, *refs):
    gs, ws, rest, o_ref = refs[:count], refs[count : 2 * count], refs[2 * count : -1], refs[-1]
    total = sum(dot_back(g[...], w[...]) for g, w in zip(gs, ws))
    if rest:
        total = total + rest[0][...]
    o_ref[...] = total.astype(bf16)


def input_grad(grads, slots, weights, ats, block, rest=()):
    n_rows = grads.shape[1]
    row_block = pl.BlockSpec((block, D), lambda r: (r, 0))
    return pl.pallas_call(
        partial(input_grad_kernel, len(slots)),
        out_shape=array((n_rows, D)),
        grid=(n_rows // block,),
        in_specs=[pl.BlockSpec((None, block, D), lambda r, s=s: (s, r, 0)) for s in slots]
        + [pl.BlockSpec((D, D), lambda r, a=a: (0, a // D)) for a in ats]
        + [row_block] * len(rest),
        out_specs=row_block,
        compiler_params=params(),
        cost_estimate=cost(1024),
    )(*[grads] * len(slots), *weights, *rest)


def state_grad_kernel(slot_ref, e_ref, g_ref, o_ref):
    o_ref[...] = dot_grad(e_ref[...], g_ref[...]).astype(bf16)


def state_grad(states, grads, slot):
    n_rows, block = states.shape[0], D // 2
    return pl.pallas_call(
        state_grad_kernel,
        out_shape=array((D, D)),
        grid_spec=pltpu.PrefetchScalarGridSpec(
            num_scalar_prefetch=1,
            grid=(D // block,),
            in_specs=[
                pl.BlockSpec((n_rows, block), lambda r, s: (0, r)),
                pl.BlockSpec((None, n_rows, D), lambda r, s: (s[0], 0, 0)),
            ],
            out_specs=pl.BlockSpec((block, D), lambda r, s: (r, 0)),
        ),
        compiler_params=params(),
        cost_estimate=cost(1024),
    )(jnp.stack([slot]).astype(jnp.int32), states, grads)


def two_heads(rows):
    low_half = lax.broadcasted_iota(jnp.int32, rows.shape, 1) < DH
    zero = jnp.zeros_like(rows)
    return jnp.concatenate([jnp.where(low_half, rows, zero), jnp.where(low_half, zero, rows)], axis=0)


def one_row(both):
    half = both.shape[0] // 2
    low_half = lax.broadcasted_iota(jnp.int32, (half, both.shape[1]), 1) < DH
    return jnp.where(low_half, both[:half], both[half:])


def masked_exp(queries, keys, valid, causal):
    scores = dot_back(queries, keys)
    place = lax.broadcasted_iota(jnp.int32, (1, scores.shape[1]), 1)
    if causal:
        rows = scores.shape[0] // 2
        spot = lax.broadcasted_iota(jnp.int32, scores.shape, 0)
        spot = jnp.where(spot >= rows, spot - rows, spot)
        spots = lax.broadcasted_iota(jnp.int32, scores.shape, 1)
        allowed = (spots <= spot) & (spots < valid)
        scores = jnp.where(allowed, scores, -1e30)
    else:
        scores = scores + jnp.where(place < valid, 0.0, -1e30)
    top = jnp.max(scores, axis=-1, keepdims=True)
    exponent = jnp.exp(scores - top)
    return exponent, 1.0 / jnp.sum(exponent, axis=-1, keepdims=True)


def attend_kernel(causal, len_ref, q_ref, k_ref, v_ref, x_ref, o_ref):
    valid = len_ref[pl.program_id(0)]
    o_ref[0] = x_ref[...]
    for at in range(0, q_ref.shape[1], LANES):
        pair = slice(at, at + LANES)
        queries = two_heads(q_ref[:, pair] * DH**-0.5)
        exponent, inverse = masked_exp(queries, k_ref[:, pair], valid, causal)
        o_ref[1, :, pair] = one_row(dot(exponent.astype(bf16), v_ref[:, pair]) * inverse).astype(bf16)


def attend_back_kernel(causal, len_ref, q_ref, k_ref, v_ref, do_ref, x_ref, dq_ref, *more):
    dkv_refs, sums_ref = more[:-1], more[-1]
    valid = len_ref[pl.program_id(0)]
    dq_ref[dq_ref.shape[0] - 1] = x_ref[...]
    sums_ref[2:8, :] = jnp.zeros((6, sums_ref.shape[1]), f32)
    for at in range(0, q_ref.shape[1], LANES):
        pair = slice(at, at + LANES)
        keys = k_ref[:, pair]
        queries = two_heads(q_ref[:, pair] * DH**-0.5)
        exponent, inverse = masked_exp(queries, keys, valid, causal)
        grads = two_heads(do_ref[:, pair])
        grad_probs = dot_back(grads, v_ref[:, pair])
        row_dot = jnp.sum(exponent * grad_probs, axis=-1, keepdims=True) * inverse
        grad_scores = (exponent * (grad_probs - row_dot)).astype(bf16)
        dq = one_row(dot(grad_scores, keys) * (inverse * DH**-0.5)).astype(bf16)
        dk = dot_grad(grad_scores, (queries * inverse).astype(bf16)).astype(bf16)
        dv = dot_grad(exponent.astype(bf16), (grads * inverse).astype(bf16)).astype(bf16)
        dq_ref[0, :, pair] = dq
        if dkv_refs:
            dkv_refs[0][0, :, pair], dkv_refs[0][1, :, pair] = dk, dv
        else:
            dq_ref[1, :, pair], dq_ref[2, :, pair] = dk, dv
        sums_ref[0:1, pair] = column_sum(dq)
        sums_ref[1:2, pair] = column_sum(dv)


def head_block(rows, at, group):
    return pl.BlockSpec((rows, LANES * group), lambda m, p, n: (m, at // group + p))


def slots_block(slots, rows, group):
    return pl.BlockSpec((slots, rows, LANES * group), lambda m, p, n: (0, m, p))


def attend(lengths, queries, keys, values, beside, seqs, causal, q_at, k_at, v_at):
    q_rows, k_rows = queries.shape[0] // seqs, keys.shape[0] // seqs
    group = PAIRS if causal else PAIRS // 2
    return pl.pallas_call(
        partial(attend_kernel, causal),
        out_shape=array((2, seqs * q_rows, D)),
        grid_spec=pltpu.PrefetchScalarGridSpec(
            num_scalar_prefetch=1,
            grid=(seqs, PAIRS // group),
            in_specs=[
                head_block(q_rows, q_at, group),
                head_block(k_rows, k_at, group),
                head_block(k_rows, v_at, group),
                head_block(q_rows, 0, group),
            ],
            out_specs=slots_block(2, q_rows, group),
        ),
        compiler_params=params(),
        cost_estimate=cost(1024),
    )(lengths, queries, keys, values, beside)


def attend_back(lengths, queries, keys, values, grads, beside, seqs, causal, q_at, k_at, v_at):
    q_rows, k_rows = queries.shape[0] // seqs, keys.shape[0] // seqs
    group = PAIRS if causal else PAIRS // 2
    slots = 4 if causal else 2
    out_shape = [array((slots, seqs * q_rows, D))]
    out_specs = [slots_block(slots, q_rows, group)]
    if not causal:
        out_shape.append(array((2, seqs * k_rows, D)))
        out_specs.append(slots_block(2, k_rows, group))
    out_shape.append(array((8 * seqs, D), f32))
    out_specs.append(head_block(8, 0, group))
    return pl.pallas_call(
        partial(attend_back_kernel, causal),
        out_shape=out_shape,
        grid_spec=pltpu.PrefetchScalarGridSpec(
            num_scalar_prefetch=1,
            grid=(seqs, PAIRS // group),
            in_specs=[
                head_block(q_rows, q_at, group),
                head_block(k_rows, k_at, group),
                head_block(k_rows, v_at, group),
                head_block(q_rows, 0, group),
                head_block(q_rows, 0, group),
            ],
            out_specs=out_specs,
        ),
        compiler_params=params(),
        cost_estimate=cost(1024),
    )(lengths, queries, keys, values, grads, beside)


def place_kernel(rows, idx_ref, *refs):
    slot = 0
    for piece in refs[:-1]:
        for j in range(piece.shape[0] // rows):
            at = pl.multiple_of(idx_ref[slot] * rows, rows)
            refs[-1][pl.ds(at, rows), :] = piece[j * rows : (j + 1) * rows, :]
            slot += 1


def place(pieces, slots):
    total, width = sum(piece.shape[0] for piece in pieces), pieces[0].shape[1]
    return pl.pallas_call(
        partial(place_kernel, total // len(slots)),
        out_shape=array((total, width), pieces[0].dtype),
        grid_spec=pltpu.PrefetchScalarGridSpec(
            num_scalar_prefetch=1,
            grid=(),
            in_specs=[pl.BlockSpec(memory_space=pltpu.VMEM)] * len(pieces),
            out_specs=pl.BlockSpec(memory_space=pltpu.VMEM),
        ),
        compiler_params=params(),
        cost_estimate=cost(1024),
    )(jnp.stack(slots).astype(jnp.int32), *pieces)


def under(first, second):
    return place([first, second], [jnp.int32(0), jnp.int32(1)])


def assemble_kernel(wide, rows, step, counts, idx_ref, *refs):
    pieces, (out_ref, held, in_sems, out_sems) = refs[: len(counts)], refs[len(counts) :]
    loads, at = [], 0
    for i, (piece, count) in enumerate(zip(pieces, counts)):
        loads.append(pltpu.make_async_copy(piece, held.at[pl.ds(at * step, count * step), :], in_sems.at[i]))
        at += count
    for load in loads:
        load.start()
    stores, copy = [], 0
    for load, count in zip(loads, counts):
        load.wait()
        for _ in range(count):
            unit, shard = idx_ref[0, copy], idx_ref[1, copy]
            if wide:
                target = out_ref.at[
                    pl.ds(pl.multiple_of(shard * rows, rows), rows), pl.ds(pl.multiple_of(unit * D, D), D)
                ]
            else:
                row = (shard * UNITS + unit) * rows
                target = out_ref.at[pl.ds(pl.multiple_of(row, rows), rows), :]
            store = pltpu.make_async_copy(held.at[pl.ds(copy * step, rows), :], target, out_sems.at[copy])
            store.start()
            stores.append(store)
            copy += 1
    for store in stores:
        store.wait()


def assemble(pieces, places, rows, step, wide):
    counts = [piece.shape[0] // step for piece in pieces]
    shards = len(places) // UNITS
    return pl.pallas_call(
        partial(assemble_kernel, wide, rows, step, counts),
        out_shape=array((shards * rows, UNITS * D) if wide else (UNITS * shards * rows, D)),
        grid_spec=pltpu.PrefetchScalarGridSpec(
            num_scalar_prefetch=1,
            grid=(),
            in_specs=[ANY] * len(pieces),
            out_specs=ANY,
            scratch_shapes=[
                pltpu.VMEM((len(places) * step, D), bf16),
                pltpu.SemaphoreType.DMA((len(pieces),)),
                pltpu.SemaphoreType.DMA((len(places),)),
            ],
        ),
        compiler_params=params(),
        cost_estimate=cost(1024),
    )(jnp.stack([jnp.stack([place[j] for place in places]) for j in range(2)]).astype(jnp.int32), *pieces)


def store_plane(step, plane, outs):
    @pl.when(step < 2)
    def _():
        outs[0][...] = plane

    @pl.when(step == 2)
    def _():
        outs[1][...] = plane

    @pl.when(step == 3)
    def _():
        outs[2][...] = plane


def planes_kernel(depth, idx_ref, *refs):
    x_mine, x_peer = refs[:depth], refs[depth : 2 * depth]
    inputs = jnp.concatenate(
        [jnp.concatenate([x[...] for x in xs], axis=1) for xs in (x_mine, x_peer)], axis=0
    )
    grads = jnp.concatenate([y[...] for y in refs[2 * depth : 2 * depth + 2]], axis=0)
    store_plane(pl.program_id(0), dot_grad(inputs, grads).astype(bf16), refs[-3:])


def sum_planes_kernel(depth, idx_ref, *refs):
    mine, peer, outs = refs[:depth], refs[depth : 2 * depth], refs[-3:]
    plane = jnp.concatenate([a[...].astype(f32) + b[...].astype(f32) for a, b in zip(mine, peer)], axis=0)
    store_plane(pl.program_id(0), plane.astype(bf16), outs)


def planes_call(kernel, table, in_specs, operands, plane, width):
    return pl.pallas_call(
        kernel,
        out_shape=[array((n * plane, width)) for n in (2, 1, 1)],
        grid_spec=pltpu.PrefetchScalarGridSpec(
            num_scalar_prefetch=1,
            grid=(4,),
            in_specs=in_specs,
            out_specs=[
                pl.BlockSpec((plane, width), lambda k, i: (jnp.minimum(k, 1), 0)),
                pl.BlockSpec((plane, width), lambda k, i: (0, 0)),
                pl.BlockSpec((plane, width), lambda k, i: (0, 0)),
            ],
        ),
        compiler_params=params(),
        cost_estimate=cost(1024),
    )(jnp.stack(table).astype(jnp.int32), *operands)


def column(spots, j):
    return jnp.stack([spot[j] for spot in spots])


def unit_planes(x_mine, x_peer, y_mine, y_peer, spots, z, stride, rows, width=D):
    depth, tokens = 4, x_mine.shape[1]
    blocks = x_mine.shape[2] // rows

    def x_spec(j):
        def at(k, i):
            block = i[0, k] + stride * i[3, j]
            return (block // blocks, 0, block % blocks)

        return pl.BlockSpec((None, tokens, rows), at)

    x_specs = [x_spec(j) for j in range(depth)]
    y_spec = pl.BlockSpec((None, tokens, width), lambda k, i: (i[1, k], 0, i[2, k]))
    table = [column(spots, j) for j in range(3)] + [jnp.stack([z, z ^ 2, z ^ 1, z ^ 3])]
    operands = [x_mine] * depth + [x_peer] * depth + [y_mine, y_peer]
    return planes_call(
        partial(planes_kernel, depth), table, x_specs * 2 + [y_spec] * 2, operands, depth * rows, width
    )


def sum_planes(mine, peer, spots, z, rows, width):
    depth = 4
    specs = [
        pl.BlockSpec((rows, width), lambda k, i, j=j: (2 * i[2, j] + i[0, k], i[1, k])) for j in range(depth)
    ]
    table = [column(spots, j) for j in range(2)] + [jnp.stack([z, z ^ 2, z ^ 1, z ^ 3])]
    return planes_call(
        partial(sum_planes_kernel, depth), table, specs * 2, [mine] * depth + [peer] * depth, depth * rows, width
    )


def adam_update(weight, first, second, grad, rate, decay):
    first = momentum_decay * first + (1.0 - momentum_decay) * grad
    second = square_decay * second + (1.0 - square_decay) * grad * grad
    update = first / fix_first / (jnp.sqrt(second / fix_second) + epsilon) + decay * weight
    return (weight - rate * update, first, second)


def adam_kernel(idx_ref, here_ref, there_ref, w_ref, m_ref, v_ref, *rest):
    w_out, m_out, v_out = rest[-3:]
    away = pl.program_id(0) ^ idx_ref[0]
    grad = jnp.where(away % 2 == 0, here_ref[...], there_ref[...]).astype(f32)
    if len(w_ref.shape) == 3:
        grad = grad[None]
    w_out[...], m_out[...], v_out[...] = adam_update(
        w_ref[...], m_ref[...], v_ref[...], grad, matrix_rate, matrix_decay
    )


def adam_units(spot, grads, state, block_shape, at, earlier=None):
    spec = pl.BlockSpec(block_shape, lambda u, i: at(u))
    rows, width = grads[0].shape[0] // 2, grads[0].shape[1]
    g_spec = pl.BlockSpec((rows, width), lambda u, i: ((u ^ i[0]) // 2, 0))
    extra = list(earlier) if earlier is not None else []
    outs = pl.pallas_call(
        adam_kernel,
        out_shape=[array(a.shape, f32) for a in state],
        grid_spec=pltpu.PrefetchScalarGridSpec(
            num_scalar_prefetch=1,
            grid=(UNITS,),
            in_specs=[g_spec] * 2 + [spec] * 3 + [ANY] * len(extra),
            out_specs=[spec] * 3,
        ),
        input_output_aliases={6 + i: i for i in range(len(extra))},
        compiler_params=params(),
        cost_estimate=cost(1024),
    )(jnp.stack([spot]).astype(jnp.int32), *grads, *state, *extra)
    return list(outs)


def hold(*values):
    return lax.optimization_barrier(values)


class Links:
    def __init__(self, n_dp, n_fsdp):
        self.n_fsdp, self.depth = n_fsdp, n_fsdp // 2
        spot = lax.axis_index("dp")
        shard = lax.axis_index("fsdp")
        self.spot, self.shard = spot, shard
        self.x, self.core = spot // 2, spot % 2
        self.z, self.y = shard // 2, shard % 2
        ids = [
            (x, c, z, y) for x in range(2) for c in range(2) for z in range(self.depth) for y in range(2)
        ]

        def number(x, c, z, y):
            return ((x * 2 + c) * self.depth + z) * 2 + y

        def perm(to):
            return [(number(*i), number(*to(*i))) for i in ids]

        flip_x = lambda x, c, z, y: (1 - x, c, z, y)
        flip_y = lambda x, c, z, y: (x, c, z, 1 - y)
        self.to_core = perm(lambda x, c, z, y: (x, 1 - c, z, y))
        self.to_x = perm(flip_x)
        self.to_y = perm(flip_y)
        self.swap1 = perm(lambda x, c, z, y: flip_y(x, c, z, y) if c == 0 else flip_x(x, c, z, y))
        self.swap2 = perm(lambda x, c, z, y: flip_x(x, c, z, y) if c == 0 else flip_y(x, c, z, y))
        self.to_z1 = perm(lambda x, c, z, y: (x, c, z ^ 1, y))
        self.to_z2 = perm(lambda x, c, z, y: (x, c, z ^ 2, y))

    def send(self, block, perm):
        return lax.ppermute(block, ("dp", "fsdp"), perm)

    def column(self, arrived):
        return place(arrived, [self.z ^ away for away in (0, 2, 1, 3)])

    def kinds(self, core):
        x, y = self.x, self.y
        return ((x, y), (x ^ core, y ^ (1 - core)), (x ^ (1 - core), y ^ core), (1 - x, 1 - y))

    def finish(self, pieces, rows, wide, more=0):
        places = [
            (ux * 2 + core, 2 * z + y)
            for core in (self.core, 1 - self.core)
            for ux, y in self.kinds(core)
            for z in range(self.depth)
        ]
        return assemble(pieces, places, rows, rows + more, wide)

    def vectors(self, here, cols):
        half = here[0].shape[0] // 2
        own, other = [
            piece.reshape(self.depth, -1, D)[:, -TAIL:, : 2 * cols] for piece in (here[0][:half], here[1][half:])
        ]
        pair = [jnp.where(self.y == 0, own, other), jnp.where(self.y == 0, other, own)]
        parts = [pair[f % 2][f // 2] for f in range(self.n_fsdp)]
        return jnp.concatenate(
            [
                jnp.concatenate([part[:, :cols] for part in parts], axis=1),
                jnp.concatenate([part[:1, cols:] for part in parts], axis=1),
            ],
            axis=0,
        )

    def plane_order(self):
        own, near, far, both = self.kinds(self.core)
        return far, both, near, own


def add_kernel(rows, count, *refs):
    ins, outs = refs[: len(rows)], refs[len(rows) :]
    total = sum(a[r : r + count, :].astype(f32) for a, r in zip(ins, rows)).astype(bf16)
    part = count // len(outs)
    for i, out in enumerate(outs):
        out[...] = total[i * part : (i + 1) * part]


def add_rows(terms, count, parts=1):
    width = terms[0][0].shape[1]
    vmem = pl.BlockSpec(memory_space=pltpu.VMEM)
    return pl.pallas_call(
        partial(add_kernel, [r for _, r in terms], count),
        out_shape=[array((count // parts, width))] * parts,
        in_specs=[vmem] * len(terms),
        out_specs=[vmem] * parts,
        compiler_params=params(),
        cost_estimate=cost(1024),
    )(*[a for a, _ in terms])


class Sum:
    def __init__(self, links, planes):
        self.links, self.parts, self.step = links, list(planes), 0

    def add(self):
        parts = self.parts
        if self.step == 1:
            got, second, kept = parts
            half = second.shape[0]
            parts[1:2] = add_rows([(second, 0), (got, half)], half)
        elif self.step == 2:
            got, got_second, kept = parts
            self.parts = add_rows([(kept, 0), (got, 0), (got_second, 0)], kept.shape[0], 2)
        elif self.step == 3:
            self.parts = add_rows([(part, 0) for part in parts], parts[0].shape[0], 2)
        elif self.step == 4:
            self.parts = add_rows([(part, 0) for part in parts], parts[0].shape[0])
        elif self.step == 5:
            self.parts = [under(*parts)]
        self.parts = list(self.parts)

    def send(self):
        links, parts = self.links, self.parts
        if self.step == 0:
            parts[0] = links.send(parts[0], links.swap2)
        elif self.step < 4:
            parts[1] = links.send(parts[1], (links.swap1, links.to_z1, links.to_z2)[self.step - 1])
        elif self.step == 4:
            parts.append(links.send(parts[0], links.to_x))
        else:
            parts.append(links.send(parts[0], links.to_core))
        self.step += 1


def advance(value, *sums):
    def held(value):
        value, *parts = hold(value, *(part for one in sums for part in one.parts))
        for one in sums:
            one.parts, parts = parts[: len(one.parts)], parts[len(one.parts) :]
        return value

    value = held(value)
    for one in sums:
        one.add()
    value = held(value)
    for one in sums:
        one.send()
    return value


def on_device(
    n_dp,
    n_fsdp,
    tokens,
    states,
    cotangent,
    seq_len,
    enc_len,
    attn_w,
    attn_m,
    attn_v,
    fc1_w,
    fc1_m,
    fc1_v,
    fc2_w,
    fc2_m,
    fc2_v,
    vec_w,
    vec_m,
    vec_v,
):
    micro, local, length, width = tokens.shape
    enc_length = states.shape[2]
    seqs = micro * local
    shard_rows = attn_w.shape[1]
    linked = n_dp == 4 and n_fsdp == 8 and vec_w.shape[0] == TAIL + 1
    token_rows = tokens.reshape(seqs * length, width)
    state_rows = states.reshape(seqs * enc_length, width)
    cotan_rows = cotangent.reshape(seqs * length, width)
    tok_lens = seq_len.reshape(seqs)
    enc_lens = enc_len.reshape(seqs)

    if linked:
        links = Links(n_dp, n_fsdp)
        spot, core = links.spot, links.core
        peer = lambda rows: links.send(rows, links.to_core)
        part_a = lax.dynamic_index_in_dim(attn_w, spot + jnp.where(spot < 2, 0, 3), 0, keepdims=False).astype(bf16)
        part_b = lax.dynamic_index_in_dim(attn_w, spot + jnp.where(spot < 3, 2, 4), 0, keepdims=False).astype(bf16)
        part_1 = lax.dynamic_slice_in_dim(fc1_w, spot * D, D, 1).astype(bf16)
        part_2 = lax.dynamic_slice_in_dim(fc2_w, spot * shard_rows, shard_rows, 0).astype(bf16)
        vec_cols = vec_w.shape[1]
        small = vec_w.astype(bf16)
        small = jnp.concatenate(
            [
                small[:TAIL],
                jnp.pad(small[TAIL:], ((0, TAIL - 1), (0, 0))),
                jnp.zeros((TAIL, D - 2 * vec_cols), bf16),
            ],
            axis=1,
        )
        part_a = jnp.concatenate([part_a, small], axis=0)

        to_z1, to_z2, swap1, swap2 = links.to_z1, links.to_z2, links.swap1, links.swap2
        send = links.send
        a_2, a_1 = send(part_a, to_z2), send(part_a, to_z1)
        part_b, a_2, a_1 = hold(part_b, a_2, a_1)
        a_3, b_2 = send(a_2, to_z1), send(part_b, to_z2)
        a_own = links.column([part_a, a_2, a_1, a_3])
        a_near = send(a_own, swap1)
        part_1, b_2, a_near = hold(part_1, b_2, a_near)

        a_here = [under(a_own, a_near)]
        a_here.append(send(a_here[0], swap2))
        b_1, c_2 = send(under(part_b, b_2), to_z1), send(part_1, to_z2)
        a_there = [peer(a_here[0])]
        part_2, b_1, c_2 = hold(part_2, b_1, c_2)
        b_own = links.column([part_b, b_2, b_1])
        b_near = send(b_own, swap1)
        c_1 = send(under(part_1, c_2), to_z1)
        part_2, c_1, b_near, a_here[1], a_there[0] = hold(part_2, c_1, b_near, a_here[1], a_there[0])

        b_here = [under(b_own, b_near)]
        b_here.append(send(b_here[0], swap2))
        c_own = links.column([part_1, c_2, c_1])
        c_near = send(c_own, swap1)
        d_2 = send(part_2, to_z2)
        a_there.append(peer(a_here[1]))
        first_w = links.finish(a_here + a_there, shard_rows, True, TAIL)
        vectors = links.vectors(a_here, vec_cols)
    else:
        vectors = lax.all_gather(vec_w.astype(bf16), "fsdp", axis=1, tiled=True)
        attn = lax.all_gather(attn_w.astype(bf16), "fsdp", axis=1, tiled=True)
        first_w = jnp.concatenate([attn[u] for u in FIRST], axis=1)
        second_w = jnp.concatenate([attn[u] for u in SECOND], axis=1)
        fc_in = lax.all_gather(fc1_w.astype(bf16), "fsdp", axis=0, tiled=True)
        fc_out = lax.all_gather(fc2_w.astype(bf16), "fsdp", axis=0, tiled=True)
    vec = vectors.astype(f32)
    zeros = jnp.zeros((1, width), f32)
    qk_bias = jnp.concatenate([vec[0:1], zeros], axis=1)
    kv_bias = jnp.concatenate([zeros, vec[4:5]], axis=1)
    fc_bias = vec[13:].reshape(1, -1)

    queries_keys = project(token_rows, first_w, qk_bias, 0)
    if linked:
        queries_keys, first_w, d_2 = hold(queries_keys, first_w, d_2)
        d_1 = send(under(part_2, d_2), to_z1)
        b_there = [peer(b_here[0])]
    cross_kv = project(state_rows, first_w, kv_bias, 2 * D)
    if linked:
        cross_kv, d_1, c_near, b_here[1], b_there[0] = hold(cross_kv, d_1, c_near, b_here[1], b_there[0])
        c_here = [under(c_own, c_near)]
        c_here.append(send(c_here[0], swap2))
        d_own = links.column([part_2, d_2, d_1])
        d_near = send(d_own, swap1)
        b_there.append(peer(b_here[1]))
        second_w = links.finish(b_here + b_there, shard_rows, True)
        c_there = [peer(c_here[0])]
    values = project(token_rows, second_w, vec[1:2], 0)
    self_in = attend(tok_lens, queries_keys, queries_keys, values, token_rows, seqs, True, 0, PAIRS, 0)
    if linked:
        self_in_peer = peer(self_in)
    normed_one, normed_one_low, unit_one, scale_one, sums_one = join(
        tok_lens, self_in, second_w, D, token_rows, vec, (2, 7, 8)
    )
    cross_q = project(normed_one_low, second_w, vec[3:4], 2 * D)
    cross_in = attend(enc_lens, cross_q, cross_kv, cross_kv, normed_one_low, seqs, False, 0, 0, PAIRS)
    normed_two, normed_two_low, unit_two, scale_two, sums_two = join(
        tok_lens, cross_in, second_w, 3 * D, normed_one, vec, (5, 9, 10)
    )
    if linked:
        normed_two_low, d_near, c_here[1], c_there[0] = hold(normed_two_low, d_near, c_here[1], c_there[0])
        d_here = [under(d_own, d_near)]
        d_here.append(send(d_here[0], swap2))
        c_there.append(peer(c_here[1]))
        fc_in = links.finish(c_here + c_there, shard_rows, True)
        d_there = [peer(d_here[0])]
        cross_in_peer = peer(cross_in)
    hidden, slope = hidden_layer(normed_two_low, fc_in, fc_bias)
    if linked:
        hidden_peer, normed_two_peer = peer(hidden), peer(normed_two_low)
        hidden, d_here[1], d_there[0] = hold(hidden, d_here[1], d_there[0])
        d_there.append(peer(d_here[1]))
        fc_out = links.finish(d_here + d_there, shard_rows, False)
    mixed, grad_three, grad_ffn, sums_three = turn(
        tok_lens, hidden, fc_out, normed_two, cotan_rows, vec, (6, 11, 12)
    )

    if linked:
        order = links.plane_order()

        def planes_of(x_mine, x_peer, y_mine, y_peer, x_at, y_at, stride, width=D):
            spots = [(x_at(ux, y), *y_at(ux)) for ux, y in order]
            slots = [a if a.ndim == 3 else a[None] for a in (x_mine, x_peer, y_mine, y_peer)]
            return unit_planes(*slots, spots, links.z, stride, shard_rows, width)

        grad_ffn_peer = peer(grad_ffn)
    grad_pre, sums_pre = hidden_back(grad_ffn, fc_out, slope)
    if linked:
        grad_pre, grad_ffn_peer = hold(grad_pre, grad_ffn_peer)
        grad_pre_peer = peer(grad_pre)
        planes = planes_of(
            hidden, hidden_peer, grad_ffn, grad_ffn_peer,
            lambda ux, y: y * UNITS + ux * 2 + core, lambda ux: (0 * ux, 0 * ux), 2 * UNITS,
        )
        sum_2 = Sum(links, planes)
        grad_pre, grad_pre_peer = hold(grad_pre, grad_pre_peer)
        grad_pre = advance(grad_pre, sum_2)
    else:
        grad_fc2 = dot_grad(hidden, grad_ffn).astype(bf16)
    grad_two, grad_cross, grad_ctx, sums_back_two = join_back(
        grad_pre, fc_in, 0, grad_three, unit_two, scale_two, vec, 9, second_w, 3 * D
    )
    if linked:
        planes = planes_of(
            normed_two_low, normed_two_peer, grad_pre, grad_pre_peer,
            lambda ux, y: y, lambda ux: (0 * ux, ux * 2 + core), 2,
        )
        sum_1 = Sum(links, planes)
        grad_ctx = advance(grad_ctx, sum_1)
    else:
        grad_fc1 = dot_grad(normed_two_low, grad_pre).astype(bf16)
    cross_grads, cross_dkv, sums_cross = attend_back(
        enc_lens, cross_q, cross_kv, cross_kv, grad_ctx, grad_cross, seqs, False, 0, 0, PAIRS
    )
    if linked:
        cross_grads = advance(cross_grads, sum_2)
        cross_grads_peer = peer(cross_grads)
    grad_one, grad_self, grad_ctx, sums_back_one = join_back(
        cross_grads, second_w, 2 * D, grad_two, unit_one, scale_one, vec, 7, second_w, D
    )
    if linked:
        grad_ctx, cross_grads_peer = hold(grad_ctx, cross_grads_peer)
        planes_t = planes_of(
            cross_in, cross_in_peer, cross_grads, cross_grads_peer,
            lambda ux, y: core * 2 * links.depth + y, lambda ux: (core + 0 * ux, ux), 2, D // 2,
        )
        grad_ctx, *planes_t = hold(grad_ctx, *planes_t)
    self_grads, sums_self = attend_back(
        tok_lens, queries_keys, queries_keys, values, grad_ctx, grad_self, seqs, True, 0, PAIRS, 0
    )
    sums_cross = sums_cross.reshape(seqs, 8, width).sum(axis=0)
    sums_self = sums_self.reshape(seqs, 8, width).sum(axis=0)
    grad_vec = jnp.concatenate(
        [
            sums_self[0:2],
            sums_back_one[2:3],
            sums_cross[0:2],
            sums_back_two[2:3],
            sums_three[4:5],
            sums_back_one[0:2],
            sums_back_two[0:2],
            sums_three[2:4],
            sums_pre.reshape(-1, width),
            sums_three[0:1],
            sums_one,
            sums_two,
            sums_three[1:2],
            jnp.broadcast_to(jnp.sum(seq_len).astype(f32), (1, width)),
        ],
        axis=0,
    )
    n_vec = vec_w.shape[0]
    if linked:
        self_grads = advance(self_grads, sum_1, sum_2)
        sum_t = Sum(links, planes_t)
        self_grads = advance(self_grads, sum_t)
        self_grads_peer, vec_peer = peer(self_grads), peer(grad_vec)
        self_grads, cross_dkv = hold(self_grads, cross_dkv)
        theirs = state_grad(state_rows, cross_dkv, 1 - core)
        theirs, self_grads_peer, vec_peer = hold(theirs, self_grads_peer, vec_peer)
        theirs = advance(theirs, sum_t, sum_2)
        grad_vec = grad_vec + vec_peer
        vec_peer = send(grad_vec, to_z1)
        planes = planes_of(
            self_in, self_in_peer, self_grads, self_grads_peer,
            lambda ux, y: y + 2 * links.depth * (ux * core), lambda ux: (ux * 2 + core, 0 * ux), 2,
        )
        sum_a = Sum(links, planes)
        theirs = advance(theirs, sum_a, sum_1)
        theirs_peer = peer(theirs)
        cross_dkv, theirs = hold(cross_dkv, theirs)
        mine = state_grad(state_rows, cross_dkv, core)
        mine, theirs_peer, vec_peer = hold(mine, theirs_peer, vec_peer)
        grad_vec = grad_vec + vec_peer
        vec_peer = send(grad_vec, to_z2)
        planes = sum_planes(
            mine, theirs_peer, [(y, ux) for ux, y in order], links.z, shard_rows, D // 2
        )
        sum_e = Sum(links, planes)
        self_grads = advance(self_grads, sum_e, sum_t, sum_2)
    else:
        grad_attn = jnp.stack(
            [dot_grad(self_in[u // 3], self_grads[u]) for u in range(4)]
            + [
                dot_grad(normed_one_low, cross_grads[0]),
                dot_grad(state_rows, cross_dkv[0]),
                dot_grad(state_rows, cross_dkv[1]),
                dot_grad(cross_in[1], cross_grads[1]),
            ]
        ).astype(bf16)
    grad_tokens = input_grad(
        self_grads, (0, 1, 2), (first_w, first_w, second_w), (0, D, 0), seqs * length, (grad_one,)
    )
    if linked:
        cross_dkv, grad_tokens, vec_peer = hold(cross_dkv, grad_tokens, vec_peer)
        cross_dkv = advance(cross_dkv, sum_1)
        grad_vec = grad_vec + vec_peer
        vec_peer = send(grad_vec, swap1)
    grad_states = input_grad(cross_dkv, (0, 1), (first_w, first_w), (2 * D, 3 * D), BLOCK)

    if linked:
        state_1, state_2 = (fc1_w, fc1_m, fc1_v), (fc2_w, fc2_m, fc2_v)
        attn_state = (attn_w, attn_m, attn_v)
        grad_states = advance(grad_states, sum_a, sum_t)
        grad_states, vec_peer = hold(grad_states, vec_peer)
        grad_vec = grad_vec + vec_peer
        vec_peer = send(grad_vec, swap2)
        grad_states = advance(grad_states, sum_e, sum_1, sum_2)
        fc2_new = adam_units(spot, sum_2.parts, state_2, (shard_rows, D), lambda u: (u, 0))
        fc2_new[0], vec_peer = hold(fc2_new[0], vec_peer)
        grad_vec = grad_vec + vec_peer
        fc2_new[0] = advance(fc2_new[0], sum_a, sum_t, sum_1)
        fc1_new = adam_units(spot, sum_1.parts, state_1, (shard_rows, D), lambda u: (0, u))
        fc1_new[0] = advance(fc1_new[0], sum_e, sum_t)
        fc1_new[0] = advance(fc1_new[0], sum_a)
        attn_new = adam_units(
            spot, sum_t.parts, attn_state, (1, shard_rows, D // 2), lambda u: (4 + 3 * (u % 2), 0, u // 2)
        )
        attn_new[0] = advance(attn_new[0], sum_e)
        attn_new[0] = advance(attn_new[0], sum_a)
        attn_new[0] = advance(attn_new[0], sum_e)
        attn_new[0] = advance(attn_new[0], sum_a)
        attn_new[0] = advance(attn_new[0], sum_e)
        attn_new = adam_units(
            spot, sum_a.parts, attn_state, (1, shard_rows, D), lambda u: (u, 0, 0), attn_new
        )
        attn_new = adam_units(
            spot, sum_e.parts, attn_state, (1, shard_rows, D // 2), lambda u: (5 + u % 2, 0, u // 2), attn_new
        )
    else:
        grad_vec = lax.psum(grad_vec, ("dp", "fsdp"))

        def owned(grad, dim):
            part = lax.psum_scatter(grad, "fsdp", scatter_dimension=dim, tiled=True)
            return lax.psum(part, "dp").astype(f32)

        attn_new = adam_update(attn_w, attn_m, attn_v, owned(grad_attn, 1), matrix_rate, matrix_decay)
        fc1_new = adam_update(fc1_w, fc1_m, fc1_v, owned(grad_fc1, 0), matrix_rate, matrix_decay)
        fc2_new = adam_update(fc2_w, fc2_m, fc2_v, owned(grad_fc2, 0), matrix_rate, matrix_decay)
    stats = grad_vec[n_vec:]
    stream_rms = jnp.sqrt(jnp.sum(stats[:4], axis=1) / (stats[4, 0] * D))
    cols = vec_w.shape[1]
    vec_grad = lax.dynamic_slice_in_dim(grad_vec[:n_vec], lax.axis_index("fsdp") * cols, cols, 1)
    vec_new = adam_update(vec_w, vec_m, vec_v, vec_grad, vector_rate, 0.0)
    return (
        mixed.reshape(tokens.shape),
        grad_tokens.reshape(tokens.shape),
        grad_states.reshape(states.shape),
        stream_rms,
        *attn_new,
        *fc1_new,
        *fc2_new,
        *vec_new,
    )


def solution(mesh):
    rows = P(None, ("dp", "fsdp"), None, None)
    lens = P(None, ("dp", "fsdp"))
    attn, fc, vec = P(None, "fsdp", None), P("fsdp", None), P(None, "fsdp")
    state = (attn,) * 3 + (fc,) * 6 + (vec,) * 3
    return jax.shard_map(
        partial(on_device, mesh.shape["dp"], mesh.shape["fsdp"]),
        mesh=mesh,
        in_specs=(rows, rows, rows, lens, lens) + state,
        out_specs=(rows, rows, rows, P()) + state,
        check_vma=False,
    )
```

time: 782 us -> 490 us (0.63)
  matrix products: 102 us -> 0 us
  waiting for transfers between devices: 196 us -> 109 us
  Pallas kernels: 288 us -> 233 us
  starting transfers between devices: 122 us -> 80.7 us
  other arithmetic: 33.8 us -> 5.39 us
  local copies, waits for them, and re-layouts: 31.2 us -> 52.9 us
    dot_general x19 -> x0, matrix products: 102 us -> none  [the longest x10 48.2 us: dot_back(): lax.dot_general(left, right, (((1,), (1,)), ((), ())), preferred_element_...]
    ppermute x94 -> x69, waiting for transfers between devices: 196 us -> 109 us  [send(): return lax.ppermute(block, ('dp', 'fsdp'), perm)]
    pallas_call x31 -> x69, Pallas kernels: 288 us -> 233 us  [the longest x5 29 us: planes_call(): pl.pallas_call(kernel, out_shape=[array((n * plane, width)) for n in (2,...]
    ppermute x94 -> x69, starting transfers between devices: 122 us -> 80.7 us  [send(): return lax.ppermute(block, ('dp', 'fsdp'), perm)]
    unnamed x129 -> x238, local copies, waits for them, and re-layouts: 23.6 us -> 41.3 us
    convert_element_type x16 -> x1, other arithmetic: 17.3 us -> 0.71 us  [on_device(): small = vec_w.astype(bf16)]
    reduce_sum x13 -> x4, other arithmetic: 8.68 us -> 0.77 us  [the longest x1 0.63 us: on_device(): jnp.sum(seq_len).astype(f32)]
  transfers between devices with their start and end apart: 94 -> 69, of which waited for: 27 -> 23; matrix products, arithmetic and copies ran while one was open for 14% -> 3% of each run, Pallas kernels for 33% -> 43%
where the time goes in v2:
time: 490 us; the launch traced here: 485 us
  Pallas kernels  233 us (48%)
  waiting for transfers between devices  109 us (22%)
  starting transfers between devices  80.7 us (16%)
  local copies, waits for them, and re-layouts  52.9 us (11%)
  other arithmetic  5.39 us (1%)
    ppermute x69, waiting for transfers between devices, send(): return lax.ppermute(block, ('dp', 'fsdp'), perm)  109 us
    ppermute x69, starting transfers between devices, send(): return lax.ppermute(block, ('dp', 'fsdp'), perm)  80.7 us
    unnamed x238, local copies, waits for them, and re-layouts  41.3 us
    pallas_call x5, Pallas kernels, planes_call(): pl.pallas_call(kernel, out_shape=[array((n * plane, width)) for n in (2,...  29 us
    pallas_call x2, Pallas kernels, attend_back(): pl.pallas_call(partial(attend_back_kernel, causal), out_shape=out_shape,...  29 us
    pallas_call x4, Pallas kernels, assemble(): pl.pallas_call(partial(assemble_kernel, wide, rows, step, counts), out_sh...  24 us
    pallas_call x5, Pallas kernels, adam_units(): pl.pallas_call(adam_kernel, out_shape=[array(a.shape, f32) for a in state...  21.5 us
    pallas_call x2, Pallas kernels, input_grad(): pl.pallas_call(partial(input_grad_kernel, len(slots)), out_shape=array((n...  18.6 us
  transfers between devices with their start and end apart: 69, of which 23 were waited for; matrix products, arithmetic and copies ran while one was open for 3% of the time, Pallas kernels for 43%

profile of v2, /device:TPU:0, one launch (start us, length us, event | category | flops | bytes accessed | tf_op | source)
XLA Modules:
  0.0 485.5 jit_solution(12396066264780377434)
XLA Ops:
  2.7 4.1 collective-permute-start
  8.4 11.9 %collective-permute-done.refs_1_ = bf16[144,1024]{1,0:T(8,128)(2,1)S(1)} collective-permute-done((bf16[144,1024]{1,0:T(8,128)(2,1)S(1)}, bf16[144,1024]{1,0:T(8,128)(2,1)S(1)}, u32[]{:S(2)}, u32[]{:S(2)}) %collective-permute-start) | collective-permute-done | bytes 294944 | tf_op jit(solution)/shard_map/ppermute | solution.py:726
  22.0 6.4 %collective-permute-done.2.refs_3_ = bf16[144,1024]{1,0:T(8,128)(2,1)S(1)} collective-permute-done((bf16[144,1024]{1,0:T(8,128)(2,1)S(1)}, bf16[144,1024]{1,0:T(8,128)(2,1)S(1)}, u32[]{:S(2)}, u32[]{:S(2)}) %collective-permute-start.2) | collective-permute-done | bytes 294944 | tf_op jit(solution)/shard_map/ppermute | solution.py:726
  30.3 3.3 collective-permute-start.3
  35.4 9.5 %collective-permute-done.3.refs_1_ = bf16[128,1024]{1,0:T(8,128)(2,1)S(1)} collective-permute-done((bf16[128,1024]{1,0:T(8,128)(2,1)S(1)}, bf16[128,1024]{1,0:T(8,128)(2,1)S(1)}, u32[]{:S(2)}, u32[]{:S(2)}) %collective-permute-start.3) | collective-permute-done | bytes 262176 | tf_op jit(solution)/shard_map/ppermute | solution.py:726
  52.6 3.4 collective-permute-start.6
  57.8 12.6 %collective-permute-done.6.refs_1_ = bf16[128,1024]{1,0:T(8,128)(2,1)S(1)} collective-permute-done((bf16[128,1024]{1,0:T(8,128)(2,1)}, bf16[128,1024]{1,0:T(8,128)(2,1)S(1)}, u32[]{:S(2)}, u32[]{:S(2)}) %collective-permute-start.6) | collective-permute-done | bytes 262176 | tf_op jit(solution)/shard_map/ppermute | solution.py:726
  79.4 4.0 collective-permute-start.7
  83.7 10.5 %collective-permute-done.7.refs_2_ = bf16[256,1024]{1,0:T(8,128)(2,1)} collective-permute-done((bf16[256,1024]{1,0:T(8,128)(2,1)}, bf16[256,1024]{1,0:T(8,128)(2,1)}, u32[]{:S(2)}, u32[]{:S(2)}) %collective-permute-start.7) | collective-permute-done | bytes 524320 | tf_op jit(solution)/shard_map/ppermute | solution.py:726
  105.2 6.7 %shard_map.293.w_ref.refs_3_.refs_4_.refs_2_ = bf16[1024,4096]{1,0:T(8,128)(2,1)} custom-call(s32[2,32]{1,0:T(2,128)S(1)} %pad_add_fusion.5.idx_ref, bf16[1152,1024]{1,0:T(8,128)(2,1)S(1)} %shard_map.289.refs_0_, bf16[1152,1024]{1,0:T(8,128)(2,1)} %collective-permute-done.9.refs_1_, bf16[1152,1024]{1,0:T(8,128)(2,1)} %collective-permute-done.10.refs_2_, ...), custom_call_target="tpu_custom_call" | custom-call | bytes 1024 | tf_op jit(solution)/shard_map/pallas_call | solution.py:552
  111.9 3.4 copy-done.1
  119.6 12.8 %shard_map.296.k_ref.v_ref = bf16[2048,2048]{1,0:T(8,128)(2,1)} custom-call(bf16[2048,1024]{1,0:T(8,128)(2,1)S(1)} %bitcast.126, bf16[1024,4096]{1,0:T(8,128)(2,1)} %shard_map.293.w_ref.refs_3_.refs_4_.refs_2_, f32[1,2048]{1,0:T(1,128)S(1)} %concatenate.30.b_ref), custom_call_target="tpu_custom_call" | custom-call | bytes 1024 | tf_op jit(solution)/shard_map/pallas_call | solution.py:111
  142.3 6.4 %shard_map.299.w_ref.after_ref.refs_5_ = bf16[1024,4096]{1,0:T(8,128)(2,1)} custom-call(s32[2,32]{1,0:T(2,128)S(1)} %pad_add_fusion.5.idx_ref, bf16[1024,1024]{1,0:T(8,128)(2,1)} %shard_map.295.refs_0_, bf16[1024,1024]{1,0:T(8,128)(2,1)} %collective-permute-done.15.refs_1_, bf16[1024,1024]{1,0:T(8,128)(2,1)} %collective-permute-done.16.refs_2_, ...), custom_call_target="tpu_custom_call" | custom-call | bytes 1024 | tf_op jit(solution)/shard_map/pallas_call | solution.py:552
  148.7 3.4 copy-done
  155.5 3.3 shard_map.302
  159.8 10.7 %shard_map.304.x_ref.refs_0_.refs_1_.refs_2_.refs_3_ = bf16[2,256,1024]{2,1,0:T(8,128)(2,1)S(1)} custom-call(s32[2]{0:T(128)S(1)} %bitcast.150, bf16[256,1024]{1,0:T(8,128)(2,1)S(1)} %shard_map.303.q_ref, bf16[2048,2048]{1,0:T(8,128)(2,1)} %shard_map.296.k_ref.v_ref, bf16[2048,2048]{1,0:T(8,128)(2,1)} %shard_map.296.k_ref.v_ref, ...), custom_call_target="tpu_custom_call" | custom-call | bytes 1024 | tf_op jit(solution)/shard_map/pallas_call | solution.py:442
  170.5 3.2 shard_map.305
  180.4 6.1 %shard_map.308.w_ref = bf16[1024,4096]{1,0:T(8,128)(2,1)} custom-call(s32[2,32]{1,0:T(2,128)S(1)} %pad_add_fusion.5.idx_ref, bf16[1024,1024]{1,0:T(8,128)(2,1)S(1)} %shard_map.307.refs_0_, bf16[1024,1024]{1,0:T(8,128)(2,1)} %collective-permute-done.19.refs_1_, bf16[1024,1024]{1,0:T(8,128)(2,1)} %collective-permute-done.20.refs_2_, ...), custom_call_target="tpu_custom_call" | custom-call | bytes 1024 | tf_op jit(solution)/shard_map/pallas_call | solution.py:552
  186.5 6.8 %shard_map.309 = (bf16[256,4096]{1,0:T(8,128)(2,1)S(1)}, bf16[256,4096]{1,0:T(8,128)(2,1)S(1)}) custom-call(bf16[256,1024]{1,0:T(8,128)(2,1)S(1)} %get-tuple-element.338.x_ref, bf16[1024,4096]{1,0:T(8,128)(2,1)} %shard_map.308.w_ref, f32[1,4096]{1,0:T(1,128)S(1)} %bitcast.144), custom_call_target="tpu_custom_call" | custom-call | bytes 1024 | tf_op jit(solution)/shard_map/pallas_call | solution.py:189
  193.3 10.7 %collective-permute-done.22.refs_1_ = bf16[1024,1024]{1,0:T(8,128)(2,1)S(1)} collective-permute-done((bf16[1024,1024]{1,0:T(8,128)(2,1)S(1)}, bf16[1024,1024]{1,0:T(8,128)(2,1)S(1)}, u32[]{:S(2)}, u32[]{:S(2)}) %collective-permute-start.22) | collective-permute-done | bytes 2097184 | tf_op jit(solution)/shard_map/ppermute | solution.py:726
  204.1 4.1 collective-permute-done.24.refs_3_
  208.2 4.8 shard_map.311.w_ref
  213.1 8.4 %shard_map.312 = (bf16[256,1024]{1,0:T(8,128)(2,1)}, f32[256,1024]{1,0:T(8,128)S(1)}, bf16[256,1024]{1,0:T(8,128)(2,1)S(1)}, f32[8,1024]{1,0:T(8,128)S(1)}) custom-call(s32[2]{0:T(128)S(1)} %bitcast.148, bf16[256,4096]{1,0:T(8,128)(2,1)S(1)} %get-tuple-element.343.x_ref, bf16[4096,1024]{1,0:T(8,128)(2,1)} %shard_map.311.w_ref, f32[256,1024]{1,0:T(8,128)S(1)} %copy-done.43, ...), custom_call_target="tpu_custom_call" | custom-call | bytes 1024 | tf_op jit(solution)/shard_map/pallas_call | solution.py:230
  222.0 6.8 %shard_map.313 = (bf16[256,4096]{1,0:T(8,128)(2,1)}, f32[1,4096]{1,0:T(1,128)S(1)}) custom-call(bf16[256,1024]{1,0:T(8,128)(2,1)S(1)} %get-tuple-element.348.e_ref, bf16[4096,1024]{1,0:T(8,128)(2,1)} %shard_map.311.w_ref, bf16[256,4096]{1,0:T(8,128)(2,1)S(1)} %get-tuple-element.349.slope_ref), custom_call_target="tpu_custom_call" | custom-call | bytes 1024 | tf_op jit(solution)/shard_map/pallas_call | solution.py:260
  232.9 7.0 %shard_map.314 = (bf16[1024,1024]{1,0:T(8,128)(2,1)}, bf16[512,1024]{1,0:T(8,128)(2,1)S(1)}, bf16[512,1024]{1,0:T(8,128)(2,1)S(1)}) custom-call(s32[4,4]{1,0:T(4,128)S(1)} %get-tuple-element.651.idx_ref, bf16[1,256,4096]{2,1,0:T(8,128)(2,1)S(1)} %bitcast.122, bf16[1,256,4096]{2,1,0:T(8,128)(2,1)S(1)} %bitcast.123, bf16[1,256,4096]{2,1,0:T(8,128)(2,1)S(1)} %bitcast.124, ...), custom_call_target="tpu_custom_call" | custom-call | bytes 1024 | tf_op jit(solution)/shard_map/pallas_call | solution.py:601
  241.7 8.1 %shard_map.315 = (f32[256,1024]{1,0:T(8,128)S(1)}, bf16[256,1024]{1,0:T(8,128)(2,1)S(1)}, bf16[256,1024]{1,0:T(8,128)(2,1)S(1)}, f32[8,1024]{1,0:T(8,128)S(1)}) custom-call(bf16[256,4096]{1,0:T(8,128)(2,1)} %get-tuple-element.357.g_ref, bf16[1024,4096]{1,0:T(8,128)(2,1)} %shard_map.308.w_ref, f32[256,1024]{1,0:T(8,128)S(1)} %copy-done.64, ...), custom_call_target="tpu_custom_call" | custom-call | bytes 1024 | tf_op jit(solution)/shard_map/pallas_call | solution.py:299
  249.9 7.5 %shard_map.316 = (bf16[1024,1024]{1,0:T(8,128)(2,1)}, bf16[512,1024]{1,0:T(8,128)(2,1)S(1)}, bf16[512,1024]{1,0:T(8,128)(2,1)S(1)}) custom-call(s32[4,4]{1,0:T(4,128)S(1)} %get-tuple-element.649.idx_ref, bf16[1,256,1024]{2,1,0:T(8,128)(2,1)S(1)} %bitcast.129, bf16[1,256,1024]{2,1,0:T(8,128)(2,1)S(1)} %bitcast.130, bf16[1,256,1024]{2,1,0:T(8,128)(2,1)S(1)} %bitcast.131, ...), custom_call_target="tpu_custom_call" | custom-call | bytes 1024 | tf_op jit(solution)/shard_map/pallas_call | solution.py:601
  258.9 21.0 %shard_map.317 = (bf16[2,256,1024]{2,1,0:T(8,128)(2,1)S(1)}, bf16[2,2048,1024]{2,1,0:T(8,128)(2,1)}, f32[16,1024]{1,0:T(8,128)S(1)}) custom-call(s32[2]{0:T(128)S(1)} %bitcast.151, bf16[256,1024]{1,0:T(8,128)(2,1)S(1)} %copy-done.21, bf16[2048,2048]{1,0:T(8,128)(2,1)} %shard_map.296.k_ref.v_ref, bf16[2048,2048]{1,0:T(8,128)(2,1)} %shard_map.296.k_ref.v_ref, ...), custom_call_target="tpu_custom_call" | custom-call | bytes 1024 | tf_op jit(solution)/shard_map/pallas_call | solution.py:472
  281.9 4.0 shard_map.319
  286.9 4.5 shard_map.320
  291.5 8.0 %shard_map.321 = (bf16[4,256,1024]{2,1,0:T(8,128)(2,1)S(1)}, f32[16,1024]{1,0:T(8,128)S(1)}) custom-call(s32[2]{0:T(128)S(1)} %bitcast.149, bf16[256,2048]{1,0:T(8,128)(2,1)S(1)} %copy-done.12, bf16[256,2048]{1,0:T(8,128)(2,1)S(1)} %copy-done.12, bf16[256,1024]{1,0:T(8,128)(2,1)S(1)} %copy-done.19, bf16[256,1024]{1,0:T(8,128)(2,1)S(1)} %get-tuple-element.386.do_ref, ...), custom_call_target="tpu_custom_call" | custom-call | bytes 1024 | tf_op jit(solution)/shard_map/pallas_call | solution.py:472
  318.9 7.5 %shard_map.324 = bf16[1024,1024]{1,0:T(8,128)(2,1)S(1)} custom-call(s32[1]{0:T(128)} %bitcast.75.slot_ref, bf16[2048,1024]{1,0:T(8,128)(2,1)S(1)} %bitcast.127, bf16[2,2048,1024]{2,1,0:T(8,128)(2,1)} %get-tuple-element.487.g_ref.refs_0_.refs_1_), custom_call_target="tpu_custom_call" | custom-call | bytes 1024 | tf_op jit(solution)/shard_map/pallas_call | solution.py:349
  329.2 4.4 collective-permute-done.36.refs_1_
  336.6 6.6 %shard_map.327 = (bf16[1024,1024]{1,0:T(8,128)(2,1)S(1)}, bf16[512,1024]{1,0:T(8,128)(2,1)S(1)}, bf16[512,1024]{1,0:T(8,128)(2,1)S(1)}) custom-call(s32[4,4]{1,0:T(4,128)S(1)} %copy-done.84, bf16[2,256,1024]{2,1,0:T(8,128)(2,1)S(1)} %shard_map.301.x_ref.refs_0_.refs_1_.refs_2_.refs_3_, ...), custom_call_target="tpu_custom_call" | custom-call | bytes 1024 | tf_op jit(solution)/shard_map/pallas_call | solution.py:601
  355.2 7.1 %shard_map.329.refs_0_.refs_1_.refs_2_.refs_3_ = bf16[1024,1024]{1,0:T(8,128)(2,1)S(1)} custom-call(s32[1]{0:T(128)} %bitcast.93.slot_ref, bf16[2048,1024]{1,0:T(8,128)(2,1)S(1)} %bitcast.128, bf16[2,2048,1024]{2,1,0:T(8,128)(2,1)} %get-tuple-element.487.g_ref.refs_0_.refs_1_), custom_call_target="tpu_custom_call" | custom-call | bytes 1024 | tf_op jit(solution)/shard_map/pallas_call | solution.py:349
  363.0 3.3 shard_map.330
  373.1 5.7 %shard_map.333 = bf16[256,1024]{1,0:T(8,128)(2,1)} custom-call(bf16[4,256,1024]{2,1,0:T(8,128)(2,1)S(1)} %get-tuple-element.475.refs_8_.refs_0_.refs_1_.refs_2_, bf16[4,256,1024]{2,1,0:T(8,128)(2,1)S(1)} %get-tuple-element.475.refs_8_.refs_0_.refs_1_.refs_2_, bf16[4,256,1024]{2,1,0:T(8,128)(2,1)S(1)} %get-tuple-element.475.refs_8_.refs_0_.refs_1_.refs_2_, ...), custom_call_target="tpu_custom_call" | custom-call | bytes 1024 | tf_op jit(solution)/shard_map/pallas_call | solution.py:330
  381.6 12.9 %shard_map.335 = bf16[2048,1024]{1,0:T(8,128)(2,1)} custom-call(bf16[2,2048,1024]{2,1,0:T(8,128)(2,1)S(1)} %bitcast.121, bf16[2,2048,1024]{2,1,0:T(8,128)(2,1)S(1)} %bitcast.121, bf16[1024,4096]{1,0:T(8,128)(2,1)} %shard_map.293.w_ref.refs_3_.refs_4_.refs_2_, bf16[1024,4096]{1,0:T(8,128)(2,1)} %shard_map.293.w_ref.refs_3_.refs_4_.refs_2_), custom_call_target="tpu_custom_call" | custom-call | bytes 1024 | tf_op jit(solution)/shard_map/pallas_call | solution.py:330
  396.6 3.4 collective-permute-start.50
  401.2 9.6 %collective-permute-done.48 = f32[22,1024]{1,0:T(8,128)S(1)} collective-permute-done((f32[22,1024]{1,0:T(8,128)S(1)}, f32[22,1024]{1,0:T(8,128)S(1)}, u32[]{:S(2)}, u32[]{:S(2)}) %collective-permute-start.48) | collective-permute-done | bytes 90144 | tf_op jit(solution)/shard_map/ppermute | solution.py:726
  419.5 3.7 shard_map.341
  433.5 3.9 shard_map.345
  443.0 4.2 shard_map.348
  447.2 3.9 collective-permute-done.61.refs_1_
  451.2 4.7 collective-permute-done.63.refs_1_
  457.9 6.5 %collective-permute-done.64.refs_1_ = bf16[128,512]{1,0:T(8,128)(2,1)S(1)} collective-permute-done((bf16[128,512]{1,0:T(8,128)(2,1)S(1)}, bf16[128,512]{1,0:T(8,128)(2,1)S(1)}, u32[]{:S(2)}, u32[]{:S(2)}) %collective-permute-start.64) | collective-permute-done | bytes 131104 | tf_op jit(solution)/shard_map/ppermute | solution.py:726
  475.6 5.4 %shard_map.355 = (f32[8,128,1024]{2,1,0:T(8,128)}, f32[8,128,1024]{2,1,0:T(8,128)}, f32[8,128,1024]{2,1,0:T(8,128)}) custom-call(s32[1]{0:T(128)} %bitcast.88.idx_ref, bf16[256,1024]{1,0:T(8,128)(2,1)S(1)} %shard_map.353.here_ref, ...), custom_call_target="tpu_custom_call", output_to_operand_aliasing={{0}: (6, {}), {1}: (7, {}), {2}: (8, {})} | custom-call | bytes 1024 | tf_op jit(solution)/shard_map/pallas_call | solution.py:677
  481.1 4.2 shard_map.356
  (468 shorter events, 161.2 us)
Async XLA Ops:
  2.7 17.5 %collective-permute-start = (bf16[144,1024]{1,0:T(8,128)(2,1)S(1)}, bf16[144,1024]{1,0:T(8,128)(2,1)S(1)}, u32[]{:S(2)}, u32[]{:S(2)}) collective-permute-start(bf16[144,1024]{1,0:T(8,128)(2,1)S(1)} %fusion.6.refs_0_), channel_id=1, source_target_pairs={{0,4},{1,5},{2,6},{3,7},{4,0},{5,1},{6,2},{7,3},{8,12},{9,13},{10,... | collective-permute-start | bytes 884744 | tf_op jit(solution)/shard_map/ppermute | solution.py:726
  6.8 13.6 %collective-permute-start.1 = (bf16[144,1024]{1,0:T(8,128)(2,1)S(1)}, bf16[144,1024]{1,0:T(8,128)(2,1)S(1)}, u32[]{:S(2)}, u32[]{:S(2)}) collective-permute-start(bf16[144,1024]{1,0:T(8,128)(2,1)S(1)} %fusion.6.refs_0_), channel_id=1, source_target_pairs={{0,2},{1,3},{2,0},{3,1},{4,6},{5,7},{6,4},{7,5},{8,10},{9,11},{10,... | collective-permute-start | bytes 884744 | tf_op jit(solution)/shard_map/ppermute | solution.py:726
  29.0 16.6 %collective-permute-start.4 = (bf16[576,1024]{1,0:T(8,128)(2,1)S(1)}, bf16[576,1024]{1,0:T(8,128)(2,1)S(1)}, u32[]{:S(2)}, u32[]{:S(2)}) collective-permute-start(bf16[576,1024]{1,0:T(8,128)(2,1)S(1)} %shard_map.288.refs_0_), channel_id=1, source_target_pairs={{0,1},{1,0},{2,3},{3,2},{4,5},{5,4},{6,7},{7,6},{8,24},{9,25},{10,... | collective-permute-start | bytes 3538952 | tf_op jit(solution)/shard_map/ppermute | solution.py:726
  30.3 14.6 %collective-permute-start.3 = (bf16[128,1024]{1,0:T(8,128)(2,1)S(1)}, bf16[128,1024]{1,0:T(8,128)(2,1)S(1)}, u32[]{:S(2)}, u32[]{:S(2)}) collective-permute-start(bf16[128,1024]{1,0:T(8,128)(2,1)S(1)} %get-tuple-element.315.refs_0_), channel_id=1, source_target_pairs={{0,4},{1,5},{2,6},{3,7},{4,0},{5,1},{6,2},{7,3},{8,12},{9,13},{10,... | collective-permute-start | bytes 786440 | tf_op jit(solution)/shard_map/ppermute | solution.py:726
  48.6 45.7 %collective-permute-start.9 = (bf16[1152,1024]{1,0:T(8,128)(2,1)S(1)}, bf16[1152,1024]{1,0:T(8,128)(2,1)}, u32[]{:S(2)}, u32[]{:S(2)}) collective-permute-start(bf16[1152,1024]{1,0:T(8,128)(2,1)S(1)} %shard_map.289.refs_0_), channel_id=1, source_target_pairs={{0,16},{1,17},{2,18},{3,19},{4,20},{5,21},{6,22},{7,23},{8,9},{9,8... | collective-permute-start | bytes 7077896 | tf_op jit(solution)/shard_map/ppermute | solution.py:726
  49.6 44.7 %collective-permute-start.10 = (bf16[1152,1024]{1,0:T(8,128)(2,1)S(1)}, bf16[1152,1024]{1,0:T(8,128)(2,1)}, u32[]{:S(2)}, u32[]{:S(2)}) collective-permute-start(bf16[1152,1024]{1,0:T(8,128)(2,1)S(1)} %shard_map.289.refs_0_), channel_id=1, source_target_pairs={{0,8},{1,9},{2,10},{3,11},{4,12},{5,13},{6,14},{7,15},{8,0},{9,1},... | collective-permute-start | bytes 7077896 | tf_op jit(solution)/shard_map/ppermute | solution.py:726
  51.0 20.1 %collective-permute-start.5 = (bf16[256,1024]{1,0:T(8,128)(2,1)}, bf16[256,1024]{1,0:T(8,128)(2,1)S(1)}, u32[]{:S(2)}, u32[]{:S(2)}) collective-permute-start(bf16[256,1024]{1,0:T(8,128)(2,1)} %shard_map.290), channel_id=1, source_target_pairs={{0,2},{1,3},{2,0},{3,1},{4,6},{5,7},{6,4},{7,5},{8,10},{9,11},{10,... | collective-permute-start | bytes 1572872 | tf_op jit(solution)/shard_map/ppermute | solution.py:726
  52.6 17.8 %collective-permute-start.6 = (bf16[128,1024]{1,0:T(8,128)(2,1)}, bf16[128,1024]{1,0:T(8,128)(2,1)S(1)}, u32[]{:S(2)}, u32[]{:S(2)}) collective-permute-start(bf16[128,1024]{1,0:T(8,128)(2,1)} %dynamic-slice_convert_fusion.1.refs_0_), channel_id=1, source_target_pairs={{0,4},{1,5},{2,6},{3,7},{4,0},{5,1},{6,2},{7,3},{8,12},{9,13},{10,... | collective-permute-start | bytes 786440 | tf_op jit(solution)/shard_map/ppermute | solution.py:726
  75.5 18.8 %collective-permute-start.8 = (bf16[512,1024]{1,0:T(8,128)(2,1)S(1)}, bf16[512,1024]{1,0:T(8,128)(2,1)}, u32[]{:S(2)}, u32[]{:S(2)}) collective-permute-start(bf16[512,1024]{1,0:T(8,128)(2,1)S(1)} %shard_map.292.refs_0_), channel_id=1, source_target_pairs={{0,1},{1,0},{2,3},{3,2},{4,5},{5,4},{6,7},{7,6},{8,24},{9,25},{10,... | collective-permute-start | bytes 3145736 | tf_op jit(solution)/shard_map/ppermute | solution.py:726
  79.4 14.9 %collective-permute-start.7 = (bf16[256,1024]{1,0:T(8,128)(2,1)}, bf16[256,1024]{1,0:T(8,128)(2,1)}, u32[]{:S(2)}, u32[]{:S(2)}) collective-permute-start(bf16[256,1024]{1,0:T(8,128)(2,1)} %shard_map.291), channel_id=1, source_target_pairs={{0,2},{1,3},{2,0},{3,1},{4,6},{5,7},{6,4},{7,5},{8,10},{9,11},{10,... | collective-permute-start | bytes 1572872 | tf_op jit(solution)/shard_map/ppermute | solution.py:726
  94.3 10.9 %collective-permute-start.11 = (bf16[1152,1024]{1,0:T(8,128)(2,1)}, bf16[1152,1024]{1,0:T(8,128)(2,1)S(1)}, u32[]{:S(2)}, u32[]{:S(2)}) collective-permute-start(bf16[1152,1024]{1,0:T(8,128)(2,1)} %collective-permute-done.9.refs_1_), channel_id=1, source_target_pairs={{0,8},{1,9},{2,10},{3,11},{4,12},{5,13},{6,14},{7,15},{8,0},{9,1},... | collective-permute-start | bytes 7077896 | tf_op jit(solution)/shard_map/ppermute | solution.py:726
  99.0 37.6 %collective-permute-start.15 = (bf16[1024,1024]{1,0:T(8,128)(2,1)}, bf16[1024,1024]{1,0:T(8,128)(2,1)}, u32[]{:S(2)}, u32[]{:S(2)}) collective-permute-start(bf16[1024,1024]{1,0:T(8,128)(2,1)} %shard_map.295.refs_0_), channel_id=1, source_target_pairs={{0,16},{1,17},{2,18},{3,19},{4,20},{5,21},{6,22},{7,23},{8,9},{9,8... | collective-permute-start | bytes 6291464 | tf_op jit(solution)/shard_map/ppermute | solution.py:726
  100.5 36.1 %collective-permute-start.16 = (bf16[1024,1024]{1,0:T(8,128)(2,1)}, bf16[1024,1024]{1,0:T(8,128)(2,1)}, u32[]{:S(2)}, u32[]{:S(2)}) collective-permute-start(bf16[1024,1024]{1,0:T(8,128)(2,1)} %shard_map.295.refs_0_), channel_id=1, source_target_pairs={{0,8},{1,9},{2,10},{3,11},{4,12},{5,13},{6,14},{7,15},{8,0},{9,1},... | collective-permute-start | bytes 6291464 | tf_op jit(solution)/shard_map/ppermute | solution.py:726
  100.8 16.4 %collective-permute-start.12 = (bf16[128,1024]{1,0:T(8,128)(2,1)S(1)}, bf16[128,1024]{1,0:T(8,128)(2,1)S(1)}, u32[]{:S(2)}, u32[]{:S(2)}) collective-permute-start(bf16[128,1024]{1,0:T(8,128)(2,1)S(1)} %copy-done.24), channel_id=1, source_target_pairs={{0,4},{1,5},{2,6},{3,7},{4,0},{5,1},{6,2},{7,3},{8,12},{9,13},{10,... | collective-permute-start | bytes 786440 | tf_op jit(solution)/shard_map/ppermute | solution.py:726
  103.6 28.8 %collective-permute-start.14 = (bf16[512,1024]{1,0:T(8,128)(2,1)S(1)}, bf16[512,1024]{1,0:T(8,128)(2,1)S(1)}, u32[]{:S(2)}, u32[]{:S(2)}) collective-permute-start(bf16[512,1024]{1,0:T(8,128)(2,1)S(1)} %shard_map.298.refs_0_), channel_id=1, source_target_pairs={{0,1},{1,0},{2,3},{3,2},{4,5},{5,4},{6,7},{7,6},{8,24},{9,25},{10,... | collective-permute-start | bytes 3145736 | tf_op jit(solution)/shard_map/ppermute | solution.py:726
  117.8 18.9 %collective-permute-start.13 = (bf16[256,1024]{1,0:T(8,128)(2,1)S(1)}, bf16[256,1024]{1,0:T(8,128)(2,1)S(1)}, u32[]{:S(2)}, u32[]{:S(2)}) collective-permute-start(bf16[256,1024]{1,0:T(8,128)(2,1)S(1)} %shard_map.297), channel_id=1, source_target_pairs={{0,2},{1,3},{2,0},{3,1},{4,6},{5,7},{6,4},{7,5},{8,10},{9,11},{10,... | collective-permute-start | bytes 1572872 | tf_op jit(solution)/shard_map/ppermute | solution.py:726
  138.6 37.4 %collective-permute-start.19 = (bf16[1024,1024]{1,0:T(8,128)(2,1)S(1)}, bf16[1024,1024]{1,0:T(8,128)(2,1)}, u32[]{:S(2)}, u32[]{:S(2)}) collective-permute-start(bf16[1024,1024]{1,0:T(8,128)(2,1)S(1)} %shard_map.307.refs_0_), channel_id=1, source_target_pairs={{0,16},{1,17},{2,18},{3,19},{4,20},{5,21},{6,22},{7,23},{8,9},{9,8... | collective-permute-start | bytes 6291464 | tf_op jit(solution)/shard_map/ppermute | solution.py:726
  140.1 35.9 %collective-permute-start.20 = (bf16[1024,1024]{1,0:T(8,128)(2,1)S(1)}, bf16[1024,1024]{1,0:T(8,128)(2,1)}, u32[]{:S(2)}, u32[]{:S(2)}) collective-permute-start(bf16[1024,1024]{1,0:T(8,128)(2,1)S(1)} %shard_map.307.refs_0_), channel_id=1, source_target_pairs={{0,8},{1,9},{2,10},{3,11},{4,12},{5,13},{6,14},{7,15},{8,0},{9,1},... | collective-permute-start | bytes 6291464 | tf_op jit(solution)/shard_map/ppermute | solution.py:726
  141.0 34.8 %collective-permute-start.18 = (bf16[512,1024]{1,0:T(8,128)(2,1)S(1)}, bf16[512,1024]{1,0:T(8,128)(2,1)}, u32[]{:S(2)}, u32[]{:S(2)}) collective-permute-start(bf16[512,1024]{1,0:T(8,128)(2,1)S(1)} %shard_map.306.refs_0_), channel_id=1, source_target_pairs={{0,1},{1,0},{2,3},{3,2},{4,5},{5,4},{6,7},{7,6},{8,24},{9,25},{10,... | collective-permute-start | bytes 3145736 | tf_op jit(solution)/shard_map/ppermute | solution.py:726
  177.9 26.1 %collective-permute-start.22 = (bf16[1024,1024]{1,0:T(8,128)(2,1)S(1)}, bf16[1024,1024]{1,0:T(8,128)(2,1)S(1)}, u32[]{:S(2)}, u32[]{:S(2)}) collective-permute-start(bf16[1024,1024]{1,0:T(8,128)(2,1)S(1)} %shard_map.310.refs_0_), channel_id=1, source_target_pairs={{0,16},{1,17},{2,18},{3,19},{4,20},{5,21},{6,22},{7,23},{8,9},{9,8... | collective-permute-start | bytes 6291464 | tf_op jit(solution)/shard_map/ppermute | solution.py:726
  179.5 24.5 %collective-permute-start.23 = (bf16[1024,1024]{1,0:T(8,128)(2,1)S(1)}, bf16[1024,1024]{1,0:T(8,128)(2,1)S(1)}, u32[]{:S(2)}, u32[]{:S(2)}) collective-permute-start(bf16[1024,1024]{1,0:T(8,128)(2,1)S(1)} %shard_map.310.refs_0_), channel_id=1, source_target_pairs={{0,8},{1,9},{2,10},{3,11},{4,12},{5,13},{6,14},{7,15},{8,0},{9,1},... | collective-permute-start | bytes 6291464 | tf_op jit(solution)/shard_map/ppermute | solution.py:726
  229.6 10.4 %collective-permute-start.26 = (bf16[256,4096]{1,0:T(8,128)(2,1)}, bf16[256,4096]{1,0:T(8,128)(2,1)}, u32[]{:S(2)}, u32[]{:S(2)}) collective-permute-start(bf16[256,4096]{1,0:T(8,128)(2,1)} %get-tuple-element.357.g_ref), channel_id=1, source_target_pairs={{0,8},{1,9},{2,10},{3,11},{4,12},{5,13},{6,14},{7,15},{8,0},{9,1},... | collective-permute-start | bytes 6291464 | tf_op jit(solution)/shard_map/ppermute | solution.py:726
  240.0 40.0 %collective-permute-start.29 = (bf16[1024,1024]{1,0:T(8,128)(2,1)}, bf16[1024,1024]{1,0:T(8,128)(2,1)S(1)}, u32[]{:S(2)}, u32[]{:S(2)}) collective-permute-start(bf16[1024,1024]{1,0:T(8,128)(2,1)} %get-tuple-element.369), channel_id=1, source_target_pairs={{0,16},{1,17},{2,18},{3,19},{4,20},{5,21},{6,22},{7,23},{8,9},{9,8... | collective-permute-start | bytes 6291464 | tf_op jit(solution)/shard_map/ppermute | solution.py:726
  257.4 42.1 %collective-permute-start.32 = (bf16[1024,1024]{1,0:T(8,128)(2,1)}, bf16[1024,1024]{1,0:T(8,128)(2,1)S(1)}, u32[]{:S(2)}, u32[]{:S(2)}) collective-permute-start(bf16[1024,1024]{1,0:T(8,128)(2,1)} %get-tuple-element.389), channel_id=1, source_target_pairs={{0,16},{1,17},{2,18},{3,19},{4,20},{5,21},{6,22},{7,23},{8,9},{9,8... | collective-permute-start | bytes 6291464 | tf_op jit(solution)/shard_map/ppermute | solution.py:726
  281.4 18.1 %collective-permute-start.33 = (bf16[512,1024]{1,0:T(8,128)(2,1)S(1)}, bf16[512,1024]{1,0:T(8,128)(2,1)}, u32[]{:S(2)}, u32[]{:S(2)}) collective-permute-start(bf16[512,1024]{1,0:T(8,128)(2,1)S(1)} %shard_map.318), channel_id=1, source_target_pairs={{0,1},{1,0},{2,3},{3,2},{4,5},{5,4},{6,7},{7,6},{8,24},{9,25},{10,... | collective-permute-start | bytes 3145736 | tf_op jit(solution)/shard_map/ppermute | solution.py:726
  304.4 22.0 %collective-permute-start.34 = (bf16[4,256,1024]{2,1,0:T(8,128)(2,1)S(1)}, bf16[4,256,1024]{2,1,0:T(8,128)(2,1)}, u32[]{:S(2)}, u32[]{:S(2)}) collective-permute-start(bf16[4,256,1024]{2,1,0:T(8,128)(2,1)S(1)} %get-tuple-element.475.refs_8_.refs_0_.refs_1_.refs_2_), channel_id=1, source_target_pairs={{0,8},{1,9},{2,10},{3,11},{4,12},{5,13},{6,14},{7,15},{8,0},{9,1},... | collective-permute-start | bytes 6291464 | tf_op jit(solution)/shard_map/ppermute | solution.py:726
  305.7 30.9 %collective-permute-start.38 = (bf16[2,256,1024]{2,1,0:T(8,128)(2,1)S(1)}, bf16[2,256,1024]{2,1,0:T(8,128)(2,1)}, u32[]{:S(2)}, u32[]{:S(2)}) collective-permute-start(bf16[2,256,1024]{2,1,0:T(8,128)(2,1)S(1)} %shard_map.301.x_ref.refs_0_.refs_1_.refs_2_.refs_3_), channel_id=1, source_target_pairs={{0,8},{1,9},{2,10},{3,11},{4,12},{5,13},{6,14},{7,15},{8,0},{9,1},... | collective-permute-start | bytes 3145736 | tf_op jit(solution)/shard_map/ppermute | solution.py:726
  307.5 26.1 %collective-permute-start.36 = (bf16[1024,512]{1,0:T(8,128)(2,1)}, bf16[1024,512]{1,0:T(8,128)(2,1)}, u32[]{:S(2)}, u32[]{:S(2)}) collective-permute-start(bf16[1024,512]{1,0:T(8,128)(2,1)} %copy-done.94), channel_id=1, source_target_pairs={{0,16},{1,17},{2,18},{3,19},{4,20},{5,21},{6,22},{7,23},{8,9},{9,8... | collective-permute-start | bytes 3145736 | tf_op jit(solution)/shard_map/ppermute | solution.py:726
  308.8 36.4 %collective-permute-start.39 = (bf16[512,1024]{1,0:T(8,128)(2,1)}, bf16[512,1024]{1,0:T(8,128)(2,1)}, u32[]{:S(2)}, u32[]{:S(2)}) collective-permute-start(bf16[512,1024]{1,0:T(8,128)(2,1)} %copy-done.58), channel_id=1, source_target_pairs={{0,1},{1,0},{2,3},{3,2},{4,5},{5,4},{6,7},{7,6},{8,24},{9,25},{10,... | collective-permute-start | bytes 3145736 | tf_op jit(solution)/shard_map/ppermute | solution.py:726
  315.0 14.2 %collective-permute-start.37 = (bf16[256,1024]{1,0:T(8,128)(2,1)}, bf16[256,1024]{1,0:T(8,128)(2,1)S(1)}, u32[]{:S(2)}, u32[]{:S(2)}) collective-permute-start(bf16[256,1024]{1,0:T(8,128)(2,1)} %copy-done.95), channel_id=1, source_target_pairs={{0,2},{1,3},{2,0},{3,1},{4,6},{5,7},{6,4},{7,5},{8,10},{9,11},{10,... | collective-permute-start | bytes 1572872 | tf_op jit(solution)/shard_map/ppermute | solution.py:726
  348.9 14.1 %collective-permute-start.40 = (bf16[1024,1024]{1,0:T(8,128)(2,1)S(1)}, bf16[1024,1024]{1,0:T(8,128)(2,1)S(1)}, u32[]{:S(2)}, u32[]{:S(2)}) collective-permute-start(bf16[1024,1024]{1,0:T(8,128)(2,1)S(1)} %shard_map.324), channel_id=1, source_target_pairs={{0,8},{1,9},{2,10},{3,11},{4,12},{5,13},{6,14},{7,15},{8,0},{9,1},... | collective-permute-start | bytes 6291464 | tf_op jit(solution)/shard_map/ppermute | solution.py:726
  348.9 45.6 %collective-permute-start.46 = (bf16[1024,1024]{1,0:T(8,128)(2,1)}, bf16[1024,1024]{1,0:T(8,128)(2,1)S(1)}, u32[]{:S(2)}, u32[]{:S(2)}) collective-permute-start(bf16[1024,1024]{1,0:T(8,128)(2,1)} %copy-done.93), channel_id=1, source_target_pairs={{0,16},{1,17},{2,18},{3,19},{4,20},{5,21},{6,22},{7,23},{8,9},{9,8... | collective-permute-start | bytes 6291464 | tf_op jit(solution)/shard_map/ppermute | solution.py:726
  350.3 16.8 %collective-permute-start.42 = (bf16[512,512]{1,0:T(8,128)(2,1)S(1)}, bf16[512,512]{1,0:T(8,128)(2,1)S(1)}, u32[]{:S(2)}, u32[]{:S(2)}) collective-permute-start(bf16[512,512]{1,0:T(8,128)(2,1)S(1)} %copy-done.81), channel_id=1, source_target_pairs={{0,1},{1,0},{2,3},{3,2},{4,5},{5,4},{6,7},{7,6},{8,24},{9,25},{10,... | collective-permute-start | bytes 1572872 | tf_op jit(solution)/shard_map/ppermute | solution.py:726
  351.3 15.8 %collective-permute-start.43 = (bf16[128,1024]{1,0:T(8,128)(2,1)}, bf16[128,1024]{1,0:T(8,128)(2,1)S(1)}, u32[]{:S(2)}, u32[]{:S(2)}) collective-permute-start(bf16[128,1024]{1,0:T(8,128)(2,1)} %copy-done.96), channel_id=1, source_target_pairs={{0,4},{1,5},{2,6},{3,7},{4,0},{5,1},{6,2},{7,3},{8,12},{9,13},{10,... | collective-permute-start | bytes 786440 | tf_op jit(solution)/shard_map/ppermute | solution.py:726
  362.3 19.1 %collective-permute-start.45 = (bf16[256,1024]{1,0:T(8,128)(2,1)}, bf16[256,1024]{1,0:T(8,128)(2,1)S(1)}, u32[]{:S(2)}, u32[]{:S(2)}) collective-permute-start(bf16[256,1024]{1,0:T(8,128)(2,1)} %get-tuple-element.481), channel_id=1, source_target_pairs={{0,2},{1,3},{2,0},{3,1},{4,6},{5,7},{6,4},{7,5},{8,10},{9,11},{10,... | collective-permute-start | bytes 1572872 | tf_op jit(solution)/shard_map/ppermute | solution.py:726
  368.7 42.1 %collective-permute-start.49 = (bf16[1024,512]{1,0:T(8,128)(2,1)}, bf16[1024,512]{1,0:T(8,128)(2,1)S(1)}, u32[]{:S(2)}, u32[]{:S(2)}) collective-permute-start(bf16[1024,512]{1,0:T(8,128)(2,1)} %get-tuple-element.504), channel_id=1, source_target_pairs={{0,16},{1,17},{2,18},{3,19},{4,20},{5,21},{6,22},{7,23},{8,9},{9,8... | collective-permute-start | bytes 3145736 | tf_op jit(solution)/shard_map/ppermute | solution.py:726
  369.5 25.0 %collective-permute-start.47 = (bf16[256,512]{1,0:T(8,128)(2,1)S(1)}, bf16[256,512]{1,0:T(8,128)(2,1)S(1)}, u32[]{:S(2)}, u32[]{:S(2)}) collective-permute-start(bf16[256,512]{1,0:T(8,128)(2,1)S(1)} %get-tuple-element.492), channel_id=1, source_target_pairs={{0,2},{1,3},{2,0},{3,1},{4,6},{5,7},{6,4},{7,5},{8,10},{9,11},{10,... | collective-permute-start | bytes 786440 | tf_op jit(solution)/shard_map/ppermute | solution.py:726
  371.0 10.4 %collective-permute-start.44 = (f32[22,1024]{1,0:T(8,128)S(1)}, f32[22,1024]{1,0:T(8,128)S(1)}, u32[]{:S(2)}, u32[]{:S(2)}) collective-permute-start(f32[22,1024]{1,0:T(8,128)S(1)} %add.172), channel_id=1, source_target_pairs={{0,4},{1,5},{2,6},{3,7},{4,0},{5,1},{6,2},{7,3},{8,12},{9,13},{10,... | collective-permute-start | bytes 270344 | tf_op jit(solution)/shard_map/ppermute | solution.py:726
  394.9 29.6 %collective-permute-start.54 = (bf16[512,1024]{1,0:T(8,128)(2,1)S(1)}, bf16[512,1024]{1,0:T(8,128)(2,1)S(1)}, u32[]{:S(2)}, u32[]{:S(2)}) collective-permute-start(bf16[512,1024]{1,0:T(8,128)(2,1)S(1)} %shard_map.336), channel_id=1, source_target_pairs={{0,1},{1,0},{2,3},{3,2},{4,5},{5,4},{6,7},{7,6},{8,24},{9,25},{10,... | collective-permute-start | bytes 3145736 | tf_op jit(solution)/shard_map/ppermute | solution.py:726
  396.0 14.8 %collective-permute-start.51 = (bf16[128,1024]{1,0:T(8,128)(2,1)S(1)}, bf16[128,1024]{1,0:T(8,128)(2,1)S(1)}, u32[]{:S(2)}, u32[]{:S(2)}) collective-permute-start(bf16[128,1024]{1,0:T(8,128)(2,1)S(1)} %shard_map.332.refs_0_), channel_id=1, source_target_pairs={{0,16},{1,17},{2,18},{3,19},{4,20},{5,21},{6,22},{7,23},{8,24},{9,... | collective-permute-start | bytes 786440 | tf_op jit(solution)/shard_map/ppermute | solution.py:726
  396.6 14.2 %collective-permute-start.50 = (bf16[128,1024]{1,0:T(8,128)(2,1)S(1)}, bf16[128,1024]{1,0:T(8,128)(2,1)S(1)}, u32[]{:S(2)}, u32[]{:S(2)}) collective-permute-start(bf16[128,1024]{1,0:T(8,128)(2,1)S(1)} %get-tuple-element.508), channel_id=1, source_target_pairs={{0,4},{1,5},{2,6},{3,7},{4,0},{5,1},{6,2},{7,3},{8,12},{9,13},{10,... | collective-permute-start | bytes 786440 | tf_op jit(solution)/shard_map/ppermute | solution.py:726
  400.0 10.7 %collective-permute-start.48 = (f32[22,1024]{1,0:T(8,128)S(1)}, f32[22,1024]{1,0:T(8,128)S(1)}, u32[]{:S(2)}, u32[]{:S(2)}) collective-permute-start(f32[22,1024]{1,0:T(8,128)S(1)} %add.173), channel_id=1, source_target_pairs={{0,1},{1,0},{2,3},{3,2},{4,5},{5,4},{6,7},{7,6},{8,24},{9,25},{10,... | collective-permute-start | bytes 270344 | tf_op jit(solution)/shard_map/ppermute | solution.py:726
  425.6 11.8 %collective-permute-start.58 = (bf16[512,512]{1,0:T(8,128)(2,1)S(1)}, bf16[512,512]{1,0:T(8,128)(2,1)S(1)}, u32[]{:S(2)}, u32[]{:S(2)}) collective-permute-start(bf16[512,512]{1,0:T(8,128)(2,1)S(1)} %shard_map.338), channel_id=1, source_target_pairs={{0,1},{1,0},{2,3},{3,2},{4,5},{5,4},{6,7},{7,6},{8,24},{9,25},{10,... | collective-permute-start | bytes 1572872 | tf_op jit(solution)/shard_map/ppermute | solution.py:726
  426.6 15.0 %collective-permute-start.62 = (bf16[256,1024]{1,0:T(8,128)(2,1)S(1)}, bf16[256,1024]{1,0:T(8,128)(2,1)S(1)}, u32[]{:S(2)}, u32[]{:S(2)}) collective-permute-start(bf16[256,1024]{1,0:T(8,128)(2,1)S(1)} %get-tuple-element.566), channel_id=1, source_target_pairs={{0,2},{1,3},{2,0},{3,1},{4,6},{5,7},{6,4},{7,5},{8,10},{9,11},{10,... | collective-permute-start | bytes 1572872 | tf_op jit(solution)/shard_map/ppermute | solution.py:726
  438.2 12.9 %collective-permute-start.61 = (bf16[256,512]{1,0:T(8,128)(2,1)S(1)}, bf16[256,512]{1,0:T(8,128)(2,1)S(1)}, u32[]{:S(2)}, u32[]{:S(2)}) collective-permute-start(bf16[256,512]{1,0:T(8,128)(2,1)S(1)} %get-tuple-element.557), channel_id=1, source_target_pairs={{0,2},{1,3},{2,0},{3,1},{4,6},{5,7},{6,4},{7,5},{8,10},{9,11},{10,... | collective-permute-start | bytes 786440 | tf_op jit(solution)/shard_map/ppermute | solution.py:726
  441.7 14.1 %collective-permute-start.63 = (bf16[128,1024]{1,0:T(8,128)(2,1)S(1)}, bf16[128,1024]{1,0:T(8,128)(2,1)S(1)}, u32[]{:S(2)}, u32[]{:S(2)}) collective-permute-start(bf16[128,1024]{1,0:T(8,128)(2,1)S(1)} %get-tuple-element.573), channel_id=1, source_target_pairs={{0,4},{1,5},{2,6},{3,7},{4,0},{5,1},{6,2},{7,3},{8,12},{9,13},{10,... | collective-permute-start | bytes 786440 | tf_op jit(solution)/shard_map/ppermute | solution.py:726
  455.9 11.0 %collective-permute-start.65 = (bf16[128,1024]{1,0:T(8,128)(2,1)S(1)}, bf16[128,1024]{1,0:T(8,128)(2,1)S(1)}, u32[]{:S(2)}, u32[]{:S(2)}) collective-permute-start(bf16[128,1024]{1,0:T(8,128)(2,1)S(1)} %shard_map.351.refs_0_), channel_id=1, source_target_pairs={{0,16},{1,17},{2,18},{3,19},{4,20},{5,21},{6,22},{7,23},{8,24},{9,... | collective-permute-start | bytes 786440 | tf_op jit(solution)/shard_map/ppermute | solution.py:726
  470.0 11.1 %collective-permute-start.67 = (bf16[256,512]{1,0:T(8,128)(2,1)S(1)}, bf16[256,512]{1,0:T(8,128)(2,1)S(1)}, u32[]{:S(2)}, u32[]{:S(2)}) collective-permute-start(bf16[256,512]{1,0:T(8,128)(2,1)S(1)} %shard_map.354.here_ref), channel_id=1, source_target_pairs={{0,8},{1,9},{2,10},{3,11},{4,12},{5,13},{6,14},{7,15},{8,0},{9,1},... | collective-permute-start | bytes 786440 | tf_op jit(solution)/shard_map/ppermute | solution.py:726
  (132 other events, 938.7 us)

commit v3 on v2

--- a/solution.py
+++ b/solution.py
@@ -29,12 +29,12 @@
 f32 = jnp.float32
 bf16 = jnp.bfloat16
 ANY = pl.BlockSpec(memory_space=pl.ANY)
-VMEM_BYTES = 44 * 1024 * 1024
+MIB = 1024 * 1024
 FIRST, SECOND = (0, 1, 5, 6), (2, 3, 4, 7)
 
 
-def params(**more):
-    return pltpu.CompilerParams(vmem_limit_bytes=VMEM_BYTES, **more)
+def params(mib):
+    return pltpu.CompilerParams(vmem_limit_bytes=mib * MIB)
 
 
 def cost(nbytes):
@@ -47,6 +47,10 @@
 
 def whole(shape):
     return pl.BlockSpec(shape, lambda *at: (0,) * len(shape))
+
+
+def far(values):
+    return pltpu.with_memory_space_constraint(values, pltpu.HBM)
 
 
 def dot(left, right):
@@ -118,7 +122,7 @@
             pl.BlockSpec((1, BLOCK), lambda n: (0, n)),
         ],
         out_specs=pl.BlockSpec((n_rows, BLOCK), lambda n: (0, n)),
-        compiler_params=params(),
+        compiler_params=params(22),
         cost_estimate=cost(1024),
     )(rows, weights, bias)
 
@@ -170,7 +174,7 @@
             out_specs=[whole((n_rows, D))] * 3 + [whole((n_rows, LANES)), whole((1, D))],
             scratch_shapes=[pltpu.VMEM((n_rows, D), f32)],
         ),
-        compiler_params=params(),
+        compiler_params=params(12),
         cost_estimate=cost(1024),
     )(lengths, rows, weights, residual, vec)
 
@@ -196,7 +200,7 @@
             pl.BlockSpec((1, BLOCK), lambda n: (0, n)),
         ],
         out_specs=[out_spec] * 2,
-        compiler_params=params(),
+        compiler_params=params(14),
         cost_estimate=cost(1024),
     )(rows, weights, bias)
 
@@ -243,7 +247,7 @@
             out_specs=[whole((n_rows, D))] * 3 + [whole((8, D))],
             scratch_shapes=[pltpu.VMEM((n_rows, D), f32)],
         ),
-        compiler_params=params(),
+        compiler_params=params(14),
         cost_estimate=cost(1024),
     )(lengths, rows, weights, residual, cotangent, vec)
 
@@ -263,7 +267,7 @@
         grid=(width // BLOCK,),
         in_specs=[whole((n_rows, D)), pl.BlockSpec((BLOCK, D), lambda n: (n, 0)), block],
         out_specs=[block, pl.BlockSpec((1, BLOCK), lambda n: (0, n))],
-        compiler_params=params(),
+        compiler_params=params(14),
         cost_estimate=cost(1024),
     )(grads, weights, slope)
 
@@ -311,9 +315,9 @@
         ],
         out_specs=[whole((n_rows, D))] * 3 + [whole((8, D))],
         scratch_shapes=[pltpu.VMEM((n_rows, D), f32)],
-        compiler_params=params(),
-        cost_estimate=cost(1024),
-    )(grads, weights, above, unit, scale, vec, after)
+        compiler_params=params(18),
+        cost_estimate=cost(1024),
+    )(grads, far(weights), above, far(unit), scale, vec, far(after))
 
 
 def input_grad_kernel(count, *refs):
@@ -335,9 +339,9 @@
         + [pl.BlockSpec((D, D), lambda r, a=a: (0, a // D)) for a in ats]
         + [row_block] * len(rest),
         out_specs=row_block,
-        compiler_params=params(),
-        cost_estimate=cost(1024),
-    )(*[grads] * len(slots), *weights, *rest)
+        compiler_params=params(22),
+        cost_estimate=cost(1024),
+    )(*[far(grads)] * len(slots), *[far(w) for w in weights], *rest)
 
 
 def state_grad_kernel(slot_ref, e_ref, g_ref, o_ref):
@@ -358,9 +362,9 @@
             ],
             out_specs=pl.BlockSpec((block, D), lambda r, s: (r, 0)),
         ),
-        compiler_params=params(),
-        cost_estimate=cost(1024),
-    )(jnp.stack([slot]).astype(jnp.int32), states, grads)
+        compiler_params=params(18),
+        cost_estimate=cost(1024),
+    )(jnp.stack([slot]).astype(jnp.int32), states, far(grads))
 
 
 def two_heads(rows):
@@ -453,7 +457,7 @@
             ],
             out_specs=slots_block(2, q_rows, group),
         ),
-        compiler_params=params(),
+        compiler_params=params(20),
         cost_estimate=cost(1024),
     )(lengths, queries, keys, values, beside)
 
@@ -484,7 +488,7 @@
             ],
             out_specs=out_specs,
         ),
-        compiler_params=params(),
+        compiler_params=params(22),
         cost_estimate=cost(1024),
     )(lengths, queries, keys, values, grads, beside)
 
@@ -509,7 +513,7 @@
             in_specs=[pl.BlockSpec(memory_space=pltpu.VMEM)] * len(pieces),
             out_specs=pl.BlockSpec(memory_space=pltpu.VMEM),
         ),
-        compiler_params=params(),
+        compiler_params=params(6),
         cost_estimate=cost(1024),
     )(jnp.stack(slots).astype(jnp.int32), *pieces)
 
@@ -563,7 +567,7 @@
                 pltpu.SemaphoreType.DMA((len(places),)),
             ],
         ),
-        compiler_params=params(),
+        compiler_params=params(10),
         cost_estimate=cost(1024),
     )(jnp.stack([jnp.stack([place[j] for place in places]) for j in range(2)]).astype(jnp.int32), *pieces)
 
@@ -611,7 +615,7 @@
                 pl.BlockSpec((plane, width), lambda k, i: (0, 0)),
             ],
         ),
-        compiler_params=params(),
+        compiler_params=params(13),
         cost_estimate=cost(1024),
     )(jnp.stack(table).astype(jnp.int32), *operands)
 
@@ -634,6 +638,8 @@
     x_specs = [x_spec(j) for j in range(depth)]
     y_spec = pl.BlockSpec((None, tokens, width), lambda k, i: (i[1, k], 0, i[2, k]))
     table = [column(spots, j) for j in range(3)] + [jnp.stack([z, z ^ 2, z ^ 1, z ^ 3])]
+    if x_peer.shape[2] > 2 * D:
+        x_mine, x_peer = far(x_mine), far(x_peer)
     operands = [x_mine] * depth + [x_peer] * depth + [y_mine, y_peer]
     return planes_call(
         partial(planes_kernel, depth), table, x_specs * 2 + [y_spec] * 2, operands, depth * rows, width
@@ -674,6 +680,7 @@
     rows, width = grads[0].shape[0] // 2, grads[0].shape[1]
     g_spec = pl.BlockSpec((rows, width), lambda u, i: ((u ^ i[0]) // 2, 0))
     extra = list(earlier) if earlier is not None else []
+    state = [far(a) for a in state]
     outs = pl.pallas_call(
         adam_kernel,
         out_shape=[array(a.shape, f32) for a in state],
@@ -684,14 +691,18 @@
             out_specs=[spec] * 3,
         ),
         input_output_aliases={6 + i: i for i in range(len(extra))},
-        compiler_params=params(),
+        compiler_params=params(8),
         cost_estimate=cost(1024),
     )(jnp.stack([spot]).astype(jnp.int32), *grads, *state, *extra)
     return list(outs)
 
 
+CLOCK = []
+
+
 def hold(*values):
-    return lax.optimization_barrier(values)
+    CLOCK[0], *held = lax.optimization_barrier((CLOCK[0], *values))
+    return held
 
 
 class Links:
@@ -743,9 +754,17 @@
 
     def vectors(self, here, cols):
         half = here[0].shape[0] // 2
-        own, other = [
-            piece.reshape(self.depth, -1, D)[:, -TAIL:, : 2 * cols] for piece in (here[0][:half], here[1][half:])
-        ]
+        step = half // self.depth
+
+        def tails(piece, first):
+            return jnp.stack(
+                [
+                    lax.slice(piece, (first + (z + 1) * step - TAIL, 0), (first + (z + 1) * step, 2 * cols))
+                    for z in range(self.depth)
+                ]
+            )
+
+        own, other = tails(here[0], 0), tails(here[1], half)
         pair = [jnp.where(self.y == 0, own, other), jnp.where(self.y == 0, other, own)]
         parts = [pair[f % 2][f // 2] for f in range(self.n_fsdp)]
         return jnp.concatenate(
@@ -777,7 +796,7 @@
         out_shape=[array((count // parts, width))] * parts,
         in_specs=[vmem] * len(terms),
         out_specs=[vmem] * parts,
-        compiler_params=params(),
+        compiler_params=params(8),
         cost_estimate=cost(1024),
     )(*[a for a, _ in terms])
 
@@ -816,20 +835,56 @@
         self.step += 1
 
 
-def advance(value, *sums):
-    def held(value):
-        value, *parts = hold(value, *(part for one in sums for part in one.parts))
-        for one in sums:
-            one.parts, parts = parts[: len(one.parts)], parts[len(one.parts) :]
-        return value
-
-    value = held(value)
+def land(sums, *values):
+    parts = hold(*values, *(part for one in sums for part in one.parts))
+    values, parts = parts[: len(values)], parts[len(values) :]
+    for one in sums:
+        one.parts, parts = parts[: len(one.parts)], parts[len(one.parts) :]
+    return values
+
+
+def add(*sums):
     for one in sums:
         one.add()
-    value = held(value)
+
+
+def go(*sums):
     for one in sums:
         one.send()
-    return value
+
+
+PLAN = (
+    ("", "give grad_ffn", "give hidden"),
+    ("hidden", "land grad_ffn", "land hidden", "give grad_pre", "give normed_two_low"),
+    ("planes_2", "land grad_pre", "land normed_two_low", "sum 2"),
+    ("two",),
+    ("planes_1",),
+    ("", "sum 1"),
+    ("cross", "sum 2", "give cross_grads"),
+    ("one", "land cross_grads"),
+    ("self",),
+    ("planes_t", "sum 1", "sum 2", "give self_grads", "vec c"),
+    ("", "sum t"),
+    ("theirs", "land self_grads", "land vec", "sum 2", "give theirs"),
+    ("planes_a", "vec z1", "sum 1", "sum t"),
+    ("", "sum a"),
+    ("mine", "land theirs", "land vec", "vec z2", "sum t"),
+    ("planes_e", "sum 2"),
+    ("tokens", "vec s1", "sum 1", "sum e", "land vec"),
+    ("", "sum a", "sum t", "sum 2"),
+    ("states", "land vec", "vec s2"),
+    ("", "sum 1"),
+    ("adam_2", "sum e", "sum a"),
+    ("", "sum t", "sum 1"),
+    ("adam_1", "sum e", "sum t", "land vec"),
+    ("", "sum a"),
+    ("adam_t", "sum e"),
+    ("", "sum a"),
+    ("", "sum e"),
+    ("", "sum a", "sum e"),
+    ("adam_e",),
+    ("adam_a",),
+)
 
 
 def on_device(
@@ -886,27 +941,32 @@
 
         to_z1, to_z2, swap1, swap2 = links.to_z1, links.to_z2, links.swap1, links.swap2
         send = links.send
+        CLOCK[:] = [vec_m]
         a_2, a_1 = send(part_a, to_z2), send(part_a, to_z1)
-        part_b, a_2, a_1 = hold(part_b, a_2, a_1)
-        a_3, b_2 = send(a_2, to_z1), send(part_b, to_z2)
+        part_a, part_b, a_2, a_1 = hold(part_a, part_b, a_2, a_1)
+
+        a_3, b_2, b_1 = send(a_2, to_z1), send(part_b, to_z2), send(part_b, to_z1)
+        (a_3,) = hold(a_3)
         a_own = links.column([part_a, a_2, a_1, a_3])
         a_near = send(a_own, swap1)
-        part_1, b_2, a_near = hold(part_1, b_2, a_near)
+        part_b, part_1, b_2, b_1, a_near = hold(part_b, part_1, b_2, b_1, a_near)
 
         a_here = [under(a_own, a_near)]
         a_here.append(send(a_here[0], swap2))
-        b_1, c_2 = send(under(part_b, b_2), to_z1), send(part_1, to_z2)
-        a_there = [peer(a_here[0])]
-        part_2, b_1, c_2 = hold(part_2, b_1, c_2)
-        b_own = links.column([part_b, b_2, b_1])
+        b_3, c_2 = send(b_2, to_z1), send(part_1, to_z2)
+        part_1, b_3, c_2 = hold(part_1, b_3, c_2)
+        b_own = links.column([part_b, b_2, b_1, b_3])
         b_near = send(b_own, swap1)
         c_1 = send(under(part_1, c_2), to_z1)
-        part_2, c_1, b_near, a_here[1], a_there[0] = hold(part_2, c_1, b_near, a_here[1], a_there[0])
-
+        a_there = [peer(a_here[0])]
+        part_1, c_1 = hold(part_1, c_1)
+        c_own = links.column([part_1, c_2, c_1])
+        c_own, part_2, b_own, b_near, *held = hold(c_own, part_2, b_own, b_near, *a_here, a_there[0])
+        a_here, a_there = held[:2], held[2:]
+
+        c_near = send(c_own, swap1)
         b_here = [under(b_own, b_near)]
         b_here.append(send(b_here[0], swap2))
-        c_own = links.column([part_1, c_2, c_1])
-        c_near = send(c_own, swap1)
         d_2 = send(part_2, to_z2)
         a_there.append(peer(a_here[1]))
         first_w = links.finish(a_here + a_there, shard_rows, True, TAIL)
@@ -926,15 +986,16 @@
 
     queries_keys = project(token_rows, first_w, qk_bias, 0)
     if linked:
-        queries_keys, first_w, d_2 = hold(queries_keys, first_w, d_2)
+        queries_keys, first_w, part_2, d_2 = hold(queries_keys, first_w, part_2, d_2)
         d_1 = send(under(part_2, d_2), to_z1)
         b_there = [peer(b_here[0])]
     cross_kv = project(state_rows, first_w, kv_bias, 2 * D)
     if linked:
-        cross_kv, d_1, c_near, b_here[1], b_there[0] = hold(cross_kv, d_1, c_near, b_here[1], b_there[0])
+        cross_kv, d_1 = hold(cross_kv, d_1)
+        d_own = links.column([part_2, d_2, d_1])
+        d_own, c_own, c_near, b_here[1], b_there[0] = hold(d_own, c_own, c_near, b_here[1], b_there[0])
         c_here = [under(c_own, c_near)]
         c_here.append(send(c_here[0], swap2))
-        d_own = links.column([part_2, d_2, d_1])
         d_near = send(d_own, swap1)
         b_there.append(peer(b_here[1]))
         second_w = links.finish(b_here + b_there, shard_rows, True)
@@ -952,7 +1013,9 @@
         tok_lens, cross_in, second_w, 3 * D, normed_one, vec, (5, 9, 10)
     )
     if linked:
-        normed_two_low, d_near, c_here[1], c_there[0] = hold(normed_two_low, d_near, c_here[1], c_there[0])
+        normed_two_low, d_own, d_near, c_here[1], c_there[0] = hold(
+            normed_two_low, d_own, d_near, c_here[1], c_there[0]
+        )
         d_here = [under(d_own, d_near)]
         d_here.append(send(d_here[0], swap2))
         c_there.append(peer(c_here[1]))
@@ -961,181 +1024,225 @@
         cross_in_peer = peer(cross_in)
     hidden, slope = hidden_layer(normed_two_low, fc_in, fc_bias)
     if linked:
-        hidden_peer, normed_two_peer = peer(hidden), peer(normed_two_low)
-        hidden, d_here[1], d_there[0] = hold(hidden, d_here[1], d_there[0])
+        hidden, normed_two_low, d_here[1], d_there[0] = hold(hidden, normed_two_low, d_here[1], d_there[0])
         d_there.append(peer(d_here[1]))
         fc_out = links.finish(d_here + d_there, shard_rows, False)
     mixed, grad_three, grad_ffn, sums_three = turn(
         tok_lens, hidden, fc_out, normed_two, cotan_rows, vec, (6, 11, 12)
     )
 
+    env = dict(
+        hidden=hidden, normed_two_low=normed_two_low, grad_three=grad_three, grad_ffn=grad_ffn, self_in=self_in,
+        cross_in=cross_in, sums_three=sums_three,
+    )
+
+    def k_hidden(e):
+        e["grad_pre"], e["sums_pre"] = hidden_back(e["grad_ffn"], fc_out, slope)
+
+    def k_two(e):
+        e["grad_two"], e["grad_cross"], e["grad_ctx"], e["sums_two"] = join_back(
+            e["grad_pre"], fc_in, 0, grad_three, unit_two, scale_two, vec, 9, second_w, 3 * D
+        )
+
+    def k_cross(e):
+        e["cross_grads"], e["cross_dkv"], e["sums_cross"] = attend_back(
+            enc_lens, cross_q, cross_kv, cross_kv, e["grad_ctx"], e["grad_cross"], seqs, False, 0, 0, PAIRS
+        )
+
+    def k_one(e):
+        e["grad_one"], e["grad_self"], e["grad_ctx"], e["sums_one"] = join_back(
+            e["cross_grads"], second_w, 2 * D, e["grad_two"], unit_one, scale_one, vec, 7, second_w, D
+        )
+
+    def k_self(e):
+        e["self_grads"], sums_self = attend_back(
+            tok_lens, queries_keys, queries_keys, values, e["grad_ctx"], e["grad_self"], seqs, True, 0, PAIRS, 0
+        )
+        sums_cross = e["sums_cross"].reshape(seqs, 8, width).sum(axis=0)
+        sums_self = sums_self.reshape(seqs, 8, width).sum(axis=0)
+        last = e["sums_three"]
+        e["grad_vec"] = jnp.concatenate(
+            [
+                sums_self[0:2],
+                e["sums_one"][2:3],
+                sums_cross[0:2],
+                e["sums_two"][2:3],
+                last[4:5],
+                e["sums_one"][0:2],
+                e["sums_two"][0:2],
+                last[2:4],
+                e["sums_pre"].reshape(-1, width),
+                last[0:1],
+                sums_one,
+                sums_two,
+                last[1:2],
+                jnp.broadcast_to(jnp.sum(seq_len).astype(f32), (1, width)),
+            ],
+            axis=0,
+        )
+
+    def k_states(e):
+        e["grad_states"] = input_grad(e["cross_dkv"], (0, 1), (first_w, first_w), (2 * D, 3 * D), BLOCK)
+
+    def k_tokens(e):
+        e["grad_tokens"] = input_grad(
+            e["self_grads"], (0, 1, 2), (first_w, first_w, second_w), (0, D, 0), seqs * length, (e["grad_one"],)
+        )
+
+    kernels = {
+        "hidden": (k_hidden, ("grad_ffn",), ("grad_pre", "sums_pre")),
+        "two": (k_two, ("grad_pre",), ("grad_two", "grad_cross", "grad_ctx", "sums_two")),
+        "cross": (k_cross, ("grad_ctx", "grad_cross"), ("cross_grads", "cross_dkv", "sums_cross")),
+        "one": (k_one, ("cross_grads",), ("grad_one", "grad_self", "grad_ctx", "sums_one")),
+        "self": (k_self, ("grad_ctx", "grad_self"), ("self_grads", "grad_vec")),
+        "states": (k_states, ("cross_dkv",), ("grad_states",)),
+        "tokens": (k_tokens, ("self_grads",), ("grad_tokens",)),
+    }
+    n_vec = vec_w.shape[0]
     if linked:
         order = links.plane_order()
-
-        def planes_of(x_mine, x_peer, y_mine, y_peer, x_at, y_at, stride, width=D):
+        sums = {}
+
+        def planes_of(name, x_mine, x_peer, y_mine, y_peer, x_at, y_at, stride, wide=D):
             spots = [(x_at(ux, y), *y_at(ux)) for ux, y in order]
             slots = [a if a.ndim == 3 else a[None] for a in (x_mine, x_peer, y_mine, y_peer)]
-            return unit_planes(*slots, spots, links.z, stride, shard_rows, width)
-
-        grad_ffn_peer = peer(grad_ffn)
-    grad_pre, sums_pre = hidden_back(grad_ffn, fc_out, slope)
-    if linked:
-        grad_pre, grad_ffn_peer = hold(grad_pre, grad_ffn_peer)
-        grad_pre_peer = peer(grad_pre)
-        planes = planes_of(
-            hidden, hidden_peer, grad_ffn, grad_ffn_peer,
-            lambda ux, y: y * UNITS + ux * 2 + core, lambda ux: (0 * ux, 0 * ux), 2 * UNITS,
+            sums[name] = Sum(links, unit_planes(*slots, spots, links.z, stride, shard_rows, wide))
+
+        def k_planes_2(e):
+            planes_of(
+                "2", e["hidden"], e["hidden_peer"], e["grad_ffn"], e["grad_ffn_peer"],
+                lambda ux, y: y * UNITS + ux * 2 + core, lambda ux: (0 * ux, 0 * ux), 2 * UNITS,
+            )
+
+        def k_planes_1(e):
+            planes_of(
+                "1", e["normed_two_low"], e["normed_two_low_peer"], e["grad_pre"], e["grad_pre_peer"],
+                lambda ux, y: y, lambda ux: (0 * ux, ux * 2 + core), 2,
+            )
+
+        def k_planes_t(e):
+            planes_of(
+                "t", e["cross_in"], e["cross_in_peer"], e["cross_grads"], e["cross_grads_peer"],
+                lambda ux, y: core * 2 * links.depth + y, lambda ux: (core + 0 * ux, ux), 2, D // 2,
+            )
+
+        def k_planes_a(e):
+            planes_of(
+                "a", e["self_in"], e["self_in_peer"], e["self_grads"], e["self_grads_peer"],
+                lambda ux, y: y + 2 * links.depth * (ux * core), lambda ux: (ux * 2 + core, 0 * ux), 2,
+            )
+
+        def k_theirs(e):
+            e["theirs"] = state_grad(state_rows, e["cross_dkv"], 1 - core)
+
+        def k_mine(e):
+            e["mine"] = state_grad(state_rows, e["cross_dkv"], core)
+
+        def k_planes_e(e):
+            spots = [(y, ux) for ux, y in order]
+            sums["e"] = Sum(links, sum_planes(e["mine"], e["theirs_peer"], spots, links.z, shard_rows, D // 2))
+
+        states_of = {"1": (fc1_w, fc1_m, fc1_v), "2": (fc2_w, fc2_m, fc2_v)}
+        whole_unit, half_unit = (1, shard_rows, D), (1, shard_rows, D // 2)
+        ways = {
+            "2": ((shard_rows, D), lambda u: (u, 0)),
+            "1": ((shard_rows, D), lambda u: (0, u)),
+            "a": (whole_unit, lambda u: (u, 0, 0)),
+            "t": (half_unit, lambda u: (4 + 3 * (u % 2), 0, u // 2)),
+            "e": (half_unit, lambda u: (5 + u % 2, 0, u // 2)),
+        }
+
+        def k_adam(name):
+            def kernel(e):
+                place_of = name if name in states_of else "attn"
+                state = states_of.get(name, (attn_w, attn_m, attn_v))
+                e[place_of] = adam_units(spot, sums[name].parts, state, *ways[name], e.get(place_of))
+
+            return kernel
+
+        kernels |= {
+            "planes_2": (k_planes_2, ("hidden", "hidden_peer", "grad_ffn", "grad_ffn_peer"), ()),
+            "planes_1": (k_planes_1, ("normed_two_low", "normed_two_low_peer", "grad_pre", "grad_pre_peer"), ()),
+            "planes_t": (k_planes_t, ("cross_in", "cross_in_peer", "cross_grads", "cross_grads_peer"), ()),
+            "planes_a": (k_planes_a, ("self_in", "self_in_peer", "self_grads", "self_grads_peer"), ()),
+            "theirs": (k_theirs, ("cross_dkv",), ("theirs",)),
+            "mine": (k_mine, ("cross_dkv",), ("mine",)),
+            "planes_e": (k_planes_e, ("mine", "theirs_peer"), ()),
+        }
+        for name in "21ate":
+            kernels["adam_" + name] = (k_adam(name), (), ())
+        env |= {"self_in_peer": self_in_peer, "cross_in_peer": cross_in_peer}
+        vec_perms = {"c": links.to_core, "z1": to_z1, "z2": to_z2, "s1": swap1, "s2": swap2}
+        CLOCK[:] = [CLOCK[0]]
+        for at, (kernel, *events) in enumerate(PLAN):
+            if kernel:
+                kernels[kernel][0](env)
+            moved = [event[4:] for event in events if event.startswith("sum ")]
+            made = [name[-1] for name in (kernel,) if name.startswith("planes")]
+            landing = [event[5:] for event in events if event.startswith("land ")]
+            names = set(kernels[kernel][2]) if kernel else set()
+            for later in PLAN[at + 1 :]:
+                if later[0]:
+                    names |= set(kernels[later[0]][1])
+                    break
+            names |= {name + "_peer" for name in landing}
+            names |= {event[5:] for event in events if event.startswith("give ")}
+            if "vec" in landing or any(event.startswith("vec ") for event in events):
+                names |= {"grad_vec"}
+            names = sorted(name for name in names if name in env)
+            here = [sums[name] for name in sorted({*moved, *made})]
+            arrays = [env[name] for name in names]
+            if kernel.startswith("adam"):
+                place_of = kernel[5:] if kernel[5:] in states_of else "attn"
+                arrays.append(env[place_of][0])
+            held = land(here, *arrays)
+            env.update(zip(names, held))
+            if kernel.startswith("adam"):
+                env[place_of][0] = held[-1]
+            if "vec" in landing:
+                env["grad_vec"] = env["grad_vec"] + env["vec_peer"]
+            add(*[sums[name] for name in moved])
+            if moved:
+                held = land(here, *[env[name] for name in names])
+                env.update(zip(names, held))
+            go(*[sums[name] for name in moved])
+            for event in events:
+                if event.startswith("give "):
+                    env[event[5:] + "_peer"] = peer(env[event[5:]])
+                elif event.startswith("vec "):
+                    env["vec_peer"] = send(env["grad_vec"], vec_perms[event[4:]])
+        fc1_new, fc2_new, attn_new = env["1"], env["2"], env["attn"]
+        grad_vec = env["grad_vec"]
+    else:
+        for name in ("hidden", "two", "cross", "one", "self", "states", "tokens"):
+            kernels[name][0](env)
+        self_grads, cross_grads, cross_dkv = env["self_grads"], env["cross_grads"], env["cross_dkv"]
+        grad_vec = lax.psum(env["grad_vec"], ("dp", "fsdp"))
+
+        def owned(inputs, grads, dim):
+            part = dot_grad(inputs, grads).astype(bf16)
+            part = lax.psum_scatter(part, "fsdp", scatter_dimension=dim, tiled=True)
+            return lax.psum(part, "dp").astype(f32)
+
+        grad_attn = jnp.stack(
+            [owned(self_in[u // 3], self_grads[u], 0) for u in range(4)]
+            + [
+                owned(normed_one_low, cross_grads[0], 0),
+                owned(state_rows, cross_dkv[0], 0),
+                owned(state_rows, cross_dkv[1], 0),
+                owned(cross_in[1], cross_grads[1], 0),
+            ]
         )
-        sum_2 = Sum(links, planes)
-        grad_pre, grad_pre_peer = hold(grad_pre, grad_pre_peer)
-        grad_pre = advance(grad_pre, sum_2)
-    else:
-        grad_fc2 = dot_grad(hidden, grad_ffn).astype(bf16)
-    grad_two, grad_cross, grad_ctx, sums_back_two = join_back(
-        grad_pre, fc_in, 0, grad_three, unit_two, scale_two, vec, 9, second_w, 3 * D
-    )
-    if linked:
-        planes = planes_of(
-            normed_two_low, normed_two_peer, grad_pre, grad_pre_peer,
-            lambda ux, y: y, lambda ux: (0 * ux, ux * 2 + core), 2,
-        )
-        sum_1 = Sum(links, planes)
-        grad_ctx = advance(grad_ctx, sum_1)
-    else:
-        grad_fc1 = dot_grad(normed_two_low, grad_pre).astype(bf16)
-    cross_grads, cross_dkv, sums_cross = attend_back(
-        enc_lens, cross_q, cross_kv, cross_kv, grad_ctx, grad_cross, seqs, False, 0, 0, PAIRS
-    )
-    if linked:
-        cross_grads = advance(cross_grads, sum_2)
-        cross_grads_peer = peer(cross_grads)
-    grad_one, grad_self, grad_ctx, sums_back_one = join_back(
-        cross_grads, second_w, 2 * D, grad_two, unit_one, scale_one, vec, 7, second_w, D
-    )
-    if linked:
-        grad_ctx, cross_grads_peer = hold(grad_ctx, cross_grads_peer)
-        planes_t = planes_of(
-            cross_in, cross_in_peer, cross_grads, cross_grads_peer,
-            lambda ux, y: core * 2 * links.depth + y, lambda ux: (core + 0 * ux, ux), 2, D // 2,
-        )
-        grad_ctx, *planes_t = hold(grad_ctx, *planes_t)
-    self_grads, sums_self = attend_back(
-        tok_lens, queries_keys, queries_keys, values, grad_ctx, grad_self, seqs, True, 0, PAIRS, 0
-    )
-    sums_cross = sums_cross.reshape(seqs, 8, width).sum(axis=0)
-    sums_self = sums_self.reshape(seqs, 8, width).sum(axis=0)
-    grad_vec = jnp.concatenate(
-        [
-            sums_self[0:2],
-            sums_back_one[2:3],
-            sums_cross[0:2],
-            sums_back_two[2:3],
-            sums_three[4:5],
-            sums_back_one[0:2],
-            sums_back_two[0:2],
-            sums_three[2:4],
-            sums_pre.reshape(-1, width),
-            sums_three[0:1],
-            sums_one,
-            sums_two,
-            sums_three[1:2],
-            jnp.broadcast_to(jnp.sum(seq_len).astype(f32), (1, width)),
-        ],
-        axis=0,
-    )
-    n_vec = vec_w.shape[0]
-    if linked:
-        self_grads = advance(self_grads, sum_1, sum_2)
-        sum_t = Sum(links, planes_t)
-        self_grads = advance(self_grads, sum_t)
-        self_grads_peer, vec_peer = peer(self_grads), peer(grad_vec)
-        self_grads, cross_dkv = hold(self_grads, cross_dkv)
-        theirs = state_grad(state_rows, cross_dkv, 1 - core)
-        theirs, self_grads_peer, vec_peer = hold(theirs, self_grads_peer, vec_peer)
-        theirs = advance(theirs, sum_t, sum_2)
-        grad_vec = grad_vec + vec_peer
-        vec_peer = send(grad_vec, to_z1)
-        planes = planes_of(
-            self_in, self_in_peer, self_grads, self_grads_peer,
-            lambda ux, y: y + 2 * links.depth * (ux * core), lambda ux: (ux * 2 + core, 0 * ux), 2,
-        )
-        sum_a = Sum(links, planes)
-        theirs = advance(theirs, sum_a, sum_1)
-        theirs_peer = peer(theirs)
-        cross_dkv, theirs = hold(cross_dkv, theirs)
-        mine = state_grad(state_rows, cross_dkv, core)
-        mine, theirs_peer, vec_peer = hold(mine, theirs_peer, vec_peer)
-        grad_vec = grad_vec + vec_peer
-        vec_peer = send(grad_vec, to_z2)
-        planes = sum_planes(
-            mine, theirs_peer, [(y, ux) for ux, y in order], links.z, shard_rows, D // 2
-        )
-        sum_e = Sum(links, planes)
-        self_grads = advance(self_grads, sum_e, sum_t, sum_2)
-    else:
-        grad_attn = jnp.stack(
-            [dot_grad(self_in[u // 3], self_grads[u]) for u in range(4)]
-            + [
-                dot_grad(normed_one_low, cross_grads[0]),
-                dot_grad(state_rows, cross_dkv[0]),
-                dot_grad(state_rows, cross_dkv[1]),
-                dot_grad(cross_in[1], cross_grads[1]),
-            ]
-        ).astype(bf16)
-    grad_tokens = input_grad(
-        self_grads, (0, 1, 2), (first_w, first_w, second_w), (0, D, 0), seqs * length, (grad_one,)
-    )
-    if linked:
-        cross_dkv, grad_tokens, vec_peer = hold(cross_dkv, grad_tokens, vec_peer)
-        cross_dkv = advance(cross_dkv, sum_1)
-        grad_vec = grad_vec + vec_peer
-        vec_peer = send(grad_vec, swap1)
-    grad_states = input_grad(cross_dkv, (0, 1), (first_w, first_w), (2 * D, 3 * D), BLOCK)
-
-    if linked:
-        state_1, state_2 = (fc1_w, fc1_m, fc1_v), (fc2_w, fc2_m, fc2_v)
-        attn_state = (attn_w, attn_m, attn_v)
-        grad_states = advance(grad_states, sum_a, sum_t)
-        grad_states, vec_peer = hold(grad_states, vec_peer)
-        grad_vec = grad_vec + vec_peer
-        vec_peer = send(grad_vec, swap2)
-        grad_states = advance(grad_states, sum_e, sum_1, sum_2)
-        fc2_new = adam_units(spot, sum_2.parts, state_2, (shard_rows, D), lambda u: (u, 0))
-        fc2_new[0], vec_peer = hold(fc2_new[0], vec_peer)
-        grad_vec = grad_vec + vec_peer
-        fc2_new[0] = advance(fc2_new[0], sum_a, sum_t, sum_1)
-        fc1_new = adam_units(spot, sum_1.parts, state_1, (shard_rows, D), lambda u: (0, u))
-        fc1_new[0] = advance(fc1_new[0], sum_e, sum_t)
-        fc1_new[0] = advance(fc1_new[0], sum_a)
-        attn_new = adam_units(
-            spot, sum_t.parts, attn_state, (1, shard_rows, D // 2), lambda u: (4 + 3 * (u % 2), 0, u // 2)
-        )
-        attn_new[0] = advance(attn_new[0], sum_e)
-        attn_new[0] = advance(attn_new[0], sum_a)
-        attn_new[0] = advance(attn_new[0], sum_e)
-        attn_new[0] = advance(attn_new[0], sum_a)
-        attn_new[0] = advance(attn_new[0], sum_e)
-        attn_new = adam_units(
-            spot, sum_a.parts, attn_state, (1, shard_rows, D), lambda u: (u, 0, 0), attn_new
-        )
-        attn_new = adam_units(
-            spot, sum_e.parts, attn_state, (1, shard_rows, D // 2), lambda u: (5 + u % 2, 0, u // 2), attn_new
-        )
-    else:
-        grad_vec = lax.psum(grad_vec, ("dp", "fsdp"))
-
-        def owned(grad, dim):
-            part = lax.psum_scatter(grad, "fsdp", scatter_dimension=dim, tiled=True)
-            return lax.psum(part, "dp").astype(f32)
-
-        attn_new = adam_update(attn_w, attn_m, attn_v, owned(grad_attn, 1), matrix_rate, matrix_decay)
-        fc1_new = adam_update(fc1_w, fc1_m, fc1_v, owned(grad_fc1, 0), matrix_rate, matrix_decay)
-        fc2_new = adam_update(fc2_w, fc2_m, fc2_v, owned(grad_fc2, 0), matrix_rate, matrix_decay)
+        grad_fc1, grad_fc2 = owned(normed_two_low, env["grad_pre"], 0), owned(hidden, grad_ffn, 0)
+        attn_new = adam_update(attn_w, attn_m, attn_v, grad_attn, matrix_rate, matrix_decay)
+        fc1_new = adam_update(fc1_w, fc1_m, fc1_v, grad_fc1, matrix_rate, matrix_decay)
+        fc2_new = adam_update(fc2_w, fc2_m, fc2_v, grad_fc2, matrix_rate, matrix_decay)
+    grad_tokens, grad_states = env["grad_tokens"], env["grad_states"]
     stats = grad_vec[n_vec:]
     stream_rms = jnp.sqrt(jnp.sum(stats[:4], axis=1) / (stats[4, 0] * D))
     cols = vec_w.shape[1]
     vec_grad = lax.dynamic_slice_in_dim(grad_vec[:n_vec], lax.axis_index("fsdp") * cols, cols, 1)
-    vec_new = adam_update(vec_w, vec_m, vec_v, vec_grad, vector_rate, 0.0)
+    vec_new = adam_update(vec_w, CLOCK[0] if linked else vec_m, vec_v, vec_grad, vector_rate, 0.0)
     return (
         mixed.reshape(tokens.shape),
         grad_tokens.reshape(tokens.shape),

time: 490 us -> 461 us (0.941)
  waiting for transfers between devices: 109 us -> 142 us
  local copies, waits for them, and re-layouts: 52.9 us -> 26.2 us
  Pallas kernels: 233 us -> 207 us
  starting transfers between devices: 80.7 us -> 73.2 us
    ppermute x69 -> x70, waiting for transfers between devices: 109 us -> 142 us  [send(): return lax.ppermute(block, ('dp', 'fsdp'), perm)]
    unnamed x238 -> x154, local copies, waits for them, and re-layouts: 41.3 us -> 20.2 us
    pallas_call x4, Pallas kernels: 24 us -> 10.8 us  [assemble(): pl.pallas_call(partial(assemble_kernel, wide, rows, step, counts), out_sh...]
    ppermute x69 -> x70, starting transfers between devices: 80.7 us -> 73.2 us  [send(): return lax.ppermute(block, ('dp', 'fsdp'), perm)]
    pallas_call x5, Pallas kernels: 21.5 us -> 28.5 us  [adam_units(): pl.pallas_call(adam_kernel, out_shape=[array(a.shape, f32) for a in state...]
    pallas_call x16 -> x15, Pallas kernels: 17.2 us -> 12.3 us  [place(): pl.pallas_call(partial(place_kernel, total // len(slots)), out_shape=arra...]
  transfers between devices with their start and end apart: 69 -> 70, of which waited for: 23 -> 33; matrix products, arithmetic and copies ran while one was open for 3% -> 2% of each run, Pallas kernels for 43% -> 41%
where the time goes in v3:
time: 461 us; the launch traced here: 457 us
  Pallas kernels  207 us (45%)
  waiting for transfers between devices  142 us (31%)
  starting transfers between devices  73.2 us (16%)
  local copies, waits for them, and re-layouts  26.2 us (6%)
    ppermute x70, waiting for transfers between devices, send(): return lax.ppermute(block, ('dp', 'fsdp'), perm)  142 us
    ppermute x70, starting transfers between devices, send(): return lax.ppermute(block, ('dp', 'fsdp'), perm)  73.2 us
    pallas_call x5, Pallas kernels, adam_units(): pl.pallas_call(adam_kernel, out_shape=[array(a.shape, f32) for a in state...  28.5 us
    pallas_call x2, Pallas kernels, attend_back(): pl.pallas_call(partial(attend_back_kernel, causal), out_shape=out_shape,...  27.7 us
    pallas_call x5, Pallas kernels, planes_call(): pl.pallas_call(kernel, out_shape=[array((n * plane, width)) for n in (2,...  27.3 us
    unnamed x154, local copies, waits for them, and re-layouts  20.2 us
    pallas_call x2, Pallas kernels, input_grad(): pl.pallas_call(partial(input_grad_kernel, len(slots)), out_shape=array((n...  19.9 us
    pallas_call x2, Pallas kernels, state_grad(): pl.pallas_call(state_grad_kernel, out_shape=array((D, D)), grid_spec=pltp...  14.2 us
  transfers between devices with their start and end apart: 70, of which 33 were waited for; matrix products, arithmetic and copies ran while one was open for 2% of the time, Pallas kernels for 41%

profile of v3, /device:TPU:0, one launch (start us, length us, event | category | flops | bytes accessed | tf_op | source)
XLA Modules:
  0.0 456.7 jit_solution(11867010436316177962)
XLA Ops:
  2.7 4.1 collective-permute-start
  8.4 11.9 %collective-permute-done.refs_1_ = bf16[144,1024]{1,0:T(8,128)(2,1)S(1)} collective-permute-done((bf16[144,1024]{1,0:T(8,128)(2,1)S(1)}, bf16[144,1024]{1,0:T(8,128)(2,1)S(1)}, u32[]{:S(2)}, u32[]{:S(2)}) %collective-permute-start) | collective-permute-done | bytes 294944 | tf_op jit(solution)/shard_map/ppermute | solution.py:737
  22.0 6.4 %collective-permute-done.2.refs_3_ = bf16[144,1024]{1,0:T(8,128)(2,1)S(1)} collective-permute-done((bf16[144,1024]{1,0:T(8,128)(2,1)S(1)}, bf16[144,1024]{1,0:T(8,128)(2,1)S(1)}, u32[]{:S(2)}, u32[]{:S(2)}) %collective-permute-start.2) | collective-permute-done | bytes 294944 | tf_op jit(solution)/shard_map/ppermute | solution.py:737
  30.4 3.3 collective-permute-start.3
  36.5 8.5 %collective-permute-done.3.refs_1_ = bf16[128,1024]{1,0:T(8,128)(2,1)S(1)} collective-permute-done((bf16[128,1024]{1,0:T(8,128)(2,1)S(1)}, bf16[128,1024]{1,0:T(8,128)(2,1)S(1)}, u32[]{:S(2)}, u32[]{:S(2)}) %collective-permute-start.3) | collective-permute-done | bytes 262176 | tf_op jit(solution)/shard_map/ppermute | solution.py:737
  51.3 3.4 collective-permute-start.7
  54.6 9.2 %collective-permute-done.6.refs_3_ = bf16[128,1024]{1,0:T(8,128)(2,1)S(1)} collective-permute-done((bf16[128,1024]{1,0:T(8,128)(2,1)S(1)}, bf16[128,1024]{1,0:T(8,128)(2,1)S(1)}, u32[]{:S(2)}, u32[]{:S(2)}) %collective-permute-start.6) | collective-permute-done | bytes 262176 | tf_op jit(solution)/shard_map/ppermute | solution.py:737
  63.9 3.1 collective-permute-done.7.refs_1_
  72.3 9.5 %collective-permute-done.8.refs_2_ = bf16[256,1024]{1,0:T(8,128)(2,1)} collective-permute-done((bf16[256,1024]{1,0:T(8,128)(2,1)}, bf16[256,1024]{1,0:T(8,128)(2,1)}, u32[]{:S(2)}, u32[]{:S(2)}) %collective-permute-start.8) | collective-permute-done | bytes 524320 | tf_op jit(solution)/shard_map/ppermute | solution.py:737
  97.5 4.0 shard_map.293.w_ref.refs_3_.refs_4_.refs_2_
  103.4 5.1 %collective-permute-done.13.refs_1_ = bf16[128,1024]{1,0:T(8,128)(2,1)S(1)} collective-permute-done((bf16[128,1024]{1,0:T(8,128)(2,1)S(1)}, bf16[128,1024]{1,0:T(8,128)(2,1)S(1)}, u32[]{:S(2)}, u32[]{:S(2)}) %collective-permute-start.13) | collective-permute-done | bytes 262176 | tf_op jit(solution)/shard_map/ppermute | solution.py:737
  109.8 9.9 %shard_map.295.k_ref.v_ref = bf16[2048,2048]{1,0:T(8,128)(2,1)S(1)} custom-call(bf16[2048,1024]{1,0:T(8,128)(2,1)S(1)} %bitcast.138, bf16[1024,4096]{1,0:T(8,128)(2,1)S(1)} %shard_map.293.w_ref.refs_3_.refs_4_.refs_2_, f32[1,2048]{1,0:T(1,128)S(1)} %concatenate.30.b_ref), custom_call_target="tpu_custom_call" | custom-call | bytes 1024 | tf_op jit(solution)/shard_map/pallas_call | solution.py:115
  122.7 6.6 %collective-permute-done.16.refs_1_ = bf16[1024,1024]{1,0:T(8,128)(2,1)S(1)} collective-permute-done((bf16[1024,1024]{1,0:T(8,128)(2,1)S(1)}, bf16[1024,1024]{1,0:T(8,128)(2,1)S(1)}, u32[]{:S(2)}, u32[]{:S(2)}) %collective-permute-start.16) | collective-permute-done | bytes 2097184 | tf_op jit(solution)/shard_map/ppermute | solution.py:737
  142.7 9.9 %shard_map.304.x_ref.refs_0_.refs_1_.refs_2_.refs_3_ = bf16[2,256,1024]{2,1,0:T(8,128)(2,1)S(1)} custom-call(s32[2]{0:T(128)S(1)} %bitcast.162, bf16[256,1024]{1,0:T(8,128)(2,1)S(1)} %shard_map.303.q_ref, bf16[2048,2048]{1,0:T(8,128)(2,1)S(1)} %shard_map.295.k_ref.v_ref, bf16[2048,2048]{1,0:T(8,128)(2,1)S(1)} %shard_map.295.k_ref.v_ref, ...), custom_call_target="tpu_custom_call" | custom-call | bytes 1024 | tf_op jit(solution)/shard_map/pallas_call | solution.py:446
  154.3 3.7 collective-permute-done.19.refs_1_
  158.0 9.4 %collective-permute-done.20.refs_1_ = bf16[1024,1024]{1,0:T(8,128)(2,1)S(1)} collective-permute-done((bf16[1024,1024]{1,0:T(8,128)(2,1)S(1)}, bf16[1024,1024]{1,0:T(8,128)(2,1)S(1)}, u32[]{:S(2)}, u32[]{:S(2)}) %collective-permute-start.20) | collective-permute-done | bytes 2097184 | tf_op jit(solution)/shard_map/ppermute | solution.py:737
  173.9 5.3 %shard_map.308 = (bf16[256,4096]{1,0:T(8,128)(2,1)S(1)}, bf16[256,4096]{1,0:T(8,128)(2,1)S(1)}) custom-call(bf16[256,1024]{1,0:T(8,128)(2,1)S(1)} %get-tuple-element.520.x_ref, bf16[1024,4096]{1,0:T(8,128)(2,1)S(1)} %shard_map.307.w_ref, f32[1,4096]{1,0:T(1,128)S(1)} %bitcast.156), custom_call_target="tpu_custom_call" | custom-call | bytes 1024 | tf_op jit(solution)/shard_map/pallas_call | solution.py:193
  179.2 15.1 %collective-permute-done.23.refs_1_ = bf16[1024,1024]{1,0:T(8,128)(2,1)S(1)} collective-permute-done((bf16[1024,1024]{1,0:T(8,128)(2,1)S(1)}, bf16[1024,1024]{1,0:T(8,128)(2,1)S(1)}, u32[]{:S(2)}, u32[]{:S(2)}) %collective-permute-start.23) | collective-permute-done | bytes 2097184 | tf_op jit(solution)/shard_map/ppermute | solution.py:737
  194.2 4.2 collective-permute-done.25.refs_3_
  200.7 6.0 %shard_map.311 = (bf16[256,1024]{1,0:T(8,128)(2,1)}, f32[256,1024]{1,0:T(8,128)S(1)}, bf16[256,1024]{1,0:T(8,128)(2,1)S(1)}, f32[8,1024]{1,0:T(8,128)S(1)}) custom-call(s32[2]{0:T(128)S(1)} %bitcast.160, bf16[256,4096]{1,0:T(8,128)(2,1)S(1)} %get-tuple-element.499.x_ref, bf16[4096,1024]{1,0:T(8,128)(2,1)S(1)} %shard_map.310.w_ref, ...), custom_call_target="tpu_custom_call" | custom-call | bytes 1024 | tf_op jit(solution)/shard_map/pallas_call | solution.py:234
  207.2 4.2 shard_map.312
  216.4 6.5 %shard_map.313 = (bf16[1024,1024]{1,0:T(8,128)(2,1)S(1)}, bf16[512,1024]{1,0:T(8,128)(2,1)S(1)}, bf16[512,1024]{1,0:T(8,128)(2,1)S(1)}) custom-call(s32[4,4]{1,0:T(4,128)S(1)} %get-tuple-element.893.idx_ref, bf16[1,256,4096]{2,1,0:T(8,128)(2,1)} %bitcast.134, bf16[1,256,4096]{2,1,0:T(8,128)(2,1)} %bitcast.135, bf16[1,256,4096]{2,1,0:T(8,128)(2,1)} %bitcast.136, ...), custom_call_target="tpu_custom_call" | custom-call | bytes 1024 | tf_op jit(solution)/shard_map/pallas_call | solution.py:605
  224.4 9.0 %shard_map.314 = (f32[256,1024]{1,0:T(8,128)S(1)}, bf16[256,1024]{1,0:T(8,128)(2,1)S(1)}, bf16[256,1024]{1,0:T(8,128)(2,1)S(1)}, f32[8,1024]{1,0:T(8,128)S(1)}) custom-call(bf16[256,4096]{1,0:T(8,128)(2,1)} %get-tuple-element.522.g_ref, bf16[1024,4096]{1,0:T(8,128)(2,1)} %copy-done.4, f32[256,1024]{1,0:T(8,128)S(1)} %copy-done.38, f32[256,1024]{1,0:T(8,128)} %copy-done.36, ...), custom_call_target="tpu_custom_call" | custom-call | bytes 1024 | tf_op jit(solution)/shard_map/pallas_call | solution.py:303
  233.4 7.5 %shard_map.315 = (bf16[1024,1024]{1,0:T(8,128)(2,1)}, bf16[512,1024]{1,0:T(8,128)(2,1)S(1)}, bf16[512,1024]{1,0:T(8,128)(2,1)S(1)}) custom-call(s32[4,4]{1,0:T(4,128)S(1)} %get-tuple-element.891.idx_ref, bf16[1,256,1024]{2,1,0:T(8,128)(2,1)S(1)} %bitcast.141, bf16[1,256,1024]{2,1,0:T(8,128)(2,1)S(1)} %bitcast.142, bf16[1,256,1024]{2,1,0:T(8,128)(2,1)S(1)} %bitcast.143, ...), custom_call_target="tpu_custom_call" | custom-call | bytes 1024 | tf_op jit(solution)/shard_map/pallas_call | solution.py:605
  244.4 19.6 %shard_map.316 = (bf16[2,256,1024]{2,1,0:T(8,128)(2,1)}, bf16[2,2048,1024]{2,1,0:T(8,128)(2,1)S(1)}, f32[16,1024]{1,0:T(8,128)S(1)}) custom-call(s32[2]{0:T(128)S(1)} %bitcast.163, bf16[256,1024]{1,0:T(8,128)(2,1)S(1)} %shard_map.303.q_ref, bf16[2048,2048]{1,0:T(8,128)(2,1)S(1)} %bitcast.133, bf16[2048,2048]{1,0:T(8,128)(2,1)S(1)} %bitcast.133, ...), custom_call_target="tpu_custom_call" | custom-call | bytes 1024 | tf_op jit(solution)/shard_map/pallas_call | solution.py:476
  264.0 3.4 copy-done.3
  274.9 4.5 shard_map.318
  280.5 8.1 %shard_map.319 = (bf16[4,256,1024]{2,1,0:T(8,128)(2,1)S(1)}, f32[16,1024]{1,0:T(8,128)S(1)}) custom-call(s32[2]{0:T(128)S(1)} %bitcast.161, bf16[256,2048]{1,0:T(8,128)(2,1)S(1)} %copy-done.13, bf16[256,2048]{1,0:T(8,128)(2,1)S(1)} %copy-done.13, bf16[256,1024]{1,0:T(8,128)(2,1)S(1)} %shard_map.300.v_ref, bf16[256,1024]{1,0:T(8,128)(2,1)S(1)} %get-tuple-element.554.do_ref, ...), custom_call_target="tpu_custom_call" | custom-call | bytes 1024 | tf_op jit(solution)/shard_map/pallas_call | solution.py:476
  290.4 5.3 %shard_map.320 = (bf16[1024,512]{1,0:T(8,128)(2,1)S(1)}, bf16[512,512]{1,0:T(8,128)(2,1)S(1)}, bf16[512,512]{1,0:T(8,128)(2,1)S(1)}) custom-call(s32[4,4]{1,0:T(4,128)S(1)} %copy-done.49, bf16[2,256,1024]{2,1,0:T(8,128)(2,1)S(1)} %copy-done.9, bf16[2,256,1024]{2,1,0:T(8,128)(2,1)S(1)} %copy-done.9, bf16[2,256,1024]{2,1,0:T(8,128)(2,1)S(1)} %copy-done.9, ...), custom_call_target="tpu_custom_call" | custom-call | bytes 1024 | tf_op jit(solution)/shard_map/pallas_call | solution.py:605
  305.6 7.1 %shard_map.323 = bf16[1024,1024]{1,0:T(8,128)(2,1)S(1)} custom-call(s32[1]{0:T(128)} %bitcast.83.slot_ref, bf16[2048,1024]{1,0:T(8,128)(2,1)S(1)} %bitcast.139, bf16[2,2048,1024]{2,1,0:T(8,128)(2,1)} %copy-done.3), custom_call_target="tpu_custom_call" | custom-call | bytes 1024 | tf_op jit(solution)/shard_map/pallas_call | solution.py:353
  312.7 3.1 collective-permute-done.38.refs_1_
  316.0 5.6 %shard_map.325 = (bf16[1024,1024]{1,0:T(8,128)(2,1)S(1)}, bf16[512,1024]{1,0:T(8,128)(2,1)S(1)}, bf16[512,1024]{1,0:T(8,128)(2,1)S(1)}) custom-call(s32[4,4]{1,0:T(4,128)S(1)} %copy-done.48, bf16[2,256,1024]{2,1,0:T(8,128)(2,1)S(1)} %shard_map.301.x_ref.refs_0_.refs_1_.refs_2_.refs_3_, ...), custom_call_target="tpu_custom_call" | custom-call | bytes 1024 | tf_op jit(solution)/shard_map/pallas_call | solution.py:605
  321.6 4.1 collective-permute-done.40.refs_1_
  332.1 3.6 collective-permute-done.42
  338.1 7.1 %shard_map.328.refs_0_.refs_1_.refs_2_.refs_3_ = bf16[1024,1024]{1,0:T(8,128)(2,1)S(1)} custom-call(s32[1]{0:T(128)} %bitcast.99.slot_ref, bf16[2048,1024]{1,0:T(8,128)(2,1)S(1)} %bitcast.140, bf16[2,2048,1024]{2,1,0:T(8,128)(2,1)} %copy-done.3), custom_call_target="tpu_custom_call" | custom-call | bytes 1024 | tf_op jit(solution)/shard_map/pallas_call | solution.py:353
  350.8 4.2 collective-permute-start.49
  355.0 6.0 %shard_map.332 = bf16[256,1024]{1,0:T(8,128)(2,1)} custom-call(bf16[4,256,1024]{2,1,0:T(8,128)(2,1)} %copy-done.10, bf16[4,256,1024]{2,1,0:T(8,128)(2,1)} %copy-done.10, bf16[4,256,1024]{2,1,0:T(8,128)(2,1)} %copy-done.10, bf16[1024,4096]{1,0:T(8,128)(2,1)} %copy-done.1, bf16[1024,4096]{1,0:T(8,128)(2,1)} %copy-done.1, bf16[1024,4096]{1,0:T(8,128)(2,1)} %copy-done, ...), custom_call_target="tpu_custom_call" | custom-call | bytes 1024 | tf_op jit(solution)/shard_map/pallas_call | solution.py:334
  367.5 2.9 collective-permute-start.51
  370.6 13.9 %shard_map.337 = bf16[2048,1024]{1,0:T(8,128)(2,1)} custom-call(bf16[2,2048,1024]{2,1,0:T(8,128)(2,1)} %copy-done.3, bf16[2,2048,1024]{2,1,0:T(8,128)(2,1)} %copy-done.3, bf16[1024,4096]{1,0:T(8,128)(2,1)} %copy-done.1, bf16[1024,4096]{1,0:T(8,128)(2,1)} %copy-done.1), custom_call_target="tpu_custom_call" | custom-call | bytes 1024 | tf_op jit(solution)/shard_map/pallas_call | solution.py:334
  387.1 3.1 collective-permute-start.56
  390.2 6.5 %shard_map.339 = (f32[512,1024]{1,0:T(8,128)}, f32[512,1024]{1,0:T(8,128)}, f32[512,1024]{1,0:T(8,128)}) custom-call(s32[1]{0:T(128)} %bitcast.94.idx_ref, bf16[256,1024]{1,0:T(8,128)(2,1)S(1)} %shard_map.334.here_ref, bf16[256,1024]{1,0:T(8,128)(2,1)S(1)} %collective-permute-done.52.there_ref, f32[512,1024]{1,0:T(8,128)} %w_ref.5, f32[512,1024]{1,0:T(8,128)} %m_ref.5, ...), custom_call_target="tpu_custom_call" | custom-call | bytes 1024 | tf_op jit(solution)/shard_map/pallas_call | solution.py:684
  403.3 6.5 %shard_map.344 = (f32[128,4096]{1,0:T(8,128)}, f32[128,4096]{1,0:T(8,128)}, f32[128,4096]{1,0:T(8,128)}) custom-call(s32[1]{0:T(128)} %bitcast.94.idx_ref, bf16[256,1024]{1,0:T(8,128)(2,1)S(1)} %shard_map.342.here_ref, bf16[256,1024]{1,0:T(8,128)(2,1)S(1)} %collective-permute-done.58.there_ref, f32[128,4096]{1,0:T(8,128)} %w_ref.6, f32[128,4096]{1,0:T(8,128)} %m_ref.6, ...), custom_call_target="tpu_custom_call" | custom-call | bytes 1024 | tf_op jit(solution)/shard_map/pallas_call | solution.py:684
  414.6 4.5 shard_map.348
  419.1 5.2 %collective-permute-done.63.refs_1_ = bf16[256,512]{1,0:T(8,128)(2,1)S(1)} collective-permute-done((bf16[256,512]{1,0:T(8,128)(2,1)S(1)}, bf16[256,512]{1,0:T(8,128)(2,1)S(1)}, u32[]{:S(2)}, u32[]{:S(2)}) %collective-permute-start.63) | collective-permute-done | bytes 262176 | tf_op jit(solution)/shard_map/ppermute | solution.py:737
  425.5 6.4 %collective-permute-done.64.refs_1_ = bf16[128,1024]{1,0:T(8,128)(2,1)S(1)} collective-permute-done((bf16[128,1024]{1,0:T(8,128)(2,1)S(1)}, bf16[128,1024]{1,0:T(8,128)(2,1)S(1)}, u32[]{:S(2)}, u32[]{:S(2)}) %collective-permute-start.64) | collective-permute-done | bytes 262176 | tf_op jit(solution)/shard_map/ppermute | solution.py:737
  434.8 6.4 %collective-permute-done.67.refs_1_ = bf16[128,512]{1,0:T(8,128)(2,1)S(1)} collective-permute-done((bf16[128,512]{1,0:T(8,128)(2,1)S(1)}, bf16[128,512]{1,0:T(8,128)(2,1)S(1)}, u32[]{:S(2)}, u32[]{:S(2)}) %collective-permute-start.67) | collective-permute-done | bytes 131104 | tf_op jit(solution)/shard_map/ppermute | solution.py:737
  444.8 4.5 shard_map.354
  449.3 6.5 %shard_map.355 = (f32[8,128,1024]{2,1,0:T(8,128)}, f32[8,128,1024]{2,1,0:T(8,128)}, f32[8,128,1024]{2,1,0:T(8,128)}) custom-call(s32[1]{0:T(128)} %bitcast.94.idx_ref, bf16[256,1024]{1,0:T(8,128)(2,1)S(1)} %shard_map.352.here_ref, ...), custom_call_target="tpu_custom_call", output_to_operand_aliasing={{0}: (6, {}), {1}: (7, {}), {2}: (8, {})} | custom-call | bytes 1024 | tf_op jit(solution)/shard_map/pallas_call | solution.py:684
  (384 shorter events, 139.4 us)
Async XLA Ops:
  2.7 17.5 %collective-permute-start = (bf16[144,1024]{1,0:T(8,128)(2,1)S(1)}, bf16[144,1024]{1,0:T(8,128)(2,1)S(1)}, u32[]{:S(2)}, u32[]{:S(2)}) collective-permute-start(bf16[144,1024]{1,0:T(8,128)(2,1)S(1)} %fusion.6.refs_0_), channel_id=1, source_target_pairs={{0,4},{1,5},{2,6},{3,7},{4,0},{5,1},{6,2},{7,3},{8,12},{9,13},{10,... | collective-permute-start | bytes 884744 | tf_op jit(solution)/shard_map/ppermute | solution.py:737
  6.8 13.6 %collective-permute-start.1 = (bf16[144,1024]{1,0:T(8,128)(2,1)S(1)}, bf16[144,1024]{1,0:T(8,128)(2,1)S(1)}, u32[]{:S(2)}, u32[]{:S(2)}) collective-permute-start(bf16[144,1024]{1,0:T(8,128)(2,1)S(1)} %fusion.6.refs_0_), channel_id=1, source_target_pairs={{0,2},{1,3},{2,0},{3,1},{4,6},{5,7},{6,4},{7,5},{8,10},{9,11},{10,... | collective-permute-start | bytes 884744 | tf_op jit(solution)/shard_map/ppermute | solution.py:737
  29.0 17.1 %collective-permute-start.5 = (bf16[576,1024]{1,0:T(8,128)(2,1)S(1)}, bf16[576,1024]{1,0:T(8,128)(2,1)S(1)}, u32[]{:S(2)}, u32[]{:S(2)}) collective-permute-start(bf16[576,1024]{1,0:T(8,128)(2,1)S(1)} %shard_map.288.refs_0_), channel_id=1, source_target_pairs={{0,1},{1,0},{2,3},{3,2},{4,5},{5,4},{6,7},{7,6},{8,24},{9,25},{10,... | collective-permute-start | bytes 3538952 | tf_op jit(solution)/shard_map/ppermute | solution.py:737
  30.4 14.7 %collective-permute-start.3 = (bf16[128,1024]{1,0:T(8,128)(2,1)S(1)}, bf16[128,1024]{1,0:T(8,128)(2,1)S(1)}, u32[]{:S(2)}, u32[]{:S(2)}) collective-permute-start(bf16[128,1024]{1,0:T(8,128)(2,1)S(1)} %get-tuple-element.446.refs_0_), channel_id=1, source_target_pairs={{0,4},{1,5},{2,6},{3,7},{4,0},{5,1},{6,2},{7,3},{8,12},{9,13},{10,... | collective-permute-start | bytes 786440 | tf_op jit(solution)/shard_map/ppermute | solution.py:737
  33.6 11.8 %collective-permute-start.4 = (bf16[128,1024]{1,0:T(8,128)(2,1)S(1)}, bf16[128,1024]{1,0:T(8,128)(2,1)S(1)}, u32[]{:S(2)}, u32[]{:S(2)}) collective-permute-start(bf16[128,1024]{1,0:T(8,128)(2,1)S(1)} %get-tuple-element.446.refs_0_), channel_id=1, source_target_pairs={{0,2},{1,3},{2,0},{3,1},{4,6},{5,7},{6,4},{7,5},{8,10},{9,11},{10,... | collective-permute-start | bytes 786440 | tf_op jit(solution)/shard_map/ppermute | solution.py:737
  49.1 40.0 %collective-permute-start.10 = (bf16[1152,1024]{1,0:T(8,128)(2,1)S(1)}, bf16[1152,1024]{1,0:T(8,128)(2,1)}, u32[]{:S(2)}, u32[]{:S(2)}) collective-permute-start(bf16[1152,1024]{1,0:T(8,128)(2,1)S(1)} %shard_map.292.refs_0_), channel_id=1, source_target_pairs={{0,16},{1,17},{2,18},{3,19},{4,20},{5,21},{6,22},{7,23},{8,9},{9,8... | collective-permute-start | bytes 7077896 | tf_op jit(solution)/shard_map/ppermute | solution.py:737
  49.7 39.4 %collective-permute-start.11 = (bf16[1152,1024]{1,0:T(8,128)(2,1)S(1)}, bf16[1152,1024]{1,0:T(8,128)(2,1)}, u32[]{:S(2)}, u32[]{:S(2)}) collective-permute-start(bf16[1152,1024]{1,0:T(8,128)(2,1)S(1)} %shard_map.292.refs_0_), channel_id=1, source_target_pairs={{0,8},{1,9},{2,10},{3,11},{4,12},{5,13},{6,14},{7,15},{8,0},{9,1},... | collective-permute-start | bytes 7077896 | tf_op jit(solution)/shard_map/ppermute | solution.py:737
  49.7 14.1 %collective-permute-start.6 = (bf16[128,1024]{1,0:T(8,128)(2,1)S(1)}, bf16[128,1024]{1,0:T(8,128)(2,1)S(1)}, u32[]{:S(2)}, u32[]{:S(2)}) collective-permute-start(bf16[128,1024]{1,0:T(8,128)(2,1)S(1)} %copy-done.43), channel_id=1, source_target_pairs={{0,2},{1,3},{2,0},{3,1},{4,6},{5,7},{6,4},{7,5},{8,10},{9,11},{10,... | collective-permute-start | bytes 786440 | tf_op jit(solution)/shard_map/ppermute | solution.py:737
  51.3 15.7 %collective-permute-start.7 = (bf16[128,1024]{1,0:T(8,128)(2,1)S(1)}, bf16[128,1024]{1,0:T(8,128)(2,1)S(1)}, u32[]{:S(2)}, u32[]{:S(2)}) collective-permute-start(bf16[128,1024]{1,0:T(8,128)(2,1)S(1)} %dynamic-slice_convert_fusion.1.refs_0_), channel_id=1, source_target_pairs={{0,4},{1,5},{2,6},{3,7},{4,0},{5,1},{6,2},{7,3},{8,12},{9,13},{10,... | collective-permute-start | bytes 786440 | tf_op jit(solution)/shard_map/ppermute | solution.py:737
  67.6 19.9 %collective-permute-start.9 = (bf16[512,1024]{1,0:T(8,128)(2,1)S(1)}, bf16[512,1024]{1,0:T(8,128)(2,1)}, u32[]{:S(2)}, u32[]{:S(2)}) collective-permute-start(bf16[512,1024]{1,0:T(8,128)(2,1)S(1)} %shard_map.291.refs_0_), channel_id=1, source_target_pairs={{0,1},{1,0},{2,3},{3,2},{4,5},{5,4},{6,7},{7,6},{8,24},{9,25},{10,... | collective-permute-start | bytes 3145736 | tf_op jit(solution)/shard_map/ppermute | solution.py:737
  70.6 11.1 %collective-permute-start.8 = (bf16[256,1024]{1,0:T(8,128)(2,1)}, bf16[256,1024]{1,0:T(8,128)(2,1)}, u32[]{:S(2)}, u32[]{:S(2)}) collective-permute-start(bf16[256,1024]{1,0:T(8,128)(2,1)} %shard_map.289), channel_id=1, source_target_pairs={{0,2},{1,3},{2,0},{3,1},{4,6},{5,7},{6,4},{7,5},{8,10},{9,11},{10,... | collective-permute-start | bytes 1572872 | tf_op jit(solution)/shard_map/ppermute | solution.py:737
  92.0 37.3 %collective-permute-start.16 = (bf16[1024,1024]{1,0:T(8,128)(2,1)S(1)}, bf16[1024,1024]{1,0:T(8,128)(2,1)S(1)}, u32[]{:S(2)}, u32[]{:S(2)}) collective-permute-start(bf16[1024,1024]{1,0:T(8,128)(2,1)S(1)} %shard_map.298.refs_0_), channel_id=1, source_target_pairs={{0,16},{1,17},{2,18},{3,19},{4,20},{5,21},{6,22},{7,23},{8,9},{9,8... | collective-permute-start | bytes 6291464 | tf_op jit(solution)/shard_map/ppermute | solution.py:737
  92.6 36.8 %collective-permute-start.17 = (bf16[1024,1024]{1,0:T(8,128)(2,1)S(1)}, bf16[1024,1024]{1,0:T(8,128)(2,1)S(1)}, u32[]{:S(2)}, u32[]{:S(2)}) collective-permute-start(bf16[1024,1024]{1,0:T(8,128)(2,1)S(1)} %shard_map.298.refs_0_), channel_id=1, source_target_pairs={{0,8},{1,9},{2,10},{3,11},{4,12},{5,13},{6,14},{7,15},{8,0},{9,1},... | collective-permute-start | bytes 6291464 | tf_op jit(solution)/shard_map/ppermute | solution.py:737
  93.7 14.7 %collective-permute-start.13 = (bf16[128,1024]{1,0:T(8,128)(2,1)S(1)}, bf16[128,1024]{1,0:T(8,128)(2,1)S(1)}, u32[]{:S(2)}, u32[]{:S(2)}) collective-permute-start(bf16[128,1024]{1,0:T(8,128)(2,1)S(1)} %dynamic-slice_convert_fusion.refs_0_), channel_id=1, source_target_pairs={{0,4},{1,5},{2,6},{3,7},{4,0},{5,1},{6,2},{7,3},{8,12},{9,13},{10,... | collective-permute-start | bytes 786440 | tf_op jit(solution)/shard_map/ppermute | solution.py:737
  95.8 27.0 %collective-permute-start.15 = (bf16[512,1024]{1,0:T(8,128)(2,1)S(1)}, bf16[512,1024]{1,0:T(8,128)(2,1)S(1)}, u32[]{:S(2)}, u32[]{:S(2)}) collective-permute-start(bf16[512,1024]{1,0:T(8,128)(2,1)S(1)} %shard_map.290.refs_0_), channel_id=1, source_target_pairs={{0,1},{1,0},{2,3},{3,2},{4,5},{5,4},{6,7},{7,6},{8,24},{9,25},{10,... | collective-permute-start | bytes 3145736 | tf_op jit(solution)/shard_map/ppermute | solution.py:737
  109.1 13.0 %collective-permute-start.14 = (bf16[256,1024]{1,0:T(8,128)(2,1)S(1)}, bf16[256,1024]{1,0:T(8,128)(2,1)S(1)}, u32[]{:S(2)}, u32[]{:S(2)}) collective-permute-start(bf16[256,1024]{1,0:T(8,128)(2,1)S(1)} %shard_map.296), channel_id=1, source_target_pairs={{0,2},{1,3},{2,0},{3,1},{4,6},{5,7},{6,4},{7,5},{8,10},{9,11},{10,... | collective-permute-start | bytes 1572872 | tf_op jit(solution)/shard_map/ppermute | solution.py:737
  130.1 37.3 %collective-permute-start.20 = (bf16[1024,1024]{1,0:T(8,128)(2,1)S(1)}, bf16[1024,1024]{1,0:T(8,128)(2,1)S(1)}, u32[]{:S(2)}, u32[]{:S(2)}) collective-permute-start(bf16[1024,1024]{1,0:T(8,128)(2,1)S(1)} %shard_map.306.refs_0_), channel_id=1, source_target_pairs={{0,16},{1,17},{2,18},{3,19},{4,20},{5,21},{6,22},{7,23},{8,9},{9,8... | collective-permute-start | bytes 6291464 | tf_op jit(solution)/shard_map/ppermute | solution.py:737
  130.6 36.8 %collective-permute-start.21 = (bf16[1024,1024]{1,0:T(8,128)(2,1)S(1)}, bf16[1024,1024]{1,0:T(8,128)(2,1)S(1)}, u32[]{:S(2)}, u32[]{:S(2)}) collective-permute-start(bf16[1024,1024]{1,0:T(8,128)(2,1)S(1)} %shard_map.306.refs_0_), channel_id=1, source_target_pairs={{0,8},{1,9},{2,10},{3,11},{4,12},{5,13},{6,14},{7,15},{8,0},{9,1},... | collective-permute-start | bytes 6291464 | tf_op jit(solution)/shard_map/ppermute | solution.py:737
  131.9 26.1 %collective-permute-start.19 = (bf16[512,1024]{1,0:T(8,128)(2,1)S(1)}, bf16[512,1024]{1,0:T(8,128)(2,1)S(1)}, u32[]{:S(2)}, u32[]{:S(2)}) collective-permute-start(bf16[512,1024]{1,0:T(8,128)(2,1)S(1)} %shard_map.297.refs_0_), channel_id=1, source_target_pairs={{0,1},{1,0},{2,3},{3,2},{4,5},{5,4},{6,7},{7,6},{8,24},{9,25},{10,... | collective-permute-start | bytes 3145736 | tf_op jit(solution)/shard_map/ppermute | solution.py:737
  168.1 26.1 %collective-permute-start.23 = (bf16[1024,1024]{1,0:T(8,128)(2,1)S(1)}, bf16[1024,1024]{1,0:T(8,128)(2,1)S(1)}, u32[]{:S(2)}, u32[]{:S(2)}) collective-permute-start(bf16[1024,1024]{1,0:T(8,128)(2,1)S(1)} %shard_map.309.refs_0_), channel_id=1, source_target_pairs={{0,16},{1,17},{2,18},{3,19},{4,20},{5,21},{6,22},{7,23},{8,9},{9,8... | collective-permute-start | bytes 6291464 | tf_op jit(solution)/shard_map/ppermute | solution.py:737
  168.7 25.6 %collective-permute-start.24 = (bf16[1024,1024]{1,0:T(8,128)(2,1)S(1)}, bf16[1024,1024]{1,0:T(8,128)(2,1)S(1)}, u32[]{:S(2)}, u32[]{:S(2)}) collective-permute-start(bf16[1024,1024]{1,0:T(8,128)(2,1)S(1)} %shard_map.309.refs_0_), channel_id=1, source_target_pairs={{0,8},{1,9},{2,10},{3,11},{4,12},{5,13},{6,14},{7,15},{8,0},{9,1},... | collective-permute-start | bytes 6291464 | tf_op jit(solution)/shard_map/ppermute | solution.py:737
  213.7 10.2 %collective-permute-start.28 = (bf16[256,4096]{1,0:T(8,128)(2,1)}, bf16[256,4096]{1,0:T(8,128)(2,1)}, u32[]{:S(2)}, u32[]{:S(2)}) collective-permute-start(bf16[256,4096]{1,0:T(8,128)(2,1)} %get-tuple-element.522.g_ref), channel_id=1, source_target_pairs={{0,8},{1,9},{2,10},{3,11},{4,12},{5,13},{6,14},{7,15},{8,0},{9,1},... | collective-permute-start | bytes 6291464 | tf_op jit(solution)/shard_map/ppermute | solution.py:737
  223.9 43.5 %collective-permute-start.30 = (bf16[1024,1024]{1,0:T(8,128)(2,1)S(1)}, bf16[1024,1024]{1,0:T(8,128)(2,1)S(1)}, u32[]{:S(2)}, u32[]{:S(2)}) collective-permute-start(bf16[1024,1024]{1,0:T(8,128)(2,1)S(1)} %get-tuple-element.533), channel_id=1, source_target_pairs={{0,16},{1,17},{2,18},{3,19},{4,20},{5,21},{6,22},{7,23},{8,9},{9,8... | collective-permute-start | bytes 6291464 | tf_op jit(solution)/shard_map/ppermute | solution.py:737
  242.8 52.9 %collective-permute-start.33 = (bf16[1024,1024]{1,0:T(8,128)(2,1)}, bf16[1024,1024]{1,0:T(8,128)(2,1)}, u32[]{:S(2)}, u32[]{:S(2)}) collective-permute-start(bf16[1024,1024]{1,0:T(8,128)(2,1)} %get-tuple-element.569), channel_id=1, source_target_pairs={{0,16},{1,17},{2,18},{3,19},{4,20},{5,21},{6,22},{7,23},{8,9},{9,8... | collective-permute-start | bytes 6291464 | tf_op jit(solution)/shard_map/ppermute | solution.py:737
  269.0 11.4 %collective-permute-start.31 = (bf16[2,256,1024]{2,1,0:T(8,128)(2,1)}, bf16[2,256,1024]{2,1,0:T(8,128)(2,1)}, u32[]{:S(2)}, u32[]{:S(2)}) collective-permute-start(bf16[2,256,1024]{2,1,0:T(8,128)(2,1)} %get-tuple-element.577.g_ref.refs_8_), channel_id=1, source_target_pairs={{0,8},{1,9},{2,10},{3,11},{4,12},{5,13},{6,14},{7,15},{8,0},{9,1},... | collective-permute-start | bytes 3145736 | tf_op jit(solution)/shard_map/ppermute | solution.py:737
  269.4 20.9 %collective-permute-start.32 = (bf16[2,256,1024]{2,1,0:T(8,128)(2,1)S(1)}, bf16[2,256,1024]{2,1,0:T(8,128)(2,1)}, u32[]{:S(2)}, u32[]{:S(2)}) collective-permute-start(bf16[2,256,1024]{2,1,0:T(8,128)(2,1)S(1)} %copy-done.9), channel_id=1, source_target_pairs={{0,8},{1,9},{2,10},{3,11},{4,12},{5,13},{6,14},{7,15},{8,0},{9,1},... | collective-permute-start | bytes 3145736 | tf_op jit(solution)/shard_map/ppermute | solution.py:737
  269.6 26.1 %collective-permute-start.34 = (bf16[512,1024]{1,0:T(8,128)(2,1)}, bf16[512,1024]{1,0:T(8,128)(2,1)}, u32[]{:S(2)}, u32[]{:S(2)}) collective-permute-start(bf16[512,1024]{1,0:T(8,128)(2,1)} %shard_map.317), channel_id=1, source_target_pairs={{0,1},{1,0},{2,3},{3,2},{4,5},{5,4},{6,7},{7,6},{8,24},{9,25},{10,... | collective-permute-start | bytes 3145736 | tf_op jit(solution)/shard_map/ppermute | solution.py:737
  299.7 16.1 %collective-permute-start.35 = (bf16[4,256,1024]{2,1,0:T(8,128)(2,1)S(1)}, bf16[4,256,1024]{2,1,0:T(8,128)(2,1)S(1)}, u32[]{:S(2)}, u32[]{:S(2)}) collective-permute-start(bf16[4,256,1024]{2,1,0:T(8,128)(2,1)S(1)} %copy-done.11), channel_id=1, source_target_pairs={{0,8},{1,9},{2,10},{3,11},{4,12},{5,13},{6,14},{7,15},{8,0},{9,1},... | collective-permute-start | bytes 6291464 | tf_op jit(solution)/shard_map/ppermute | solution.py:737
  300.3 25.5 %collective-permute-start.40 = (bf16[1024,512]{1,0:T(8,128)(2,1)S(1)}, bf16[1024,512]{1,0:T(8,128)(2,1)S(1)}, u32[]{:S(2)}, u32[]{:S(2)}) collective-permute-start(bf16[1024,512]{1,0:T(8,128)(2,1)S(1)} %get-tuple-element.632), channel_id=1, source_target_pairs={{0,16},{1,17},{2,18},{3,19},{4,20},{5,21},{6,22},{7,23},{8,9},{9,8... | collective-permute-start | bytes 3145736 | tf_op jit(solution)/shard_map/ppermute | solution.py:737
  300.8 25.0 %collective-permute-start.39 = (bf16[512,1024]{1,0:T(8,128)(2,1)S(1)}, bf16[512,1024]{1,0:T(8,128)(2,1)S(1)}, u32[]{:S(2)}, u32[]{:S(2)}) collective-permute-start(bf16[512,1024]{1,0:T(8,128)(2,1)S(1)} %shard_map.321), channel_id=1, source_target_pairs={{0,1},{1,0},{2,3},{3,2},{4,5},{5,4},{6,7},{7,6},{8,24},{9,25},{10,... | collective-permute-start | bytes 3145736 | tf_op jit(solution)/shard_map/ppermute | solution.py:737
  302.1 13.7 %collective-permute-start.38 = (bf16[256,1024]{1,0:T(8,128)(2,1)S(1)}, bf16[256,1024]{1,0:T(8,128)(2,1)S(1)}, u32[]{:S(2)}, u32[]{:S(2)}) collective-permute-start(bf16[256,1024]{1,0:T(8,128)(2,1)S(1)} %get-tuple-element.607), channel_id=1, source_target_pairs={{0,2},{1,3},{2,0},{3,1},{4,6},{5,7},{6,4},{7,5},{8,10},{9,11},{10,... | collective-permute-start | bytes 1572872 | tf_op jit(solution)/shard_map/ppermute | solution.py:737
  315.9 29.3 %collective-permute-start.41 = (bf16[1024,1024]{1,0:T(8,128)(2,1)S(1)}, bf16[1024,1024]{1,0:T(8,128)(2,1)S(1)}, u32[]{:S(2)}, u32[]{:S(2)}) collective-permute-start(bf16[1024,1024]{1,0:T(8,128)(2,1)S(1)} %shard_map.323), channel_id=1, source_target_pairs={{0,8},{1,9},{2,10},{3,11},{4,12},{5,13},{6,14},{7,15},{8,0},{9,1},... | collective-permute-start | bytes 6291464 | tf_op jit(solution)/shard_map/ppermute | solution.py:737
  327.9 35.0 %collective-permute-start.48 = (bf16[1024,1024]{1,0:T(8,128)(2,1)S(1)}, bf16[1024,1024]{1,0:T(8,128)(2,1)S(1)}, u32[]{:S(2)}, u32[]{:S(2)}) collective-permute-start(bf16[1024,1024]{1,0:T(8,128)(2,1)S(1)} %get-tuple-element.711), channel_id=1, source_target_pairs={{0,16},{1,17},{2,18},{3,19},{4,20},{5,21},{6,22},{7,23},{8,9},{9,8... | collective-permute-start | bytes 6291464 | tf_op jit(solution)/shard_map/ppermute | solution.py:737
  328.6 16.6 %collective-permute-start.43 = (bf16[512,512]{1,0:T(8,128)(2,1)S(1)}, bf16[512,512]{1,0:T(8,128)(2,1)S(1)}, u32[]{:S(2)}, u32[]{:S(2)}) collective-permute-start(bf16[512,512]{1,0:T(8,128)(2,1)S(1)} %shard_map.327), channel_id=1, source_target_pairs={{0,1},{1,0},{2,3},{3,2},{4,5},{5,4},{6,7},{7,6},{8,24},{9,25},{10,... | collective-permute-start | bytes 1572872 | tf_op jit(solution)/shard_map/ppermute | solution.py:737
  331.4 29.6 %collective-permute-start.46 = (bf16[256,1024]{1,0:T(8,128)(2,1)S(1)}, bf16[256,1024]{1,0:T(8,128)(2,1)S(1)}, u32[]{:S(2)}, u32[]{:S(2)}) collective-permute-start(bf16[256,1024]{1,0:T(8,128)(2,1)S(1)} %get-tuple-element.691), channel_id=1, source_target_pairs={{0,2},{1,3},{2,0},{3,1},{4,6},{5,7},{6,4},{7,5},{8,10},{9,11},{10,... | collective-permute-start | bytes 1572872 | tf_op jit(solution)/shard_map/ppermute | solution.py:737
  335.6 14.3 %collective-permute-start.44 = (bf16[128,1024]{1,0:T(8,128)(2,1)S(1)}, bf16[128,1024]{1,0:T(8,128)(2,1)S(1)}, u32[]{:S(2)}, u32[]{:S(2)}) collective-permute-start(bf16[128,1024]{1,0:T(8,128)(2,1)S(1)} %get-tuple-element.673), channel_id=1, source_target_pairs={{0,4},{1,5},{2,6},{3,7},{4,0},{5,1},{6,2},{7,3},{8,12},{9,13},{10,... | collective-permute-start | bytes 786440 | tf_op jit(solution)/shard_map/ppermute | solution.py:737
  349.9 15.7 %collective-permute-start.47 = (bf16[128,1024]{1,0:T(8,128)(2,1)S(1)}, bf16[128,1024]{1,0:T(8,128)(2,1)S(1)}, u32[]{:S(2)}, u32[]{:S(2)}) collective-permute-start(bf16[128,1024]{1,0:T(8,128)(2,1)S(1)} %shard_map.331.refs_0_), channel_id=1, source_target_pairs={{0,16},{1,17},{2,18},{3,19},{4,20},{5,21},{6,22},{7,23},{8,24},{9,... | collective-permute-start | bytes 786440 | tf_op jit(solution)/shard_map/ppermute | solution.py:737
  350.8 14.8 %collective-permute-start.49 = (bf16[256,512]{1,0:T(8,128)(2,1)S(1)}, bf16[256,512]{1,0:T(8,128)(2,1)S(1)}, u32[]{:S(2)}, u32[]{:S(2)}) collective-permute-start(bf16[256,512]{1,0:T(8,128)(2,1)S(1)} %get-tuple-element.715), channel_id=1, source_target_pairs={{0,2},{1,3},{2,0},{3,1},{4,6},{5,7},{6,4},{7,5},{8,10},{9,11},{10,... | collective-permute-start | bytes 786440 | tf_op jit(solution)/shard_map/ppermute | solution.py:737
  361.5 35.2 %collective-permute-start.54 = (bf16[1024,512]{1,0:T(8,128)(2,1)S(1)}, bf16[1024,512]{1,0:T(8,128)(2,1)S(1)}, u32[]{:S(2)}, u32[]{:S(2)}) collective-permute-start(bf16[1024,512]{1,0:T(8,128)(2,1)S(1)} %get-tuple-element.743), channel_id=1, source_target_pairs={{0,16},{1,17},{2,18},{3,19},{4,20},{5,21},{6,22},{7,23},{8,9},{9,8... | collective-permute-start | bytes 3145736 | tf_op jit(solution)/shard_map/ppermute | solution.py:737
  366.5 30.2 %collective-permute-start.53 = (bf16[512,1024]{1,0:T(8,128)(2,1)S(1)}, bf16[512,1024]{1,0:T(8,128)(2,1)S(1)}, u32[]{:S(2)}, u32[]{:S(2)}) collective-permute-start(bf16[512,1024]{1,0:T(8,128)(2,1)S(1)} %shard_map.335), channel_id=1, source_target_pairs={{0,1},{1,0},{2,3},{3,2},{4,5},{5,4},{6,7},{7,6},{8,24},{9,25},{10,... | collective-permute-start | bytes 3145736 | tf_op jit(solution)/shard_map/ppermute | solution.py:737
  367.5 22.7 %collective-permute-start.52 = (bf16[256,1024]{1,0:T(8,128)(2,1)S(1)}, bf16[256,1024]{1,0:T(8,128)(2,1)S(1)}, u32[]{:S(2)}, u32[]{:S(2)}) collective-permute-start(bf16[256,1024]{1,0:T(8,128)(2,1)S(1)} %shard_map.334.here_ref), channel_id=1, source_target_pairs={{0,8},{1,9},{2,10},{3,11},{4,12},{5,13},{6,14},{7,15},{8,0},{9,1},... | collective-permute-start | bytes 1572872 | tf_op jit(solution)/shard_map/ppermute | solution.py:737
  367.5 18.1 %collective-permute-start.51 = (bf16[128,1024]{1,0:T(8,128)(2,1)S(1)}, bf16[128,1024]{1,0:T(8,128)(2,1)S(1)}, u32[]{:S(2)}, u32[]{:S(2)}) collective-permute-start(bf16[128,1024]{1,0:T(8,128)(2,1)S(1)} %get-tuple-element.733), channel_id=1, source_target_pairs={{0,4},{1,5},{2,6},{3,7},{4,0},{5,1},{6,2},{7,3},{8,12},{9,13},{10,... | collective-permute-start | bytes 786440 | tf_op jit(solution)/shard_map/ppermute | solution.py:737
  370.5 15.1 %collective-permute-start.50 = (f32[22,1024]{1,0:T(8,128)S(1)}, f32[22,1024]{1,0:T(8,128)S(1)}, u32[]{:S(2)}, u32[]{:S(2)}) collective-permute-start(f32[22,1024]{1,0:T(8,128)S(1)} %add.173), channel_id=1, source_target_pairs={{0,1},{1,0},{2,3},{3,2},{4,5},{5,4},{6,7},{7,6},{8,24},{9,25},{10,... | collective-permute-start | bytes 270344 | tf_op jit(solution)/shard_map/ppermute | solution.py:737
  385.6 11.6 %collective-permute-start.55 = (bf16[128,1024]{1,0:T(8,128)(2,1)S(1)}, bf16[128,1024]{1,0:T(8,128)(2,1)S(1)}, u32[]{:S(2)}, u32[]{:S(2)}) collective-permute-start(bf16[128,1024]{1,0:T(8,128)(2,1)S(1)} %shard_map.338.refs_0_), channel_id=1, source_target_pairs={{0,16},{1,17},{2,18},{3,19},{4,20},{5,21},{6,22},{7,23},{8,24},{9,... | collective-permute-start | bytes 786440 | tf_op jit(solution)/shard_map/ppermute | solution.py:737
  399.2 10.6 %collective-permute-start.59 = (bf16[512,512]{1,0:T(8,128)(2,1)S(1)}, bf16[512,512]{1,0:T(8,128)(2,1)S(1)}, u32[]{:S(2)}, u32[]{:S(2)}) collective-permute-start(bf16[512,512]{1,0:T(8,128)(2,1)S(1)} %shard_map.341), channel_id=1, source_target_pairs={{0,1},{1,0},{2,3},{3,2},{4,5},{5,4},{6,7},{7,6},{8,24},{9,25},{10,... | collective-permute-start | bytes 1572872 | tf_op jit(solution)/shard_map/ppermute | solution.py:737
  400.3 13.8 %collective-permute-start.61 = (bf16[256,1024]{1,0:T(8,128)(2,1)S(1)}, bf16[256,1024]{1,0:T(8,128)(2,1)S(1)}, u32[]{:S(2)}, u32[]{:S(2)}) collective-permute-start(bf16[256,1024]{1,0:T(8,128)(2,1)S(1)} %get-tuple-element.786), channel_id=1, source_target_pairs={{0,2},{1,3},{2,0},{3,1},{4,6},{5,7},{6,4},{7,5},{8,10},{9,11},{10,... | collective-permute-start | bytes 1572872 | tf_op jit(solution)/shard_map/ppermute | solution.py:737
  412.4 11.9 %collective-permute-start.63 = (bf16[256,512]{1,0:T(8,128)(2,1)S(1)}, bf16[256,512]{1,0:T(8,128)(2,1)S(1)}, u32[]{:S(2)}, u32[]{:S(2)}) collective-permute-start(bf16[256,512]{1,0:T(8,128)(2,1)S(1)} %get-tuple-element.796), channel_id=1, source_target_pairs={{0,2},{1,3},{2,0},{3,1},{4,6},{5,7},{6,4},{7,5},{8,10},{9,11},{10,... | collective-permute-start | bytes 786440 | tf_op jit(solution)/shard_map/ppermute | solution.py:737
  414.2 17.7 %collective-permute-start.64 = (bf16[128,1024]{1,0:T(8,128)(2,1)S(1)}, bf16[128,1024]{1,0:T(8,128)(2,1)S(1)}, u32[]{:S(2)}, u32[]{:S(2)}) collective-permute-start(bf16[128,1024]{1,0:T(8,128)(2,1)S(1)} %get-tuple-element.804), channel_id=1, source_target_pairs={{0,4},{1,5},{2,6},{3,7},{4,0},{5,1},{6,2},{7,3},{8,12},{9,13},{10,... | collective-permute-start | bytes 786440 | tf_op jit(solution)/shard_map/ppermute | solution.py:737
  (92 other events, 693.2 us)

commit v4 on v3

--- a/solution.py
+++ b/solution.py
@@ -43,6 +43,10 @@
 
 def array(shape, kind=bf16):
     return jax.ShapeDtypeStruct(shape, kind)
+
+
+def far_array(shape, kind=bf16):
+    return pltpu.HBM(shape, kind)
 
 
 def whole(shape):
@@ -158,7 +162,7 @@
         out_shape=[
             array((n_rows, D), f32),
             array((n_rows, D)),
-            array((n_rows, D), f32),
+            far_array((n_rows, D), f32),
             array((n_rows, LANES), f32),
             array((1, D), f32),
         ],
@@ -233,7 +237,7 @@
     n_rows, depth = rows.shape
     return pl.pallas_call(
         partial(turn_kernel, n_rows // lengths.shape[0], rows_at),
-        out_shape=[array((n_rows, D)), array((n_rows, D), f32), array((n_rows, D)), array((8, D), f32)],
+        out_shape=[array((n_rows, D)), far_array((n_rows, D), f32), array((n_rows, D)), array((8, D), f32)],
         grid_spec=pltpu.PrefetchScalarGridSpec(
             num_scalar_prefetch=1,
             grid=(depth // BLOCK,),
@@ -263,7 +267,7 @@
     block = pl.BlockSpec((n_rows, BLOCK), lambda n: (0, n))
     return pl.pallas_call(
         hidden_back_kernel,
-        out_shape=[array((n_rows, width)), array((1, width), f32)],
+        out_shape=[far_array((n_rows, width)), array((1, width), f32)],
         grid=(width // BLOCK,),
         in_specs=[whole((n_rows, D)), pl.BlockSpec((BLOCK, D), lambda n: (n, 0)), block],
         out_specs=[block, pl.BlockSpec((1, BLOCK), lambda n: (0, n))],
@@ -302,7 +306,7 @@
     )
     return pl.pallas_call(
         partial(join_back_kernel, row_at),
-        out_shape=[array((n_rows, D), f32), array((n_rows, D)), array((n_rows, D)), array((8, D), f32)],
+        out_shape=[far_array((n_rows, D), f32), array((n_rows, D)), array((n_rows, D)), array((8, D), f32)],
         grid=(width // BLOCK,),
         in_specs=[
             g_spec,
@@ -317,7 +321,7 @@
         scratch_shapes=[pltpu.VMEM((n_rows, D), f32)],
         compiler_params=params(18),
         cost_estimate=cost(1024),
-    )(grads, far(weights), above, far(unit), scale, vec, far(after))
+    )(grads, far(weights), far(above), far(unit), scale, vec, far(after))
 
 
 def input_grad_kernel(count, *refs):
@@ -466,10 +470,10 @@
     q_rows, k_rows = queries.shape[0] // seqs, keys.shape[0] // seqs
     group = PAIRS if causal else PAIRS // 2
     slots = 4 if causal else 2
-    out_shape = [array((slots, seqs * q_rows, D))]
+    out_shape = [(far_array if causal else array)((slots, seqs * q_rows, D))]
     out_specs = [slots_block(slots, q_rows, group)]
     if not causal:
-        out_shape.append(array((2, seqs * k_rows, D)))
+        out_shape.append(far_array((2, seqs * k_rows, D)))
         out_specs.append(slots_block(2, k_rows, group))
     out_shape.append(array((8 * seqs, D), f32))
     out_specs.append(head_block(8, 0, group))
@@ -490,7 +494,7 @@
         ),
         compiler_params=params(22),
         cost_estimate=cost(1024),
-    )(lengths, queries, keys, values, grads, beside)
+    )(lengths, queries, keys if causal else far(keys), values if causal else far(values), grads, beside)
 
 
 def place_kernel(rows, idx_ref, *refs):

time: 461 us -> 456 us (0.989)
  local copies, waits for them, and re-layouts: 26.2 us -> 17.7 us
  Pallas kernels: 207 us -> 213 us
    unnamed x154 -> x142, local copies, waits for them, and re-layouts: 20.2 us -> 9.51 us
  transfers between devices with their start and end apart: 70 -> 70, of which waited for: 33 -> 33; matrix products, arithmetic and copies ran while one was open for 2% -> 2% of each run, Pallas kernels for 41% -> 42%
where the time goes in v4:
time: 456 us; the launch traced here: 452 us
  Pallas kernels  213 us (47%)
  waiting for transfers between devices  140 us (31%)
  starting transfers between devices  73.5 us (16%)
  local copies, waits for them, and re-layouts  17.7 us (4%)
    ppermute x70, waiting for transfers between devices, send(): return lax.ppermute(block, ('dp', 'fsdp'), perm)  140 us
    ppermute x70, starting transfers between devices, send(): return lax.ppermute(block, ('dp', 'fsdp'), perm)  73.5 us
    pallas_call x2, Pallas kernels, attend_back(): pl.pallas_call(partial(attend_back_kernel, causal), out_shape=out_shape,...  29.9 us
    pallas_call x5, Pallas kernels, adam_units(): pl.pallas_call(adam_kernel, out_shape=[array(a.shape, f32) for a in state...  28.5 us
    pallas_call x5, Pallas kernels, planes_call(): pl.pallas_call(kernel, out_shape=[array((n * plane, width)) for n in (2,...  26.6 us
    pallas_call x2, Pallas kernels, input_grad(): pl.pallas_call(partial(input_grad_kernel, len(slots)), out_shape=array((n...  19.9 us
    pallas_call x2, Pallas kernels, join_back(): pl.pallas_call(partial(join_back_kernel, row_at), out_shape=[far_array((n...  15.2 us
    pallas_call x2, Pallas kernels, state_grad(): pl.pallas_call(state_grad_kernel, out_shape=array((D, D)), grid_spec=pltp...  14.2 us
  transfers between devices with their start and end apart: 70, of which 33 were waited for; matrix products, arithmetic and copies ran while one was open for 2% of the time, Pallas kernels for 42%

profile of v4, /device:TPU:0, one launch (start us, length us, event | category | flops | bytes accessed | tf_op | source)
XLA Modules:
  0.0 452.3 jit_solution(10443749547071801864)
XLA Ops:
  2.7 4.1 collective-permute-start
  8.4 11.9 %collective-permute-done.refs_1_ = bf16[144,1024]{1,0:T(8,128)(2,1)S(1)} collective-permute-done((bf16[144,1024]{1,0:T(8,128)(2,1)S(1)}, bf16[144,1024]{1,0:T(8,128)(2,1)S(1)}, u32[]{:S(2)}, u32[]{:S(2)}) %collective-permute-start) | collective-permute-done | bytes 294944 | tf_op jit(solution)/shard_map/ppermute | solution.py:741
  22.0 6.4 %collective-permute-done.2.refs_3_ = bf16[144,1024]{1,0:T(8,128)(2,1)S(1)} collective-permute-done((bf16[144,1024]{1,0:T(8,128)(2,1)S(1)}, bf16[144,1024]{1,0:T(8,128)(2,1)S(1)}, u32[]{:S(2)}, u32[]{:S(2)}) %collective-permute-start.2) | collective-permute-done | bytes 294944 | tf_op jit(solution)/shard_map/ppermute | solution.py:741
  30.4 3.3 collective-permute-start.3
  36.5 8.5 %collective-permute-done.3.refs_1_ = bf16[128,1024]{1,0:T(8,128)(2,1)S(1)} collective-permute-done((bf16[128,1024]{1,0:T(8,128)(2,1)S(1)}, bf16[128,1024]{1,0:T(8,128)(2,1)S(1)}, u32[]{:S(2)}, u32[]{:S(2)}) %collective-permute-start.3) | collective-permute-done | bytes 262176 | tf_op jit(solution)/shard_map/ppermute | solution.py:741
  51.3 3.4 collective-permute-start.7
  54.6 9.2 %collective-permute-done.6.refs_3_ = bf16[128,1024]{1,0:T(8,128)(2,1)S(1)} collective-permute-done((bf16[128,1024]{1,0:T(8,128)(2,1)S(1)}, bf16[128,1024]{1,0:T(8,128)(2,1)S(1)}, u32[]{:S(2)}, u32[]{:S(2)}) %collective-permute-start.6) | collective-permute-done | bytes 262176 | tf_op jit(solution)/shard_map/ppermute | solution.py:741
  63.9 3.1 collective-permute-done.7.refs_1_
  72.3 9.5 %collective-permute-done.8.refs_2_ = bf16[256,1024]{1,0:T(8,128)(2,1)} collective-permute-done((bf16[256,1024]{1,0:T(8,128)(2,1)}, bf16[256,1024]{1,0:T(8,128)(2,1)}, u32[]{:S(2)}, u32[]{:S(2)}) %collective-permute-start.8) | collective-permute-done | bytes 524320 | tf_op jit(solution)/shard_map/ppermute | solution.py:741
  97.5 4.0 shard_map.293.w_ref.refs_3_.refs_4_.refs_2_
  103.4 5.1 %collective-permute-done.13.refs_1_ = bf16[128,1024]{1,0:T(8,128)(2,1)S(1)} collective-permute-done((bf16[128,1024]{1,0:T(8,128)(2,1)S(1)}, bf16[128,1024]{1,0:T(8,128)(2,1)S(1)}, u32[]{:S(2)}, u32[]{:S(2)}) %collective-permute-start.13) | collective-permute-done | bytes 262176 | tf_op jit(solution)/shard_map/ppermute | solution.py:741
  109.8 9.9 %shard_map.295.k_ref.v_ref = bf16[2048,2048]{1,0:T(8,128)(2,1)S(1)} custom-call(bf16[2048,1024]{1,0:T(8,128)(2,1)S(1)} %bitcast.136, bf16[1024,4096]{1,0:T(8,128)(2,1)S(1)} %shard_map.293.w_ref.refs_3_.refs_4_.refs_2_, f32[1,2048]{1,0:T(1,128)S(1)} %concatenate.30.b_ref), custom_call_target="tpu_custom_call" | custom-call | bytes 1024 | tf_op jit(solution)/shard_map/pallas_call | solution.py:119
  122.7 6.6 %collective-permute-done.16.refs_1_ = bf16[1024,1024]{1,0:T(8,128)(2,1)S(1)} collective-permute-done((bf16[1024,1024]{1,0:T(8,128)(2,1)S(1)}, bf16[1024,1024]{1,0:T(8,128)(2,1)S(1)}, u32[]{:S(2)}, u32[]{:S(2)}) %collective-permute-start.16) | collective-permute-done | bytes 2097184 | tf_op jit(solution)/shard_map/ppermute | solution.py:741
  136.6 2.7 shard_map.301.x_ref.refs_0_.refs_1_.refs_2_.refs_3_
  142.7 9.9 %shard_map.304.x_ref.refs_0_.refs_1_.refs_2_.refs_3_ = bf16[2,256,1024]{2,1,0:T(8,128)(2,1)S(1)} custom-call(s32[2]{0:T(128)S(1)} %bitcast.161, bf16[256,1024]{1,0:T(8,128)(2,1)S(1)} %shard_map.303.q_ref, bf16[2048,2048]{1,0:T(8,128)(2,1)S(1)} %shard_map.295.k_ref.v_ref, bf16[2048,2048]{1,0:T(8,128)(2,1)S(1)} %shard_map.295.k_ref.v_ref, ...), custom_call_target="tpu_custom_call" | custom-call | bytes 1024 | tf_op jit(solution)/shard_map/pallas_call | solution.py:450
  155.2 2.8 collective-permute-done.19.refs_1_
  158.0 9.4 %collective-permute-done.20.refs_1_ = bf16[1024,1024]{1,0:T(8,128)(2,1)S(1)} collective-permute-done((bf16[1024,1024]{1,0:T(8,128)(2,1)S(1)}, bf16[1024,1024]{1,0:T(8,128)(2,1)S(1)}, u32[]{:S(2)}, u32[]{:S(2)}) %collective-permute-start.20) | collective-permute-done | bytes 2097184 | tf_op jit(solution)/shard_map/ppermute | solution.py:741
  173.9 5.3 %shard_map.308 = (bf16[256,4096]{1,0:T(8,128)(2,1)S(1)}, bf16[256,4096]{1,0:T(8,128)(2,1)S(1)}) custom-call(bf16[256,1024]{1,0:T(8,128)(2,1)S(1)} %get-tuple-element.520.x_ref, bf16[1024,4096]{1,0:T(8,128)(2,1)S(1)} %shard_map.307.w_ref, f32[1,4096]{1,0:T(1,128)S(1)} %bitcast.155), custom_call_target="tpu_custom_call" | custom-call | bytes 1024 | tf_op jit(solution)/shard_map/pallas_call | solution.py:197
  179.2 15.1 %collective-permute-done.23.refs_1_ = bf16[1024,1024]{1,0:T(8,128)(2,1)S(1)} collective-permute-done((bf16[1024,1024]{1,0:T(8,128)(2,1)S(1)}, bf16[1024,1024]{1,0:T(8,128)(2,1)S(1)}, u32[]{:S(2)}, u32[]{:S(2)}) %collective-permute-start.23) | collective-permute-done | bytes 2097184 | tf_op jit(solution)/shard_map/ppermute | solution.py:741
  194.2 4.2 collective-permute-done.25.refs_3_
  200.7 6.3 %shard_map.311 = (bf16[256,1024]{1,0:T(8,128)(2,1)}, f32[256,1024]{1,0:T(8,128)}, bf16[256,1024]{1,0:T(8,128)(2,1)S(1)}, f32[8,1024]{1,0:T(8,128)S(1)}) custom-call(s32[2]{0:T(128)S(1)} %bitcast.159, bf16[256,4096]{1,0:T(8,128)(2,1)S(1)} %get-tuple-element.499.x_ref, bf16[4096,1024]{1,0:T(8,128)(2,1)S(1)} %shard_map.310.w_ref, ...), custom_call_target="tpu_custom_call" | custom-call | bytes 1024 | tf_op jit(solution)/shard_map/pallas_call | solution.py:238
  207.5 4.2 shard_map.312
  214.9 6.2 %shard_map.313 = (bf16[1024,1024]{1,0:T(8,128)(2,1)S(1)}, bf16[512,1024]{1,0:T(8,128)(2,1)S(1)}, bf16[512,1024]{1,0:T(8,128)(2,1)S(1)}) custom-call(s32[4,4]{1,0:T(4,128)S(1)} %get-tuple-element.893.idx_ref, bf16[1,256,4096]{2,1,0:T(8,128)(2,1)} %bitcast.132, bf16[1,256,4096]{2,1,0:T(8,128)(2,1)} %bitcast.133, bf16[1,256,4096]{2,1,0:T(8,128)(2,1)} %bitcast.134, ...), custom_call_target="tpu_custom_call" | custom-call | bytes 1024 | tf_op jit(solution)/shard_map/pallas_call | solution.py:609
  222.6 9.8 %shard_map.314 = (f32[256,1024]{1,0:T(8,128)}, bf16[256,1024]{1,0:T(8,128)(2,1)S(1)}, bf16[256,1024]{1,0:T(8,128)(2,1)S(1)}, f32[8,1024]{1,0:T(8,128)S(1)}) custom-call(bf16[256,4096]{1,0:T(8,128)(2,1)S(1)} %copy-done.15, bf16[1024,4096]{1,0:T(8,128)(2,1)} %copy-done.3, f32[256,1024]{1,0:T(8,128)} %get-tuple-element.508.dr_ref, ...), custom_call_target="tpu_custom_call" | custom-call | bytes 1024 | tf_op jit(solution)/shard_map/pallas_call | solution.py:307
  232.4 7.4 %shard_map.315 = (bf16[1024,1024]{1,0:T(8,128)(2,1)}, bf16[512,1024]{1,0:T(8,128)(2,1)S(1)}, bf16[512,1024]{1,0:T(8,128)(2,1)S(1)}) custom-call(s32[4,4]{1,0:T(4,128)S(1)} %get-tuple-element.891.idx_ref, bf16[1,256,1024]{2,1,0:T(8,128)(2,1)S(1)} %bitcast.139, bf16[1,256,1024]{2,1,0:T(8,128)(2,1)S(1)} %bitcast.140, bf16[1,256,1024]{2,1,0:T(8,128)(2,1)S(1)} %bitcast.141, ...), custom_call_target="tpu_custom_call" | custom-call | bytes 1024 | tf_op jit(solution)/shard_map/pallas_call | solution.py:609
  242.3 20.9 %shard_map.316 = (bf16[2,256,1024]{2,1,0:T(8,128)(2,1)}, bf16[2,2048,1024]{2,1,0:T(8,128)(2,1)}, f32[16,1024]{1,0:T(8,128)S(1)}) custom-call(s32[2]{0:T(128)S(1)} %bitcast.162, bf16[256,1024]{1,0:T(8,128)(2,1)S(1)} %shard_map.303.q_ref, bf16[2048,2048]{1,0:T(8,128)(2,1)} %copy-done.2, bf16[2048,2048]{1,0:T(8,128)(2,1)} %copy-done.2, ...), custom_call_target="tpu_custom_call" | custom-call | bytes 1024 | tf_op jit(solution)/shard_map/pallas_call | solution.py:480
  271.6 5.4 %shard_map.318 = (f32[256,1024]{1,0:T(8,128)}, bf16[256,1024]{1,0:T(8,128)(2,1)S(1)}, bf16[256,1024]{1,0:T(8,128)(2,1)S(1)}, f32[8,1024]{1,0:T(8,128)S(1)}) custom-call(bf16[2,256,1024]{2,1,0:T(8,128)(2,1)} %get-tuple-element.577.g_ref.refs_8_, bf16[1024,4096]{1,0:T(8,128)(2,1)} %copy-done, f32[256,1024]{1,0:T(8,128)} %get-tuple-element.545.dr_ref, ...), custom_call_target="tpu_custom_call" | custom-call | bytes 1024 | tf_op jit(solution)/shard_map/pallas_call | solution.py:307
  277.1 9.0 %shard_map.319 = (bf16[4,256,1024]{2,1,0:T(8,128)(2,1)}, f32[16,1024]{1,0:T(8,128)S(1)}) custom-call(s32[2]{0:T(128)S(1)} %bitcast.160, bf16[256,2048]{1,0:T(8,128)(2,1)S(1)} %copy-done.11, bf16[256,2048]{1,0:T(8,128)(2,1)S(1)} %copy-done.11, bf16[256,1024]{1,0:T(8,128)(2,1)S(1)} %copy-done.17, bf16[256,1024]{1,0:T(8,128)(2,1)S(1)} %get-tuple-element.554.do_ref, ...), custom_call_target="tpu_custom_call" | custom-call | bytes 1024 | tf_op jit(solution)/shard_map/pallas_call | solution.py:480
  286.6 5.2 %shard_map.320 = (bf16[1024,512]{1,0:T(8,128)(2,1)S(1)}, bf16[512,512]{1,0:T(8,128)(2,1)S(1)}, bf16[512,512]{1,0:T(8,128)(2,1)S(1)}) custom-call(s32[4,4]{1,0:T(4,128)S(1)} %copy-done.41, bf16[2,256,1024]{2,1,0:T(8,128)(2,1)S(1)} %copy-done.8, bf16[2,256,1024]{2,1,0:T(8,128)(2,1)S(1)} %copy-done.8, bf16[2,256,1024]{2,1,0:T(8,128)(2,1)S(1)} %copy-done.8, ...), custom_call_target="tpu_custom_call" | custom-call | bytes 1024 | tf_op jit(solution)/shard_map/pallas_call | solution.py:609
  301.6 7.1 %shard_map.323 = bf16[1024,1024]{1,0:T(8,128)(2,1)S(1)} custom-call(s32[1]{0:T(128)} %bitcast.83.slot_ref, bf16[2048,1024]{1,0:T(8,128)(2,1)S(1)} %bitcast.137, bf16[2,2048,1024]{2,1,0:T(8,128)(2,1)} %get-tuple-element.728.g_ref.refs_0_.refs_1_), custom_call_target="tpu_custom_call" | custom-call | bytes 1024 | tf_op jit(solution)/shard_map/pallas_call | solution.py:357
  308.7 3.2 collective-permute-done.38.refs_1_
  312.2 5.6 %shard_map.325 = (bf16[1024,1024]{1,0:T(8,128)(2,1)S(1)}, bf16[512,1024]{1,0:T(8,128)(2,1)S(1)}, bf16[512,1024]{1,0:T(8,128)(2,1)S(1)}) custom-call(s32[4,4]{1,0:T(4,128)S(1)} %copy-done.40, bf16[2,256,1024]{2,1,0:T(8,128)(2,1)S(1)} %shard_map.301.x_ref.refs_0_.refs_1_.refs_2_.refs_3_, ...), custom_call_target="tpu_custom_call" | custom-call | bytes 1024 | tf_op jit(solution)/shard_map/pallas_call | solution.py:609
  317.8 4.1 collective-permute-done.40.refs_1_
  328.2 3.7 collective-permute-done.42
  334.0 7.1 %shard_map.328.refs_0_.refs_1_.refs_2_.refs_3_ = bf16[1024,1024]{1,0:T(8,128)(2,1)S(1)} custom-call(s32[1]{0:T(128)} %bitcast.99.slot_ref, bf16[2048,1024]{1,0:T(8,128)(2,1)S(1)} %bitcast.138, bf16[2,2048,1024]{2,1,0:T(8,128)(2,1)} %get-tuple-element.728.g_ref.refs_0_.refs_1_), custom_call_target="tpu_custom_call" | custom-call | bytes 1024 | tf_op jit(solution)/shard_map/pallas_call | solution.py:357
  347.1 4.1 collective-permute-start.49
  351.2 6.0 %shard_map.332 = bf16[256,1024]{1,0:T(8,128)(2,1)} custom-call(bf16[4,256,1024]{2,1,0:T(8,128)(2,1)} %get-tuple-element.687.refs_8_.refs_0_.refs_1_.refs_2_, bf16[4,256,1024]{2,1,0:T(8,128)(2,1)} %get-tuple-element.687.refs_8_.refs_0_.refs_1_.refs_2_, bf16[4,256,1024]{2,1,0:T(8,128)(2,1)} %get-tuple-element.687.refs_8_.refs_0_.refs_1_.refs_2_, ...), custom_call_target="tpu_custom_call" | custom-call | bytes 1024 | tf_op jit(solution)/shard_map/pallas_call | solution.py:338
  363.3 3.0 collective-permute-start.51
  366.5 13.9 %shard_map.337 = bf16[2048,1024]{1,0:T(8,128)(2,1)} custom-call(bf16[2,2048,1024]{2,1,0:T(8,128)(2,1)} %get-tuple-element.728.g_ref.refs_0_.refs_1_, bf16[2,2048,1024]{2,1,0:T(8,128)(2,1)} %get-tuple-element.728.g_ref.refs_0_.refs_1_, bf16[1024,4096]{1,0:T(8,128)(2,1)} %copy-done.1, bf16[1024,4096]{1,0:T(8,128)(2,1)} %copy-done.1), custom_call_target="tpu_custom_call" | custom-call | bytes 1024 | tf_op jit(solution)/shard_map/pallas_call | solution.py:338
  383.2 3.1 collective-permute-start.56
  386.3 6.5 %shard_map.339 = (f32[512,1024]{1,0:T(8,128)}, f32[512,1024]{1,0:T(8,128)}, f32[512,1024]{1,0:T(8,128)}) custom-call(s32[1]{0:T(128)} %bitcast.94.idx_ref, bf16[256,1024]{1,0:T(8,128)(2,1)S(1)} %shard_map.334.here_ref, bf16[256,1024]{1,0:T(8,128)(2,1)S(1)} %collective-permute-done.52.there_ref, f32[512,1024]{1,0:T(8,128)} %w_ref.5, f32[512,1024]{1,0:T(8,128)} %m_ref.5, ...), custom_call_target="tpu_custom_call" | custom-call | bytes 1024 | tf_op jit(solution)/shard_map/pallas_call | solution.py:688
  399.3 6.5 %shard_map.344 = (f32[128,4096]{1,0:T(8,128)}, f32[128,4096]{1,0:T(8,128)}, f32[128,4096]{1,0:T(8,128)}) custom-call(s32[1]{0:T(128)} %bitcast.94.idx_ref, bf16[256,1024]{1,0:T(8,128)(2,1)S(1)} %shard_map.342.here_ref, bf16[256,1024]{1,0:T(8,128)(2,1)S(1)} %collective-permute-done.58.there_ref, f32[128,4096]{1,0:T(8,128)} %w_ref.6, f32[128,4096]{1,0:T(8,128)} %m_ref.6, ...), custom_call_target="tpu_custom_call" | custom-call | bytes 1024 | tf_op jit(solution)/shard_map/pallas_call | solution.py:688
  410.5 4.5 shard_map.348
  414.9 5.5 %collective-permute-done.63.refs_1_ = bf16[256,512]{1,0:T(8,128)(2,1)S(1)} collective-permute-done((bf16[256,512]{1,0:T(8,128)(2,1)S(1)}, bf16[256,512]{1,0:T(8,128)(2,1)S(1)}, u32[]{:S(2)}, u32[]{:S(2)}) %collective-permute-start.63) | collective-permute-done | bytes 262176 | tf_op jit(solution)/shard_map/ppermute | solution.py:741
  421.6 5.9 %collective-permute-done.64.refs_1_ = bf16[128,1024]{1,0:T(8,128)(2,1)S(1)} collective-permute-done((bf16[128,1024]{1,0:T(8,128)(2,1)S(1)}, bf16[128,1024]{1,0:T(8,128)(2,1)S(1)}, u32[]{:S(2)}, u32[]{:S(2)}) %collective-permute-start.64) | collective-permute-done | bytes 262176 | tf_op jit(solution)/shard_map/ppermute | solution.py:741
  430.8 6.0 %collective-permute-done.67.refs_1_ = bf16[128,512]{1,0:T(8,128)(2,1)S(1)} collective-permute-done((bf16[128,512]{1,0:T(8,128)(2,1)S(1)}, bf16[128,512]{1,0:T(8,128)(2,1)S(1)}, u32[]{:S(2)}, u32[]{:S(2)}) %collective-permute-start.67) | collective-permute-done | bytes 131104 | tf_op jit(solution)/shard_map/ppermute | solution.py:741
  440.4 4.5 shard_map.354
  444.9 6.5 %shard_map.355 = (f32[8,128,1024]{2,1,0:T(8,128)}, f32[8,128,1024]{2,1,0:T(8,128)}, f32[8,128,1024]{2,1,0:T(8,128)}) custom-call(s32[1]{0:T(128)} %bitcast.94.idx_ref, bf16[256,1024]{1,0:T(8,128)(2,1)S(1)} %shard_map.352.here_ref, ...), custom_call_target="tpu_custom_call", output_to_operand_aliasing={{0}: (6, {}), {1}: (7, {}), {2}: (8, {})} | custom-call | bytes 1024 | tf_op jit(solution)/shard_map/pallas_call | solution.py:688
  (371 shorter events, 133.6 us)
Async XLA Ops:
  2.7 17.5 %collective-permute-start = (bf16[144,1024]{1,0:T(8,128)(2,1)S(1)}, bf16[144,1024]{1,0:T(8,128)(2,1)S(1)}, u32[]{:S(2)}, u32[]{:S(2)}) collective-permute-start(bf16[144,1024]{1,0:T(8,128)(2,1)S(1)} %fusion.6.refs_0_), channel_id=1, source_target_pairs={{0,4},{1,5},{2,6},{3,7},{4,0},{5,1},{6,2},{7,3},{8,12},{9,13},{10,... | collective-permute-start | bytes 884744 | tf_op jit(solution)/shard_map/ppermute | solution.py:741
  6.8 13.6 %collective-permute-start.1 = (bf16[144,1024]{1,0:T(8,128)(2,1)S(1)}, bf16[144,1024]{1,0:T(8,128)(2,1)S(1)}, u32[]{:S(2)}, u32[]{:S(2)}) collective-permute-start(bf16[144,1024]{1,0:T(8,128)(2,1)S(1)} %fusion.6.refs_0_), channel_id=1, source_target_pairs={{0,2},{1,3},{2,0},{3,1},{4,6},{5,7},{6,4},{7,5},{8,10},{9,11},{10,... | collective-permute-start | bytes 884744 | tf_op jit(solution)/shard_map/ppermute | solution.py:741
  29.0 17.1 %collective-permute-start.5 = (bf16[576,1024]{1,0:T(8,128)(2,1)S(1)}, bf16[576,1024]{1,0:T(8,128)(2,1)S(1)}, u32[]{:S(2)}, u32[]{:S(2)}) collective-permute-start(bf16[576,1024]{1,0:T(8,128)(2,1)S(1)} %shard_map.288.refs_0_), channel_id=1, source_target_pairs={{0,1},{1,0},{2,3},{3,2},{4,5},{5,4},{6,7},{7,6},{8,24},{9,25},{10,... | collective-permute-start | bytes 3538952 | tf_op jit(solution)/shard_map/ppermute | solution.py:741
  30.4 14.7 %collective-permute-start.3 = (bf16[128,1024]{1,0:T(8,128)(2,1)S(1)}, bf16[128,1024]{1,0:T(8,128)(2,1)S(1)}, u32[]{:S(2)}, u32[]{:S(2)}) collective-permute-start(bf16[128,1024]{1,0:T(8,128)(2,1)S(1)} %get-tuple-element.446.refs_0_), channel_id=1, source_target_pairs={{0,4},{1,5},{2,6},{3,7},{4,0},{5,1},{6,2},{7,3},{8,12},{9,13},{10,... | collective-permute-start | bytes 786440 | tf_op jit(solution)/shard_map/ppermute | solution.py:741
  33.6 11.8 %collective-permute-start.4 = (bf16[128,1024]{1,0:T(8,128)(2,1)S(1)}, bf16[128,1024]{1,0:T(8,128)(2,1)S(1)}, u32[]{:S(2)}, u32[]{:S(2)}) collective-permute-start(bf16[128,1024]{1,0:T(8,128)(2,1)S(1)} %get-tuple-element.446.refs_0_), channel_id=1, source_target_pairs={{0,2},{1,3},{2,0},{3,1},{4,6},{5,7},{6,4},{7,5},{8,10},{9,11},{10,... | collective-permute-start | bytes 786440 | tf_op jit(solution)/shard_map/ppermute | solution.py:741
  49.1 40.0 %collective-permute-start.10 = (bf16[1152,1024]{1,0:T(8,128)(2,1)S(1)}, bf16[1152,1024]{1,0:T(8,128)(2,1)}, u32[]{:S(2)}, u32[]{:S(2)}) collective-permute-start(bf16[1152,1024]{1,0:T(8,128)(2,1)S(1)} %shard_map.292.refs_0_), channel_id=1, source_target_pairs={{0,16},{1,17},{2,18},{3,19},{4,20},{5,21},{6,22},{7,23},{8,9},{9,8... | collective-permute-start | bytes 7077896 | tf_op jit(solution)/shard_map/ppermute | solution.py:741
  49.7 39.4 %collective-permute-start.11 = (bf16[1152,1024]{1,0:T(8,128)(2,1)S(1)}, bf16[1152,1024]{1,0:T(8,128)(2,1)}, u32[]{:S(2)}, u32[]{:S(2)}) collective-permute-start(bf16[1152,1024]{1,0:T(8,128)(2,1)S(1)} %shard_map.292.refs_0_), channel_id=1, source_target_pairs={{0,8},{1,9},{2,10},{3,11},{4,12},{5,13},{6,14},{7,15},{8,0},{9,1},... | collective-permute-start | bytes 7077896 | tf_op jit(solution)/shard_map/ppermute | solution.py:741
  49.7 14.1 %collective-permute-start.6 = (bf16[128,1024]{1,0:T(8,128)(2,1)S(1)}, bf16[128,1024]{1,0:T(8,128)(2,1)S(1)}, u32[]{:S(2)}, u32[]{:S(2)}) collective-permute-start(bf16[128,1024]{1,0:T(8,128)(2,1)S(1)} %copy-done.35), channel_id=1, source_target_pairs={{0,2},{1,3},{2,0},{3,1},{4,6},{5,7},{6,4},{7,5},{8,10},{9,11},{10,... | collective-permute-start | bytes 786440 | tf_op jit(solution)/shard_map/ppermute | solution.py:741
  51.3 15.7 %collective-permute-start.7 = (bf16[128,1024]{1,0:T(8,128)(2,1)S(1)}, bf16[128,1024]{1,0:T(8,128)(2,1)S(1)}, u32[]{:S(2)}, u32[]{:S(2)}) collective-permute-start(bf16[128,1024]{1,0:T(8,128)(2,1)S(1)} %dynamic-slice_convert_fusion.1.refs_0_), channel_id=1, source_target_pairs={{0,4},{1,5},{2,6},{3,7},{4,0},{5,1},{6,2},{7,3},{8,12},{9,13},{10,... | collective-permute-start | bytes 786440 | tf_op jit(solution)/shard_map/ppermute | solution.py:741
  67.6 19.9 %collective-permute-start.9 = (bf16[512,1024]{1,0:T(8,128)(2,1)S(1)}, bf16[512,1024]{1,0:T(8,128)(2,1)}, u32[]{:S(2)}, u32[]{:S(2)}) collective-permute-start(bf16[512,1024]{1,0:T(8,128)(2,1)S(1)} %shard_map.291.refs_0_), channel_id=1, source_target_pairs={{0,1},{1,0},{2,3},{3,2},{4,5},{5,4},{6,7},{7,6},{8,24},{9,25},{10,... | collective-permute-start | bytes 3145736 | tf_op jit(solution)/shard_map/ppermute | solution.py:741
  70.6 11.1 %collective-permute-start.8 = (bf16[256,1024]{1,0:T(8,128)(2,1)}, bf16[256,1024]{1,0:T(8,128)(2,1)}, u32[]{:S(2)}, u32[]{:S(2)}) collective-permute-start(bf16[256,1024]{1,0:T(8,128)(2,1)} %shard_map.289), channel_id=1, source_target_pairs={{0,2},{1,3},{2,0},{3,1},{4,6},{5,7},{6,4},{7,5},{8,10},{9,11},{10,... | collective-permute-start | bytes 1572872 | tf_op jit(solution)/shard_map/ppermute | solution.py:741
  92.0 37.3 %collective-permute-start.16 = (bf16[1024,1024]{1,0:T(8,128)(2,1)S(1)}, bf16[1024,1024]{1,0:T(8,128)(2,1)S(1)}, u32[]{:S(2)}, u32[]{:S(2)}) collective-permute-start(bf16[1024,1024]{1,0:T(8,128)(2,1)S(1)} %shard_map.298.refs_0_), channel_id=1, source_target_pairs={{0,16},{1,17},{2,18},{3,19},{4,20},{5,21},{6,22},{7,23},{8,9},{9,8... | collective-permute-start | bytes 6291464 | tf_op jit(solution)/shard_map/ppermute | solution.py:741
  92.6 36.8 %collective-permute-start.17 = (bf16[1024,1024]{1,0:T(8,128)(2,1)S(1)}, bf16[1024,1024]{1,0:T(8,128)(2,1)S(1)}, u32[]{:S(2)}, u32[]{:S(2)}) collective-permute-start(bf16[1024,1024]{1,0:T(8,128)(2,1)S(1)} %shard_map.298.refs_0_), channel_id=1, source_target_pairs={{0,8},{1,9},{2,10},{3,11},{4,12},{5,13},{6,14},{7,15},{8,0},{9,1},... | collective-permute-start | bytes 6291464 | tf_op jit(solution)/shard_map/ppermute | solution.py:741
  93.7 14.7 %collective-permute-start.13 = (bf16[128,1024]{1,0:T(8,128)(2,1)S(1)}, bf16[128,1024]{1,0:T(8,128)(2,1)S(1)}, u32[]{:S(2)}, u32[]{:S(2)}) collective-permute-start(bf16[128,1024]{1,0:T(8,128)(2,1)S(1)} %dynamic-slice_convert_fusion.refs_0_), channel_id=1, source_target_pairs={{0,4},{1,5},{2,6},{3,7},{4,0},{5,1},{6,2},{7,3},{8,12},{9,13},{10,... | collective-permute-start | bytes 786440 | tf_op jit(solution)/shard_map/ppermute | solution.py:741
  95.8 27.0 %collective-permute-start.15 = (bf16[512,1024]{1,0:T(8,128)(2,1)S(1)}, bf16[512,1024]{1,0:T(8,128)(2,1)S(1)}, u32[]{:S(2)}, u32[]{:S(2)}) collective-permute-start(bf16[512,1024]{1,0:T(8,128)(2,1)S(1)} %shard_map.290.refs_0_), channel_id=1, source_target_pairs={{0,1},{1,0},{2,3},{3,2},{4,5},{5,4},{6,7},{7,6},{8,24},{9,25},{10,... | collective-permute-start | bytes 3145736 | tf_op jit(solution)/shard_map/ppermute | solution.py:741
  109.1 13.0 %collective-permute-start.14 = (bf16[256,1024]{1,0:T(8,128)(2,1)S(1)}, bf16[256,1024]{1,0:T(8,128)(2,1)S(1)}, u32[]{:S(2)}, u32[]{:S(2)}) collective-permute-start(bf16[256,1024]{1,0:T(8,128)(2,1)S(1)} %shard_map.296), channel_id=1, source_target_pairs={{0,2},{1,3},{2,0},{3,1},{4,6},{5,7},{6,4},{7,5},{8,10},{9,11},{10,... | collective-permute-start | bytes 1572872 | tf_op jit(solution)/shard_map/ppermute | solution.py:741
  130.1 37.3 %collective-permute-start.20 = (bf16[1024,1024]{1,0:T(8,128)(2,1)S(1)}, bf16[1024,1024]{1,0:T(8,128)(2,1)S(1)}, u32[]{:S(2)}, u32[]{:S(2)}) collective-permute-start(bf16[1024,1024]{1,0:T(8,128)(2,1)S(1)} %shard_map.306.refs_0_), channel_id=1, source_target_pairs={{0,16},{1,17},{2,18},{3,19},{4,20},{5,21},{6,22},{7,23},{8,9},{9,8... | collective-permute-start | bytes 6291464 | tf_op jit(solution)/shard_map/ppermute | solution.py:741
  130.6 36.8 %collective-permute-start.21 = (bf16[1024,1024]{1,0:T(8,128)(2,1)S(1)}, bf16[1024,1024]{1,0:T(8,128)(2,1)S(1)}, u32[]{:S(2)}, u32[]{:S(2)}) collective-permute-start(bf16[1024,1024]{1,0:T(8,128)(2,1)S(1)} %shard_map.306.refs_0_), channel_id=1, source_target_pairs={{0,8},{1,9},{2,10},{3,11},{4,12},{5,13},{6,14},{7,15},{8,0},{9,1},... | collective-permute-start | bytes 6291464 | tf_op jit(solution)/shard_map/ppermute | solution.py:741
  131.9 26.1 %collective-permute-start.19 = (bf16[512,1024]{1,0:T(8,128)(2,1)S(1)}, bf16[512,1024]{1,0:T(8,128)(2,1)S(1)}, u32[]{:S(2)}, u32[]{:S(2)}) collective-permute-start(bf16[512,1024]{1,0:T(8,128)(2,1)S(1)} %shard_map.297.refs_0_), channel_id=1, source_target_pairs={{0,1},{1,0},{2,3},{3,2},{4,5},{5,4},{6,7},{7,6},{8,24},{9,25},{10,... | collective-permute-start | bytes 3145736 | tf_op jit(solution)/shard_map/ppermute | solution.py:741
  168.1 26.1 %collective-permute-start.23 = (bf16[1024,1024]{1,0:T(8,128)(2,1)S(1)}, bf16[1024,1024]{1,0:T(8,128)(2,1)S(1)}, u32[]{:S(2)}, u32[]{:S(2)}) collective-permute-start(bf16[1024,1024]{1,0:T(8,128)(2,1)S(1)} %shard_map.309.refs_0_), channel_id=1, source_target_pairs={{0,16},{1,17},{2,18},{3,19},{4,20},{5,21},{6,22},{7,23},{8,9},{9,8... | collective-permute-start | bytes 6291464 | tf_op jit(solution)/shard_map/ppermute | solution.py:741
  168.7 25.6 %collective-permute-start.24 = (bf16[1024,1024]{1,0:T(8,128)(2,1)S(1)}, bf16[1024,1024]{1,0:T(8,128)(2,1)S(1)}, u32[]{:S(2)}, u32[]{:S(2)}) collective-permute-start(bf16[1024,1024]{1,0:T(8,128)(2,1)S(1)} %shard_map.309.refs_0_), channel_id=1, source_target_pairs={{0,8},{1,9},{2,10},{3,11},{4,12},{5,13},{6,14},{7,15},{8,0},{9,1},... | collective-permute-start | bytes 6291464 | tf_op jit(solution)/shard_map/ppermute | solution.py:741
  222.1 41.1 %collective-permute-start.30 = (bf16[1024,1024]{1,0:T(8,128)(2,1)S(1)}, bf16[1024,1024]{1,0:T(8,128)(2,1)S(1)}, u32[]{:S(2)}, u32[]{:S(2)}) collective-permute-start(bf16[1024,1024]{1,0:T(8,128)(2,1)S(1)} %get-tuple-element.533), channel_id=1, source_target_pairs={{0,16},{1,17},{2,18},{3,19},{4,20},{5,21},{6,22},{7,23},{8,9},{9,8... | collective-permute-start | bytes 6291464 | tf_op jit(solution)/shard_map/ppermute | solution.py:741
  240.7 51.0 %collective-permute-start.33 = (bf16[1024,1024]{1,0:T(8,128)(2,1)}, bf16[1024,1024]{1,0:T(8,128)(2,1)}, u32[]{:S(2)}, u32[]{:S(2)}) collective-permute-start(bf16[1024,1024]{1,0:T(8,128)(2,1)} %get-tuple-element.569), channel_id=1, source_target_pairs={{0,16},{1,17},{2,18},{3,19},{4,20},{5,21},{6,22},{7,23},{8,9},{9,8... | collective-permute-start | bytes 6291464 | tf_op jit(solution)/shard_map/ppermute | solution.py:741
  264.8 12.2 %collective-permute-start.31 = (bf16[2,256,1024]{2,1,0:T(8,128)(2,1)}, bf16[2,256,1024]{2,1,0:T(8,128)(2,1)}, u32[]{:S(2)}, u32[]{:S(2)}) collective-permute-start(bf16[2,256,1024]{2,1,0:T(8,128)(2,1)} %get-tuple-element.577.g_ref.refs_8_), channel_id=1, source_target_pairs={{0,8},{1,9},{2,10},{3,11},{4,12},{5,13},{6,14},{7,15},{8,0},{9,1},... | collective-permute-start | bytes 3145736 | tf_op jit(solution)/shard_map/ppermute | solution.py:741
  265.2 21.3 %collective-permute-start.32 = (bf16[2,256,1024]{2,1,0:T(8,128)(2,1)S(1)}, bf16[2,256,1024]{2,1,0:T(8,128)(2,1)S(1)}, u32[]{:S(2)}, u32[]{:S(2)}) collective-permute-start(bf16[2,256,1024]{2,1,0:T(8,128)(2,1)S(1)} %copy-done.8), channel_id=1, source_target_pairs={{0,8},{1,9},{2,10},{3,11},{4,12},{5,13},{6,14},{7,15},{8,0},{9,1},... | collective-permute-start | bytes 3145736 | tf_op jit(solution)/shard_map/ppermute | solution.py:741
  265.4 26.4 %collective-permute-start.34 = (bf16[512,1024]{1,0:T(8,128)(2,1)}, bf16[512,1024]{1,0:T(8,128)(2,1)}, u32[]{:S(2)}, u32[]{:S(2)}) collective-permute-start(bf16[512,1024]{1,0:T(8,128)(2,1)} %shard_map.317), channel_id=1, source_target_pairs={{0,1},{1,0},{2,3},{3,2},{4,5},{5,4},{6,7},{7,6},{8,24},{9,25},{10,... | collective-permute-start | bytes 3145736 | tf_op jit(solution)/shard_map/ppermute | solution.py:741
  295.7 16.2 %collective-permute-start.35 = (bf16[4,256,1024]{2,1,0:T(8,128)(2,1)S(1)}, bf16[4,256,1024]{2,1,0:T(8,128)(2,1)S(1)}, u32[]{:S(2)}, u32[]{:S(2)}) collective-permute-start(bf16[4,256,1024]{2,1,0:T(8,128)(2,1)S(1)} %copy-done.9), channel_id=1, source_target_pairs={{0,8},{1,9},{2,10},{3,11},{4,12},{5,13},{6,14},{7,15},{8,0},{9,1},... | collective-permute-start | bytes 6291464 | tf_op jit(solution)/shard_map/ppermute | solution.py:741
  296.3 25.6 %collective-permute-start.40 = (bf16[1024,512]{1,0:T(8,128)(2,1)S(1)}, bf16[1024,512]{1,0:T(8,128)(2,1)S(1)}, u32[]{:S(2)}, u32[]{:S(2)}) collective-permute-start(bf16[1024,512]{1,0:T(8,128)(2,1)S(1)} %get-tuple-element.632), channel_id=1, source_target_pairs={{0,16},{1,17},{2,18},{3,19},{4,20},{5,21},{6,22},{7,23},{8,9},{9,8... | collective-permute-start | bytes 3145736 | tf_op jit(solution)/shard_map/ppermute | solution.py:741
  296.8 25.1 %collective-permute-start.39 = (bf16[512,1024]{1,0:T(8,128)(2,1)S(1)}, bf16[512,1024]{1,0:T(8,128)(2,1)S(1)}, u32[]{:S(2)}, u32[]{:S(2)}) collective-permute-start(bf16[512,1024]{1,0:T(8,128)(2,1)S(1)} %shard_map.321), channel_id=1, source_target_pairs={{0,1},{1,0},{2,3},{3,2},{4,5},{5,4},{6,7},{7,6},{8,24},{9,25},{10,... | collective-permute-start | bytes 3145736 | tf_op jit(solution)/shard_map/ppermute | solution.py:741
  298.3 13.7 %collective-permute-start.38 = (bf16[256,1024]{1,0:T(8,128)(2,1)S(1)}, bf16[256,1024]{1,0:T(8,128)(2,1)S(1)}, u32[]{:S(2)}, u32[]{:S(2)}) collective-permute-start(bf16[256,1024]{1,0:T(8,128)(2,1)S(1)} %get-tuple-element.607), channel_id=1, source_target_pairs={{0,2},{1,3},{2,0},{3,1},{4,6},{5,7},{6,4},{7,5},{8,10},{9,11},{10,... | collective-permute-start | bytes 1572872 | tf_op jit(solution)/shard_map/ppermute | solution.py:741
  312.1 29.0 %collective-permute-start.41 = (bf16[1024,1024]{1,0:T(8,128)(2,1)S(1)}, bf16[1024,1024]{1,0:T(8,128)(2,1)S(1)}, u32[]{:S(2)}, u32[]{:S(2)}) collective-permute-start(bf16[1024,1024]{1,0:T(8,128)(2,1)S(1)} %shard_map.323), channel_id=1, source_target_pairs={{0,8},{1,9},{2,10},{3,11},{4,12},{5,13},{6,14},{7,15},{8,0},{9,1},... | collective-permute-start | bytes 6291464 | tf_op jit(solution)/shard_map/ppermute | solution.py:741
  324.1 34.9 %collective-permute-start.48 = (bf16[1024,1024]{1,0:T(8,128)(2,1)S(1)}, bf16[1024,1024]{1,0:T(8,128)(2,1)S(1)}, u32[]{:S(2)}, u32[]{:S(2)}) collective-permute-start(bf16[1024,1024]{1,0:T(8,128)(2,1)S(1)} %get-tuple-element.711), channel_id=1, source_target_pairs={{0,16},{1,17},{2,18},{3,19},{4,20},{5,21},{6,22},{7,23},{8,9},{9,8... | collective-permute-start | bytes 6291464 | tf_op jit(solution)/shard_map/ppermute | solution.py:741
  324.5 16.6 %collective-permute-start.43 = (bf16[512,512]{1,0:T(8,128)(2,1)S(1)}, bf16[512,512]{1,0:T(8,128)(2,1)S(1)}, u32[]{:S(2)}, u32[]{:S(2)}) collective-permute-start(bf16[512,512]{1,0:T(8,128)(2,1)S(1)} %shard_map.327), channel_id=1, source_target_pairs={{0,1},{1,0},{2,3},{3,2},{4,5},{5,4},{6,7},{7,6},{8,24},{9,25},{10,... | collective-permute-start | bytes 1572872 | tf_op jit(solution)/shard_map/ppermute | solution.py:741
  327.5 29.7 %collective-permute-start.46 = (bf16[256,1024]{1,0:T(8,128)(2,1)S(1)}, bf16[256,1024]{1,0:T(8,128)(2,1)S(1)}, u32[]{:S(2)}, u32[]{:S(2)}) collective-permute-start(bf16[256,1024]{1,0:T(8,128)(2,1)S(1)} %get-tuple-element.691), channel_id=1, source_target_pairs={{0,2},{1,3},{2,0},{3,1},{4,6},{5,7},{6,4},{7,5},{8,10},{9,11},{10,... | collective-permute-start | bytes 1572872 | tf_op jit(solution)/shard_map/ppermute | solution.py:741
  332.0 13.8 %collective-permute-start.44 = (bf16[128,1024]{1,0:T(8,128)(2,1)S(1)}, bf16[128,1024]{1,0:T(8,128)(2,1)S(1)}, u32[]{:S(2)}, u32[]{:S(2)}) collective-permute-start(bf16[128,1024]{1,0:T(8,128)(2,1)S(1)} %get-tuple-element.673), channel_id=1, source_target_pairs={{0,4},{1,5},{2,6},{3,7},{4,0},{5,1},{6,2},{7,3},{8,12},{9,13},{10,... | collective-permute-start | bytes 786440 | tf_op jit(solution)/shard_map/ppermute | solution.py:741
  345.8 15.6 %collective-permute-start.47 = (bf16[128,1024]{1,0:T(8,128)(2,1)S(1)}, bf16[128,1024]{1,0:T(8,128)(2,1)S(1)}, u32[]{:S(2)}, u32[]{:S(2)}) collective-permute-start(bf16[128,1024]{1,0:T(8,128)(2,1)S(1)} %shard_map.331.refs_0_), channel_id=1, source_target_pairs={{0,16},{1,17},{2,18},{3,19},{4,20},{5,21},{6,22},{7,23},{8,24},{9,... | collective-permute-start | bytes 786440 | tf_op jit(solution)/shard_map/ppermute | solution.py:741
  347.1 14.4 %collective-permute-start.49 = (bf16[256,512]{1,0:T(8,128)(2,1)S(1)}, bf16[256,512]{1,0:T(8,128)(2,1)S(1)}, u32[]{:S(2)}, u32[]{:S(2)}) collective-permute-start(bf16[256,512]{1,0:T(8,128)(2,1)S(1)} %get-tuple-element.715), channel_id=1, source_target_pairs={{0,2},{1,3},{2,0},{3,1},{4,6},{5,7},{6,4},{7,5},{8,10},{9,11},{10,... | collective-permute-start | bytes 786440 | tf_op jit(solution)/shard_map/ppermute | solution.py:741
  357.7 35.1 %collective-permute-start.54 = (bf16[1024,512]{1,0:T(8,128)(2,1)S(1)}, bf16[1024,512]{1,0:T(8,128)(2,1)S(1)}, u32[]{:S(2)}, u32[]{:S(2)}) collective-permute-start(bf16[1024,512]{1,0:T(8,128)(2,1)S(1)} %get-tuple-element.743), channel_id=1, source_target_pairs={{0,16},{1,17},{2,18},{3,19},{4,20},{5,21},{6,22},{7,23},{8,9},{9,8... | collective-permute-start | bytes 3145736 | tf_op jit(solution)/shard_map/ppermute | solution.py:741
  362.4 30.4 %collective-permute-start.53 = (bf16[512,1024]{1,0:T(8,128)(2,1)S(1)}, bf16[512,1024]{1,0:T(8,128)(2,1)S(1)}, u32[]{:S(2)}, u32[]{:S(2)}) collective-permute-start(bf16[512,1024]{1,0:T(8,128)(2,1)S(1)} %shard_map.335), channel_id=1, source_target_pairs={{0,1},{1,0},{2,3},{3,2},{4,5},{5,4},{6,7},{7,6},{8,24},{9,25},{10,... | collective-permute-start | bytes 3145736 | tf_op jit(solution)/shard_map/ppermute | solution.py:741
  363.3 23.0 %collective-permute-start.52 = (bf16[256,1024]{1,0:T(8,128)(2,1)S(1)}, bf16[256,1024]{1,0:T(8,128)(2,1)S(1)}, u32[]{:S(2)}, u32[]{:S(2)}) collective-permute-start(bf16[256,1024]{1,0:T(8,128)(2,1)S(1)} %shard_map.334.here_ref), channel_id=1, source_target_pairs={{0,8},{1,9},{2,10},{3,11},{4,12},{5,13},{6,14},{7,15},{8,0},{9,1},... | collective-permute-start | bytes 1572872 | tf_op jit(solution)/shard_map/ppermute | solution.py:741
  363.3 18.4 %collective-permute-start.51 = (bf16[128,1024]{1,0:T(8,128)(2,1)S(1)}, bf16[128,1024]{1,0:T(8,128)(2,1)S(1)}, u32[]{:S(2)}, u32[]{:S(2)}) collective-permute-start(bf16[128,1024]{1,0:T(8,128)(2,1)S(1)} %get-tuple-element.733), channel_id=1, source_target_pairs={{0,4},{1,5},{2,6},{3,7},{4,0},{5,1},{6,2},{7,3},{8,12},{9,13},{10,... | collective-permute-start | bytes 786440 | tf_op jit(solution)/shard_map/ppermute | solution.py:741
  366.3 15.4 %collective-permute-start.50 = (f32[22,1024]{1,0:T(8,128)S(1)}, f32[22,1024]{1,0:T(8,128)S(1)}, u32[]{:S(2)}, u32[]{:S(2)}) collective-permute-start(f32[22,1024]{1,0:T(8,128)S(1)} %add.173), channel_id=1, source_target_pairs={{0,1},{1,0},{2,3},{3,2},{4,5},{5,4},{6,7},{7,6},{8,24},{9,25},{10,... | collective-permute-start | bytes 270344 | tf_op jit(solution)/shard_map/ppermute | solution.py:741
  381.8 11.6 %collective-permute-start.55 = (bf16[128,1024]{1,0:T(8,128)(2,1)S(1)}, bf16[128,1024]{1,0:T(8,128)(2,1)S(1)}, u32[]{:S(2)}, u32[]{:S(2)}) collective-permute-start(bf16[128,1024]{1,0:T(8,128)(2,1)S(1)} %shard_map.338.refs_0_), channel_id=1, source_target_pairs={{0,16},{1,17},{2,18},{3,19},{4,20},{5,21},{6,22},{7,23},{8,24},{9,... | collective-permute-start | bytes 786440 | tf_op jit(solution)/shard_map/ppermute | solution.py:741
  383.2 10.1 %collective-permute-start.56 = (bf16[128,512]{1,0:T(8,128)(2,1)S(1)}, bf16[128,512]{1,0:T(8,128)(2,1)S(1)}, u32[]{:S(2)}, u32[]{:S(2)}) collective-permute-start(bf16[128,512]{1,0:T(8,128)(2,1)S(1)} %get-tuple-element.758), channel_id=1, source_target_pairs={{0,4},{1,5},{2,6},{3,7},{4,0},{5,1},{6,2},{7,3},{8,12},{9,13},{10,... | collective-permute-start | bytes 393224 | tf_op jit(solution)/shard_map/ppermute | solution.py:741
  395.2 10.6 %collective-permute-start.59 = (bf16[512,512]{1,0:T(8,128)(2,1)S(1)}, bf16[512,512]{1,0:T(8,128)(2,1)S(1)}, u32[]{:S(2)}, u32[]{:S(2)}) collective-permute-start(bf16[512,512]{1,0:T(8,128)(2,1)S(1)} %shard_map.341), channel_id=1, source_target_pairs={{0,1},{1,0},{2,3},{3,2},{4,5},{5,4},{6,7},{7,6},{8,24},{9,25},{10,... | collective-permute-start | bytes 1572872 | tf_op jit(solution)/shard_map/ppermute | solution.py:741
  396.5 13.5 %collective-permute-start.61 = (bf16[256,1024]{1,0:T(8,128)(2,1)S(1)}, bf16[256,1024]{1,0:T(8,128)(2,1)S(1)}, u32[]{:S(2)}, u32[]{:S(2)}) collective-permute-start(bf16[256,1024]{1,0:T(8,128)(2,1)S(1)} %get-tuple-element.786), channel_id=1, source_target_pairs={{0,2},{1,3},{2,0},{3,1},{4,6},{5,7},{6,4},{7,5},{8,10},{9,11},{10,... | collective-permute-start | bytes 1572872 | tf_op jit(solution)/shard_map/ppermute | solution.py:741
  408.4 12.0 %collective-permute-start.63 = (bf16[256,512]{1,0:T(8,128)(2,1)S(1)}, bf16[256,512]{1,0:T(8,128)(2,1)S(1)}, u32[]{:S(2)}, u32[]{:S(2)}) collective-permute-start(bf16[256,512]{1,0:T(8,128)(2,1)S(1)} %get-tuple-element.796), channel_id=1, source_target_pairs={{0,2},{1,3},{2,0},{3,1},{4,6},{5,7},{6,4},{7,5},{8,10},{9,11},{10,... | collective-permute-start | bytes 786440 | tf_op jit(solution)/shard_map/ppermute | solution.py:741
  410.1 17.4 %collective-permute-start.64 = (bf16[128,1024]{1,0:T(8,128)(2,1)S(1)}, bf16[128,1024]{1,0:T(8,128)(2,1)S(1)}, u32[]{:S(2)}, u32[]{:S(2)}) collective-permute-start(bf16[128,1024]{1,0:T(8,128)(2,1)S(1)} %get-tuple-element.804), channel_id=1, source_target_pairs={{0,4},{1,5},{2,6},{3,7},{4,0},{5,1},{6,2},{7,3},{8,12},{9,13},{10,... | collective-permute-start | bytes 786440 | tf_op jit(solution)/shard_map/ppermute | solution.py:741
  (86 other events, 665.9 us)

commit v5 on v4

--- a/solution.py
+++ b/solution.py
@@ -677,6 +677,44 @@
     w_out[...], m_out[...], v_out[...] = adam_update(
         w_ref[...], m_ref[...], v_ref[...], grad, matrix_rate, matrix_decay
     )
+
+
+def adam_pair_kernel(cuts, idx_ref, here_ref, there_ref, w_ref, m_ref, v_ref, *rest):
+    w_out, m_out, v_out = rest[-3:]
+    for unit, cut in enumerate(cuts):
+        grad = jnp.where(idx_ref[0] % 2 == unit, here_ref[...], there_ref[...]).astype(f32)
+        if len(w_ref.shape) == 3:
+            grad = grad[None]
+        w_out[cut], m_out[cut], v_out[cut] = adam_update(
+            w_ref[cut], m_ref[cut], v_ref[cut], grad, matrix_rate, matrix_decay
+        )
+
+
+def adam_pairs(spot, grads, state, block_shape, dim, earlier=None):
+    pair = tuple(2 * n if d == dim else n for d, n in enumerate(block_shape))
+    spec = pl.BlockSpec(pair, lambda p, i: tuple(p if d == dim else 0 for d in range(len(pair))))
+    cuts = [
+        tuple(slice(k * n, (k + 1) * n) if d == dim else slice(None) for d, n in enumerate(block_shape))
+        for k in range(2)
+    ]
+    rows, width = grads[0].shape[0] // 2, grads[0].shape[1]
+    g_spec = pl.BlockSpec((rows, width), lambda p, i: (p ^ (i[0] // 2), 0))
+    extra = list(earlier) if earlier is not None else []
+    state = [far(a) for a in state]
+    outs = pl.pallas_call(
+        partial(adam_pair_kernel, cuts),
+        out_shape=[array(a.shape, f32) for a in state],
+        grid_spec=pltpu.PrefetchScalarGridSpec(
+            num_scalar_prefetch=1,
+            grid=(UNITS // 2,),
+            in_specs=[g_spec] * 2 + [spec] * 3 + [ANY] * len(extra),
+            out_specs=[spec] * 3,
+        ),
+        input_output_aliases={6 + i: i for i in range(len(extra))},
+        compiler_params=params(18),
+        cost_estimate=cost(1024),
+    )(jnp.stack([spot]).astype(jnp.int32), *grads, *state, *extra)
+    return list(outs)
 
 
 def adam_units(spot, grads, state, block_shape, at, earlier=None):
@@ -1156,11 +1194,16 @@
             "e": (half_unit, lambda u: (5 + u % 2, 0, u // 2)),
         }
 
+        pairs = {"a": (whole_unit, 0), "2": ((shard_rows, D), 0), "1": ((shard_rows, D), 1)}
+
         def k_adam(name):
             def kernel(e):
                 place_of = name if name in states_of else "attn"
                 state = states_of.get(name, (attn_w, attn_m, attn_v))
-                e[place_of] = adam_units(spot, sums[name].parts, state, *ways[name], e.get(place_of))
+                if name in pairs:
+                    e[place_of] = adam_pairs(spot, sums[name].parts, state, *pairs[name], e.get(place_of))
+                else:
+                    e[place_of] = adam_units(spot, sums[name].parts, state, *ways[name], e.get(place_of))
 
             return kernel
 

time: 456 us -> 454 us (level)
    pallas_call x5 -> x2, Pallas kernels: 28.5 us -> 8.94 us  [adam_units(): pl.pallas_call(adam_kernel, out_shape=[array(a.shape, f32) for a in state...]
    pallas_call x0 -> x3, Pallas kernels: none -> 16.7 us  [adam_pairs(): pl.pallas_call(partial(adam_pair_kernel, cuts), out_shape=[array(a.shape,...]
  transfers between devices with their start and end apart: 70 -> 70, of which waited for: 33 -> 35; matrix products, arithmetic and copies ran while one was open for 2% -> 2% of each run, Pallas kernels for 42% -> 42%
where the time goes in v5:
time: 454 us; the launch traced here: 450 us
  Pallas kernels  210 us (46%)
  waiting for transfers between devices  139 us (31%)
  starting transfers between devices  74.5 us (16%)
  local copies, waits for them, and re-layouts  17.7 us (4%)
    ppermute x70, waiting for transfers between devices, send(): return lax.ppermute(block, ('dp', 'fsdp'), perm)  139 us
    ppermute x70, starting transfers between devices, send(): return lax.ppermute(block, ('dp', 'fsdp'), perm)  74.5 us
    pallas_call x2, Pallas kernels, attend_back(): pl.pallas_call(partial(attend_back_kernel, causal), out_shape=out_shape,...  29.9 us
    pallas_call x5, Pallas kernels, planes_call(): pl.pallas_call(kernel, out_shape=[array((n * plane, width)) for n in (2,...  26.6 us
    pallas_call x2, Pallas kernels, input_grad(): pl.pallas_call(partial(input_grad_kernel, len(slots)), out_shape=array((n...  19.9 us
    pallas_call x3, Pallas kernels, adam_pairs(): pl.pallas_call(partial(adam_pair_kernel, cuts), out_shape=[array(a.shape,...  16.7 us
    pallas_call x2, Pallas kernels, join_back(): pl.pallas_call(partial(join_back_kernel, row_at), out_shape=[far_array((n...  15.2 us
    pallas_call x2, Pallas kernels, state_grad(): pl.pallas_call(state_grad_kernel, out_shape=array((D, D)), grid_spec=pltp...  14.2 us
  transfers between devices with their start and end apart: 70, of which 35 were waited for; matrix products, arithmetic and copies ran while one was open for 2% of the time, Pallas kernels for 42%

profile of v5, /device:TPU:0, one launch (start us, length us, event | category | flops | bytes accessed | tf_op | source)
XLA Modules:
  0.0 449.9 jit_solution(12462847522234053085)
XLA Ops:
  2.7 4.1 collective-permute-start
  8.4 11.9 %collective-permute-done.refs_1_ = bf16[144,1024]{1,0:T(8,128)(2,1)S(1)} collective-permute-done((bf16[144,1024]{1,0:T(8,128)(2,1)S(1)}, bf16[144,1024]{1,0:T(8,128)(2,1)S(1)}, u32[]{:S(2)}, u32[]{:S(2)}) %collective-permute-start) | collective-permute-done | bytes 294944 | tf_op jit(solution)/shard_map/ppermute | solution.py:779
  22.0 6.4 %collective-permute-done.2.refs_3_ = bf16[144,1024]{1,0:T(8,128)(2,1)S(1)} collective-permute-done((bf16[144,1024]{1,0:T(8,128)(2,1)S(1)}, bf16[144,1024]{1,0:T(8,128)(2,1)S(1)}, u32[]{:S(2)}, u32[]{:S(2)}) %collective-permute-start.2) | collective-permute-done | bytes 294944 | tf_op jit(solution)/shard_map/ppermute | solution.py:779
  30.4 3.3 collective-permute-start.3
  36.5 8.5 %collective-permute-done.3.refs_1_ = bf16[128,1024]{1,0:T(8,128)(2,1)S(1)} collective-permute-done((bf16[128,1024]{1,0:T(8,128)(2,1)S(1)}, bf16[128,1024]{1,0:T(8,128)(2,1)S(1)}, u32[]{:S(2)}, u32[]{:S(2)}) %collective-permute-start.3) | collective-permute-done | bytes 262176 | tf_op jit(solution)/shard_map/ppermute | solution.py:779
  51.3 3.4 collective-permute-start.7
  54.6 9.2 %collective-permute-done.6.refs_3_ = bf16[128,1024]{1,0:T(8,128)(2,1)S(1)} collective-permute-done((bf16[128,1024]{1,0:T(8,128)(2,1)S(1)}, bf16[128,1024]{1,0:T(8,128)(2,1)S(1)}, u32[]{:S(2)}, u32[]{:S(2)}) %collective-permute-start.6) | collective-permute-done | bytes 262176 | tf_op jit(solution)/shard_map/ppermute | solution.py:779
  63.9 3.1 collective-permute-done.7.refs_1_
  72.3 9.5 %collective-permute-done.8.refs_2_ = bf16[256,1024]{1,0:T(8,128)(2,1)} collective-permute-done((bf16[256,1024]{1,0:T(8,128)(2,1)}, bf16[256,1024]{1,0:T(8,128)(2,1)}, u32[]{:S(2)}, u32[]{:S(2)}) %collective-permute-start.8) | collective-permute-done | bytes 524320 | tf_op jit(solution)/shard_map/ppermute | solution.py:779
  97.5 4.0 shard_map.293.w_ref.refs_3_.refs_4_.refs_2_
  103.4 5.1 %collective-permute-done.13.refs_1_ = bf16[128,1024]{1,0:T(8,128)(2,1)S(1)} collective-permute-done((bf16[128,1024]{1,0:T(8,128)(2,1)S(1)}, bf16[128,1024]{1,0:T(8,128)(2,1)S(1)}, u32[]{:S(2)}, u32[]{:S(2)}) %collective-permute-start.13) | collective-permute-done | bytes 262176 | tf_op jit(solution)/shard_map/ppermute | solution.py:779
  109.8 9.9 %shard_map.295.k_ref.v_ref = bf16[2048,2048]{1,0:T(8,128)(2,1)S(1)} custom-call(bf16[2048,1024]{1,0:T(8,128)(2,1)S(1)} %bitcast.136, bf16[1024,4096]{1,0:T(8,128)(2,1)S(1)} %shard_map.293.w_ref.refs_3_.refs_4_.refs_2_, f32[1,2048]{1,0:T(1,128)S(1)} %concatenate.30.b_ref), custom_call_target="tpu_custom_call" | custom-call | bytes 1024 | tf_op jit(solution)/shard_map/pallas_call | solution.py:119
  122.7 6.6 %collective-permute-done.16.refs_1_ = bf16[1024,1024]{1,0:T(8,128)(2,1)S(1)} collective-permute-done((bf16[1024,1024]{1,0:T(8,128)(2,1)S(1)}, bf16[1024,1024]{1,0:T(8,128)(2,1)S(1)}, u32[]{:S(2)}, u32[]{:S(2)}) %collective-permute-start.16) | collective-permute-done | bytes 2097184 | tf_op jit(solution)/shard_map/ppermute | solution.py:779
  136.6 2.7 shard_map.301.x_ref.refs_0_.refs_1_.refs_2_.refs_3_
  142.7 9.9 %shard_map.304.x_ref.refs_0_.refs_1_.refs_2_.refs_3_ = bf16[2,256,1024]{2,1,0:T(8,128)(2,1)S(1)} custom-call(s32[2]{0:T(128)S(1)} %bitcast.161, bf16[256,1024]{1,0:T(8,128)(2,1)S(1)} %shard_map.303.q_ref, bf16[2048,2048]{1,0:T(8,128)(2,1)S(1)} %shard_map.295.k_ref.v_ref, bf16[2048,2048]{1,0:T(8,128)(2,1)S(1)} %shard_map.295.k_ref.v_ref, ...), custom_call_target="tpu_custom_call" | custom-call | bytes 1024 | tf_op jit(solution)/shard_map/pallas_call | solution.py:450
  155.2 2.8 collective-permute-done.19.refs_1_
  158.0 9.4 %collective-permute-done.20.refs_1_ = bf16[1024,1024]{1,0:T(8,128)(2,1)S(1)} collective-permute-done((bf16[1024,1024]{1,0:T(8,128)(2,1)S(1)}, bf16[1024,1024]{1,0:T(8,128)(2,1)S(1)}, u32[]{:S(2)}, u32[]{:S(2)}) %collective-permute-start.20) | collective-permute-done | bytes 2097184 | tf_op jit(solution)/shard_map/ppermute | solution.py:779
  173.9 5.3 %shard_map.308 = (bf16[256,4096]{1,0:T(8,128)(2,1)S(1)}, bf16[256,4096]{1,0:T(8,128)(2,1)S(1)}) custom-call(bf16[256,1024]{1,0:T(8,128)(2,1)S(1)} %get-tuple-element.520.x_ref, bf16[1024,4096]{1,0:T(8,128)(2,1)S(1)} %shard_map.307.w_ref, f32[1,4096]{1,0:T(1,128)S(1)} %bitcast.155), custom_call_target="tpu_custom_call" | custom-call | bytes 1024 | tf_op jit(solution)/shard_map/pallas_call | solution.py:197
  179.2 15.1 %collective-permute-done.23.refs_1_ = bf16[1024,1024]{1,0:T(8,128)(2,1)S(1)} collective-permute-done((bf16[1024,1024]{1,0:T(8,128)(2,1)S(1)}, bf16[1024,1024]{1,0:T(8,128)(2,1)S(1)}, u32[]{:S(2)}, u32[]{:S(2)}) %collective-permute-start.23) | collective-permute-done | bytes 2097184 | tf_op jit(solution)/shard_map/ppermute | solution.py:779
  194.2 4.2 collective-permute-done.25.refs_3_
  200.7 6.3 %shard_map.311 = (bf16[256,1024]{1,0:T(8,128)(2,1)}, f32[256,1024]{1,0:T(8,128)}, bf16[256,1024]{1,0:T(8,128)(2,1)S(1)}, f32[8,1024]{1,0:T(8,128)S(1)}) custom-call(s32[2]{0:T(128)S(1)} %bitcast.159, bf16[256,4096]{1,0:T(8,128)(2,1)S(1)} %get-tuple-element.499.x_ref, bf16[4096,1024]{1,0:T(8,128)(2,1)S(1)} %shard_map.310.w_ref, ...), custom_call_target="tpu_custom_call" | custom-call | bytes 1024 | tf_op jit(solution)/shard_map/pallas_call | solution.py:238
  207.5 4.2 shard_map.312
  214.9 6.2 %shard_map.313 = (bf16[1024,1024]{1,0:T(8,128)(2,1)S(1)}, bf16[512,1024]{1,0:T(8,128)(2,1)S(1)}, bf16[512,1024]{1,0:T(8,128)(2,1)S(1)}) custom-call(s32[4,4]{1,0:T(4,128)S(1)} %get-tuple-element.893.idx_ref, bf16[1,256,4096]{2,1,0:T(8,128)(2,1)} %bitcast.132, bf16[1,256,4096]{2,1,0:T(8,128)(2,1)} %bitcast.133, bf16[1,256,4096]{2,1,0:T(8,128)(2,1)} %bitcast.134, ...), custom_call_target="tpu_custom_call" | custom-call | bytes 1024 | tf_op jit(solution)/shard_map/pallas_call | solution.py:609
  222.6 9.8 %shard_map.314 = (f32[256,1024]{1,0:T(8,128)}, bf16[256,1024]{1,0:T(8,128)(2,1)S(1)}, bf16[256,1024]{1,0:T(8,128)(2,1)S(1)}, f32[8,1024]{1,0:T(8,128)S(1)}) custom-call(bf16[256,4096]{1,0:T(8,128)(2,1)S(1)} %copy-done.15, bf16[1024,4096]{1,0:T(8,128)(2,1)} %copy-done.3, f32[256,1024]{1,0:T(8,128)} %get-tuple-element.508.dr_ref, ...), custom_call_target="tpu_custom_call" | custom-call | bytes 1024 | tf_op jit(solution)/shard_map/pallas_call | solution.py:307
  232.4 7.4 %shard_map.315 = (bf16[1024,1024]{1,0:T(8,128)(2,1)}, bf16[512,1024]{1,0:T(8,128)(2,1)S(1)}, bf16[512,1024]{1,0:T(8,128)(2,1)S(1)}) custom-call(s32[4,4]{1,0:T(4,128)S(1)} %get-tuple-element.891.idx_ref, bf16[1,256,1024]{2,1,0:T(8,128)(2,1)S(1)} %bitcast.139, bf16[1,256,1024]{2,1,0:T(8,128)(2,1)S(1)} %bitcast.140, bf16[1,256,1024]{2,1,0:T(8,128)(2,1)S(1)} %bitcast.141, ...), custom_call_target="tpu_custom_call" | custom-call | bytes 1024 | tf_op jit(solution)/shard_map/pallas_call | solution.py:609
  242.3 20.9 %shard_map.316 = (bf16[2,256,1024]{2,1,0:T(8,128)(2,1)}, bf16[2,2048,1024]{2,1,0:T(8,128)(2,1)}, f32[16,1024]{1,0:T(8,128)S(1)}) custom-call(s32[2]{0:T(128)S(1)} %bitcast.162, bf16[256,1024]{1,0:T(8,128)(2,1)S(1)} %shard_map.303.q_ref, bf16[2048,2048]{1,0:T(8,128)(2,1)} %copy-done.2, bf16[2048,2048]{1,0:T(8,128)(2,1)} %copy-done.2, ...), custom_call_target="tpu_custom_call" | custom-call | bytes 1024 | tf_op jit(solution)/shard_map/pallas_call | solution.py:480
  271.6 5.4 %shard_map.318 = (f32[256,1024]{1,0:T(8,128)}, bf16[256,1024]{1,0:T(8,128)(2,1)S(1)}, bf16[256,1024]{1,0:T(8,128)(2,1)S(1)}, f32[8,1024]{1,0:T(8,128)S(1)}) custom-call(bf16[2,256,1024]{2,1,0:T(8,128)(2,1)} %get-tuple-element.577.g_ref.refs_8_, bf16[1024,4096]{1,0:T(8,128)(2,1)} %copy-done, f32[256,1024]{1,0:T(8,128)} %get-tuple-element.545.dr_ref, ...), custom_call_target="tpu_custom_call" | custom-call | bytes 1024 | tf_op jit(solution)/shard_map/pallas_call | solution.py:307
  277.1 9.0 %shard_map.319 = (bf16[4,256,1024]{2,1,0:T(8,128)(2,1)}, f32[16,1024]{1,0:T(8,128)S(1)}) custom-call(s32[2]{0:T(128)S(1)} %bitcast.160, bf16[256,2048]{1,0:T(8,128)(2,1)S(1)} %copy-done.11, bf16[256,2048]{1,0:T(8,128)(2,1)S(1)} %copy-done.11, bf16[256,1024]{1,0:T(8,128)(2,1)S(1)} %copy-done.17, bf16[256,1024]{1,0:T(8,128)(2,1)S(1)} %get-tuple-element.554.do_ref, ...), custom_call_target="tpu_custom_call" | custom-call | bytes 1024 | tf_op jit(solution)/shard_map/pallas_call | solution.py:480
  286.6 5.2 %shard_map.320 = (bf16[1024,512]{1,0:T(8,128)(2,1)S(1)}, bf16[512,512]{1,0:T(8,128)(2,1)S(1)}, bf16[512,512]{1,0:T(8,128)(2,1)S(1)}) custom-call(s32[4,4]{1,0:T(4,128)S(1)} %copy-done.41, bf16[2,256,1024]{2,1,0:T(8,128)(2,1)S(1)} %copy-done.8, bf16[2,256,1024]{2,1,0:T(8,128)(2,1)S(1)} %copy-done.8, bf16[2,256,1024]{2,1,0:T(8,128)(2,1)S(1)} %copy-done.8, ...), custom_call_target="tpu_custom_call" | custom-call | bytes 1024 | tf_op jit(solution)/shard_map/pallas_call | solution.py:609
  301.6 7.1 %shard_map.323 = bf16[1024,1024]{1,0:T(8,128)(2,1)S(1)} custom-call(s32[1]{0:T(128)} %bitcast.83.slot_ref, bf16[2048,1024]{1,0:T(8,128)(2,1)S(1)} %bitcast.137, bf16[2,2048,1024]{2,1,0:T(8,128)(2,1)} %get-tuple-element.728.g_ref.refs_0_.refs_1_), custom_call_target="tpu_custom_call" | custom-call | bytes 1024 | tf_op jit(solution)/shard_map/pallas_call | solution.py:357
  308.7 3.2 collective-permute-done.38.refs_1_
  312.2 5.6 %shard_map.325 = (bf16[1024,1024]{1,0:T(8,128)(2,1)S(1)}, bf16[512,1024]{1,0:T(8,128)(2,1)S(1)}, bf16[512,1024]{1,0:T(8,128)(2,1)S(1)}) custom-call(s32[4,4]{1,0:T(4,128)S(1)} %copy-done.40, bf16[2,256,1024]{2,1,0:T(8,128)(2,1)S(1)} %shard_map.301.x_ref.refs_0_.refs_1_.refs_2_.refs_3_, ...), custom_call_target="tpu_custom_call" | custom-call | bytes 1024 | tf_op jit(solution)/shard_map/pallas_call | solution.py:609
  317.8 4.1 collective-permute-done.40.refs_1_
  328.2 3.7 collective-permute-done.42
  334.0 7.1 %shard_map.328.refs_0_.refs_1_.refs_2_.refs_3_ = bf16[1024,1024]{1,0:T(8,128)(2,1)S(1)} custom-call(s32[1]{0:T(128)} %bitcast.99.slot_ref, bf16[2048,1024]{1,0:T(8,128)(2,1)S(1)} %bitcast.138, bf16[2,2048,1024]{2,1,0:T(8,128)(2,1)} %get-tuple-element.728.g_ref.refs_0_.refs_1_), custom_call_target="tpu_custom_call" | custom-call | bytes 1024 | tf_op jit(solution)/shard_map/pallas_call | solution.py:357
  347.1 4.1 collective-permute-start.49
  351.2 6.0 %shard_map.332 = bf16[256,1024]{1,0:T(8,128)(2,1)} custom-call(bf16[4,256,1024]{2,1,0:T(8,128)(2,1)} %get-tuple-element.687.refs_8_.refs_0_.refs_1_.refs_2_, bf16[4,256,1024]{2,1,0:T(8,128)(2,1)} %get-tuple-element.687.refs_8_.refs_0_.refs_1_.refs_2_, bf16[4,256,1024]{2,1,0:T(8,128)(2,1)} %get-tuple-element.687.refs_8_.refs_0_.refs_1_.refs_2_, ...), custom_call_target="tpu_custom_call" | custom-call | bytes 1024 | tf_op jit(solution)/shard_map/pallas_call | solution.py:338
  363.3 3.0 collective-permute-start.51
  366.5 13.9 %shard_map.337 = bf16[2048,1024]{1,0:T(8,128)(2,1)} custom-call(bf16[2,2048,1024]{2,1,0:T(8,128)(2,1)} %get-tuple-element.728.g_ref.refs_0_.refs_1_, bf16[2,2048,1024]{2,1,0:T(8,128)(2,1)} %get-tuple-element.728.g_ref.refs_0_.refs_1_, bf16[1024,4096]{1,0:T(8,128)(2,1)} %copy-done.1, bf16[1024,4096]{1,0:T(8,128)(2,1)} %copy-done.1), custom_call_target="tpu_custom_call" | custom-call | bytes 1024 | tf_op jit(solution)/shard_map/pallas_call | solution.py:338
  383.2 3.1 collective-permute-start.56
  386.3 5.6 %shard_map.339 = (f32[512,1024]{1,0:T(8,128)}, f32[512,1024]{1,0:T(8,128)}, f32[512,1024]{1,0:T(8,128)}) custom-call(s32[1]{0:T(128)} %bitcast.94.idx_ref, bf16[256,1024]{1,0:T(8,128)(2,1)S(1)} %shard_map.334.here_ref, bf16[256,1024]{1,0:T(8,128)(2,1)S(1)} %collective-permute-done.52.there_ref, f32[512,1024]{1,0:T(8,128)} %w_ref.5, f32[512,1024]{1,0:T(8,128)} %m_ref.5, ...), custom_call_target="tpu_custom_call" | custom-call | bytes 1024 | tf_op jit(solution)/shard_map/pallas_call | solution.py:704
  398.4 5.6 %shard_map.344 = (f32[128,4096]{1,0:T(8,128)}, f32[128,4096]{1,0:T(8,128)}, f32[128,4096]{1,0:T(8,128)}) custom-call(s32[1]{0:T(128)} %bitcast.94.idx_ref, bf16[256,1024]{1,0:T(8,128)(2,1)S(1)} %shard_map.342.here_ref, bf16[256,1024]{1,0:T(8,128)(2,1)S(1)} %collective-permute-done.58.there_ref, f32[128,4096]{1,0:T(8,128)} %w_ref.6, f32[128,4096]{1,0:T(8,128)} %m_ref.6, ...), custom_call_target="tpu_custom_call" | custom-call | bytes 1024 | tf_op jit(solution)/shard_map/pallas_call | solution.py:704
  410.2 4.5 shard_map.348
  414.7 5.3 %collective-permute-done.63.refs_1_ = bf16[256,512]{1,0:T(8,128)(2,1)S(1)} collective-permute-done((bf16[256,512]{1,0:T(8,128)(2,1)S(1)}, bf16[256,512]{1,0:T(8,128)(2,1)S(1)}, u32[]{:S(2)}, u32[]{:S(2)}) %collective-permute-start.63) | collective-permute-done | bytes 262176 | tf_op jit(solution)/shard_map/ppermute | solution.py:779
  421.1 4.9 %collective-permute-done.64.refs_1_ = bf16[128,1024]{1,0:T(8,128)(2,1)S(1)} collective-permute-done((bf16[128,1024]{1,0:T(8,128)(2,1)S(1)}, bf16[128,1024]{1,0:T(8,128)(2,1)S(1)}, u32[]{:S(2)}, u32[]{:S(2)}) %collective-permute-start.64) | collective-permute-done | bytes 262176 | tf_op jit(solution)/shard_map/ppermute | solution.py:779
  429.9 5.5 %collective-permute-done.67.refs_1_ = bf16[128,512]{1,0:T(8,128)(2,1)S(1)} collective-permute-done((bf16[128,512]{1,0:T(8,128)(2,1)S(1)}, bf16[128,512]{1,0:T(8,128)(2,1)S(1)}, u32[]{:S(2)}, u32[]{:S(2)}) %collective-permute-start.67) | collective-permute-done | bytes 131104 | tf_op jit(solution)/shard_map/ppermute | solution.py:779
  439.0 4.5 shard_map.354
  443.5 5.6 %shard_map.355 = (f32[8,128,1024]{2,1,0:T(8,128)}, f32[8,128,1024]{2,1,0:T(8,128)}, f32[8,128,1024]{2,1,0:T(8,128)}) custom-call(s32[1]{0:T(128)} %bitcast.94.idx_ref, bf16[256,1024]{1,0:T(8,128)(2,1)S(1)} %shard_map.352.here_ref, ...), custom_call_target="tpu_custom_call", output_to_operand_aliasing={{0}: (6, {}), {1}: (7, {}), {2}: (8, {})} | custom-call | bytes 1024 | tf_op jit(solution)/shard_map/pallas_call | solution.py:704
  (371 shorter events, 135.7 us)
Async XLA Ops:
  2.7 17.5 %collective-permute-start = (bf16[144,1024]{1,0:T(8,128)(2,1)S(1)}, bf16[144,1024]{1,0:T(8,128)(2,1)S(1)}, u32[]{:S(2)}, u32[]{:S(2)}) collective-permute-start(bf16[144,1024]{1,0:T(8,128)(2,1)S(1)} %fusion.6.refs_0_), channel_id=1, source_target_pairs={{0,4},{1,5},{2,6},{3,7},{4,0},{5,1},{6,2},{7,3},{8,12},{9,13},{10,... | collective-permute-start | bytes 884744 | tf_op jit(solution)/shard_map/ppermute | solution.py:779
  6.8 13.6 %collective-permute-start.1 = (bf16[144,1024]{1,0:T(8,128)(2,1)S(1)}, bf16[144,1024]{1,0:T(8,128)(2,1)S(1)}, u32[]{:S(2)}, u32[]{:S(2)}) collective-permute-start(bf16[144,1024]{1,0:T(8,128)(2,1)S(1)} %fusion.6.refs_0_), channel_id=1, source_target_pairs={{0,2},{1,3},{2,0},{3,1},{4,6},{5,7},{6,4},{7,5},{8,10},{9,11},{10,... | collective-permute-start | bytes 884744 | tf_op jit(solution)/shard_map/ppermute | solution.py:779
  29.0 17.1 %collective-permute-start.5 = (bf16[576,1024]{1,0:T(8,128)(2,1)S(1)}, bf16[576,1024]{1,0:T(8,128)(2,1)S(1)}, u32[]{:S(2)}, u32[]{:S(2)}) collective-permute-start(bf16[576,1024]{1,0:T(8,128)(2,1)S(1)} %shard_map.288.refs_0_), channel_id=1, source_target_pairs={{0,1},{1,0},{2,3},{3,2},{4,5},{5,4},{6,7},{7,6},{8,24},{9,25},{10,... | collective-permute-start | bytes 3538952 | tf_op jit(solution)/shard_map/ppermute | solution.py:779
  30.4 14.7 %collective-permute-start.3 = (bf16[128,1024]{1,0:T(8,128)(2,1)S(1)}, bf16[128,1024]{1,0:T(8,128)(2,1)S(1)}, u32[]{:S(2)}, u32[]{:S(2)}) collective-permute-start(bf16[128,1024]{1,0:T(8,128)(2,1)S(1)} %get-tuple-element.446.refs_0_), channel_id=1, source_target_pairs={{0,4},{1,5},{2,6},{3,7},{4,0},{5,1},{6,2},{7,3},{8,12},{9,13},{10,... | collective-permute-start | bytes 786440 | tf_op jit(solution)/shard_map/ppermute | solution.py:779
  33.6 11.8 %collective-permute-start.4 = (bf16[128,1024]{1,0:T(8,128)(2,1)S(1)}, bf16[128,1024]{1,0:T(8,128)(2,1)S(1)}, u32[]{:S(2)}, u32[]{:S(2)}) collective-permute-start(bf16[128,1024]{1,0:T(8,128)(2,1)S(1)} %get-tuple-element.446.refs_0_), channel_id=1, source_target_pairs={{0,2},{1,3},{2,0},{3,1},{4,6},{5,7},{6,4},{7,5},{8,10},{9,11},{10,... | collective-permute-start | bytes 786440 | tf_op jit(solution)/shard_map/ppermute | solution.py:779
  49.1 40.0 %collective-permute-start.10 = (bf16[1152,1024]{1,0:T(8,128)(2,1)S(1)}, bf16[1152,1024]{1,0:T(8,128)(2,1)}, u32[]{:S(2)}, u32[]{:S(2)}) collective-permute-start(bf16[1152,1024]{1,0:T(8,128)(2,1)S(1)} %shard_map.292.refs_0_), channel_id=1, source_target_pairs={{0,16},{1,17},{2,18},{3,19},{4,20},{5,21},{6,22},{7,23},{8,9},{9,8... | collective-permute-start | bytes 7077896 | tf_op jit(solution)/shard_map/ppermute | solution.py:779
  49.7 39.4 %collective-permute-start.11 = (bf16[1152,1024]{1,0:T(8,128)(2,1)S(1)}, bf16[1152,1024]{1,0:T(8,128)(2,1)}, u32[]{:S(2)}, u32[]{:S(2)}) collective-permute-start(bf16[1152,1024]{1,0:T(8,128)(2,1)S(1)} %shard_map.292.refs_0_), channel_id=1, source_target_pairs={{0,8},{1,9},{2,10},{3,11},{4,12},{5,13},{6,14},{7,15},{8,0},{9,1},... | collective-permute-start | bytes 7077896 | tf_op jit(solution)/shard_map/ppermute | solution.py:779
  49.7 14.1 %collective-permute-start.6 = (bf16[128,1024]{1,0:T(8,128)(2,1)S(1)}, bf16[128,1024]{1,0:T(8,128)(2,1)S(1)}, u32[]{:S(2)}, u32[]{:S(2)}) collective-permute-start(bf16[128,1024]{1,0:T(8,128)(2,1)S(1)} %copy-done.35), channel_id=1, source_target_pairs={{0,2},{1,3},{2,0},{3,1},{4,6},{5,7},{6,4},{7,5},{8,10},{9,11},{10,... | collective-permute-start | bytes 786440 | tf_op jit(solution)/shard_map/ppermute | solution.py:779
  51.3 15.7 %collective-permute-start.7 = (bf16[128,1024]{1,0:T(8,128)(2,1)S(1)}, bf16[128,1024]{1,0:T(8,128)(2,1)S(1)}, u32[]{:S(2)}, u32[]{:S(2)}) collective-permute-start(bf16[128,1024]{1,0:T(8,128)(2,1)S(1)} %dynamic-slice_convert_fusion.1.refs_0_), channel_id=1, source_target_pairs={{0,4},{1,5},{2,6},{3,7},{4,0},{5,1},{6,2},{7,3},{8,12},{9,13},{10,... | collective-permute-start | bytes 786440 | tf_op jit(solution)/shard_map/ppermute | solution.py:779
  67.6 19.9 %collective-permute-start.9 = (bf16[512,1024]{1,0:T(8,128)(2,1)S(1)}, bf16[512,1024]{1,0:T(8,128)(2,1)}, u32[]{:S(2)}, u32[]{:S(2)}) collective-permute-start(bf16[512,1024]{1,0:T(8,128)(2,1)S(1)} %shard_map.291.refs_0_), channel_id=1, source_target_pairs={{0,1},{1,0},{2,3},{3,2},{4,5},{5,4},{6,7},{7,6},{8,24},{9,25},{10,... | collective-permute-start | bytes 3145736 | tf_op jit(solution)/shard_map/ppermute | solution.py:779
  70.6 11.1 %collective-permute-start.8 = (bf16[256,1024]{1,0:T(8,128)(2,1)}, bf16[256,1024]{1,0:T(8,128)(2,1)}, u32[]{:S(2)}, u32[]{:S(2)}) collective-permute-start(bf16[256,1024]{1,0:T(8,128)(2,1)} %shard_map.289), channel_id=1, source_target_pairs={{0,2},{1,3},{2,0},{3,1},{4,6},{5,7},{6,4},{7,5},{8,10},{9,11},{10,... | collective-permute-start | bytes 1572872 | tf_op jit(solution)/shard_map/ppermute | solution.py:779
  92.0 37.3 %collective-permute-start.16 = (bf16[1024,1024]{1,0:T(8,128)(2,1)S(1)}, bf16[1024,1024]{1,0:T(8,128)(2,1)S(1)}, u32[]{:S(2)}, u32[]{:S(2)}) collective-permute-start(bf16[1024,1024]{1,0:T(8,128)(2,1)S(1)} %shard_map.298.refs_0_), channel_id=1, source_target_pairs={{0,16},{1,17},{2,18},{3,19},{4,20},{5,21},{6,22},{7,23},{8,9},{9,8... | collective-permute-start | bytes 6291464 | tf_op jit(solution)/shard_map/ppermute | solution.py:779
  92.6 36.8 %collective-permute-start.17 = (bf16[1024,1024]{1,0:T(8,128)(2,1)S(1)}, bf16[1024,1024]{1,0:T(8,128)(2,1)S(1)}, u32[]{:S(2)}, u32[]{:S(2)}) collective-permute-start(bf16[1024,1024]{1,0:T(8,128)(2,1)S(1)} %shard_map.298.refs_0_), channel_id=1, source_target_pairs={{0,8},{1,9},{2,10},{3,11},{4,12},{5,13},{6,14},{7,15},{8,0},{9,1},... | collective-permute-start | bytes 6291464 | tf_op jit(solution)/shard_map/ppermute | solution.py:779
  93.7 14.7 %collective-permute-start.13 = (bf16[128,1024]{1,0:T(8,128)(2,1)S(1)}, bf16[128,1024]{1,0:T(8,128)(2,1)S(1)}, u32[]{:S(2)}, u32[]{:S(2)}) collective-permute-start(bf16[128,1024]{1,0:T(8,128)(2,1)S(1)} %dynamic-slice_convert_fusion.refs_0_), channel_id=1, source_target_pairs={{0,4},{1,5},{2,6},{3,7},{4,0},{5,1},{6,2},{7,3},{8,12},{9,13},{10,... | collective-permute-start | bytes 786440 | tf_op jit(solution)/shard_map/ppermute | solution.py:779
  95.8 27.0 %collective-permute-start.15 = (bf16[512,1024]{1,0:T(8,128)(2,1)S(1)}, bf16[512,1024]{1,0:T(8,128)(2,1)S(1)}, u32[]{:S(2)}, u32[]{:S(2)}) collective-permute-start(bf16[512,1024]{1,0:T(8,128)(2,1)S(1)} %shard_map.290.refs_0_), channel_id=1, source_target_pairs={{0,1},{1,0},{2,3},{3,2},{4,5},{5,4},{6,7},{7,6},{8,24},{9,25},{10,... | collective-permute-start | bytes 3145736 | tf_op jit(solution)/shard_map/ppermute | solution.py:779
  109.1 13.0 %collective-permute-start.14 = (bf16[256,1024]{1,0:T(8,128)(2,1)S(1)}, bf16[256,1024]{1,0:T(8,128)(2,1)S(1)}, u32[]{:S(2)}, u32[]{:S(2)}) collective-permute-start(bf16[256,1024]{1,0:T(8,128)(2,1)S(1)} %shard_map.296), channel_id=1, source_target_pairs={{0,2},{1,3},{2,0},{3,1},{4,6},{5,7},{6,4},{7,5},{8,10},{9,11},{10,... | collective-permute-start | bytes 1572872 | tf_op jit(solution)/shard_map/ppermute | solution.py:779
  130.1 37.3 %collective-permute-start.20 = (bf16[1024,1024]{1,0:T(8,128)(2,1)S(1)}, bf16[1024,1024]{1,0:T(8,128)(2,1)S(1)}, u32[]{:S(2)}, u32[]{:S(2)}) collective-permute-start(bf16[1024,1024]{1,0:T(8,128)(2,1)S(1)} %shard_map.306.refs_0_), channel_id=1, source_target_pairs={{0,16},{1,17},{2,18},{3,19},{4,20},{5,21},{6,22},{7,23},{8,9},{9,8... | collective-permute-start | bytes 6291464 | tf_op jit(solution)/shard_map/ppermute | solution.py:779
  130.6 36.8 %collective-permute-start.21 = (bf16[1024,1024]{1,0:T(8,128)(2,1)S(1)}, bf16[1024,1024]{1,0:T(8,128)(2,1)S(1)}, u32[]{:S(2)}, u32[]{:S(2)}) collective-permute-start(bf16[1024,1024]{1,0:T(8,128)(2,1)S(1)} %shard_map.306.refs_0_), channel_id=1, source_target_pairs={{0,8},{1,9},{2,10},{3,11},{4,12},{5,13},{6,14},{7,15},{8,0},{9,1},... | collective-permute-start | bytes 6291464 | tf_op jit(solution)/shard_map/ppermute | solution.py:779
  131.9 26.1 %collective-permute-start.19 = (bf16[512,1024]{1,0:T(8,128)(2,1)S(1)}, bf16[512,1024]{1,0:T(8,128)(2,1)S(1)}, u32[]{:S(2)}, u32[]{:S(2)}) collective-permute-start(bf16[512,1024]{1,0:T(8,128)(2,1)S(1)} %shard_map.297.refs_0_), channel_id=1, source_target_pairs={{0,1},{1,0},{2,3},{3,2},{4,5},{5,4},{6,7},{7,6},{8,24},{9,25},{10,... | collective-permute-start | bytes 3145736 | tf_op jit(solution)/shard_map/ppermute | solution.py:779
  168.1 26.1 %collective-permute-start.23 = (bf16[1024,1024]{1,0:T(8,128)(2,1)S(1)}, bf16[1024,1024]{1,0:T(8,128)(2,1)S(1)}, u32[]{:S(2)}, u32[]{:S(2)}) collective-permute-start(bf16[1024,1024]{1,0:T(8,128)(2,1)S(1)} %shard_map.309.refs_0_), channel_id=1, source_target_pairs={{0,16},{1,17},{2,18},{3,19},{4,20},{5,21},{6,22},{7,23},{8,9},{9,8... | collective-permute-start | bytes 6291464 | tf_op jit(solution)/shard_map/ppermute | solution.py:779
  168.7 25.6 %collective-permute-start.24 = (bf16[1024,1024]{1,0:T(8,128)(2,1)S(1)}, bf16[1024,1024]{1,0:T(8,128)(2,1)S(1)}, u32[]{:S(2)}, u32[]{:S(2)}) collective-permute-start(bf16[1024,1024]{1,0:T(8,128)(2,1)S(1)} %shard_map.309.refs_0_), channel_id=1, source_target_pairs={{0,8},{1,9},{2,10},{3,11},{4,12},{5,13},{6,14},{7,15},{8,0},{9,1},... | collective-permute-start | bytes 6291464 | tf_op jit(solution)/shard_map/ppermute | solution.py:779
  222.1 41.1 %collective-permute-start.30 = (bf16[1024,1024]{1,0:T(8,128)(2,1)S(1)}, bf16[1024,1024]{1,0:T(8,128)(2,1)S(1)}, u32[]{:S(2)}, u32[]{:S(2)}) collective-permute-start(bf16[1024,1024]{1,0:T(8,128)(2,1)S(1)} %get-tuple-element.533), channel_id=1, source_target_pairs={{0,16},{1,17},{2,18},{3,19},{4,20},{5,21},{6,22},{7,23},{8,9},{9,8... | collective-permute-start | bytes 6291464 | tf_op jit(solution)/shard_map/ppermute | solution.py:779
  240.7 51.0 %collective-permute-start.33 = (bf16[1024,1024]{1,0:T(8,128)(2,1)}, bf16[1024,1024]{1,0:T(8,128)(2,1)}, u32[]{:S(2)}, u32[]{:S(2)}) collective-permute-start(bf16[1024,1024]{1,0:T(8,128)(2,1)} %get-tuple-element.569), channel_id=1, source_target_pairs={{0,16},{1,17},{2,18},{3,19},{4,20},{5,21},{6,22},{7,23},{8,9},{9,8... | collective-permute-start | bytes 6291464 | tf_op jit(solution)/shard_map/ppermute | solution.py:779
  264.8 12.2 %collective-permute-start.31 = (bf16[2,256,1024]{2,1,0:T(8,128)(2,1)}, bf16[2,256,1024]{2,1,0:T(8,128)(2,1)}, u32[]{:S(2)}, u32[]{:S(2)}) collective-permute-start(bf16[2,256,1024]{2,1,0:T(8,128)(2,1)} %get-tuple-element.577.g_ref.refs_8_), channel_id=1, source_target_pairs={{0,8},{1,9},{2,10},{3,11},{4,12},{5,13},{6,14},{7,15},{8,0},{9,1},... | collective-permute-start | bytes 3145736 | tf_op jit(solution)/shard_map/ppermute | solution.py:779
  265.2 21.3 %collective-permute-start.32 = (bf16[2,256,1024]{2,1,0:T(8,128)(2,1)S(1)}, bf16[2,256,1024]{2,1,0:T(8,128)(2,1)S(1)}, u32[]{:S(2)}, u32[]{:S(2)}) collective-permute-start(bf16[2,256,1024]{2,1,0:T(8,128)(2,1)S(1)} %copy-done.8), channel_id=1, source_target_pairs={{0,8},{1,9},{2,10},{3,11},{4,12},{5,13},{6,14},{7,15},{8,0},{9,1},... | collective-permute-start | bytes 3145736 | tf_op jit(solution)/shard_map/ppermute | solution.py:779
  265.4 26.4 %collective-permute-start.34 = (bf16[512,1024]{1,0:T(8,128)(2,1)}, bf16[512,1024]{1,0:T(8,128)(2,1)}, u32[]{:S(2)}, u32[]{:S(2)}) collective-permute-start(bf16[512,1024]{1,0:T(8,128)(2,1)} %shard_map.317), channel_id=1, source_target_pairs={{0,1},{1,0},{2,3},{3,2},{4,5},{5,4},{6,7},{7,6},{8,24},{9,25},{10,... | collective-permute-start | bytes 3145736 | tf_op jit(solution)/shard_map/ppermute | solution.py:779
  295.7 16.2 %collective-permute-start.35 = (bf16[4,256,1024]{2,1,0:T(8,128)(2,1)S(1)}, bf16[4,256,1024]{2,1,0:T(8,128)(2,1)S(1)}, u32[]{:S(2)}, u32[]{:S(2)}) collective-permute-start(bf16[4,256,1024]{2,1,0:T(8,128)(2,1)S(1)} %copy-done.9), channel_id=1, source_target_pairs={{0,8},{1,9},{2,10},{3,11},{4,12},{5,13},{6,14},{7,15},{8,0},{9,1},... | collective-permute-start | bytes 6291464 | tf_op jit(solution)/shard_map/ppermute | solution.py:779
  296.3 25.6 %collective-permute-start.40 = (bf16[1024,512]{1,0:T(8,128)(2,1)S(1)}, bf16[1024,512]{1,0:T(8,128)(2,1)S(1)}, u32[]{:S(2)}, u32[]{:S(2)}) collective-permute-start(bf16[1024,512]{1,0:T(8,128)(2,1)S(1)} %get-tuple-element.632), channel_id=1, source_target_pairs={{0,16},{1,17},{2,18},{3,19},{4,20},{5,21},{6,22},{7,23},{8,9},{9,8... | collective-permute-start | bytes 3145736 | tf_op jit(solution)/shard_map/ppermute | solution.py:779
  296.8 25.1 %collective-permute-start.39 = (bf16[512,1024]{1,0:T(8,128)(2,1)S(1)}, bf16[512,1024]{1,0:T(8,128)(2,1)S(1)}, u32[]{:S(2)}, u32[]{:S(2)}) collective-permute-start(bf16[512,1024]{1,0:T(8,128)(2,1)S(1)} %shard_map.321), channel_id=1, source_target_pairs={{0,1},{1,0},{2,3},{3,2},{4,5},{5,4},{6,7},{7,6},{8,24},{9,25},{10,... | collective-permute-start | bytes 3145736 | tf_op jit(solution)/shard_map/ppermute | solution.py:779
  298.3 13.7 %collective-permute-start.38 = (bf16[256,1024]{1,0:T(8,128)(2,1)S(1)}, bf16[256,1024]{1,0:T(8,128)(2,1)S(1)}, u32[]{:S(2)}, u32[]{:S(2)}) collective-permute-start(bf16[256,1024]{1,0:T(8,128)(2,1)S(1)} %get-tuple-element.607), channel_id=1, source_target_pairs={{0,2},{1,3},{2,0},{3,1},{4,6},{5,7},{6,4},{7,5},{8,10},{9,11},{10,... | collective-permute-start | bytes 1572872 | tf_op jit(solution)/shard_map/ppermute | solution.py:779
  312.1 29.0 %collective-permute-start.41 = (bf16[1024,1024]{1,0:T(8,128)(2,1)S(1)}, bf16[1024,1024]{1,0:T(8,128)(2,1)S(1)}, u32[]{:S(2)}, u32[]{:S(2)}) collective-permute-start(bf16[1024,1024]{1,0:T(8,128)(2,1)S(1)} %shard_map.323), channel_id=1, source_target_pairs={{0,8},{1,9},{2,10},{3,11},{4,12},{5,13},{6,14},{7,15},{8,0},{9,1},... | collective-permute-start | bytes 6291464 | tf_op jit(solution)/shard_map/ppermute | solution.py:779
  324.1 34.9 %collective-permute-start.48 = (bf16[1024,1024]{1,0:T(8,128)(2,1)S(1)}, bf16[1024,1024]{1,0:T(8,128)(2,1)S(1)}, u32[]{:S(2)}, u32[]{:S(2)}) collective-permute-start(bf16[1024,1024]{1,0:T(8,128)(2,1)S(1)} %get-tuple-element.711), channel_id=1, source_target_pairs={{0,16},{1,17},{2,18},{3,19},{4,20},{5,21},{6,22},{7,23},{8,9},{9,8... | collective-permute-start | bytes 6291464 | tf_op jit(solution)/shard_map/ppermute | solution.py:779
  324.5 16.6 %collective-permute-start.43 = (bf16[512,512]{1,0:T(8,128)(2,1)S(1)}, bf16[512,512]{1,0:T(8,128)(2,1)S(1)}, u32[]{:S(2)}, u32[]{:S(2)}) collective-permute-start(bf16[512,512]{1,0:T(8,128)(2,1)S(1)} %shard_map.327), channel_id=1, source_target_pairs={{0,1},{1,0},{2,3},{3,2},{4,5},{5,4},{6,7},{7,6},{8,24},{9,25},{10,... | collective-permute-start | bytes 1572872 | tf_op jit(solution)/shard_map/ppermute | solution.py:779
  327.5 29.7 %collective-permute-start.46 = (bf16[256,1024]{1,0:T(8,128)(2,1)S(1)}, bf16[256,1024]{1,0:T(8,128)(2,1)S(1)}, u32[]{:S(2)}, u32[]{:S(2)}) collective-permute-start(bf16[256,1024]{1,0:T(8,128)(2,1)S(1)} %get-tuple-element.691), channel_id=1, source_target_pairs={{0,2},{1,3},{2,0},{3,1},{4,6},{5,7},{6,4},{7,5},{8,10},{9,11},{10,... | collective-permute-start | bytes 1572872 | tf_op jit(solution)/shard_map/ppermute | solution.py:779
  332.0 13.8 %collective-permute-start.44 = (bf16[128,1024]{1,0:T(8,128)(2,1)S(1)}, bf16[128,1024]{1,0:T(8,128)(2,1)S(1)}, u32[]{:S(2)}, u32[]{:S(2)}) collective-permute-start(bf16[128,1024]{1,0:T(8,128)(2,1)S(1)} %get-tuple-element.673), channel_id=1, source_target_pairs={{0,4},{1,5},{2,6},{3,7},{4,0},{5,1},{6,2},{7,3},{8,12},{9,13},{10,... | collective-permute-start | bytes 786440 | tf_op jit(solution)/shard_map/ppermute | solution.py:779
  345.8 15.6 %collective-permute-start.47 = (bf16[128,1024]{1,0:T(8,128)(2,1)S(1)}, bf16[128,1024]{1,0:T(8,128)(2,1)S(1)}, u32[]{:S(2)}, u32[]{:S(2)}) collective-permute-start(bf16[128,1024]{1,0:T(8,128)(2,1)S(1)} %shard_map.331.refs_0_), channel_id=1, source_target_pairs={{0,16},{1,17},{2,18},{3,19},{4,20},{5,21},{6,22},{7,23},{8,24},{9,... | collective-permute-start | bytes 786440 | tf_op jit(solution)/shard_map/ppermute | solution.py:779
  347.1 14.4 %collective-permute-start.49 = (bf16[256,512]{1,0:T(8,128)(2,1)S(1)}, bf16[256,512]{1,0:T(8,128)(2,1)S(1)}, u32[]{:S(2)}, u32[]{:S(2)}) collective-permute-start(bf16[256,512]{1,0:T(8,128)(2,1)S(1)} %get-tuple-element.715), channel_id=1, source_target_pairs={{0,2},{1,3},{2,0},{3,1},{4,6},{5,7},{6,4},{7,5},{8,10},{9,11},{10,... | collective-permute-start | bytes 786440 | tf_op jit(solution)/shard_map/ppermute | solution.py:779
  357.7 34.2 %collective-permute-start.54 = (bf16[1024,512]{1,0:T(8,128)(2,1)S(1)}, bf16[1024,512]{1,0:T(8,128)(2,1)S(1)}, u32[]{:S(2)}, u32[]{:S(2)}) collective-permute-start(bf16[1024,512]{1,0:T(8,128)(2,1)S(1)} %get-tuple-element.743), channel_id=1, source_target_pairs={{0,16},{1,17},{2,18},{3,19},{4,20},{5,21},{6,22},{7,23},{8,9},{9,8... | collective-permute-start | bytes 3145736 | tf_op jit(solution)/shard_map/ppermute | solution.py:779
  362.4 29.5 %collective-permute-start.53 = (bf16[512,1024]{1,0:T(8,128)(2,1)S(1)}, bf16[512,1024]{1,0:T(8,128)(2,1)S(1)}, u32[]{:S(2)}, u32[]{:S(2)}) collective-permute-start(bf16[512,1024]{1,0:T(8,128)(2,1)S(1)} %shard_map.335), channel_id=1, source_target_pairs={{0,1},{1,0},{2,3},{3,2},{4,5},{5,4},{6,7},{7,6},{8,24},{9,25},{10,... | collective-permute-start | bytes 3145736 | tf_op jit(solution)/shard_map/ppermute | solution.py:779
  363.3 23.0 %collective-permute-start.52 = (bf16[256,1024]{1,0:T(8,128)(2,1)S(1)}, bf16[256,1024]{1,0:T(8,128)(2,1)S(1)}, u32[]{:S(2)}, u32[]{:S(2)}) collective-permute-start(bf16[256,1024]{1,0:T(8,128)(2,1)S(1)} %shard_map.334.here_ref), channel_id=1, source_target_pairs={{0,8},{1,9},{2,10},{3,11},{4,12},{5,13},{6,14},{7,15},{8,0},{9,1},... | collective-permute-start | bytes 1572872 | tf_op jit(solution)/shard_map/ppermute | solution.py:779
  363.3 18.4 %collective-permute-start.51 = (bf16[128,1024]{1,0:T(8,128)(2,1)S(1)}, bf16[128,1024]{1,0:T(8,128)(2,1)S(1)}, u32[]{:S(2)}, u32[]{:S(2)}) collective-permute-start(bf16[128,1024]{1,0:T(8,128)(2,1)S(1)} %get-tuple-element.733), channel_id=1, source_target_pairs={{0,4},{1,5},{2,6},{3,7},{4,0},{5,1},{6,2},{7,3},{8,12},{9,13},{10,... | collective-permute-start | bytes 786440 | tf_op jit(solution)/shard_map/ppermute | solution.py:779
  366.3 15.4 %collective-permute-start.50 = (f32[22,1024]{1,0:T(8,128)S(1)}, f32[22,1024]{1,0:T(8,128)S(1)}, u32[]{:S(2)}, u32[]{:S(2)}) collective-permute-start(f32[22,1024]{1,0:T(8,128)S(1)} %add.173), channel_id=1, source_target_pairs={{0,1},{1,0},{2,3},{3,2},{4,5},{5,4},{6,7},{7,6},{8,24},{9,25},{10,... | collective-permute-start | bytes 270344 | tf_op jit(solution)/shard_map/ppermute | solution.py:779
  381.8 10.9 %collective-permute-start.55 = (bf16[128,1024]{1,0:T(8,128)(2,1)S(1)}, bf16[128,1024]{1,0:T(8,128)(2,1)S(1)}, u32[]{:S(2)}, u32[]{:S(2)}) collective-permute-start(bf16[128,1024]{1,0:T(8,128)(2,1)S(1)} %shard_map.338.refs_0_), channel_id=1, source_target_pairs={{0,16},{1,17},{2,18},{3,19},{4,20},{5,21},{6,22},{7,23},{8,24},{9,... | collective-permute-start | bytes 786440 | tf_op jit(solution)/shard_map/ppermute | solution.py:779
  383.2 9.5 %collective-permute-start.56 = (bf16[128,512]{1,0:T(8,128)(2,1)S(1)}, bf16[128,512]{1,0:T(8,128)(2,1)S(1)}, u32[]{:S(2)}, u32[]{:S(2)}) collective-permute-start(bf16[128,512]{1,0:T(8,128)(2,1)S(1)} %get-tuple-element.758), channel_id=1, source_target_pairs={{0,4},{1,5},{2,6},{3,7},{4,0},{5,1},{6,2},{7,3},{8,12},{9,13},{10,... | collective-permute-start | bytes 393224 | tf_op jit(solution)/shard_map/ppermute | solution.py:779
  394.3 10.5 %collective-permute-start.59 = (bf16[512,512]{1,0:T(8,128)(2,1)S(1)}, bf16[512,512]{1,0:T(8,128)(2,1)S(1)}, u32[]{:S(2)}, u32[]{:S(2)}) collective-permute-start(bf16[512,512]{1,0:T(8,128)(2,1)S(1)} %shard_map.341), channel_id=1, source_target_pairs={{0,1},{1,0},{2,3},{3,2},{4,5},{5,4},{6,7},{7,6},{8,24},{9,25},{10,... | collective-permute-start | bytes 1572872 | tf_op jit(solution)/shard_map/ppermute | solution.py:779
  395.6 13.5 %collective-permute-start.61 = (bf16[256,1024]{1,0:T(8,128)(2,1)S(1)}, bf16[256,1024]{1,0:T(8,128)(2,1)S(1)}, u32[]{:S(2)}, u32[]{:S(2)}) collective-permute-start(bf16[256,1024]{1,0:T(8,128)(2,1)S(1)} %get-tuple-element.786), channel_id=1, source_target_pairs={{0,2},{1,3},{2,0},{3,1},{4,6},{5,7},{6,4},{7,5},{8,10},{9,11},{10,... | collective-permute-start | bytes 1572872 | tf_op jit(solution)/shard_map/ppermute | solution.py:779
  407.4 12.5 %collective-permute-start.63 = (bf16[256,512]{1,0:T(8,128)(2,1)S(1)}, bf16[256,512]{1,0:T(8,128)(2,1)S(1)}, u32[]{:S(2)}, u32[]{:S(2)}) collective-permute-start(bf16[256,512]{1,0:T(8,128)(2,1)S(1)} %get-tuple-element.796), channel_id=1, source_target_pairs={{0,2},{1,3},{2,0},{3,1},{4,6},{5,7},{6,4},{7,5},{8,10},{9,11},{10,... | collective-permute-start | bytes 786440 | tf_op jit(solution)/shard_map/ppermute | solution.py:779
  409.2 16.9 %collective-permute-start.64 = (bf16[128,1024]{1,0:T(8,128)(2,1)S(1)}, bf16[128,1024]{1,0:T(8,128)(2,1)S(1)}, u32[]{:S(2)}, u32[]{:S(2)}) collective-permute-start(bf16[128,1024]{1,0:T(8,128)(2,1)S(1)} %get-tuple-element.804), channel_id=1, source_target_pairs={{0,4},{1,5},{2,6},{3,7},{4,0},{5,1},{6,2},{7,3},{8,12},{9,13},{10,... | collective-permute-start | bytes 786440 | tf_op jit(solution)/shard_map/ppermute | solution.py:779
  (86 other events, 662.5 us)
